TPU v7x, 32 devices: a whole 2x2x4 slice. The times are simulated.
32 devices in a mesh: seq: 8 (over z, y), head: 4 (over x, core).
Axes of the slice: x: 2, y: 2, z: 4, core: 2. Of those that a mesh axis runs over, the one named last changes fastest.
Arguments:
- tokens: float32 [2, 4096, 2048], P(None, 'seq', 'head'), may hold values from -6 to 6
- norm_gain: bfloat16 [2048], P('seq'), may hold values from 0.5 to 1.5
- w_z: bfloat16 [2048, 4096], P('seq', 'head'), may hold values from -0.125 to 0.125
- w_x: bfloat16 [2048, 4096], P('seq', 'head'), may hold values from -0.125 to 0.125
- w_bc: bfloat16 [2048, 256], P('seq'), may hold values from -0.125 to 0.125
- w_dt: bfloat16 [2048, 64], P('seq', 'head'), may hold values from -0.125 to 0.125
- conv_x: bfloat16 [4, 4096], P(None, 'head'), may hold values from -3 to 3
- conv_bc: bfloat16 [4, 256], replicated, may hold values from -3 to 3
- dt_bias: float32 [64], P('head'), may hold values from -1 to 1
- decay_rate: float32 [64], P('head'), may hold values from 0.00024414062 to 0.05
- skip_gain: float32 [64], P('head'), may hold values from 0.5 to 1.5
- gate_gain: bfloat16 [4096], P('head'), may hold values from 0.5 to 1.5
- w_out: bfloat16 [4096, 2048], P('head', 'seq'), may hold values from -0.09375 to 0.09375
- grad_out: float32 [2, 4096, 2048], P(None, 'seq', 'head'), may hold values from -6 to 6
Outputs:
- mixed_out: float32 [2, 4096, 2048], P(None, 'seq', 'head')
- grad_tokens: float32 [2, 4096, 2048], P(None, 'seq', 'head')
- grad_norm_gain: float32 [2048], P('seq')
- grad_w_z: float32 [2048, 4096], P('seq', 'head')
- grad_w_x: float32 [2048, 4096], P('seq', 'head')
- grad_w_bc: float32 [2048, 256], P('seq')
- grad_w_dt: float32 [2048, 64], P('seq', 'head')
- grad_conv_x: float32 [4, 4096], P(None, 'head')
- grad_conv_bc: float32 [4, 256], replicated
- grad_dt_bias: float32 [64], P('head')
- grad_decay_rate: float32 [64], P('head')
- grad_skip_gain: float32 [64], P('head')
- grad_gate_gain: float32 [4096], P('head')
- grad_w_out: float32 [4096, 2048], P('head', 'seq')
All inputs are finite; a program needn't handle non-finite values.
Results may differ from a plain program's by a relative error of at most 0.012.
The roundings to bfloat16 on the way count: a program that leaves them out, or rounds other values in their place, can miss the bound.
Values may be sent and summed in bfloat16 or wider, within the bound.
No kernel may reach another device: no remote copies, remote signals or barrier semaphores. Data moves between devices by JAX's collectives and lax.ppermute only.
A program may use at most 256 MiB of HBM per device.

v0:
```python
import jax
import jax.numpy as jnp
from jax import lax
from jax.sharding import PartitionSpec as P

D = 2048
P_SIZE = 64
N = 128
KERNEL = 4
SPAN = 256
MB = 2
SEQS_MB = 1
DI = 4096


EPS = 1e-05
HIGHEST = lax.Precision.HIGHEST


def passed_along(block, axis, distance):
    devices = range(lax.axis_size(axis))
    route = [(i - distance, i) for i in devices if i - distance in devices]
    return lax.ppermute(block, axis, route)


def carried_in(array, axis, combine, identity, reverse):
    devices, here = (lax.axis_size(axis), lax.axis_index(axis))
    everything = jax.tree.map(lambda part: lax.all_gather(part, axis), array)
    start = jax.tree.map(
        lambda part, zero: jnp.broadcast_to(jnp.asarray(zero, part.dtype), part.shape),
        array,
        identity,
    )

    def hop(k, before):
        at = devices - 1 - k if reverse else k
        reached = at > here if reverse else at < here
        new = combine(before, jax.tree.map(lambda part: part[at], everything))
        return jax.tree.map(lambda a, b: jnp.where(reached, a, b), new, before)

    return lax.fori_loop(0, devices, hop, start)


def silu_slope(value):
    logistic = jax.nn.sigmoid(value)
    return logistic * (1.0 + value * (1.0 - logistic))


def chain_state(earlier, later):
    return (earlier[0] * later[0], later[0][..., None, None] * earlier[1] + later[1])


def contract_rows(left, right):
    return lax.dot_general(
        left, right, (((0,), (0,)), ((), ())), preferred_element_type=jnp.float32
    )


def contract_cols(left, right):
    return lax.dot_general(
        left, right, (((1,), (1,)), ((), ())), preferred_element_type=jnp.float32
    )


def local_scan(inner, bmat, cmat, dt_raw, dt_bias, decay_rate, skip_gain):
    batch, length, heads, width = inner.shape
    block = min(SPAN, length)
    count = length // block
    steps = jax.nn.softplus(dt_raw + dt_bias)
    rates = steps * -decay_rate

    def split(array):
        return jnp.moveaxis(array.reshape((batch, count, block) + array.shape[2:]), 1, 0)

    def merge(array):
        return jnp.moveaxis(array, 0, 1).reshape((batch, length) + array.shape[3:])

    positions = lax.broadcasted_iota(jnp.int32, (block, block), 0)
    causal = positions >= lax.broadcasted_iota(jnp.int32, (block, block), 1)

    def one_block(carry, pieces):
        state, offset = carry
        part_inner, part_b, part_c, part_steps, part_rates = pieces
        within = jnp.cumsum(part_rates, axis=1)
        scores = jnp.einsum("btn,bsn->bts", part_c, part_b, precision=HIGHEST)
        gaps = within[:, :, None, :] - within[:, None, :, :]
        weights = jnp.exp(jnp.where(causal[None, :, :, None], gaps, -jnp.inf)) * scores[..., None]
        driven = part_inner * part_steps[..., None]
        inside = jnp.einsum("btsh,bshp->bthp", weights, driven, precision=HIGHEST)
        carried = jnp.exp(within)[..., None] * jnp.einsum(
            "btn,bhpn->bthp", part_c, state, precision=HIGHEST
        )
        tail = jnp.exp(within[:, -1:, :] - within)
        new_state = jnp.exp(within[:, -1])[:, :, None, None] * state + jnp.einsum(
            "bsh,bshp,bsn->bhpn", tail, driven, part_b, precision=HIGHEST
        )
        return (
            (new_state, offset + within[:, -1]),
            (inside + carried, offset[:, None, :] + within),
        )

    start = (
        jnp.zeros((batch, heads, width, bmat.shape[-1]), jnp.float32),
        jnp.zeros((batch, heads), jnp.float32),
    )
    final_pair, results = lax.scan(
        jax.checkpoint(one_block),
        start,
        (split(inner), split(bmat), split(cmat), split(steps), split(rates)),
    )
    return (merge(results[0]) + skip_gain[:, None] * inner, final_pair[0], merge(results[1]))


def fetch(norm_gain, w_z, w_x, w_bc, w_dt, w_out):
    return (
        lax.all_gather(norm_gain, "seq", axis=0, tiled=True),
        lax.all_gather(w_z, "seq", axis=0, tiled=True),
        lax.all_gather(w_x, "seq", axis=0, tiled=True),
        lax.all_gather(w_bc, "seq", axis=0, tiled=True),
        lax.all_gather(w_dt, "seq", axis=0, tiled=True),
        lax.all_gather(w_out, "seq", axis=1, tiled=True),
    )


def body(
    tokens,
    norm_gain,
    w_z,
    w_x,
    w_bc,
    w_dt,
    conv_x,
    conv_bc,
    dt_bias,
    decay_rate,
    skip_gain,
    gate_gain,
    w_out,
    grad_out,
):
    length = tokens.shape[1]
    own_width = tokens.shape[2]
    inner_width = w_z.shape[1]
    heads = dt_bias.shape[0]
    batch = SEQS_MB
    rows = batch * length
    margin = KERNEL - 1
    channels = inner_width + 2 * N
    conv_w = jnp.concatenate([conv_x, conv_bc], axis=1).astype(jnp.float32)
    gate_f = gate_gain.astype(jnp.float32)
    acc_gain = jnp.zeros((D,), jnp.float32)
    acc_z = jnp.zeros((D, inner_width), jnp.float32)
    acc_x = jnp.zeros((D, inner_width), jnp.float32)
    acc_bc = jnp.zeros((D, 2 * N), jnp.float32)
    acc_dt = jnp.zeros((D, heads), jnp.float32)
    acc_out = jnp.zeros((inner_width, D), jnp.float32)
    acc_conv = jnp.zeros((KERNEL, channels), jnp.float32)
    acc_gate = jnp.zeros((inner_width,), jnp.float32)
    acc_bias = jnp.zeros((heads,), jnp.float32)
    acc_rate = jnp.zeros((heads,), jnp.float32)
    acc_skip = jnp.zeros((heads,), jnp.float32)
    results = []
    grads_in = []
    for index in range(MB):
        current = fetch(norm_gain, w_z, w_x, w_bc, w_dt, w_out)
        gain_full, wz_full, wx_full, wbc_full, wdt_full, wout_full = current
        gain_f = gain_full.astype(jnp.float32)
        slab = tokens[index * batch : (index + 1) * batch]
        full = lax.all_gather(slab, "head", axis=2, tiled=True)
        scale = lax.rsqrt(jnp.mean(full * full, axis=-1) + EPS)
        normed = (full * scale[..., None] * gain_f).astype(jnp.bfloat16)
        flat = normed.reshape(rows, D)
        z_vals = jnp.dot(flat, wz_full, preferred_element_type=jnp.float32).reshape(
            batch, length, inner_width
        )
        dt_raw = jnp.dot(flat, wdt_full, preferred_element_type=jnp.float32).reshape(
            batch, length, heads
        )
        x_part = jnp.dot(flat, wx_full, preferred_element_type=jnp.float32)
        bc_part = jnp.dot(flat, wbc_full, preferred_element_type=jnp.float32)
        conv_in = (
            jnp.concatenate([x_part, bc_part], axis=1)
            .astype(jnp.bfloat16)
            .reshape(batch, length, channels)
        )
        before = passed_along(conv_in[:, length - margin :], "seq", 1)
        extended = jnp.concatenate([before, conv_in], axis=1).astype(jnp.float32)
        conv_out = conv_w[0] * extended[:, 0:length]
        for tap in range(1, KERNEL):
            conv_out = conv_out + conv_w[tap] * extended[:, tap : tap + length]
        act = jax.nn.silu(conv_out)
        inner = act[..., :inner_width].reshape(batch, length, heads, P_SIZE)
        bmat = act[..., inner_width : inner_width + N]
        cmat = act[..., inner_width + N :]
        local_vals, local_back = jax.vjp(
            local_scan, inner, bmat, cmat, dt_raw, dt_bias, decay_rate, skip_gain
        )
        y_local, s_local, cumulative = local_vals
        decay_total = jnp.exp(cumulative[:, -1])
        identity = (jnp.ones((batch, heads), jnp.float32), jnp.zeros(s_local.shape, jnp.float32))
        s_in = carried_in((decay_total, s_local), "seq", chain_state, identity, False)[1]
        growth = jnp.exp(cumulative)
        echo = growth[..., None] * jnp.einsum("btn,bhpn->bthp", cmat, s_in, precision=HIGHEST)
        ssd_out = (y_local + echo).reshape(batch, length, inner_width)
        gated = ssd_out * jax.nn.silu(z_vals)
        sumsq = lax.psum(jnp.sum(gated * gated, axis=-1), "head")
        gate_scale = lax.rsqrt(sumsq / DI + EPS)
        mixed = (gated * gate_scale[..., None] * gate_f).astype(jnp.bfloat16)
        mixed_flat = mixed.reshape(rows, inner_width)
        out_part = jnp.dot(mixed_flat, wout_full, preferred_element_type=jnp.float32)
        out_own = lax.psum_scatter(
            out_part.astype(jnp.bfloat16), "head", scatter_dimension=1, tiled=True
        ).astype(jnp.float32)
        results.append(slab + out_own.reshape(batch, length, own_width))
        cot_rows = grad_out[index * batch : (index + 1) * batch]
        cot_full = lax.all_gather(cot_rows.astype(jnp.bfloat16), "head", axis=2, tiled=True)
        cot_flat = cot_full.reshape(rows, D)
        acc_out = acc_out + contract_rows(mixed_flat, cot_flat)
        d_mixed = contract_cols(cot_flat, wout_full).reshape(batch, length, inner_width)
        acc_gate = acc_gate + jnp.sum(d_mixed * gated * gate_scale[..., None], axis=(0, 1))
        scaled_grad = d_mixed * gate_f
        inner_prod = lax.psum(jnp.sum(scaled_grad * gated, axis=-1), "head")
        d_gated = (
            gate_scale[..., None] * scaled_grad
            - gated * (gate_scale**3 * inner_prod / DI)[..., None]
        )
        d_ssd = (d_gated * jax.nn.silu(z_vals)).reshape(batch, length, heads, P_SIZE)
        d_z = (
            (d_gated * ssd_out * silu_slope(z_vals)).astype(jnp.bfloat16).reshape(rows, inner_width)
        )
        d_state_local = jnp.einsum("bth,bthp,btn->bhpn", growth, d_ssd, cmat, precision=HIGHEST)
        d_cmat_echo = jnp.einsum("bth,bthp,bhpn->btn", growth, d_ssd, s_in, precision=HIGHEST)
        d_cumulative = jnp.sum(d_ssd * echo, axis=-1)
        later = carried_in((decay_total, d_state_local), "seq", chain_state, identity, True)[1]
        tail_grad = decay_total * jnp.sum(later * s_in, axis=(2, 3))
        d_cumulative = d_cumulative.at[:, -1].add(tail_grad)
        d_inner, d_bmat, d_cmat, d_dtraw, d_bias, d_rate, d_skip = local_back(
            (d_ssd, later, d_cumulative)
        )
        acc_bias = acc_bias + d_bias
        acc_rate = acc_rate + d_rate
        acc_skip = acc_skip + d_skip
        d_bmat, d_cmat = lax.psum((d_bmat, d_cmat + d_cmat_echo), "head")
        d_act = jnp.concatenate(
            [d_inner.reshape(batch, length, inner_width), d_bmat, d_cmat], axis=-1
        )
        d_conv = (d_act * silu_slope(conv_out)).astype(jnp.bfloat16)
        after = passed_along(d_conv[:, :margin], "seq", -1)
        conv_grad_f = d_conv.astype(jnp.float32)
        ext_grad = jnp.concatenate([d_conv, after], axis=1).astype(jnp.float32)
        tap_grads = [
            jnp.sum(conv_grad_f * extended[:, tap : tap + length], axis=(0, 1))
            for tap in range(KERNEL)
        ]
        acc_conv = acc_conv + jnp.stack(tap_grads, axis=0)
        d_conv_in = conv_w[0] * ext_grad[:, margin : margin + length]
        for tap in range(1, KERNEL):
            d_conv_in = d_conv_in + conv_w[tap] * ext_grad[:, margin - tap : margin - tap + length]
        d_conv_in = d_conv_in.astype(jnp.bfloat16).reshape(rows, channels)
        d_x = d_conv_in[:, :inner_width]
        d_bc = d_conv_in[:, inner_width:]
        d_dt = d_dtraw.astype(jnp.bfloat16).reshape(rows, heads)
        acc_z = acc_z + contract_rows(flat, d_z)
        acc_x = acc_x + contract_rows(flat, d_x)
        acc_bc = acc_bc + contract_rows(flat, d_bc)
        acc_dt = acc_dt + contract_rows(flat, d_dt)
        own_terms = (
            contract_cols(d_z, wz_full)
            + contract_cols(d_x, wx_full)
            + contract_cols(d_dt, wdt_full)
        )
        d_normed = lax.psum(own_terms.astype(jnp.bfloat16), "head").astype(
            jnp.float32
        ) + contract_cols(d_bc, wbc_full)
        d_normed = d_normed.reshape(batch, length, D)
        acc_gain = acc_gain + jnp.sum(d_normed * full * scale[..., None], axis=(0, 1))
        gain_grad = d_normed * gain_f
        d_full = (
            scale[..., None] * gain_grad
            - full * (scale**3 * jnp.mean(gain_grad * full, axis=-1))[..., None]
        )
        own_grad = lax.dynamic_slice_in_dim(
            d_full, lax.axis_index("head") * own_width, own_width, 2
        )
        grads_in.append(cot_rows + own_grad)
    gain_rows, z_rows, x_rows, bc_rows, dt_rows, out_cols = (
        lax.psum_scatter(acc_gain, "seq", scatter_dimension=0, tiled=True),
        lax.psum_scatter(acc_z, "seq", scatter_dimension=0, tiled=True),
        lax.psum_scatter(acc_x, "seq", scatter_dimension=0, tiled=True),
        lax.psum_scatter(acc_bc, "seq", scatter_dimension=0, tiled=True),
        lax.psum_scatter(acc_dt, "seq", scatter_dimension=0, tiled=True),
        lax.psum_scatter(acc_out, "seq", scatter_dimension=1, tiled=True),
    )
    conv_sum, gate_sum, bias_sum, rate_sum, skip_sum = lax.psum(
        (acc_conv, acc_gate, acc_bias, acc_rate, acc_skip), "seq"
    )
    return (
        jnp.concatenate(results, axis=0),
        jnp.concatenate(grads_in, axis=0),
        gain_rows,
        z_rows,
        x_rows,
        bc_rows,
        dt_rows,
        conv_sum[:, :inner_width],
        conv_sum[:, inner_width:],
        bias_sum,
        rate_sum,
        skip_sum,
        gate_sum,
        out_cols,
    )


def solution(mesh):
    in_specs = (
        P(None, "seq", "head"),
        P("seq"),
        P("seq", "head"),
        P("seq", "head"),
        P("seq", None),
        P("seq", "head"),
        P(None, "head"),
        P(),
        P("head"),
        P("head"),
        P("head"),
        P("head"),
        P("head", "seq"),
        P(None, "seq", "head"),
    )
    out_specs = (
        P(None, "seq", "head"),
        P(None, "seq", "head"),
        P("seq"),
        P("seq", "head"),
        P("seq", "head"),
        P("seq", None),
        P("seq", "head"),
        P(None, "head"),
        P(),
        P("head"),
        P("head"),
        P("head"),
        P("head"),
        P("head", "seq"),
    )
    return jax.shard_map(body, mesh=mesh, in_specs=in_specs, out_specs=out_specs, check_vma=False)
```

profile of v0, /device:TPU:0, one launch (start us, length us, event | category | flops | bytes accessed | tf_op | source)
XLA Modules:
  0.0 1766.6 jit_solution(1687720845713073908)
XLA Ops:
  14.3 22.3 %all-gather.4 = bf16[8,1,256]{2,1,0:T(2,128)(2,1)S(1)} all-gather(bf16[1,1,256]{2,1,0:T(2,128)(2,1)S(1)} %reshape.2203), channel_id=1, replica_groups=mesh['seq'=8,'head'=4] {'seq'}, dimensions={0}, use_global_device_ids=true | all-gather | bytes 4608 | tf_op jit(solution)/shard_map/all_gather | solution.py:116
  36.6 30.5 %all_gather.74 = bf16[2048,16]{0,1:T(8,128)(2,1)S(1)} all-gather(bf16[256,16]{0,1:T(8,128)(2,1)S(1)} %copy-done.128), channel_id=1, replica_groups=mesh['seq'=8,'head'=4] {'seq'}, dimensions={0}, use_global_device_ids=true | all-gather | bytes 73728 | tf_op jit(solution)/shard_map/all_gather | solution.py:120
  69.9 14.4 all-gather.28.cloned.1.call-done
  94.5 32.2 %all-gather.22.cloned.1.call-done = bf16[2048,256]{1,0:T(8,128)(2,1)} async-done(((bf16[256,256]{1,0:T(8,128)(2,1)}), bf16[2048,256]{1,0:T(8,128)(2,1)}) %all-gather.22.cloned.1.call-update) | async-done | bytes 1048592 | tf_op jit(solution)/shard_map/all_gather | solution.py:119
  129.6 71.3 %all-gather.20.cloned.1.call-done = bf16[2048,1024]{1,0:T(8,128)(2,1)} async-done(((bf16[256,1024]{1,0:T(8,128)(2,1)}), bf16[2048,1024]{1,0:T(8,128)(2,1)}) %all-gather.20.cloned.1.call-update) | async-done | bytes 4194320 | tf_op jit(solution)/shard_map/all_gather | solution.py:118
  238.3 73.1 %while.158 = (s32[]{:T(128)}, f32[1,16,64,128]{3,2,1,0:T(8,128)S(1)}, f32[1,16]{1,0:T(1,128)S(1)}, f32[2,1,256,16,64]{2,0,4,3,1:T(2,128)}, f32[2,1,256,16]{2,0,3...) while((s32[]{:T(128)}, ...), condition=%wide.region_14.16_spmd.clone, body=%wide.region_11.15_spmd.clone.sunk | while | flops 1716920448 | bytes 22090848 | solution.py:106
  252.7 22.0 %dynamic_update_slice.168 = f32[2,1,256,16,64]{2,0,4,3,1:T(2,128)} dynamic-update-slice(f32[2,1,256,16,64]{2,0,4,3,1:T(2,128)} %get-tuple-element.3266, f32[1,1,256,16,64]{2,0,4,3,1:T(1,128)} %copy.845, s32[]{:T(128)S(6)} %copy.916, s32[]{:T(128)} %constant.405.clone.1..sunk.2, s32[]{:T(128)} %constant.405.clone.1..sunk.2, s32[]{:T(128)} %constant.405.clone.1..sunk.2, s32[]{:T(128)} %constant.405.clone.1..sunk.2) | dynamic-update-slice | bytes 2097156 | tf_op jit(solution)/shard_map/jvp()/while/body/jit(dynamic_update_index_in_dim)/dynamic_update_slice | solution.py:106
  289.3 22.0 %dynamic_update_slice.168 = f32[2,1,256,16,64]{2,0,4,3,1:T(2,128)} dynamic-update-slice(f32[2,1,256,16,64]{2,0,4,3,1:T(2,128)} %get-tuple-element.3266, f32[1,1,256,16,64]{2,0,4,3,1:T(1,128)} %copy.845, s32[]{:T(128)S(6)} %copy.916, s32[]{:T(128)} %constant.405.clone.1..sunk.2, s32[]{:T(128)} %constant.405.clone.1..sunk.2, s32[]{:T(128)} %constant.405.clone.1..sunk.2, s32[]{:T(128)} %constant.405.clone.1..sunk.2) | dynamic-update-slice | bytes 2097156 | tf_op jit(solution)/shard_map/jvp()/while/body/jit(dynamic_update_index_in_dim)/dynamic_update_slice | solution.py:106
  333.8 73.1 %while.156 = (s32[]{:T(128)}, f32[1,16,64,128]{3,2,1,0:T(8,128)S(1)}, f32[1,16]{1,0:T(1,128)S(1)}, f32[2,1,256,16,64]{2,0,4,3,1:T(2,128)}, f32[2,1,256,16]{2,0,3...) while((s32[]{:T(128)}, ...), condition=%wide.region_4.6_spmd.clone, body=%wide.region_1.5_spmd.clone.sunk | while | flops 1716920448 | bytes 22090848 | solution.py:106
  348.3 22.0 %dynamic_update_slice.165 = f32[2,1,256,16,64]{2,0,4,3,1:T(2,128)} dynamic-update-slice(f32[2,1,256,16,64]{2,0,4,3,1:T(2,128)} %get-tuple-element.3221, f32[1,1,256,16,64]{2,0,4,3,1:T(1,128)} %copy.839, s32[]{:T(128)S(6)} %copy.898, s32[]{:T(128)} %constant.405.clone.1..sunk, s32[]{:T(128)} %constant.405.clone.1..sunk, s32[]{:T(128)} %constant.405.clone.1..sunk, s32[]{:T(128)} %constant.405.clone.1..sunk) | dynamic-update-slice | bytes 2097156 | tf_op jit(solution)/shard_map/jvp()/while/body/jit(dynamic_update_index_in_dim)/dynamic_update_slice | solution.py:106
  384.8 22.0 %dynamic_update_slice.165 = f32[2,1,256,16,64]{2,0,4,3,1:T(2,128)} dynamic-update-slice(f32[2,1,256,16,64]{2,0,4,3,1:T(2,128)} %get-tuple-element.3221, f32[1,1,256,16,64]{2,0,4,3,1:T(1,128)} %copy.839, s32[]{:T(128)S(6)} %copy.898, s32[]{:T(128)} %constant.405.clone.1..sunk, s32[]{:T(128)} %constant.405.clone.1..sunk, s32[]{:T(128)} %constant.405.clone.1..sunk, s32[]{:T(128)} %constant.405.clone.1..sunk) | dynamic-update-slice | bytes 2097156 | tf_op jit(solution)/shard_map/jvp()/while/body/jit(dynamic_update_index_in_dim)/dynamic_update_slice | solution.py:106
  409.2 6.5 fusion.255
  421.5 18.7 %all_gather.83 = f32[8,1,16]{2,1,0:T(1,128)S(1)} all-gather(f32[1,1,16]{2,1,0:T(1,128)S(1)} %slice_exponential_fusion), channel_id=1, replica_groups=mesh['seq'=8,'head'=4] {'seq'}, dimensions={0}, use_global_device_ids=true | all-gather | bytes 576 | tf_op jit(solution)/shard_map/all_gather | solution.py:28
  444.1 16.8 all_gather.77
  460.9 9.7 while.159
  470.6 10.5 all-gather.34.cloned.1.call-done
  481.1 9.7 while.157
  493.9 8.7 add_add_fusion.1
  508.5 46.4 %all-gather.24.cloned.1.call-done = bf16[2048,1024]{1,0:T(8,128)(2,1)} async-done(((bf16[256,1024]{1,0:T(8,128)(2,1)}), bf16[2048,1024]{1,0:T(8,128)(2,1)}) %all-gather.24.cloned.1.call-update) | async-done | bytes 4194320 | tf_op jit(solution)/shard_map/all_gather | solution.py:117
  555.0 8.2 multiply_reduce_fusion.13
  567.9 6.1 all-reduce.9
  577.4 9.4 multiply_reduce_fusion.7
  586.8 6.0 all-reduce.8
  592.9 8.7 fusion.253
  635.7 48.4 %all-gather.40.cloned.1.call-done = f32[128,64,128]{2,1,0:T(8,128)} async-done(((f32[16,64,128]{2,1,0:T(8,128)}), f32[128,64,128]{2,1,0:T(8,128)}) %all-gather.40.cloned.1.call-update) | async-done | bytes 4194320 | tf_op jit(solution)/shard_map/all_gather | solution.py:28
  684.1 9.9 while.162
  700.2 124.8 %while.163 = (s32[]{:T(128)}, f32[1,16,64,128]{3,2,1,0:T(8,128)S(1)}, f32[1,16]{1,0:T(1,128)}, f32[2,1,256,16,64]{2,4,3,1,0:T(8,128)}, f32[2,1,256,128]{3,2,0,1:...) while((s32[]{:T(128)}, ...), condition=%wide.region_63.65_spmd.clone, body=%wide.region_50.64_spmd.clone.sunk | while | flops 3944067072 | bytes 44585628 | solution.py:106
  715.2 7.3 fusion.555
  777.6 7.3 fusion.555
  830.9 14.8 while.160
  851.8 116.9 %while.161 = (s32[]{:T(128)}, f32[1,16,64,128]{3,2,1,0:T(8,128)S(1)}, f32[1,16]{1,0:T(1,128)}, f32[2,1,256,16,64]{2,4,3,1,0:T(8,128)}, f32[2,1,256,128]{3,2,0,1:...) while((s32[]{:T(128)}, ...), condition=%wide.region_39.41_spmd.clone, body=%wide.region_26.40_spmd.clone.sunk | while | flops 3944067072 | bytes 44585628 | solution.py:106
  864.6 7.3 fusion.532
  923.2 7.3 fusion.532
  968.8 6.0 fusion.288
  982.4 6.0 convolution_convert_fusion
  988.4 7.2 multiply_convert_fusion.3
  995.9 6.7 fusion.367
  1025.0 7.0 add_bitcast_fusion.7
  1032.0 10.5 fusion.230
  1086.5 5.9 convolution_add_fusion.2
  1108.4 57.7 %all-reduce.17.cloned.1.call-done = (bf16[512,2048]{1,0:T(8,128)(2,1)}, bf16[512,2048]{1,0:T(8,128)(2,1)}) async-done(((bf16[512,2048]{1,0:T(8,128)(2,1)}, bf16[512,2048]{1,0:T(8,128)(2,1)}), (bf16[512,2048]{1,0:T(8,128)(2,1)}, bf16[512,2048]{1,0:T(8,128)(2,1)})) %all-reduce.17.cloned.1.call-update) | async-done | bytes 4194320 | tf_op jit(solution)/shard_map/psum | solution.py:272
  1169.6 6.2 fusion.227
  1175.8 38.2 %all-reduce.7 = (f32[2048]{0:T(1024)S(1)}, f32[4,1280]{1,0:T(4,128)S(1)}, f32[16]{0:T(128)}, f32[16]{0:T(128)}, f32[16]{0:T(128)}, /*index=5*/f32[1024]{0:T(1024)}) all-reduce(f32[2048]{0:T(1024)S(1)} %add.588, f32[4,1280]{1,0:T(4,128)S(1)} %maximum_add_fusion, f32[16]{0:T(128)S(1)} %add.594, ...), channel_id=8, replica_groups=mesh['seq'=8,'head'=4] {'seq'}, use_global_device_ids=true, to_apply=%region_70.72.clone | all-reduce | flops 8240 | bytes 65920
  1223.7 7.6 reduce-scatter.18.cloned.1.call-done
  1231.3 70.9 %reduce-scatter.16.cloned.1.call-done = f32[256,256]{1,0:T(8,128)} async-done(((f32[2048,256]{1,0:T(8,128)}), f32[256,256]{1,0:T(8,128)}) %reduce-scatter.16.cloned.1.call-update) | async-done | bytes 262160 | tf_op jit(solution)/shard_map/reduce_scatter | solution.py:290
  1302.2 152.2 %reduce-scatter.12.cloned.1.call-done = f32[256,1024]{1,0:T(8,128)} async-done(((f32[2048,1024]{1,0:T(8,128)}), f32[256,1024]{1,0:T(8,128)}) %reduce-scatter.12.cloned.1.call-update) | async-done | bytes 1048592 | tf_op jit(solution)/shard_map/reduce_scatter | solution.py:288
  1454.4 152.9 %reduce-scatter.20.cloned.1.call-done = f32[1024,256]{1,0:T(8,128)} async-done(((f32[1024,2048]{1,0:T(8,128)}), f32[1024,256]{1,0:T(8,128)}) %reduce-scatter.20.cloned.1.call-update) | async-done | bytes 1048592 | tf_op jit(solution)/shard_map/reduce_scatter | solution.py:292
  1607.3 152.3 %reduce-scatter.14.cloned.1.call-done = f32[256,1024]{1,0:T(8,128)} async-done(((f32[2048,1024]{1,0:T(8,128)}), f32[256,1024]{1,0:T(8,128)}) %reduce-scatter.14.cloned.1.call-update) | async-done | bytes 1048592 | tf_op jit(solution)/shard_map/reduce_scatter | solution.py:289
  (980 shorter events, 576.7 us)
Async XLA Ops:
  7.2 60.1 %all-gather.18.cloned.1.call-start = ((), (), s32[]{:S(2)}) async-start(), calls=%async_computation.7 | async-start | bytes 5242880 | tf_op jit(solution)/shard_map/all_gather | solution.py:169
  10.3 74.0 %all-gather.28.cloned.1.call-start = ((), (), s32[]{:S(2)}) async-start(), calls=%async_computation.13 | async-start | bytes 5242880 | tf_op jit(solution)/shard_map/all_gather | solution.py:169
  11.1 56.1 %copy-start.129 = (bf16[4,1024]{1,0:T(4,128)(2,1)S(1)}, bf16[4,1024]{1,0:T(4,128)(2,1)}, u32[]{:S(2)}) copy-start(bf16[4,1024]{1,0:T(4,128)(2,1)} %param.41) | copy-start | bytes 24580
  11.1 56.1 %copy-start.139 = (bf16[4,256]{1,0:T(4,128)(2,1)S(1)}, bf16[4,256]{1,0:T(4,128)(2,1)}, u32[]{:S(2)}) copy-start(bf16[4,256]{1,0:T(4,128)(2,1)} %param.42) | copy-start | bytes 6148
  11.1 115.6 %all-gather.22.cloned.1.call-start = ((), (), s32[]{:S(2)}) async-start(), calls=%async_computation.9 | async-start | bytes 1179648 | tf_op jit(solution)/shard_map/all_gather | solution.py:119
  11.8 189.0 %all-gather.20.cloned.1.call-start = ((), (), s32[]{:S(2)}) async-start(), calls=%async_computation.8 | async-start | bytes 4718592 | tf_op jit(solution)/shard_map/all_gather | solution.py:118
  12.4 396.8 %all-gather.32.cloned.1.call-start = ((), (), s32[]{:S(2)}) async-start(), calls=%async_computation.16 | async-start | bytes 2621440 | tf_op jit(solution)/shard_map/all_gather | solution.py:216
  13.6 395.6 %all-gather.26.cloned.1.call-start = ((), (), s32[]{:S(2)}) async-start(), calls=%async_computation.11 | async-start | bytes 4718592 | tf_op jit(solution)/shard_map/all_gather | solution.py:121
  14.2 446.7 %all-gather.36.cloned.1.call-start = ((), (), s32[]{:S(2)}) async-start(), calls=%async_computation.23 | async-start | bytes 4718592 | tf_op jit(solution)/shard_map/all_gather | solution.py:28
  14.3 298.0 %copy-start.130 = (f32[16]{0:T(128)}, f32[16]{0:T(128)S(1)}, u32[]{:S(2)}) copy-start(f32[16]{0:T(128)S(1)} %neg.63) | copy-start | bytes 196
  36.6 50.4 %copy-start.82 = (f32[8,1,256]{2,1,0:T(1,128)}, f32[8,1,256]{2,1,0:T(1,128)S(1)}, u32[]{:S(2)}) copy-start(f32[8,1,256]{2,1,0:T(1,128)S(1)} %convert_element_type.185) | copy-start | bytes 24580
  67.1 245.1 %copy-start.68 = (bf16[2048,16]{0,1:T(8,128)(2,1)}, bf16[2048,16]{0,1:T(8,128)(2,1)S(1)}, u32[]{:S(2)}) copy-start(bf16[2048,16]{0,1:T(8,128)(2,1)S(1)} %all_gather.74) | copy-start | bytes 196612
  67.2 149.3 %copy-start.98 = (f32[1280]{0:T(1024)}, f32[1280]{0:T(1024)S(1)}, u32[]{:S(2)}) copy-start(f32[1280]{0:T(1024)S(1)} %get-tuple-element.2308) | copy-start | bytes 15364
  67.2 149.3 %copy-start.100 = (f32[1280]{0:T(1024)}, f32[1280]{0:T(1024)S(1)}, u32[]{:S(2)}) copy-start(f32[1280]{0:T(1024)S(1)} %get-tuple-element.2309) | copy-start | bytes 15364
  67.2 149.3 %copy-start.102 = (f32[1280]{0:T(1024)}, f32[1280]{0:T(1024)S(1)}, u32[]{:S(2)}) copy-start(f32[1280]{0:T(1024)S(1)} %get-tuple-element.2310) | copy-start | bytes 15364
  67.3 149.3 %copy-start.104 = (f32[1280]{0:T(1024)}, f32[1280]{0:T(1024)S(1)}, u32[]{:S(2)}) copy-start(f32[1280]{0:T(1024)S(1)} %get-tuple-element.2311) | copy-start | bytes 15364
  91.9 471.2 %copy-start.5 = (bf16[512,2048]{1,0:T(8,128)(2,1)}, bf16[512,2048]{1,0:T(8,128)(2,1)S(1)}, u32[]{:S(2)}) copy-start(bf16[512,2048]{1,0:T(8,128)(2,1)S(1)} %get-tuple-element.2567) | copy-start | bytes 6291460
  206.3 9.1 collective-permute-start
  211.2 5.0 collective-permute-start.1
  312.2 168.9 %all-gather.34.cloned.1.call-start = ((), (), s32[]{:S(2)}) async-start(), calls=%async_computation.22 | async-start | bytes 4718592 | tf_op jit(solution)/shard_map/all_gather | solution.py:28
  333.8 75.3 %copy-start.137 = (bf16[1024]{0:T(1024)(128)(2,1)S(1)}, bf16[1024]{0:T(1024)(128)(2,1)}, u32[]{:S(2)}) copy-start(bf16[1024]{0:T(1024)(128)(2,1)} %param.46) | copy-start | bytes 6148
  407.7 147.2 %all-gather.24.cloned.1.call-start = ((), (), s32[]{:S(2)}) async-start(), calls=%async_computation.10 | async-start | bytes 4718592 | tf_op jit(solution)/shard_map/all_gather | solution.py:117
  408.4 168.9 %all-gather.30.cloned.1.call-start = ((), (), s32[]{:S(2)}) async-start(), calls=%async_computation.15 | async-start | bytes 2621440 | tf_op jit(solution)/shard_map/all_gather | solution.py:216
  409.0 275.0 %all-gather.40.cloned.1.call-start = ((), (), s32[]{:S(2)}) async-start(), calls=%async_computation.25 | async-start | bytes 4718592 | tf_op jit(solution)/shard_map/all_gather | solution.py:28
  409.1 183.8 %copy-start.75 = (f32[1024]{0:T(1024)}, f32[1024]{0:T(1024)S(1)}, u32[]{:S(2)}) copy-start(f32[1024]{0:T(1024)S(1)} %convert_element_type.160) | copy-start | bytes 12292
  416.8 27.3 %copy-start.79 = (f32[2,1,256,16]{3,2,0,1:T(8,128)}, f32[2,1,256,16]{3,2,0,1:T(8,128)S(1)}, u32[]{:S(2)}) copy-start(f32[2,1,256,16]{3,2,0,1:T(8,128)S(1)} %copy.653) | copy-start | bytes 98308
  420.8 211.3 %copy-start.73 = (f32[2,8,2,256]{3,1,2,0:T(8,128)}, f32[2,8,2,256]{3,1,2,0:T(8,128)S(1)}, u32[]{:S(2)}) copy-start(f32[2,8,2,256]{3,1,2,0:T(8,128)S(1)} %copy.778) | copy-start | bytes 98308
  440.2 187.7 %copy-start.74 = (f32[2,8,2,256]{3,1,2,0:T(8,128)}, f32[2,8,2,256]{3,1,2,0:T(8,128)S(1)}, u32[]{:S(2)}) copy-start(f32[2,8,2,256]{3,1,2,0:T(8,128)S(1)} %copy.779) | copy-start | bytes 98308
  609.5 221.4 %all-gather.38.cloned.1.call-start = ((), (), s32[]{:S(2)}) async-start(), calls=%async_computation.24 | async-start | bytes 4718592 | tf_op jit(solution)/shard_map/all_gather | solution.py:28
  631.3 52.8 %copy-start.80 = (f32[512,16]{0,1:T(8,128)}, f32[512,16]{0,1:T(8,128)S(1)}, u32[]{:S(2)}) copy-start(f32[512,16]{0,1:T(8,128)S(1)} %multiply_reduce_fusion.10) | copy-start | bytes 98308
  635.6 396.3 %all-reduce.15.cloned.1.call-start = ((), (), s32[]{:S(2)}) async-start(), calls=%async_computation.26 | async-start | bytes 2097152 | tf_op jit(solution)/shard_map/psum | solution.py:243
  705.6 35.3 %copy-start.59 = (f32[1,256,16]{1,2,0:T(8,128)}, f32[1,256,16]{1,2,0:T(8,128)S(1)}, u32[]{:S(2)}) copy-start(f32[1,256,16]{1,2,0:T(8,128)S(1)} %dynamic-slice_bitcast_fusion.55) | copy-start | bytes 49156 | tf_op jit(solution)/shard_map/transpose(jvp())/while
  767.4 36.0 %copy-start.59 = (f32[1,256,16]{1,2,0:T(8,128)}, f32[1,256,16]{1,2,0:T(8,128)S(1)}, u32[]{:S(2)}) copy-start(f32[1,256,16]{1,2,0:T(8,128)S(1)} %dynamic-slice_bitcast_fusion.55) | copy-start | bytes 49156 | tf_op jit(solution)/shard_map/transpose(jvp())/while
  856.1 33.2 %copy-start.61 = (f32[1,256,16]{1,2,0:T(8,128)}, f32[1,256,16]{1,2,0:T(8,128)S(1)}, u32[]{:S(2)}) copy-start(f32[1,256,16]{1,2,0:T(8,128)S(1)} %dynamic-slice_bitcast_fusion.48) | copy-start | bytes 49156 | tf_op jit(solution)/shard_map/transpose(jvp())/while
  914.0 33.9 %copy-start.61 = (f32[1,256,16]{1,2,0:T(8,128)}, f32[1,256,16]{1,2,0:T(8,128)S(1)}, u32[]{:S(2)}) copy-start(f32[1,256,16]{1,2,0:T(8,128)S(1)} %dynamic-slice_bitcast_fusion.48) | copy-start | bytes 49156 | tf_op jit(solution)/shard_map/transpose(jvp())/while
  974.8 130.3 %reduce-scatter.8.cloned.1.call-start = ((), (), s32[]{:S(2)}) async-start(), calls=%async_computation.12 | async-start | bytes 2621440 | tf_op jit(solution)/shard_map/reduce_scatter | solution.py:211
  980.8 124.3 %reduce-scatter.10.cloned.1.call-start = ((), (), s32[]{:S(2)}) async-start(), calls=%async_computation.14 | async-start | bytes 2621440 | tf_op jit(solution)/shard_map/reduce_scatter | solution.py:211
  995.6 170.5 %all-reduce.17.cloned.1.call-start = ((), (), s32[]{:S(2)}) async-start(), calls=%async_computation.27 | async-start | bytes 8388608 | tf_op jit(solution)/shard_map/psum | solution.py:272
  1042.5 5.6 collective-permute-start.2
  1044.1 6.2 collective-permute-start.3
  1062.6 168.6 %reduce-scatter.18.cloned.1.call-start = ((), (), s32[]{:S(2)}) async-start(), calls=%async_computation.20 | async-start | bytes 147456 | tf_op jit(solution)/shard_map/reduce_scatter | solution.py:291
  1066.2 236.0 %reduce-scatter.16.cloned.1.call-start = ((), (), s32[]{:S(2)}) async-start(), calls=%async_computation.19 | async-start | bytes 2359296 | tf_op jit(solution)/shard_map/reduce_scatter | solution.py:290
  1070.8 383.6 %reduce-scatter.12.cloned.1.call-start = ((), (), s32[]{:S(2)}) async-start(), calls=%async_computation.17 | async-start | bytes 9437184 | tf_op jit(solution)/shard_map/reduce_scatter | solution.py:288
  1081.5 525.8 %reduce-scatter.20.cloned.1.call-start = ((), (), s32[]{:S(2)}) async-start(), calls=%async_computation.21 | async-start | bytes 9437184 | tf_op jit(solution)/shard_map/reduce_scatter | solution.py:292
  1092.5 667.1 %reduce-scatter.14.cloned.1.call-start = ((), (), s32[]{:S(2)}) async-start(), calls=%async_computation.18 | async-start | bytes 9437184 | tf_op jit(solution)/shard_map/reduce_scatter | solution.py:289
  1106.7 59.3 %copy-start.58 = (bf16[2048,256]{1,0:T(8,128)(2,1)S(1)}, bf16[2048,256]{1,0:T(8,128)(2,1)}, u32[]{:S(2)}) copy-start(bf16[2048,256]{1,0:T(8,128)(2,1)} %all-gather.22.cloned.1.call-done) | copy-start | bytes 3145732
  1169.6 46.2 %copy-start.119 = (f32[512]{0:T(512)S(1)}, f32[512]{0:T(512)}, u32[]{:S(2)}) copy-start(f32[512]{0:T(512)} %copy-done.118) | copy-start | bytes 6148
  1169.6 46.2 %copy-start.121 = (f32[512]{0:T(512)S(1)}, f32[512]{0:T(512)}, u32[]{:S(2)}) copy-start(f32[512]{0:T(512)} %copy-done.120) | copy-start | bytes 6148
  (165 other events, 724.8 us)
Sparse Core Ops, SparseCore 0:
  10.4 37.1 all-gather.17
  49.7 34.4 all-gather.27
  86.4 40.2 all-gather.21
  128.7 72.1 all-gather.19
  202.3 20.8 all-gather.31
  225.0 75.0 all-gather.25
  312.3 73.1 all-gather.35
  407.8 73.2 all-gather.33
  483.3 71.6 all-gather.23
  556.4 20.9 all-gather.29
  609.6 74.4 all-gather.39
  686.1 71.6 all-gather.37
  975.0 34.7 all-reduce.14
  1012.3 31.7 reduce-scatter.7
  1046.5 31.4 reduce-scatter.9
  1080.4 85.6 all-reduce.16
  1169.8 61.3 reduce-scatter.17
  1235.2 66.9 reduce-scatter.15
  1306.4 147.9 reduce-scatter.11
  1458.9 148.3 reduce-scatter.19
  1611.5 148.0 reduce-scatter.13
where the time goes:
time: 1790 us; the launch traced here: 1770 us
  waiting for transfers between devices  829 us (46%)
  local copies, waits for them, and re-layouts  314 us (18%)
  matrix products  293 us (16%)
  other arithmetic  160 us (9%)
  blocking collectives  139 us (8%)
    reduce_scatter x1, waiting for transfers between devices, body(): lax.psum_scatter(acc_out, 'seq', scatter_dimension=1, tiled=True)  153 us
    reduce_scatter x1, waiting for transfers between devices, body(): lax.psum_scatter(acc_x, 'seq', scatter_dimension=0, tiled=True)  152 us
    reduce_scatter x1, waiting for transfers between devices, body(): lax.psum_scatter(acc_z, 'seq', scatter_dimension=0, tiled=True)  152 us
    dynamic_update_slice x32, local copies, waits for them, and re-layouts, local_scan(): lax.scan(jax.checkpoint(one_block), start, (split(inner), split(bmat), sp...  111 us
    all_gather x1, waiting for transfers between devices, fetch(): lax.all_gather(w_x, 'seq', axis=0, tiled=True)  71.3 us
    reduce_scatter x1, waiting for transfers between devices, body(): lax.psum_scatter(acc_bc, 'seq', scatter_dimension=0, tiled=True)  70.9 us
    dot_general x12, matrix products, one_block(): inside = jnp.einsum('btsh,bshp->bthp', weights, driven, precision=HIGHEST)  66.9 us
    all_gather x4, waiting for transfers between devices, carried_in(): everything = jax.tree.map(lambda part: lax.all_gather(part, axis), array)  58.9 us
  transfers between devices with their start and end apart: 25, of which 16 were waited for; matrix products, arithmetic and copies ran while one was open for 33% of the time, Pallas kernels for 0%

commit v1 on v0

v1 whole, which is shorter than its diff:
```python
import functools

import jax
import jax.numpy as jnp
from jax import lax
from jax.experimental import pallas as pl
from jax.experimental.pallas import tpu as pltpu
from jax.sharding import PartitionSpec as P

P_SIZE = 64
N = 128
KERNEL = 4
SPAN = 128
HALO = 8
LANES = 128
EPS = 1e-05
HIGHEST = lax.Precision.HIGHEST
F32 = jnp.float32
BF16 = jnp.bfloat16
NN = (((1,), (0,)), ((), ()))
NT = (((1,), (1,)), ((), ()))
TN = (((0,), (0,)), ((), ()))


def dot(left, right, dims=NN, precision=None):
    return lax.dot_general(left, right, dims, precision=precision, preferred_element_type=F32)


def silu_slope(value, logistic):
    return logistic * (1.0 + value * (1.0 - logistic))


class Ring:
    def __init__(self, size):
        self.size = size
        self.on = size == 8
        self.order = list(range(0, size, 2)) + list(range(size - 1, 0, -2))
        self.place = [self.order.index(i) for i in range(size)]

    def relative(self, block):
        if not self.on:
            return block
        place = jnp.asarray(self.place)
        return (place[block] - place[lax.axis_index("seq")]) % self.size

    def shift(self, array, by):
        order, size = self.order, self.size
        return lax.ppermute(array, "seq", [(order[i], order[(i + by) % size]) for i in range(size)])

    def gather(self, block, axis, after=None):
        if not self.on:
            return lax.all_gather(block, "seq", axis=axis, tiled=True), None
        if after is not None:
            block, _ = lax.optimization_barrier((block, after))
        half = self.size // 2
        items = [None] * self.size
        items[0] = block
        right = left = block
        for k in range(1, half):
            right, left = self.shift(right, 1), self.shift(left, -1)
            items[self.size - k], items[k] = right, left
        cut = block.shape[axis] // 2
        first = self.shift(lax.slice_in_dim(right, 0, cut, axis=axis), 1)
        second = self.shift(lax.slice_in_dim(left, cut, 2 * cut, axis=axis), -1)
        items[half] = jnp.concatenate([first, second], axis=axis)
        return jnp.concatenate(items, axis=axis), (right, left)

    def scatter(self, whole, axis, dtype=BF16, after=None):
        if not self.on:
            return lax.psum_scatter(
                whole.astype(dtype), "seq", scatter_dimension=axis, tiled=True
            ).astype(F32)
        size, half = self.size, self.size // 2
        width = whole.shape[axis] // size
        cut = width // 2

        def part(k, start=0, stop=width):
            k = k % size
            return lax.slice_in_dim(whole, k * width + start, k * width + stop, axis=axis)

        first = part(half, 0, cut).astype(dtype)
        second = part(half, cut, width).astype(dtype)
        if after is not None:
            first, second, _ = lax.optimization_barrier((first, second, after))
        first = self.shift(first, 1)
        second = self.shift(second, -1)
        right = jnp.concatenate(
            [part(half - 1, 0, cut) + first.astype(F32), part(half - 1, cut, width)], axis=axis
        ).astype(dtype)
        left = jnp.concatenate(
            [part(1 - half, 0, cut), part(1 - half, cut, width) + second.astype(F32)], axis=axis
        ).astype(dtype)
        for k in range(half - 2, -1, -1):
            right, left = self.shift(right, 1), self.shift(left, -1)
            if k:
                right = (part(k) + right.astype(F32)).astype(dtype)
                left = (part(-k) + left.astype(F32)).astype(dtype)
        return part(0) + right.astype(F32) + left.astype(F32)


def swap(array, axis, bit):
    size = lax.axis_size(axis)
    return lax.ppermute(array, axis, [(i, i ^ bit) for i in range(size)])


def head_sum(array):
    return lax.psum(array, "head")


def seq_sum(ring, array):
    if not ring.on:
        return lax.psum(array, "seq")
    bit = 1
    while bit < ring.size:
        array = array + swap(array, "seq", bit)
        bit *= 2
    return array


def seq_gather(ring, array):
    whole = jnp.zeros((ring.size,) + array.shape, array.dtype)
    whole = lax.dynamic_update_slice(
        whole, array[None], (lax.axis_index("seq"),) + (0,) * array.ndim
    )
    return seq_sum(ring, whole)


def head_gather(ring, own, after=None):
    heads = lax.axis_size("head")
    if not (ring.on and heads == 4):
        return lax.all_gather(own, "head", axis=1, tiled=True)
    here = lax.axis_index("head")
    if after is not None:
        own, _ = lax.optimization_barrier((own, after))
    far = swap(own, "head", 2)
    near = swap(own, "head", 1)
    both = swap(far, "head", 1)
    per = ring.size // heads
    width = own.shape[1] // per
    whole = jnp.zeros((own.shape[0], own.shape[1] * heads), own.dtype)
    for block, bit in ((own, 0), (near, 1), (far, 2), (both, 3)):
        for part in range(per):
            spot = ring.relative((here ^ bit) * per + part)
            whole = lax.dynamic_update_slice(
                whole, block[:, part * width : (part + 1) * width], (0, spot * width)
            )
    return whole


def head_scatter(ring, whole):
    heads = lax.axis_size("head")
    if not (ring.on and heads == 4):
        return lax.psum_scatter(
            whole.astype(BF16), "head", scatter_dimension=1, tiled=True
        ).astype(F32)
    here = lax.axis_index("head")
    per = ring.size // heads
    width = whole.shape[1] // ring.size

    def columns(bit):
        return [
            lax.dynamic_slice_in_dim(
                whole, ring.relative((here ^ bit) * per + part) * width, width, 1
            )
            for part in range(per)
        ]

    far = jnp.concatenate(columns(3), axis=1).astype(BF16)
    near = jnp.concatenate(columns(1), axis=1).astype(BF16)
    far = swap(far, "head", 1)
    near = swap(near, "head", 1)
    far = (jnp.concatenate(columns(2), axis=1) + far.astype(F32)).astype(BF16)
    far = swap(far, "head", 2)
    return jnp.concatenate(columns(0), axis=1) + near.astype(F32) + far.astype(F32)


def expand_scale(log_decay):
    return jnp.exp(log_decay)


def states_before(ring, state, log_decay, direction):
    size = ring.size
    incl_s, incl_w = state, log_decay
    excl_s, excl_w = jnp.zeros_like(state), jnp.zeros_like(log_decay)
    by = 1
    while by < size:
        if direction > 0:
            route = [(i, i + by) for i in range(size - by)]
        else:
            route = [(i + by, i) for i in range(size - by)]
        got_s = lax.ppermute(incl_s.astype(BF16), "seq", route).astype(F32)
        got_w = lax.ppermute(incl_w, "seq", route)
        excl_s = jnp.exp(excl_w) * got_s + excl_s
        excl_w = excl_w + got_w
        if 2 * by < size:
            incl_s = jnp.exp(incl_w) * got_s + incl_s
            incl_w = incl_w + got_w
        by *= 2
    return excl_s


def lane_is_low(rows):
    return lax.broadcasted_iota(jnp.int32, (rows, LANES), 1) < P_SIZE


def spread(columns, j, rows):
    low = jnp.broadcast_to(columns[:, 2 * j : 2 * j + 1], (rows, LANES))
    high = jnp.broadcast_to(columns[:, 2 * j + 1 : 2 * j + 2], (rows, LANES))
    return jnp.where(lane_is_low(rows), low, high), low, high


def triangle(rows, keep):
    first = lax.broadcasted_iota(jnp.int32, (rows, rows), 0)
    second = lax.broadcasted_iota(jnp.int32, (rows, rows), 1)
    return keep(first, second)


def decays(rates, rows):
    lower = triangle(rows, lambda t, s: t >= s)
    within = dot(lower.astype(F32), rates, NN, HIGHEST)
    upper = triangle(rows, lambda s, t: s <= t).astype(F32)
    within_t = dot(rates, upper, TN, HIGHEST)
    return within, within_t, lower


def window(column, row, keep):
    rows = row.shape[1]
    return jnp.exp(jnp.where(keep, column[:, :rows] - row, -1e30))


def scan_kernel(
    pairs, x_ref, bc_ref, halo_ref, dt_ref, cw_ref, bias_ref, rate_ref, skip_ref,
    v_ref, y_ref, st_ref, wc_ref, sb_ref, wo_ref, sl_ref, we_ref,
    hal, state, off, off_l,
):
    rows = x_ref.shape[0]
    inner = pairs * LANES

    @pl.when(pl.program_id(1) == 0)
    def _():
        hal[...] = halo_ref[0]
        state[...] = jnp.zeros_like(state)
        off[...] = jnp.zeros_like(off)
        off_l[...] = jnp.zeros_like(off_l)

    def convolve(ref, at, start):
        now = ref[:, start : start + LANES].astype(F32)
        chunk = jnp.concatenate([hal[:, at : at + LANES], now], axis=0)
        hal[:, at : at + LANES] = now[rows - HALO :]
        shift = HALO - KERNEL + 1
        out = cw_ref[0:1, at : at + LANES] * chunk[shift : shift + rows]
        for k in range(1, KERNEL):
            out = out + cw_ref[k : k + 1, at : at + LANES] * chunk[shift + k : shift + k + rows]
        v_ref[:, at : at + LANES] = out
        return out * jax.nn.sigmoid(out)

    bmat = convolve(bc_ref, inner, 0)
    cmat = convolve(bc_ref, inner + LANES, LANES)
    b_half, c_half = bmat.astype(BF16), cmat.astype(BF16)
    scores = dot(cmat, bmat, NT, HIGHEST)
    steps = jax.nn.softplus(dt_ref[...] + bias_ref[...])
    rates = steps * -rate_ref[...]
    within, within_t, lower = decays(rates, rows)
    low_lanes = lane_is_low(rows)
    st_ref[...] = steps
    wc_ref[...] = off[0:1] + within
    off[0:1] = off[0:1] + within[rows - 1 : rows]
    wo_ref[0] = off_l[0:1]
    for j in range(pairs):
        at = slice(j * LANES, (j + 1) * LANES)
        x = convolve(x_ref, j * LANES, j * LANES)
        u = x * spread(steps, j, rows)[0]
        u_half = u.astype(BF16)
        grow, low, high = spread(within, j, rows)
        end = grow[rows - 1 : rows]
        a_low = (window(low, within_t[2 * j : 2 * j + 1], lower) * scores).astype(BF16)
        a_high = (window(high, within_t[2 * j + 1 : 2 * j + 2], lower) * scores).astype(BF16)
        inside = jnp.where(low_lanes, dot(a_low, u_half), dot(a_high, u_half))
        before = state[:, at]
        carried = jnp.exp(grow) * dot(c_half, before.astype(BF16))
        y_ref[:, at] = inside + carried + skip_ref[0:1, at] * x
        tail = (u * jnp.exp(end - grow)).astype(BF16)
        sb_ref[0, :, at] = before
        after = jnp.exp(end) * before + dot(b_half, tail, TN)
        state[:, at] = after
        sl_ref[0, :, at] = after
        ends = off_l[0:1, at] + end
        off_l[0:1, at] = ends
        we_ref[0, :, at] = ends


def gate_kernel(pairs, y_ref, vc_ref, s_ref, wc_ref, z_ref, ssd_ref, sq_ref):
    rows = y_ref.shape[0]
    vc = vc_ref[...]
    c_half = (vc * jax.nn.sigmoid(vc)).astype(BF16)
    cumulative = wc_ref[...]
    total = jnp.zeros((rows, LANES), F32)
    for j in range(pairs):
        at = slice(j * LANES, (j + 1) * LANES)
        grow = jnp.exp(spread(cumulative, j, rows)[0])
        ssd = y_ref[:, at] + grow * dot(c_half, s_ref[0, :, at].astype(BF16))
        ssd_ref[:, at] = ssd
        z = z_ref[:, at]
        gated = ssd * (z * jax.nn.sigmoid(z))
        total = total + gated * gated
    sq_ref[0] = jnp.sum(total.T, axis=0, keepdims=True)


def as_column(row):
    return jnp.broadcast_to(row, (LANES, row.shape[1])).T


def inner_kernel(pairs, dm_ref, ssd_ref, z_ref, gs_ref, gg_ref, ip_ref, gate_ref):
    rows = dm_ref.shape[0]
    scale = as_column(gs_ref[0])

    @pl.when(pl.program_id(0) == 0)
    def _():
        gate_ref[...] = jnp.zeros_like(gate_ref)

    total = jnp.zeros((rows, LANES), F32)
    for j in range(pairs):
        at = slice(j * LANES, (j + 1) * LANES)
        z = z_ref[:, at]
        gated = ssd_ref[:, at] * (z * jax.nn.sigmoid(z))
        prod = dm_ref[:, at] * gated
        total = total + prod * gg_ref[0:1, at]
        gate_ref[0:1, at] += jnp.sum(prod * scale, axis=0, keepdims=True)
    ip_ref[0] = jnp.sum(total.T, axis=0, keepdims=True)


def gate_back_kernel(
    pairs, width, dm_ref, ssd_ref, z_ref, gs_ref, ip_ref, gg_ref, wc_ref, vc_ref,
    dz_ref, dy_ref, ds_ref,
):
    rows = dm_ref.shape[0]

    @pl.when(pl.program_id(1) == 0)
    def _():
        ds_ref[...] = jnp.zeros_like(ds_ref)

    scale = as_column(gs_ref[0])
    pull = as_column(gs_ref[0] * gs_ref[0] * gs_ref[0] * ip_ref[0] * (1.0 / width))
    vc = vc_ref[...]
    c_half = (vc * jax.nn.sigmoid(vc)).astype(BF16)
    cumulative = wc_ref[...]
    for j in range(pairs):
        at = slice(j * LANES, (j + 1) * LANES)
        z = z_ref[:, at]
        ssd = ssd_ref[:, at]
        logistic = jax.nn.sigmoid(z)
        opened = z * logistic
        d_gated = scale * (dm_ref[:, at] * gg_ref[0:1, at]) - ssd * opened * pull
        dz_ref[:, at] = (d_gated * ssd * silu_slope(z, logistic)).astype(BF16)
        dy = d_gated * opened
        dy_ref[:, at] = dy
        grown = (jnp.exp(spread(cumulative, j, rows)[0]) * dy).astype(BF16)
        ds_ref[0, :, at] += dot(c_half, grown, TN)


def scan_back_kernel(
    pairs, v_ref, dy_ref, st_ref, rate_ref, sb_ref, wo_ref, s_ref,
    du_ref, dbc_ref, grad,
):
    rows = v_ref.shape[0]
    inner = pairs * LANES

    @pl.when(pl.program_id(1) == 0)
    def _():
        grad[...] = jnp.zeros_like(grad)

    def act(at):
        value = v_ref[:, at : at + LANES]
        return value * jax.nn.sigmoid(value)

    bmat, cmat = act(inner), act(inner + LANES)
    b_half, c_half = bmat.astype(BF16), cmat.astype(BF16)
    scores = dot(cmat, bmat, NT, HIGHEST)
    steps = st_ref[...]
    rates = steps * -rate_ref[...]
    within, within_t, lower = decays(rates, rows)
    low_lanes = lane_is_low(rows)
    d_c = jnp.zeros((rows, LANES), F32)
    d_b = jnp.zeros((rows, LANES), F32)
    d_scores = jnp.zeros((rows, rows), F32)
    none = jnp.zeros((rows, LANES), BF16)
    for j in range(pairs):
        at = slice(j * LANES, (j + 1) * LANES)
        x = act(j * LANES)
        u = x * spread(steps, j, rows)[0]
        u_half = u.astype(BF16)
        dy = dy_ref[:, at]
        dy_half = dy.astype(BF16)
        grow, low, high = spread(within, j, rows)
        end = grow[rows - 1 : rows]
        back = jnp.exp(end - grow)
        grown = (jnp.exp(grow) * dy).astype(BF16)
        begun = sb_ref[0, :, at] + jnp.exp(wo_ref[0, :, at]) * s_ref[0, :, at]
        d_c = d_c + dot(grown, begun.astype(BF16), NT)
        later = grad[:, at]
        later_half = later.astype(BF16)
        d_b = d_b + dot((u * back).astype(BF16), later_half, NT)
        w_low = window(low, within_t[2 * j : 2 * j + 1], lower)
        w_high = window(high, within_t[2 * j + 1 : 2 * j + 2], lower)
        d_scores = d_scores + w_low * dot(jnp.where(low_lanes, dy_half, none), u_half, NT)
        d_scores = d_scores + w_high * dot(jnp.where(low_lanes, none, dy_half), u_half, NT)
        a_low = (w_low * scores).astype(BF16)
        a_high = (w_high * scores).astype(BF16)
        inside = jnp.where(low_lanes, dot(a_low, dy_half, TN), dot(a_high, dy_half, TN))
        du_ref[:, at] = inside + back * dot(b_half, later_half)
        grad[:, at] = jnp.exp(end) * later + dot(c_half, grown, TN)
    d_half = d_scores.astype(BF16)
    dbc_ref[:, :LANES] = d_b + dot(d_half, c_half, TN)
    dbc_ref[:, LANES:] = d_c + dot(d_half, b_half)


def head_picker(j, heads):
    lane = lax.broadcasted_iota(jnp.int32, (LANES, heads), 0) // P_SIZE
    head = lax.broadcasted_iota(jnp.int32, (LANES, heads), 1)
    return (lane + 2 * j == head).astype(F32)


def finish_kernel(
    pairs, v_ref, dy_ref, du_ref, ssd_ref, st_ref, wc_ref, we_ref, la_ref, se_ref, dbc_ref,
    dt_ref, bias_ref, rate_ref, skip_ref,
    dcx_ref, dbo_ref, ddt_ref, dskip_ref, dhead_ref, run,
):
    rows = v_ref.shape[0]
    heads = 2 * pairs
    inner = pairs * LANES

    @pl.when((pl.program_id(0) == 0) & (pl.program_id(1) == 0))
    def _():
        dskip_ref[...] = jnp.zeros_like(dskip_ref)
        dhead_ref[...] = jnp.zeros_like(dhead_ref)

    @pl.when(pl.program_id(1) == 0)
    def _():
        total = jnp.zeros((1, heads), F32)
        for j in range(pairs):
            at = slice(j * LANES, (j + 1) * LANES)
            both = jnp.sum(la_ref[0, :, at] * se_ref[0, :, at], axis=0, keepdims=True)
            total = total + dot(both, head_picker(j, heads), NN, HIGHEST)
        run[0:1] = total

    value_b = v_ref[:, inner : inner + LANES]
    b_half = (value_b * jax.nn.sigmoid(value_b)).astype(BF16)
    steps = st_ref[...]
    cumulative = wc_ref[...]
    moved = jnp.zeros((rows, heads), F32)
    driven = jnp.zeros((rows, heads), F32)
    d_b = dbc_ref[:, :LANES]
    for j in range(pairs):
        at = slice(j * LANES, (j + 1) * LANES)
        value = v_ref[:, at]
        logistic = jax.nn.sigmoid(value)
        x = value * logistic
        wide = spread(steps, j, rows)[0]
        u = x * wide
        dy = dy_ref[:, at]
        skip = skip_ref[0:1, at]
        tail = jnp.exp(we_ref[0, :, at] - spread(cumulative, j, rows)[0])
        later = la_ref[0, :, at].astype(BF16)
        du = du_ref[:, at] + tail * dot(b_half, later)
        d_b = d_b + dot((u * tail).astype(BF16), later, NT)
        picker = head_picker(j, heads)
        moved = moved + dot(dy * (ssd_ref[:, at] - skip * x) - u * du, picker, NN, HIGHEST)
        driven = driven + dot(x * du, picker, NN, HIGHEST)
        dskip_ref[0:1, at] += jnp.sum(dy * x, axis=0, keepdims=True)
        d_inner = wide * du + skip * dy
        dcx_ref[:, at] = (d_inner * silu_slope(value, logistic)).astype(BF16)
    dbo_ref[:, :LANES] = d_b
    dbo_ref[:, LANES:] = dbc_ref[:, LANES:]
    upper = triangle(rows, lambda t, s: s >= t).astype(F32)
    d_rates = dot(upper, moved, NN, HIGHEST) + run[0:1]
    run[0:1] = d_rates[0:1]
    d_steps = driven - rate_ref[...] * d_rates
    d_raw = d_steps * jax.nn.sigmoid(dt_ref[...] + bias_ref[...])
    ddt_ref[...] = d_raw.astype(BF16)
    dhead_ref[0:1] += jnp.sum(d_raw, axis=0, keepdims=True)
    dhead_ref[1:2] -= jnp.sum(steps * d_rates, axis=0, keepdims=True)


def conv_back_kernel(d_ref, in_ref, halo_ref, cw_ref, dx_ref, gw_ref, hal):
    rows, width = d_ref.shape

    @pl.when((pl.program_id(0) == 0) & (pl.program_id(1) == 0))
    def _():
        gw_ref[...] = jnp.zeros_like(gw_ref)

    @pl.when(pl.program_id(1) == 0)
    def _():
        hal[...] = halo_ref[0]

    for c in range(width // LANES):
        at = slice(c * LANES, (c + 1) * LANES)
        now = d_ref[:, at].astype(F32)
        chunk = jnp.concatenate([now, hal[:, at]], axis=0)
        hal[:, at] = now[:HALO]
        given = in_ref[:, at].astype(F32)
        total = jnp.zeros((rows, LANES), F32)
        for k in range(KERNEL):
            moved = chunk[KERNEL - 1 - k : KERNEL - 1 - k + rows]
            total = total + cw_ref[k : k + 1, at] * moved
            gw_ref[k : k + 1, at] += jnp.sum(given * moved, axis=0, keepdims=True)
        dx_ref[:, at] = total.astype(BF16)


def shaped(*shape, dtype=F32):
    return jax.ShapeDtypeStruct(shape, dtype)


def call(kernel, grid, ins, outs, shapes, scratch=(), flops=0, moved=0):
    return pl.pallas_call(
        kernel,
        grid=grid,
        in_specs=ins,
        out_specs=outs,
        out_shape=shapes,
        scratch_shapes=list(scratch),
        compiler_params=pltpu.CompilerParams(vmem_limit_bytes=40 * 1024 * 1024),
        cost_estimate=pl.CostEstimate(flops=flops, bytes_accessed=moved, transcendentals=0),
    )


def conv_back(d_conv, given, after, taps, batch, length, rows):
    width = d_conv.shape[1]
    count = length // rows
    turn = lambda b, i: (b * count + count - 1 - i, 0)
    block = pl.BlockSpec((rows, width), turn)
    total = batch * length
    return call(
        conv_back_kernel,
        (batch, count),
        [
            block,
            block,
            pl.BlockSpec((1, HALO, width), lambda b, i: (b, 0, 0)),
            pl.BlockSpec((KERNEL, width), lambda b, i: (0, 0)),
        ],
        [block, pl.BlockSpec((KERNEL, width), lambda b, i: (0, 0))],
        [shaped(total, width, dtype=BF16), shaped(KERNEL, width)],
        [pltpu.VMEM((HALO, width), F32)],
        flops=16 * total * width,
        moved=6 * total * width,
    )(d_conv, given, after, taps)


def body(
    tokens, norm_gain, w_z, w_x, w_bc, w_dt, conv_x, conv_bc, dt_bias, decay_rate,
    skip_gain, gate_gain, w_out, grad_out,
):
    ring = Ring(lax.axis_size("seq"))
    batch, length, own_width = tokens.shape
    model = norm_gain.shape[0] * ring.size
    total = batch * length
    inner = w_z.shape[1]
    heads = dt_bias.shape[0]
    inner_all = inner * lax.axis_size("head")
    pairs = heads // 2
    rows = min(SPAN, length)
    count = length // rows
    blocks = batch * count
    margin = KERNEL - 1
    here = lax.axis_index("head")

    slab = tokens.reshape(total, own_width)
    cot_rows = grad_out.reshape(total, own_width)
    bias_row = dt_bias.reshape(1, heads)
    rate_row = decay_rate.reshape(1, heads)
    skip_lanes = jnp.repeat(skip_gain, P_SIZE).reshape(1, inner)
    gate_f = gate_gain.astype(F32).reshape(1, inner)
    conv_xf = conv_x.astype(F32)
    conv_bcf = conv_bc.astype(F32)
    conv_w = jnp.concatenate([conv_xf, conv_bcf], axis=1)

    dt_w, _ = ring.gather(w_dt.T, 1)
    xbc_w, mark = ring.gather(jnp.concatenate([w_x, w_bc], axis=1), 0)
    z_w, mark = ring.gather(w_z, 0, mark)
    out_w, mark = ring.gather(w_out, 1, mark)

    gain = seq_gather(ring, norm_gain.astype(F32)).reshape(model)
    own_gain = lax.dynamic_slice_in_dim(gain, here * own_width, own_width)
    square = head_sum(jnp.sum(slab * slab, axis=1))
    scale = lax.rsqrt(square / model + EPS)
    own_normed = (slab * scale[:, None] * own_gain).astype(BF16)
    normed = head_gather(ring, own_normed)
    cot = head_gather(ring, cot_rows.astype(BF16), normed)

    xbc = dot(normed, xbc_w).astype(BF16)
    dt_raw = dot(normed, dt_w, NT)
    x_in, bc_in = xbc[:, :inner], xbc[:, inner:]

    def edge(array, last):
        cut = array.reshape(batch, length, -1)
        cut = cut[:, length - margin :] if last else cut[:, :margin]
        moves = [(i, i + 1) for i in range(ring.size - 1)]
        if not last:
            moves = [(b, a) for a, b in moves]
        got = lax.ppermute(cut, "seq", moves).astype(F32)
        pad = ((0, 0), (HALO - margin, 0), (0, 0)) if last else ((0, 0), (0, HALO - margin), (0, 0))
        return jnp.pad(got, pad)

    halo = edge(xbc, True)

    at = lambda b, i: (b * count + i, 0)
    back = lambda b, i: (b * count + count - 1 - i, 0)
    at3 = lambda b, i: (b * count + i, 0, 0)
    back3 = lambda b, i: (b * count + count - 1 - i, 0, 0)
    seq3 = lambda b, i: (b, 0, 0)
    fixed = lambda b, i: (0, 0)
    row_heads = pl.BlockSpec((1, heads), fixed)
    row_inner = pl.BlockSpec((1, inner), fixed)
    state_spec = pl.BlockSpec((1, N, inner), seq3)
    pair_flops = total * rows * inner

    conv_out, y_local, steps, cumulative, begun, offsets, left, left_w = call(
        functools.partial(scan_kernel, pairs),
        (batch, count),
        [
            pl.BlockSpec((rows, inner), at),
            pl.BlockSpec((rows, 2 * N), at),
            pl.BlockSpec((1, HALO, inner + 2 * N), seq3),
            pl.BlockSpec((rows, heads), at),
            pl.BlockSpec((KERNEL, inner + 2 * N), fixed),
            row_heads,
            row_heads,
            row_inner,
        ],
        [
            pl.BlockSpec((rows, inner + 2 * N), at),
            pl.BlockSpec((rows, inner), at),
            pl.BlockSpec((rows, heads), at),
            pl.BlockSpec((rows, heads), at),
            pl.BlockSpec((1, N, inner), at3),
            pl.BlockSpec((1, 1, inner), at3),
            state_spec,
            pl.BlockSpec((1, 1, inner), seq3),
        ],
        [
            shaped(total, inner + 2 * N),
            shaped(total, inner),
            shaped(total, heads),
            shaped(total, heads),
            shaped(blocks, N, inner),
            shaped(blocks, 1, inner),
            shaped(batch, N, inner),
            shaped(batch, 1, inner),
        ],
        [
            pltpu.VMEM((HALO, inner + 2 * N), F32),
            pltpu.VMEM((N, inner), F32),
            pltpu.VMEM((8, heads), F32),
            pltpu.VMEM((8, inner), F32),
        ],
        flops=20 * pair_flops,
        moved=total * inner * 20,
    )(x_in, bc_in, halo, dt_raw, conv_w, bias_row, rate_row, skip_lanes)

    came = states_before(ring, left, left_w, 1)
    z_vals = dot(normed, z_w)

    block_spec = pl.BlockSpec((rows, inner), at)
    row_out = pl.BlockSpec((1, 1, rows), at3)
    c_spec = pl.BlockSpec((rows, LANES), lambda b, i: (b * count + i, inner // LANES + 1))
    head_cols = pl.BlockSpec((rows, heads), at)
    ssd, square_g = call(
        functools.partial(gate_kernel, pairs),
        (batch, count),
        [block_spec, c_spec, state_spec, head_cols, block_spec],
        [block_spec, row_out],
        [shaped(total, inner), shaped(blocks, 1, rows)],
        flops=2 * total * inner * N,
        moved=total * inner * 12,
    )(y_local, conv_out, came, cumulative, z_vals)

    gate_scale = lax.rsqrt(head_sum(square_g) / inner_all + EPS)
    scale_col = gate_scale.reshape(total, 1)
    mixed = (ssd * (z_vals * jax.nn.sigmoid(z_vals)) * scale_col * gate_f).astype(BF16)

    g_out = ring.scatter(dot(mixed, cot, TN), 1)
    d_mixed = dot(cot, out_w, NT)
    flat_block = pl.BlockSpec((rows, inner), lambda i: (i, 0))
    flat_row = pl.BlockSpec((1, 1, rows), lambda i: (i, 0, 0))
    flat_inner = pl.BlockSpec((1, inner), lambda i: (0, 0))
    product, g_gate = call(
        functools.partial(inner_kernel, pairs),
        (blocks,),
        [flat_block, flat_block, flat_block, flat_row, flat_inner],
        [flat_row, flat_inner],
        [shaped(blocks, 1, rows), shaped(1, inner)],
        flops=10 * total * inner,
        moved=total * inner * 12,
    )(d_mixed, ssd, z_vals, gate_scale, gate_f)
    product = head_sum(product)

    d_z, d_ssd, d_left = call(
        functools.partial(gate_back_kernel, pairs, inner_all),
        (batch, count),
        [
            block_spec, block_spec, block_spec, row_out, row_out, row_inner, head_cols, c_spec,
        ],
        [block_spec, block_spec, state_spec],
        [shaped(total, inner, dtype=BF16), shaped(total, inner), shaped(batch, N, inner)],
        flops=2 * total * inner * N,
        moved=total * inner * 18,
    )(d_mixed, ssd, z_vals, gate_scale, product, gate_f, cumulative, conv_out)

    later = states_before(ring, d_left, left_w, -1)
    g_z = ring.scatter(dot(normed, d_z, TN), 0)

    v_back = pl.BlockSpec((rows, inner + 2 * N), back)
    block_back = pl.BlockSpec((rows, inner), back)
    heads_back = pl.BlockSpec((rows, heads), back)
    bc_back = pl.BlockSpec((rows, 2 * N), back)
    du_local, dbc_local = call(
        functools.partial(scan_back_kernel, pairs),
        (batch, count),
        [
            v_back, block_back, heads_back, row_heads,
            pl.BlockSpec((1, N, inner), back3),
            pl.BlockSpec((1, 1, inner), back3),
            state_spec,
        ],
        [block_back, bc_back],
        [shaped(total, inner), shaped(total, 2 * N)],
        [pltpu.VMEM((N, inner), F32)],
        flops=40 * pair_flops,
        moved=total * inner * 20,
    )(conv_out, d_ssd, steps, rate_row, begun, offsets, came)

    at_end = jnp.exp(left_w) * came + left
    d_conv_x, d_bc_part, d_dt, g_skip, g_heads = call(
        functools.partial(finish_kernel, pairs),
        (batch, count),
        [
            v_back, block_back, block_back, block_back, heads_back, heads_back,
            pl.BlockSpec((1, 1, inner), seq3), state_spec, state_spec, bc_back, heads_back,
            row_heads, row_heads, row_inner,
        ],
        [
            block_back, bc_back, heads_back, row_inner,
            pl.BlockSpec((2, heads), fixed),
        ],
        [
            shaped(total, inner, dtype=BF16),
            shaped(total, 2 * N),
            shaped(total, heads, dtype=BF16),
            shaped(1, inner),
            shaped(2, heads),
        ],
        [pltpu.VMEM((8, heads), F32)],
        flops=4 * total * inner * N,
        moved=total * inner * 22,
    )(
        conv_out, d_ssd, du_local, ssd, steps, cumulative, left_w, later, at_end, dbc_local,
        dt_raw, bias_row, rate_row, skip_lanes,
    )

    if lax.axis_size("head") == 4:
        d_bc_sum = d_bc_part + swap(d_bc_part, "head", 1)
        d_bc_sum = d_bc_sum.astype(BF16)
        d_bc_sum = d_bc_sum.astype(F32) + swap(d_bc_sum, "head", 2).astype(F32)
    else:
        d_bc_sum = head_sum(d_bc_part)
    v_bc = conv_out[:, inner:]
    d_conv_bc = (d_bc_sum * silu_slope(v_bc, jax.nn.sigmoid(v_bc))).astype(BF16)

    d_x, g_conv_x = conv_back(
        d_conv_x, x_in, edge(d_conv_x, False), conv_xf, batch, length, rows
    )
    d_bc, g_conv_bc = conv_back(
        d_conv_bc, bc_in, edge(d_conv_bc, False), conv_bcf, batch, length, rows
    )

    d_xbc = jnp.concatenate([d_x, d_bc], axis=1)
    x_w, bc_w = xbc_w[:, :inner], xbc_w[:, inner:]
    own_terms = dot(d_z, z_w, NT) + dot(d_x, x_w, NT) + dot(d_dt, dt_w)
    own_terms = own_terms + jnp.where(here == 0, 1.0, 0.0) * dot(d_bc, bc_w, NT)
    d_normed = head_scatter(ring, own_terms)
    g_xbc = ring.scatter(dot(normed, d_xbc, TN), 0)
    g_dt = ring.scatter(dot(d_dt, normed, TN), 1, F32).T

    out_own = head_scatter(ring, dot(mixed, out_w))
    mixed_out = slab + out_own

    g_gain_own = jnp.sum(d_normed * slab * scale[:, None], axis=0)
    gain_grad = d_normed * own_gain
    dots = head_sum(jnp.sum(gain_grad * slab, axis=1))
    grad_tokens = (
        cot_rows
        + scale[:, None] * gain_grad
        - slab * (scale * scale * scale * dots / model)[:, None]
    )
    g_gain = jnp.zeros((model,), F32)
    g_gain = lax.dynamic_update_slice_in_dim(g_gain, g_gain_own, here * own_width, 0)
    if lax.axis_size("head") == 4:
        g_gain = g_gain + swap(g_gain, "head", 1)
        g_gain = g_gain + swap(g_gain, "head", 2)
    else:
        g_gain = head_sum(g_gain)
    g_gain = seq_sum(ring, g_gain)
    slice_width = norm_gain.shape[0]
    g_gain = lax.dynamic_slice_in_dim(g_gain, lax.axis_index("seq") * slice_width, slice_width)

    small = jnp.concatenate(
        [
            g_conv_x.reshape(-1), g_conv_bc.reshape(-1), g_gate.reshape(-1),
            g_skip.reshape(-1), g_heads.reshape(-1),
        ]
    )
    small = seq_sum(ring, small)
    cuts = [KERNEL * inner, KERNEL * 2 * N, inner, inner, heads, heads]
    parts, start = [], 0
    for width in cuts:
        parts.append(small[start : start + width])
        start += width
    sum_x, sum_bc, sum_gate, sum_skip, sum_bias, sum_rate = parts

    return (
        mixed_out.reshape(batch, length, own_width),
        grad_tokens.reshape(batch, length, own_width),
        g_gain,
        g_z,
        g_xbc[:, :inner],
        g_xbc[:, inner:],
        g_dt,
        sum_x.reshape(KERNEL, inner),
        sum_bc.reshape(KERNEL, 2 * N),
        sum_bias,
        sum_rate,
        jnp.sum(sum_skip.reshape(heads, P_SIZE), axis=1),
        sum_gate,
        g_out,
    )


def solution(mesh):
    in_specs = (
        P(None, "seq", "head"),
        P("seq"),
        P("seq", "head"),
        P("seq", "head"),
        P("seq", None),
        P("seq", "head"),
        P(None, "head"),
        P(),
        P("head"),
        P("head"),
        P("head"),
        P("head"),
        P("head", "seq"),
        P(None, "seq", "head"),
    )
    out_specs = (
        P(None, "seq", "head"),
        P(None, "seq", "head"),
        P("seq"),
        P("seq", "head"),
        P("seq", "head"),
        P("seq", None),
        P("seq", "head"),
        P(None, "head"),
        P(),
        P("head"),
        P("head"),
        P("head"),
        P("head"),
        P("head", "seq"),
    )
    return jax.shard_map(body, mesh=mesh, in_specs=in_specs, out_specs=out_specs, check_vma=False)
```

time: 1790 us -> 702 us (0.39)
  waiting for transfers between devices: 829 us -> 215 us
  local copies, waits for them, and re-layouts: 314 us -> 51.2 us
  matrix products: 293 us -> 78.8 us
  starting transfers between devices: 11 us -> 159 us
  blocking collectives: 139 us -> 31.8 us
  other arithmetic: 160 us -> 60.6 us
  Pallas kernels: 0 us -> 81.3 us
    reduce_scatter x7 -> x0, waiting for transfers between devices: 536 us -> none  [the longest x1 153 us: body(): lax.psum_scatter(acc_out, 'seq', scatter_dimension=1, tiled=True)]
    all_gather x12 -> x0, waiting for transfers between devices: 226 us -> none  [the longest x1 71.3 us: fetch(): lax.all_gather(w_x, 'seq', axis=0, tiled=True)]
    dot_general x92 -> x13, matrix products: 293 us -> 78.8 us  [dot(): lax.dot_general(left, right, dims, precision=precision, preferred_element...]
    ppermute x4 -> x102, waiting for transfers between devices: 5.06 us -> 215 us  [the longest x64 128 us: shift(): lax.ppermute(array, 'seq', [(order[i], order[(i + by) % size]) for i in r...]
    ppermute x4 -> x102, starting transfers between devices: 9.37 us -> 159 us  [the longest x64 104 us: shift(): lax.ppermute(array, 'seq', [(order[i], order[(i + by) % size]) for i in r...]
    dynamic_update_slice x32 -> x18, local copies, waits for them, and re-layouts: 111 us -> 7.96 us  [the longest x16 7.7 us: head_gather(): lax.dynamic_update_slice(whole, block[:, part * width:(part + 1) * width]...]
    all_gather x4 -> x0, blocking collectives: 88.3 us -> none  [the longest x2 35.5 us: carried_in(): everything = jax.tree.map(lambda part: lax.all_gather(part, axis), array)]
    pallas_call x0 -> x8, Pallas kernels: none -> 81.3 us  [the longest x1 22.8 us: body(): call(functools.partial(finish_kernel, pairs), (batch, count), [v_back, bl...]
  transfers between devices with their start and end apart: 25 -> 102, of which waited for: 16 -> 31; matrix products, arithmetic and copies ran while one was open for 33% -> 26% of each run, Pallas kernels for 0% -> 12%
where the time goes in v1:
time: 702 us; the launch traced here: 691 us
  waiting for transfers between devices  215 us (31%)
  starting transfers between devices  159 us (23%)
  Pallas kernels  81.3 us (12%)
  matrix products  78.8 us (11%)
  other arithmetic  60.6 us (9%)
  local copies, waits for them, and re-layouts  51.2 us (7%)
  blocking collectives  31.8 us (5%)
  between operations  13.5 us (2%)
    ppermute x64, waiting for transfers between devices, shift(): lax.ppermute(array, 'seq', [(order[i], order[(i + by) % size]) for i in r...  128 us
    ppermute x64, starting transfers between devices, shift(): lax.ppermute(array, 'seq', [(order[i], order[(i + by) % size]) for i in r...  104 us
    dot_general x13, matrix products, dot(): lax.dot_general(left, right, dims, precision=precision, preferred_element...  78.8 us
    ppermute x25, waiting for transfers between devices, swap(): return lax.ppermute(array, axis, [(i, i ^ bit) for i in range(size)])  52.9 us
    psum x4, blocking collectives, head_sum(): return lax.psum(array, 'head')  31.8 us
    ppermute x25, starting transfers between devices, swap(): return lax.ppermute(array, axis, [(i, i ^ bit) for i in range(size)])  24.1 us
    ppermute x6, waiting for transfers between devices, states_before(): got_s = lax.ppermute(incl_s.astype(BF16), 'seq', route).astype(F32)  23.6 us
    pallas_call x1, Pallas kernels, body(): call(functools.partial(finish_kernel, pairs), (batch, count), [v_back, bl...  22.8 us
  transfers between devices with their start and end apart: 102, of which 31 were waited for; matrix products, arithmetic and copies ran while one was open for 26% of the time, Pallas kernels for 12%

profile of v1, /device:TPU:0, one launch (start us, length us, event | category | flops | bytes accessed | tf_op | source)
XLA Modules:
  0.0 691.2 jit_solution(4046568991682471154)
XLA Ops:
  14.4 6.0 psum.28
  50.8 12.5 %collective-permute-done.22 = bf16[16,128]{1,0:T(8,128)(2,1)S(1)} collective-permute-done((bf16[16,128]{1,0:T(8,128)(2,1)S(1)}, bf16[16,128]{1,0:T(8,128)(2,1)S(1)}, u32[]{:S(2)}, u32[]{:S(2)}) %collective-permute-start.22) | collective-permute-done | bytes 4128 | tf_op jit(solution)/shard_map/ppermute | solution.py:48
  69.6 9.7 %collective-permute-done.10 = bf16[256,1280]{1,0:T(8,128)(2,1)S(1)} collective-permute-done((bf16[256,1280]{1,0:T(8,128)(2,1)S(1)}, bf16[256,1280]{1,0:T(8,128)(2,1)S(1)}, u32[]{:S(2)}, u32[]{:S(2)}) %collective-permute-start.10) | collective-permute-done | bytes 655392 | tf_op jit(solution)/shard_map/ppermute | solution.py:48
  82.4 11.9 %collective-permute-done.11 = bf16[256,1280]{1,0:T(8,128)(2,1)S(1)} collective-permute-done((bf16[256,1280]{1,0:T(8,128)(2,1)S(1)}, bf16[256,1280]{1,0:T(8,128)(2,1)S(1)}, u32[]{:S(2)}, u32[]{:S(2)}) %collective-permute-start.11) | collective-permute-done | bytes 655392 | tf_op jit(solution)/shard_map/ppermute | solution.py:48
  101.9 11.9 %collective-permute-done.12 = bf16[128,1280]{1,0:T(8,128)(2,1)S(1)} collective-permute-done((bf16[128,1280]{1,0:T(8,128)(2,1)S(1)}, bf16[128,1280]{1,0:T(8,128)(2,1)S(1)}, u32[]{:S(2)}, u32[]{:S(2)}) %collective-permute-start.12) | collective-permute-done | bytes 327712 | tf_op jit(solution)/shard_map/ppermute | solution.py:48
  118.1 8.3 %convolution_convert_fusion = bf16[1024,1280]{1,0:T(8,128)(2,1)S(1)} fusion(bf16[1024,2048]{1,0:T(8,128)(2,1)S(1)} %slice_dynamic-update-slice_fusion.6, bf16[2048,1280]{1,0:T(8,128)(2,1)} %constant_dynamic-update-slice_fusion.2), kind=kOutput, calls=%fused_computation.4 | convolution fusion | flops 5370019840 | bytes 12058624 | tf_op jit(solution)/shard_map/dot_general | solution.py:26
  131.0 14.7 %shard_map.533 = (f32[1024,1280]{1,0:T(8,128)}, f32[1024,1024]{1,0:T(8,128)S(1)}, f32[1024,16]{1,0:T(8,128)S(1)}, f32[1024,16]{1,0:T(8,128)S(1)}, f32[8,128,1024...) custom-call(bf16[1024,1024]{1,0:T(8,128)(2,1)S(1)} %slice.358.x_ref.in_ref, ...), custom_call_target="tpu_custom_call" | custom-call | flops 2684354560 | bytes 20971520 | tf_op jit(solution)/shard_map/pallas_call | solution.py:617
  145.8 4.7 collective-permute-start.23
  152.5 5.3 collective-permute-start.25
  163.1 7.1 %collective-permute-start.29 = (bf16[256,1024]{1,0:T(8,128)(2,1)}, bf16[256,1024]{1,0:T(8,128)(2,1)S(1)}, u32[]{:S(2)}, u32[]{:S(2)}) collective-permute-start(bf16[256,1024]{1,0:T(8,128)(2,1)} %collective-permute-done.28), channel_id=1, source_target_pairs={{0,4},{8,0},{16,8},{24,16},{28,24},{20,28},{12,20},{4,12},{1,5},{9... | collective-permute-start | bytes 1572872 | tf_op jit(solution)/shard_map/ppermute | solution.py:48
  174.1 6.0 collective-permute-done.29
  180.0 5.4 collective-permute-start.30
  190.1 12.5 %collective-permute-done.33 = bf16[256,1024]{1,0:T(8,128)(2,1)S(1)} collective-permute-done((bf16[256,1024]{1,0:T(8,128)(2,1)S(1)}, bf16[256,1024]{1,0:T(8,128)(2,1)S(1)}, u32[]{:S(2)}, u32[]{:S(2)}) %collective-permute-start.33) | collective-permute-done | bytes 524320 | tf_op jit(solution)/shard_map/ppermute | solution.py:48
  212.0 6.9 collective-permute-start.39
  220.1 4.5 fusion.68.z_ref
  226.4 6.0 shard_map.534
  234.4 5.6 psum.29
  247.3 6.8 fusion.66
  255.1 8.3 %collective-permute-start.94 = (bf16[1024,128]{1,0:T(8,128)(2,1)}, bf16[1024,128]{1,0:T(8,128)(2,1)}, u32[]{:S(2)}, u32[]{:S(2)}) collective-permute-start(bf16[1024,128]{1,0:T(8,128)(2,1)} %get-tuple-element.112), channel_id=1, source_target_pairs={{0,8},{8,16},{16,24},{24,28},{28,20},{20,12},{12,4},{4,0},{1,9},{9... | collective-permute-start | bytes 786440 | tf_op jit(solution)/shard_map/ppermute | solution.py:48
  267.5 5.5 collective-permute-done.51
  277.5 5.3 collective-permute-done.37
  288.9 15.1 %collective-permute-done.41 = bf16[1024,256]{1,0:T(8,128)(2,1)S(1)} collective-permute-done((bf16[1024,256]{1,0:T(8,128)(2,1)S(1)}, bf16[1024,256]{1,0:T(8,128)(2,1)S(1)}, u32[]{:S(2)}, u32[]{:S(2)}) %collective-permute-start.41) | collective-permute-done | bytes 524320 | tf_op jit(solution)/shard_map/ppermute | solution.py:48
  315.3 4.7 fusion.70.dm_ref
  323.1 14.1 %psum.30.ip_ref = f32[8,1,128]{2,1,0:T(1,128)S(1)} all-reduce(f32[8,1,128]{2,1,0:T(1,128)S(1)} %get-tuple-element.53), channel_id=1, replica_groups=mesh['seq'=8,'head'=4] {'head'}, use_global_device_ids=true, to_apply=%region_3.4 | all-reduce | flops 1024 | bytes 8192 | tf_op jit(solution)/shard_map/psum | solution.py:107
  339.4 8.9 %shard_map.536 = (bf16[1024,1024]{1,0:T(8,128)(2,1)S(1)}, f32[1024,1024]{1,0:T(8,128)S(1)}, f32[2,128,1024]{2,1,0:T(8,128)S(1)}) custom-call(f32[1024,1024]{1,0:T(8,128)S(1)} %copy-done.5, f32[1024,1024]{1,0:T(8,128)} %copy-done, f32[1024,1024]{1,0:T(8,128)} %copy-done.2, f32[8,1,128]{2,1,0:T(1,128)S(1)} %add_rsqrt_fusion.gs_ref, ...), custom_call_target="tpu_custom_call" | custom-call | flops 268435456 | bytes 18874368 | tf_op jit(solution)/shard_map/pallas_call | solution.py:697
  348.4 6.9 fusion.64
  355.3 6.8 fusion.71
  362.1 4.5 fusion.69
  377.7 18.7 %shard_map.537 = (f32[1024,1024]{1,0:T(8,128)S(1)}, f32[1024,256]{1,0:T(8,128)S(1)}) custom-call(f32[1024,1280]{1,0:T(8,128)} %get-tuple-element.44.vc_ref.v_ref, f32[1024,1024]{1,0:T(8,128)S(1)} %get-tuple-element.55.dy_ref, f32[1024,16]{1,0:T(8,128)S(1)} %copy-done.15, f32[1,16]{1,0:T(1,128)S(1)} %bitcast.111, f32[8,128,1024]{2,1,0:T(8,128)} %copy-done.18, ...), custom_call_target="tpu_custom_call" | custom-call | flops 5368709120 | bytes 20971520 | tf_op jit(solution)/shard_map/pallas_call | solution.py:716
  406.0 8.5 %collective-permute-done.100 = bf16[1024,256]{1,0:T(8,128)(2,1)S(1)} collective-permute-done((bf16[1024,256]{1,0:T(8,128)(2,1)S(1)}, bf16[1024,256]{1,0:T(8,128)(2,1)S(1)}, u32[]{:S(2)}, u32[]{:S(2)}) %collective-permute-start.100) | collective-permute-done | bytes 524320 | tf_op jit(solution)/shard_map/ppermute | solution.py:48
  416.0 9.1 %collective-permute-done.68 = bf16[256,1024]{1,0:T(8,128)(2,1)S(1)} collective-permute-done((bf16[256,1024]{1,0:T(8,128)(2,1)S(1)}, bf16[256,1024]{1,0:T(8,128)(2,1)S(1)}, u32[]{:S(2)}, u32[]{:S(2)}) %collective-permute-start.68) | collective-permute-done | bytes 524320 | tf_op jit(solution)/shard_map/ppermute | solution.py:48
  429.8 7.2 %collective-permute-done.53 = bf16[2,128,1024]{2,1,0:T(8,128)(2,1)S(1)} collective-permute-done((bf16[2,128,1024]{2,1,0:T(8,128)(2,1)S(1)}, bf16[2,128,1024]{2,1,0:T(8,128)(2,1)S(1)}, u32[]{:S(2)}, u32[]{:S(2)}) %collective-permute-start.53) | collective-permute-done | bytes 524320 | tf_op jit(solution)/shard_map/ppermute | solution.py:191
  441.9 5.4 collective-permute-done.101
  455.9 16.4 %collective-permute-done.54 = bf16[2,128,1024]{2,1,0:T(8,128)(2,1)S(1)} collective-permute-done((bf16[2,128,1024]{2,1,0:T(8,128)(2,1)S(1)}, bf16[2,128,1024]{2,1,0:T(8,128)(2,1)S(1)}, u32[]{:S(2)}, u32[]{:S(2)}) %collective-permute-start.54) | collective-permute-done | bytes 524320 | tf_op jit(solution)/shard_map/ppermute | solution.py:191
  472.5 22.8 %shard_map.538 = (bf16[1024,1024]{1,0:T(8,128)(2,1)S(1)}, f32[1024,256]{1,0:T(8,128)}, bf16[1024,16]{1,0:T(8,128)(2,1)S(1)}, f32[1,1024]{1,0:T(1,128)S(1)}, f32[2,16]{1,0:T(2,128)S(1)}) custom-call(f32[1024,1280]{1,0:T(8,128)} %get-tuple-element.44.vc_ref.v_ref, f32[1024,1024]{1,0:T(8,128)S(1)} %get-tuple-element.55.dy_ref, f32[1024,1024]{1,0:T(8,128)} %copy-done.7, ...), custom_call_target="tpu_custom_call" | custom-call | flops 536870912 | bytes 23068672 | tf_op jit(solution)/shard_map/pallas_call | solution.py:733
  502.0 5.1 collective-permute-start.87
  512.1 5.7 shard_map.539
  520.0 9.0 %fusion = f32[1024,2048]{1,0:T(8,128)} fusion(bf16[1024,1024]{1,0:T(8,128)(2,1)S(1)} %get-tuple-element.63, bf16[2048,1280]{1,0:T(8,128)(2,1)} %constant_dynamic-update-slice_fusion.2), kind=kOutput, calls=%fused_computation.1 | convolution fusion | flops 4294967296 | bytes 14680064 | tf_op jit(solution)/shard_map/dot_general | solution.py:26
  538.7 6.4 collective-permute-done.57
  556.1 9.3 %fusion.65 = (bf16[2048,1280]{1,0:T(8,128)(2,1)}, f32[2048,1280]{1,0:T(8,128)}) fusion(bf16[1024,2048]{1,0:T(8,128)(2,1)S(1)} %copy-done.24, bf16[1024,256]{1,0:T(8,128)(2,1)S(1)} %get-tuple-element.66, bf16[1024,1024]{1,0:T(8,128)(2,1)S(1)} %get-tuple-element.63), kind=kOutput, calls=%fused_computation.225 | convolution fusion | flops 5376573440 | bytes 22544384 | tf_op jit(solution)/shard_map/dot_general | solution.py:26
  568.8 11.6 %multiply_add_fusion = f32[1024,2048]{1,0:T(8,128)} fusion(f32[1024,2048]{1,0:T(8,128)S(1)} %bitcast.114, f32[1024,2048]{1,0:T(8,128)} %fusion.71, f32[1024,2048]{1,0:T(8,128)} %fusion, bf16[1024,256]{1,0:T(8,128)(2,1)S(1)} %get-tuple-element.66, f32[]{:T(128)S(6)} %select_n.379, bf16[2048,1280]{1,0:T(8,128)(2,1)} %constant_dynamic-update-slice_fusion.2), kind=kOutput, calls=%fused_computation | convolution fusion | flops 1082130432 | bytes 35127300 | tf_op jit(solution)/shard_map/dot_general | solution.py:26
  589.4 11.2 %collective-permute-done.92 = f32[7200]{0:T(1024)S(1)} collective-permute-done((f32[7200]{0:T(1024)S(1)}, f32[7200]{0:T(1024)S(1)}, u32[]{:S(2)}, u32[]{:S(2)}) %collective-permute-start.92) | collective-permute-done | bytes 28832 | tf_op jit(solution)/shard_map/ppermute | solution.py:103
  616.7 10.2 %collective-permute-done.61 = bf16[1024,512]{1,0:T(8,128)(2,1)S(1)} collective-permute-done((bf16[1024,512]{1,0:T(8,128)(2,1)S(1)}, bf16[1024,512]{1,0:T(8,128)(2,1)S(1)}, u32[]{:S(2)}, u32[]{:S(2)}) %collective-permute-start.61) | collective-permute-done | bytes 1048608 | tf_op jit(solution)/shard_map/ppermute | solution.py:103
  633.5 15.7 %collective-permute-done.63 = f32[2048]{0:T(1024)S(1)} collective-permute-done((f32[2048]{0:T(1024)S(1)}, f32[2048]{0:T(1024)S(1)}, u32[]{:S(2)}, u32[]{:S(2)}) %collective-permute-start.63) | collective-permute-done | bytes 8224 | tf_op jit(solution)/shard_map/ppermute | solution.py:103
  653.5 6.1 psum.31
  661.5 6.1 collective-permute-done.65
  674.8 5.7 fusion.11
  681.1 6.2 collective-permute-done.82
  (490 shorter events, 255.4 us)
Async XLA Ops:
  0.7 36.0 %collective-permute-start.15 = (bf16[16,256]{1,0:T(8,128)(2,1)}, bf16[16,256]{1,0:T(8,128)(2,1)S(1)}, u32[]{:S(2)}, u32[]{:S(2)}) collective-permute-start(bf16[16,256]{1,0:T(8,128)(2,1)} %bitcast.133), channel_id=1, source_target_pairs={{0,4},{8,0},{16,8},{24,16},{28,24},{20,28},{12,20},{4,12},{1,5},{9... | collective-permute-start | bytes 24584 | tf_op jit(solution)/shard_map/ppermute | solution.py:48
  3.7 33.0 %collective-permute-start.18 = (bf16[16,256]{1,0:T(8,128)(2,1)}, bf16[16,256]{1,0:T(8,128)(2,1)S(1)}, u32[]{:S(2)}, u32[]{:S(2)}) collective-permute-start(bf16[16,256]{1,0:T(8,128)(2,1)} %bitcast.134), channel_id=1, source_target_pairs={{0,8},{8,16},{16,24},{24,28},{28,20},{20,12},{12,4},{4,0},{1,9},{9... | collective-permute-start | bytes 24584 | tf_op jit(solution)/shard_map/ppermute | solution.py:48
  4.5 30.5 %collective-permute-start = (f32[8,256]{1,0:T(8,128)S(1)}, f32[8,256]{1,0:T(8,128)S(1)}, u32[]{:S(2)}, u32[]{:S(2)}) collective-permute-start(f32[8,256]{1,0:T(8,128)S(1)} %dynamic_update_slice.58), channel_id=1, source_target_pairs={{0,4},{4,0},{8,12},{12,8},{16,20},{20,16},{24,28},{28,24},{1,5},{5... | collective-permute-start | bytes 24584 | tf_op jit(solution)/shard_map/ppermute | solution.py:103
  10.3 53.0 %collective-permute-start.9 = (bf16[256,1280]{1,0:T(8,128)(2,1)}, bf16[256,1280]{1,0:T(8,128)(2,1)S(1)}, u32[]{:S(2)}, u32[]{:S(2)}) collective-permute-start(bf16[256,1280]{1,0:T(8,128)(2,1)} %get-tuple-element.130), channel_id=1, source_target_pairs={{0,8},{8,16},{16,24},{24,28},{28,20},{20,12},{12,4},{4,0},{1,9},{9... | collective-permute-start | bytes 1966088 | tf_op jit(solution)/shard_map/ppermute | solution.py:48
  43.8 25.7 %collective-permute-start.3 = (bf16[1024,512]{1,0:T(8,128)(2,1)S(1)}, bf16[1024,512]{1,0:T(8,128)(2,1)S(1)}, u32[]{:S(2)}, u32[]{:S(2)}) collective-permute-start(bf16[1024,512]{1,0:T(8,128)(2,1)S(1)} %fusion.13), channel_id=1, source_target_pairs={{0,1},{1,0},{2,3},{3,2},{4,5},{5,4},{6,7},{7,6},{8,9},{9,8},{10,11... | collective-permute-start | bytes 3145736 | tf_op jit(solution)/shard_map/ppermute | solution.py:103
  43.9 25.6 %collective-permute-start.4 = (bf16[1024,512]{1,0:T(8,128)(2,1)S(1)}, bf16[1024,512]{1,0:T(8,128)(2,1)S(1)}, u32[]{:S(2)}, u32[]{:S(2)}) collective-permute-start(bf16[1024,512]{1,0:T(8,128)(2,1)S(1)} %fusion.13), channel_id=1, source_target_pairs={{0,2},{1,3},{2,0},{3,1},{4,6},{5,7},{6,4},{7,5},{8,10},{9,11},{10,... | collective-permute-start | bytes 3145736 | tf_op jit(solution)/shard_map/ppermute | solution.py:103
  46.2 18.8 %collective-permute-start.6 = (bf16[256,1280]{1,0:T(8,128)(2,1)}, bf16[256,1280]{1,0:T(8,128)(2,1)S(1)}, u32[]{:S(2)}, u32[]{:S(2)}) collective-permute-start(bf16[256,1280]{1,0:T(8,128)(2,1)} %get-tuple-element.130), channel_id=1, source_target_pairs={{0,4},{8,0},{16,8},{24,16},{28,24},{20,28},{12,20},{4,12},{1,5},{9... | collective-permute-start | bytes 1966088 | tf_op jit(solution)/shard_map/ppermute | solution.py:48
  69.5 32.3 %collective-permute-start.5 = (bf16[1024,512]{1,0:T(8,128)(2,1)S(1)}, bf16[1024,512]{1,0:T(8,128)(2,1)S(1)}, u32[]{:S(2)}, u32[]{:S(2)}) collective-permute-start(bf16[1024,512]{1,0:T(8,128)(2,1)S(1)} %collective-permute-done.4), channel_id=1, source_target_pairs={{0,1},{1,0},{2,3},{3,2},{4,5},{5,4},{6,7},{7,6},{8,9},{9,8},{10,11... | collective-permute-start | bytes 3145736 | tf_op jit(solution)/shard_map/ppermute | solution.py:103
  95.8 67.2 %collective-permute-start.28 = (bf16[256,1024]{1,0:T(8,128)(2,1)S(1)}, bf16[256,1024]{1,0:T(8,128)(2,1)}, u32[]{:S(2)}, u32[]{:S(2)}) collective-permute-start(bf16[256,1024]{1,0:T(8,128)(2,1)S(1)} %copy-done.38), channel_id=1, source_target_pairs={{0,4},{8,0},{16,8},{24,16},{28,24},{20,28},{12,20},{4,12},{1,5},{9... | collective-permute-start | bytes 1572872 | tf_op jit(solution)/shard_map/ppermute | solution.py:48
  96.3 73.9 %collective-permute-start.31 = (bf16[256,1024]{1,0:T(8,128)(2,1)S(1)}, bf16[256,1024]{1,0:T(8,128)(2,1)}, u32[]{:S(2)}, u32[]{:S(2)}) collective-permute-start(bf16[256,1024]{1,0:T(8,128)(2,1)S(1)} %copy-done.38), channel_id=1, source_target_pairs={{0,8},{8,16},{16,24},{24,28},{28,20},{20,12},{12,4},{4,0},{1,9},{9... | collective-permute-start | bytes 1572872 | tf_op jit(solution)/shard_map/ppermute | solution.py:48
  130.3 55.2 %collective-permute-start.47 = (bf16[1024,512]{1,0:T(8,128)(2,1)S(1)}, bf16[1024,512]{1,0:T(8,128)(2,1)}, u32[]{:S(2)}, u32[]{:S(2)}) collective-permute-start(bf16[1024,512]{1,0:T(8,128)(2,1)S(1)} %copy-done.32), channel_id=1, source_target_pairs={{0,1},{1,0},{2,3},{3,2},{4,5},{5,4},{6,7},{7,6},{8,9},{9,8},{10,11... | collective-permute-start | bytes 3145736 | tf_op jit(solution)/shard_map/ppermute | solution.py:103
  152.5 19.1 %collective-permute-start.25 = (bf16[2,128,1024]{2,1,0:T(8,128)(2,1)S(1)}, bf16[2,128,1024]{2,1,0:T(8,128)(2,1)S(1)}, u32[]{:S(2)}, u32[]{:S(2)}) collective-permute-start(bf16[2,128,1024]{2,1,0:T(8,128)(2,1)S(1)} %convert_element_type.231), channel_id=1, source_target_pairs={{0,4},{4,8},{8,12},{12,16},{16,20},{20,24},{24,28},{1,5},{5,9},{9,... | collective-permute-start | bytes 1572872 | tf_op jit(solution)/shard_map/ppermute | solution.py:191
  162.6 25.2 %collective-permute-start.48 = (bf16[1024,512]{1,0:T(8,128)(2,1)S(1)}, bf16[1024,512]{1,0:T(8,128)(2,1)}, u32[]{:S(2)}, u32[]{:S(2)}) collective-permute-start(bf16[1024,512]{1,0:T(8,128)(2,1)S(1)} %copy-done.32), channel_id=1, source_target_pairs={{0,2},{1,3},{2,0},{3,1},{4,6},{5,7},{6,4},{7,5},{8,10},{9,11},{10,... | collective-permute-start | bytes 3145736 | tf_op jit(solution)/shard_map/ppermute | solution.py:103
  171.8 33.5 %collective-permute-start.26 = (bf16[2,128,1024]{2,1,0:T(8,128)(2,1)S(1)}, bf16[2,128,1024]{2,1,0:T(8,128)(2,1)S(1)}, u32[]{:S(2)}, u32[]{:S(2)}) collective-permute-start(bf16[2,128,1024]{2,1,0:T(8,128)(2,1)S(1)} %fusion.42), channel_id=1, source_target_pairs={{0,8},{4,12},{8,16},{12,20},{16,24},{20,28},{1,9},{5,13},{9,17},{1... | collective-permute-start | bytes 1572872 | tf_op jit(solution)/shard_map/ppermute | solution.py:191
  180.0 25.2 %collective-permute-start.30 = (bf16[256,1024]{1,0:T(8,128)(2,1)S(1)}, bf16[256,1024]{1,0:T(8,128)(2,1)S(1)}, u32[]{:S(2)}, u32[]{:S(2)}) collective-permute-start(bf16[256,1024]{1,0:T(8,128)(2,1)S(1)} %collective-permute-done.29), channel_id=1, source_target_pairs={{0,4},{8,0},{16,8},{24,16},{28,24},{20,28},{12,20},{4,12},{1,5},{9... | collective-permute-start | bytes 1572872 | tf_op jit(solution)/shard_map/ppermute | solution.py:48
  187.8 56.7 %collective-permute-start.49 = (bf16[1024,512]{1,0:T(8,128)(2,1)}, bf16[1024,512]{1,0:T(8,128)(2,1)}, u32[]{:S(2)}, u32[]{:S(2)}) collective-permute-start(bf16[1024,512]{1,0:T(8,128)(2,1)} %collective-permute-done.48), channel_id=1, source_target_pairs={{0,1},{1,0},{2,3},{3,2},{4,5},{5,4},{6,7},{7,6},{8,9},{9,8},{10,11... | collective-permute-start | bytes 3145736 | tf_op jit(solution)/shard_map/ppermute | solution.py:103
  205.6 19.1 %collective-permute-start.27 = (bf16[2,128,1024]{2,1,0:T(8,128)(2,1)S(1)}, bf16[2,128,1024]{2,1,0:T(8,128)(2,1)S(1)}, u32[]{:S(2)}, u32[]{:S(2)}) collective-permute-start(bf16[2,128,1024]{2,1,0:T(8,128)(2,1)S(1)} %fusion.25), channel_id=1, source_target_pairs={{0,16},{4,20},{8,24},{12,28},{1,17},{5,21},{9,25},{13,29},{2,18},{... | collective-permute-start | bytes 1572872 | tf_op jit(solution)/shard_map/ppermute | solution.py:191
  209.0 55.7 %collective-permute-start.36 = (bf16[1024,256]{1,0:T(8,128)(2,1)}, bf16[1024,256]{1,0:T(8,128)(2,1)}, u32[]{:S(2)}, u32[]{:S(2)}) collective-permute-start(bf16[1024,256]{1,0:T(8,128)(2,1)} %param.58), channel_id=1, source_target_pairs={{0,4},{8,0},{16,8},{24,16},{28,24},{20,28},{12,20},{4,12},{1,5},{9... | collective-permute-start | bytes 1572872 | tf_op jit(solution)/shard_map/ppermute | solution.py:48
  212.0 55.5 %collective-permute-start.39 = (bf16[1024,256]{1,0:T(8,128)(2,1)}, bf16[1024,256]{1,0:T(8,128)(2,1)}, u32[]{:S(2)}, u32[]{:S(2)}) collective-permute-start(bf16[1024,256]{1,0:T(8,128)(2,1)} %param.58), channel_id=1, source_target_pairs={{0,8},{8,16},{16,24},{24,28},{28,20},{20,12},{12,4},{4,0},{1,9},{9... | collective-permute-start | bytes 1572872 | tf_op jit(solution)/shard_map/ppermute | solution.py:48
  255.1 17.9 %collective-permute-start.94 = (bf16[1024,128]{1,0:T(8,128)(2,1)}, bf16[1024,128]{1,0:T(8,128)(2,1)}, u32[]{:S(2)}, u32[]{:S(2)}) collective-permute-start(bf16[1024,128]{1,0:T(8,128)(2,1)} %get-tuple-element.112), channel_id=1, source_target_pairs={{0,8},{8,16},{16,24},{24,28},{28,20},{20,12},{12,4},{4,0},{1,9},{9... | collective-permute-start | bytes 786440 | tf_op jit(solution)/shard_map/ppermute | solution.py:48
  264.7 18.1 %collective-permute-start.37 = (bf16[1024,256]{1,0:T(8,128)(2,1)}, bf16[1024,256]{1,0:T(8,128)(2,1)S(1)}, u32[]{:S(2)}, u32[]{:S(2)}) collective-permute-start(bf16[1024,256]{1,0:T(8,128)(2,1)} %collective-permute-done.36), channel_id=1, source_target_pairs={{0,4},{8,0},{16,8},{24,16},{28,24},{20,28},{12,20},{4,12},{1,5},{9... | collective-permute-start | bytes 1572872 | tf_op jit(solution)/shard_map/ppermute | solution.py:48
  275.6 31.1 %collective-permute-start.95 = (bf16[1024,256]{1,0:T(8,128)(2,1)S(1)}, bf16[1024,256]{1,0:T(8,128)(2,1)S(1)}, u32[]{:S(2)}, u32[]{:S(2)}) collective-permute-start(bf16[1024,256]{1,0:T(8,128)(2,1)S(1)} %pad_maximum_fusion.8), channel_id=1, source_target_pairs={{0,8},{8,16},{16,24},{24,28},{28,20},{20,12},{12,4},{4,0},{1,9},{9... | collective-permute-start | bytes 1572872 | tf_op jit(solution)/shard_map/ppermute | solution.py:48
  282.8 22.7 %collective-permute-start.38 = (bf16[1024,256]{1,0:T(8,128)(2,1)S(1)}, bf16[1024,256]{1,0:T(8,128)(2,1)S(1)}, u32[]{:S(2)}, u32[]{:S(2)}) collective-permute-start(bf16[1024,256]{1,0:T(8,128)(2,1)S(1)} %collective-permute-done.37), channel_id=1, source_target_pairs={{0,4},{8,0},{16,8},{24,16},{28,24},{20,28},{12,20},{4,12},{1,5},{9... | collective-permute-start | bytes 1572872 | tf_op jit(solution)/shard_map/ppermute | solution.py:48
  283.3 20.7 %collective-permute-start.41 = (bf16[1024,256]{1,0:T(8,128)(2,1)S(1)}, bf16[1024,256]{1,0:T(8,128)(2,1)S(1)}, u32[]{:S(2)}, u32[]{:S(2)}) collective-permute-start(bf16[1024,256]{1,0:T(8,128)(2,1)S(1)} %collective-permute-done.40), channel_id=1, source_target_pairs={{0,8},{8,16},{16,24},{24,28},{28,20},{20,12},{12,4},{4,0},{1,9},{9... | collective-permute-start | bytes 1572872 | tf_op jit(solution)/shard_map/ppermute | solution.py:48
  288.2 108.3 %collective-permute-start.99 = (bf16[1024,256]{1,0:T(8,128)(2,1)}, bf16[1024,256]{1,0:T(8,128)(2,1)}, u32[]{:S(2)}, u32[]{:S(2)}) collective-permute-start(bf16[1024,256]{1,0:T(8,128)(2,1)} %pad_maximum_fusion.9), channel_id=1, source_target_pairs={{0,4},{8,0},{16,8},{24,16},{28,24},{20,28},{12,20},{4,12},{1,5},{9... | collective-permute-start | bytes 1572872 | tf_op jit(solution)/shard_map/ppermute | solution.py:48
  308.9 87.6 %collective-permute-start.96 = (bf16[1024,256]{1,0:T(8,128)(2,1)}, bf16[1024,256]{1,0:T(8,128)(2,1)}, u32[]{:S(2)}, u32[]{:S(2)}) collective-permute-start(bf16[1024,256]{1,0:T(8,128)(2,1)} %fusion.32), channel_id=1, source_target_pairs={{0,8},{8,16},{16,24},{24,28},{28,20},{20,12},{12,4},{4,0},{1,9},{9... | collective-permute-start | bytes 1572872 | tf_op jit(solution)/shard_map/ppermute | solution.py:48
  370.0 34.2 %collective-permute-start.52 = (bf16[2,128,1024]{2,1,0:T(8,128)(2,1)}, bf16[2,128,1024]{2,1,0:T(8,128)(2,1)S(1)}, u32[]{:S(2)}, u32[]{:S(2)}) collective-permute-start(bf16[2,128,1024]{2,1,0:T(8,128)(2,1)} %convert_element_type.244), channel_id=1, source_target_pairs={{4,0},{8,4},{12,8},{16,12},{20,16},{24,20},{28,24},{5,1},{9,5},{13... | collective-permute-start | bytes 1572872 | tf_op jit(solution)/shard_map/ppermute | solution.py:191
  372.2 28.1 %collective-permute-start.67 = (bf16[128,1024]{1,0:T(8,128)(2,1)}, bf16[128,1024]{1,0:T(8,128)(2,1)}, u32[]{:S(2)}, u32[]{:S(2)}) collective-permute-start(bf16[128,1024]{1,0:T(8,128)(2,1)} %get-tuple-element.116), channel_id=1, source_target_pairs={{0,8},{8,16},{16,24},{24,28},{28,20},{20,12},{12,4},{4,0},{1,9},{9... | collective-permute-start | bytes 786440 | tf_op jit(solution)/shard_map/ppermute | solution.py:48
  375.6 26.3 %collective-permute-start.71 = (bf16[128,1024]{1,0:T(8,128)(2,1)}, bf16[128,1024]{1,0:T(8,128)(2,1)}, u32[]{:S(2)}, u32[]{:S(2)}) collective-permute-start(bf16[128,1024]{1,0:T(8,128)(2,1)} %get-tuple-element.117), channel_id=1, source_target_pairs={{0,4},{8,0},{16,8},{24,16},{28,24},{20,28},{12,20},{4,12},{1,5},{9... | collective-permute-start | bytes 786440 | tf_op jit(solution)/shard_map/ppermute | solution.py:48
  396.5 42.8 %collective-permute-start.45 = (bf16[1024,512]{1,0:T(8,128)(2,1)}, bf16[1024,512]{1,0:T(8,128)(2,1)S(1)}, u32[]{:S(2)}, u32[]{:S(2)}) collective-permute-start(bf16[1024,512]{1,0:T(8,128)(2,1)} %pad_maximum_fusion.1), channel_id=1, source_target_pairs={{0,1},{1,0},{2,3},{3,2},{4,5},{5,4},{6,7},{7,6},{8,9},{9,8},{10,11... | collective-permute-start | bytes 3145736 | tf_op jit(solution)/shard_map/ppermute | solution.py:103
  400.4 41.5 %collective-permute-start.97 = (bf16[1024,256]{1,0:T(8,128)(2,1)S(1)}, bf16[1024,256]{1,0:T(8,128)(2,1)S(1)}, u32[]{:S(2)}, u32[]{:S(2)}) collective-permute-start(bf16[1024,256]{1,0:T(8,128)(2,1)S(1)} %get-tuple-element.84), channel_id=1, source_target_pairs={{0,8},{8,16},{16,24},{24,28},{28,20},{20,12},{12,4},{4,0},{1,9},{9... | collective-permute-start | bytes 1572872 | tf_op jit(solution)/shard_map/ppermute | solution.py:48
  403.4 45.1 %collective-permute-start.72 = (bf16[256,1024]{1,0:T(8,128)(2,1)S(1)}, bf16[256,1024]{1,0:T(8,128)(2,1)S(1)}, u32[]{:S(2)}, u32[]{:S(2)}) collective-permute-start(bf16[256,1024]{1,0:T(8,128)(2,1)S(1)} %pad_maximum_fusion.7), channel_id=1, source_target_pairs={{0,4},{8,0},{16,8},{24,16},{28,24},{20,28},{12,20},{4,12},{1,5},{9... | collective-permute-start | bytes 1572872 | tf_op jit(solution)/shard_map/ppermute | solution.py:48
  404.3 20.8 %collective-permute-start.68 = (bf16[256,1024]{1,0:T(8,128)(2,1)S(1)}, bf16[256,1024]{1,0:T(8,128)(2,1)S(1)}, u32[]{:S(2)}, u32[]{:S(2)}) collective-permute-start(bf16[256,1024]{1,0:T(8,128)(2,1)S(1)} %pad_maximum_fusion.6), channel_id=1, source_target_pairs={{0,8},{8,16},{16,24},{24,28},{28,20},{20,12},{12,4},{4,0},{1,9},{9... | collective-permute-start | bytes 1572872 | tf_op jit(solution)/shard_map/ppermute | solution.py:48
  414.5 22.5 %collective-permute-start.53 = (bf16[2,128,1024]{2,1,0:T(8,128)(2,1)S(1)}, bf16[2,128,1024]{2,1,0:T(8,128)(2,1)S(1)}, u32[]{:S(2)}, u32[]{:S(2)}) collective-permute-start(bf16[2,128,1024]{2,1,0:T(8,128)(2,1)S(1)} %fusion.41), channel_id=1, source_target_pairs={{8,0},{12,4},{16,8},{20,12},{24,16},{28,20},{9,1},{13,5},{17,9},{2... | collective-permute-start | bytes 1572872 | tf_op jit(solution)/shard_map/ppermute | solution.py:191
  425.1 22.2 %collective-permute-start.101 = (bf16[1024,256]{1,0:T(8,128)(2,1)S(1)}, bf16[1024,256]{1,0:T(8,128)(2,1)S(1)}, u32[]{:S(2)}, u32[]{:S(2)}) collective-permute-start(bf16[1024,256]{1,0:T(8,128)(2,1)S(1)} %fusion.31), channel_id=1, source_target_pairs={{0,4},{8,0},{16,8},{24,16},{28,24},{20,28},{12,20},{4,12},{1,5},{9... | collective-permute-start | bytes 1572872 | tf_op jit(solution)/shard_map/ppermute | solution.py:48
  439.3 32.9 %collective-permute-start.54 = (bf16[2,128,1024]{2,1,0:T(8,128)(2,1)S(1)}, bf16[2,128,1024]{2,1,0:T(8,128)(2,1)S(1)}, u32[]{:S(2)}, u32[]{:S(2)}) collective-permute-start(bf16[2,128,1024]{2,1,0:T(8,128)(2,1)S(1)} %fusion.29), channel_id=1, source_target_pairs={{16,0},{20,4},{24,8},{28,12},{17,1},{21,5},{25,9},{29,13},{18,2},{... | collective-permute-start | bytes 1572872 | tf_op jit(solution)/shard_map/ppermute | solution.py:191
  451.9 96.5 %collective-permute-start.73 = (bf16[256,1024]{1,0:T(8,128)(2,1)}, bf16[256,1024]{1,0:T(8,128)(2,1)}, u32[]{:S(2)}, u32[]{:S(2)}) collective-permute-start(bf16[256,1024]{1,0:T(8,128)(2,1)} %get-tuple-element.89), channel_id=1, source_target_pairs={{0,4},{8,0},{16,8},{24,16},{28,24},{20,28},{12,20},{4,12},{1,5},{9... | collective-permute-start | bytes 1572872 | tf_op jit(solution)/shard_map/ppermute | solution.py:48
  454.0 156.8 %collective-permute-start.70 = (bf16[256,1024]{1,0:T(8,128)(2,1)}, bf16[256,1024]{1,0:T(8,128)(2,1)}, u32[]{:S(2)}, u32[]{:S(2)}) collective-permute-start(bf16[256,1024]{1,0:T(8,128)(2,1)} %get-tuple-element.88), channel_id=1, source_target_pairs={{0,8},{8,16},{16,24},{24,28},{28,20},{20,12},{12,4},{4,0},{1,9},{9... | collective-permute-start | bytes 1572872 | tf_op jit(solution)/shard_map/ppermute | solution.py:48
  500.6 30.5 %collective-permute-start.56 = (f32[1024,256]{1,0:T(8,128)}, f32[1024,256]{1,0:T(8,128)}, u32[]{:S(2)}, u32[]{:S(2)}) collective-permute-start(f32[1024,256]{1,0:T(8,128)} %get-tuple-element.65), channel_id=1, source_target_pairs={{0,1},{1,0},{2,3},{3,2},{4,5},{5,4},{6,7},{7,6},{8,9},{9,8},{10,11... | collective-permute-start | bytes 3145736 | tf_op jit(solution)/shard_map/ppermute | solution.py:103
  554.0 31.5 %collective-permute-start.91 = (f32[7200]{0:T(1024)S(1)}, f32[7200]{0:T(1024)S(1)}, u32[]{:S(2)}, u32[]{:S(2)}) collective-permute-start(f32[7200]{0:T(1024)S(1)} %constant_dynamic-update-slice_fusion.40), channel_id=1, source_target_pairs={{0,4},{4,0},{8,12},{12,8},{16,20},{20,16},{24,28},{28,24},{1,5},{5... | collective-permute-start | bytes 86408 | tf_op jit(solution)/shard_map/ppermute | solution.py:103
  566.7 18.9 %collective-permute-start.75 = (bf16[128,1280]{1,0:T(8,128)(2,1)S(1)}, bf16[128,1280]{1,0:T(8,128)(2,1)S(1)}, u32[]{:S(2)}, u32[]{:S(2)}) collective-permute-start(bf16[128,1280]{1,0:T(8,128)(2,1)S(1)} %get-tuple-element.108), channel_id=1, source_target_pairs={{0,8},{8,16},{16,24},{24,28},{28,20},{20,12},{12,4},{4,0},{1,9},{9... | collective-permute-start | bytes 983048 | tf_op jit(solution)/shard_map/ppermute | solution.py:48
  568.5 19.2 %collective-permute-start.79 = (bf16[128,1280]{1,0:T(8,128)(2,1)S(1)}, bf16[128,1280]{1,0:T(8,128)(2,1)S(1)}, u32[]{:S(2)}, u32[]{:S(2)}) collective-permute-start(bf16[128,1280]{1,0:T(8,128)(2,1)S(1)} %get-tuple-element.109), channel_id=1, source_target_pairs={{0,4},{8,0},{16,8},{24,16},{28,24},{20,28},{12,20},{4,12},{1,5},{9... | collective-permute-start | bytes 983048 | tf_op jit(solution)/shard_map/ppermute | solution.py:48
  585.5 25.4 %collective-permute-start.74 = (bf16[256,1024]{1,0:T(8,128)(2,1)S(1)}, bf16[256,1024]{1,0:T(8,128)(2,1)S(1)}, u32[]{:S(2)}, u32[]{:S(2)}) collective-permute-start(bf16[256,1024]{1,0:T(8,128)(2,1)S(1)} %fusion.36), channel_id=1, source_target_pairs={{0,4},{8,0},{16,8},{24,16},{28,24},{20,28},{12,20},{4,12},{1,5},{9... | collective-permute-start | bytes 1572872 | tf_op jit(solution)/shard_map/ppermute | solution.py:48
  600.9 26.0 %collective-permute-start.61 = (bf16[1024,512]{1,0:T(8,128)(2,1)S(1)}, bf16[1024,512]{1,0:T(8,128)(2,1)S(1)}, u32[]{:S(2)}, u32[]{:S(2)}) collective-permute-start(bf16[1024,512]{1,0:T(8,128)(2,1)S(1)} %fusion.10), channel_id=1, source_target_pairs={{0,2},{1,3},{2,0},{3,1},{4,6},{5,7},{6,4},{7,5},{8,10},{9,11},{10,... | collective-permute-start | bytes 3145736 | tf_op jit(solution)/shard_map/ppermute | solution.py:103
  615.4 59.4 %collective-permute-start.44 = (bf16[1024,512]{1,0:T(8,128)(2,1)}, bf16[1024,512]{1,0:T(8,128)(2,1)}, u32[]{:S(2)}, u32[]{:S(2)}) collective-permute-start(bf16[1024,512]{1,0:T(8,128)(2,1)} %pad_maximum_fusion), channel_id=1, source_target_pairs={{0,1},{1,0},{2,3},{3,2},{4,5},{5,4},{6,7},{7,6},{8,9},{9,8},{10,11... | collective-permute-start | bytes 3145736 | tf_op jit(solution)/shard_map/ppermute | solution.py:103
  615.4 59.4 %collective-permute-start.46 = (bf16[1024,512]{1,0:T(8,128)(2,1)}, bf16[1024,512]{1,0:T(8,128)(2,1)}, u32[]{:S(2)}, u32[]{:S(2)}) collective-permute-start(bf16[1024,512]{1,0:T(8,128)(2,1)} %fusion.8), channel_id=1, source_target_pairs={{0,2},{1,3},{2,0},{3,1},{4,6},{5,7},{6,4},{7,5},{8,10},{9,11},{10,... | collective-permute-start | bytes 3145736 | tf_op jit(solution)/shard_map/ppermute | solution.py:103
  631.6 37.8 %collective-permute-start.81 = (bf16[256,1280]{1,0:T(8,128)(2,1)}, bf16[256,1280]{1,0:T(8,128)(2,1)}, u32[]{:S(2)}, u32[]{:S(2)}) collective-permute-start(bf16[256,1280]{1,0:T(8,128)(2,1)} %get-tuple-element.81), channel_id=1, source_target_pairs={{0,4},{8,0},{16,8},{24,16},{28,24},{20,28},{12,20},{4,12},{1,5},{9... | collective-permute-start | bytes 1966088 | tf_op jit(solution)/shard_map/ppermute | solution.py:48
  651.7 29.4 %collective-permute-start.78 = (bf16[256,1280]{1,0:T(8,128)(2,1)}, bf16[256,1280]{1,0:T(8,128)(2,1)}, u32[]{:S(2)}, u32[]{:S(2)}) collective-permute-start(bf16[256,1280]{1,0:T(8,128)(2,1)} %get-tuple-element.80), channel_id=1, source_target_pairs={{0,8},{8,16},{16,24},{24,28},{28,20},{20,12},{12,4},{4,0},{1,9},{9... | collective-permute-start | bytes 1966088 | tf_op jit(solution)/shard_map/ppermute | solution.py:48
  (115 other events, 1704.5 us)

commit v2 on v1

v2 whole, which is shorter than its diff:
```python
import functools

import jax
import jax.numpy as jnp
from jax import lax
from jax.experimental import pallas as pl
from jax.experimental.pallas import tpu as pltpu
from jax.sharding import PartitionSpec as P

P_SIZE = 64
N = 128
KERNEL = 4
SPAN = 128
HALO = 8
LANES = 128
EPS = 1e-05
HIGHEST = lax.Precision.HIGHEST
F32 = jnp.float32
BF16 = jnp.bfloat16
VMEM_LIMIT = 50 * 1024 * 1024
NN = (((1,), (0,)), ((), ()))
NT = (((1,), (1,)), ((), ()))
TN = (((0,), (0,)), ((), ()))


def dot(left, right, dims=NN, precision=None):
    return lax.dot_general(left, right, dims, precision=precision, preferred_element_type=F32)


def silu_slope(value, logistic):
    return logistic * (1.0 + value * (1.0 - logistic))


class Ring:
    def __init__(self, size):
        self.size = size
        self.on = size == 8 and lax.axis_size("head") == 4
        self.order = list(range(0, size, 2)) + list(range(size - 1, 0, -2))
        here = lax.axis_index("seq")
        self.line, self.side = here >> 1, here & 1
        self.place = jnp.where(self.side == 0, self.line, size - 1 - self.line)

    def spots(self):
        place = (self.place + jnp.arange(self.size, dtype=jnp.int32)) & (self.size - 1)
        side = place >> 2
        line = jnp.where(side == 1, self.size - 1 - place, place)
        bit = lax.axis_index("head") ^ line
        return 2 * jnp.where(bit == 3, 0, jnp.where(bit == 0, 3, bit)) + side

    def blocks(self):
        spot = jnp.arange(self.size, dtype=jnp.int32)
        side, bit = spot & 1, spot >> 1
        bit = jnp.where(bit == 0, 3, jnp.where(bit == 3, 0, bit))
        line = lax.axis_index("head") ^ bit
        place = jnp.where(side == 1, self.size - 1 - line, line)
        return (place - self.place) & (self.size - 1)

    def shift(self, array, by):
        order, size = self.order, self.size
        return lax.ppermute(array, "seq", [(order[i], order[(i + by) % size]) for i in range(size)])

    def hop(self, moving):
        if not self.on:
            return moving
        return self.shift(moving[0], 1), self.shift(moving[1], -1)

    def last_hop(self, moving):
        if not self.on:
            return moving
        cut = moving[0].shape[0] // 2
        return self.shift(moving[0][:cut], 1), self.shift(moving[1][cut:], -1)

    def part(self, whole, k):
        n = whole.shape[0] // self.size
        k = k % self.size
        return whole[k * n : (k + 1) * n]

    def send(self, whole):
        if not self.on:
            return None
        far = self.part(whole, self.size // 2)
        cut = far.shape[0] // 2
        return self.shift(far[:cut], 1), self.shift(far[cut:], -1)

    def add(self, whole, came, k):
        if not self.on:
            return None
        right, left = self.part(whole, k).astype(F32), self.part(whole, -k).astype(F32)
        first, second = came[0].astype(F32), came[1].astype(F32)
        if k == self.size // 2 - 1:
            cut = first.shape[0]
            right = jnp.concatenate([right[:cut] + first, right[cut:]], axis=0)
            left = jnp.concatenate([left[:cut], left[cut:] + second], axis=0)
        else:
            right, left = right + first, left + second
        return right.astype(BF16), left.astype(BF16)

    def total(self, whole, came):
        if not self.on:
            return lax.psum_scatter(whole, "seq", scatter_dimension=0, tiled=True).astype(F32)
        return self.part(whole, 0).astype(F32) + came[0].astype(F32) + came[1].astype(F32)

    def phase(self, work, *args):
        if not self.on:
            return work(*args)
        shapes = jax.eval_shape(work, *args)

        def idle(*args):
            return jax.tree.map(lambda x: jnp.zeros(x.shape, x.dtype), shapes)

        return lax.cond(lax.axis_index("seq") < self.size, work, idle, *args)


def swap(array, axis, bit):
    size = lax.axis_size(axis)
    return lax.ppermute(array, axis, [(i, i ^ bit) for i in range(size)])


def head_sum(array):
    return lax.psum(array, "head")


def seq_sum(ring, array):
    if not ring.on:
        return lax.psum(array, "seq")
    bit = 1
    while bit < ring.size:
        array = array + swap(array, "seq", bit)
        bit *= 2
    return array


def own_features(ring, block, own_width):
    if not ring.on:
        whole = lax.all_gather(block, "seq", axis=0, tiled=True)
        return lax.dynamic_slice_in_dim(whole, lax.axis_index("head") * own_width, own_width)

    def fetch(flip):
        index = lambda line, side, head: (2 * line + side) * 4 + head
        return lax.ppermute(
            block,
            ("seq", "head"),
            [
                (index(head, side ^ flip, line), index(line, side, head))
                for line in range(4)
                for side in range(2)
                for head in range(4)
            ],
        )

    same, other = fetch(0), fetch(1)
    even = ring.side == 0
    return jnp.concatenate([jnp.where(even, same, other), jnp.where(even, other, same)])


def corner(ring, own, far):
    if not ring.on:
        return lax.all_gather(own, "head", axis=1, tiled=True)
    return swap(far, "head", 1)


def beside(ring, array):
    return swap(array, "head", 1) if ring.on else array


def across(ring, array):
    return swap(array, "head", 2) if ring.on else array


def scatter_near(ring, whole):
    if not ring.on:
        return whole, None
    width = whole.shape[1] // 4
    part = lambda k: whole[:, k * width : (k + 1) * width]
    far = swap(part(0), "head", 1)
    near = swap(part(1), "head", 1)
    far = (part(2).astype(F32) + far.astype(F32)).astype(BF16)
    return far, part(3).astype(F32) + near.astype(F32)


def scatter_sum(ring, far, mine):
    if not ring.on:
        return lax.psum_scatter(far, "head", scatter_dimension=1, tiled=True).astype(F32)
    return mine + far.astype(F32)


def shift_flat(array, by):
    size = lax.axis_size("seq")
    return lax.ppermute(array, "seq", [(i, i + by) for i in range(size) if 0 <= i + by < size])


def states_scan(state, log_decay, direction):
    incl_s, incl_w = state, log_decay
    excl_s, excl_w = jnp.zeros_like(state), jnp.zeros_like(log_decay)
    by = 1
    while by < lax.axis_size("seq"):
        got_s = shift_flat(incl_s.astype(BF16), by * direction).astype(F32)
        got_w = shift_flat(incl_w, by * direction)
        excl_s = jnp.exp(excl_w) * got_s + excl_s
        excl_w = excl_w + got_w
        incl_s = jnp.exp(incl_w) * got_s + incl_s
        incl_w = incl_w + got_w
        by *= 2
    return excl_s


def log_rows(log_decay):
    high = log_decay.astype(BF16).astype(F32)
    middle = (log_decay - high).astype(BF16).astype(F32)
    low = log_decay - high - middle
    row = lax.broadcasted_iota(jnp.int32, (16, log_decay.shape[1]), 0)
    parts = jnp.where(row == 0, high, jnp.where(row == 1, middle, low))
    return jnp.where(row < 3, parts, 0.0).astype(BF16)


def log_sum(rows):
    rows = rows.astype(F32)
    return rows[0:1] + rows[1:2] + rows[2:3]


def pass_begin_kernel(even_ref, lead_ref, state_ref, log_ref, keep_ref, kept_ref, send_ref):
    even = even_ref[0] == 1
    keep_ref[...] = jnp.where(even, state_ref[0], state_ref[1])
    kept_ref[...] = jnp.where(even, log_ref[0], log_ref[1])
    send_ref[:N] = jnp.where(even, state_ref[1], state_ref[0]).astype(BF16)
    send_ref[N:] = log_rows(jnp.where(even, log_ref[1], log_ref[0]))


def pass_pair_kernel(
    even_ref, lead_ref, keep_ref, kept_ref, got_ref, first_ref, d_first_ref, both_ref, pair_ref, send_ref
):
    leads = lead_ref[0] == 1
    keep, kept = keep_ref[...], kept_ref[...]
    got, gotten = got_ref[:N].astype(F32), log_sum(got_ref[N:])
    first = jnp.where(leads, keep, got)
    both = jnp.exp(jnp.where(leads, gotten, kept)) * first + jnp.where(leads, got, keep)
    first_ref[...] = first
    d_first_ref[...] = jnp.exp(jnp.where(leads, kept, gotten))
    both_ref[...] = both
    pair_ref[...] = jnp.exp(kept + gotten)
    send_ref[:N] = both.astype(BF16)
    send_ref[N:] = log_rows(kept + gotten)


def pass_line_kernel(even_ref, lead_ref, both_ref, pair_ref, got_ref, carry_ref, before_ref, send_ref):
    carry = got_ref[:N].astype(F32)
    carry_ref[...] = carry
    before_ref[...] = jnp.exp(log_sum(got_ref[N:]))
    send_ref[...] = (pair_ref[...] * carry + both_ref[...]).astype(BF16)


def pass_far_kernel(
    even_ref, lead_ref, first_ref, d_first_ref, carry_ref, before_ref, got_ref, mine_ref, send_ref
):
    leads = lead_ref[0] == 1
    carry = before_ref[...] * got_ref[...].astype(F32) + carry_ref[...]
    further = d_first_ref[...] * carry + first_ref[...]
    mine_ref[...] = jnp.where(leads, carry, further)
    send_ref[...] = jnp.where(leads, further, carry).astype(BF16)


def pass_end_kernel(even_ref, lead_ref, mine_ref, got_ref, out_ref):
    even = even_ref[0] == 1
    mine, got = mine_ref[...], got_ref[...].astype(F32)
    out_ref[0] = jnp.where(even, mine, got)
    out_ref[1] = jnp.where(even, got, mine)


class Passing:
    def __init__(self, ring, direction, inner):
        self.direction = direction
        leads = ring.side == 0 if direction > 0 else ring.side == 1
        self.flags = [jnp.where(f, 1, 0).astype(jnp.int32).reshape(1) for f in (ring.side == 0, leads)]
        row = shaped(1, inner)
        self.state, self.row = shaped(N, inner), row
        self.sent, self.sent_log = shaped(N, inner, dtype=BF16), shaped(N + 16, inner, dtype=BF16)

    def step(self, kernel, outs, *args):
        return pl.pallas_call(
            kernel,
            in_specs=[pl.BlockSpec(memory_space=pltpu.SMEM)] * 2
            + [pl.BlockSpec(memory_space=pltpu.VMEM)] * len(args),
            out_specs=jax.tree.map(lambda _: pl.BlockSpec(memory_space=pltpu.VMEM), outs),
            out_shape=outs,
            compiler_params=pltpu.CompilerParams(vmem_limit_bytes=VMEM_LIMIT),
        )(*self.flags, *args)

    def begin(self, state, log_decay):
        return self.step(pass_begin_kernel, [self.state, self.row, self.sent_log], state, log_decay)

    def pair(self, held):
        keep, kept, send = held
        got = swap(send, "seq", 1)
        outs = [self.state, self.row, self.state, self.row, self.sent_log]
        return self.step(pass_pair_kernel, outs, keep, kept, got)

    def next_line(self, held):
        first, d_first, both, pair, send = held
        got = shift_flat(send, 2 * self.direction)
        outs = [self.state, self.row, self.sent]
        return (first, d_first, *self.step(pass_line_kernel, outs, both, pair, got))

    def further_lines(self, held):
        first, d_first, carry, before, send = held
        got = shift_flat(send, 4 * self.direction)
        outs = [self.state, self.sent]
        return self.step(pass_far_kernel, outs, first, d_first, carry, before, got)

    def end(self, held):
        mine, send = held
        out = shaped(2, *self.state.shape)
        return self.step(pass_end_kernel, out, mine, swap(send, "seq", 1))


def lane_is_low(rows):
    return lax.broadcasted_iota(jnp.int32, (rows, LANES), 1) < P_SIZE


def spread(columns, j, rows):
    low = jnp.broadcast_to(columns[:, 2 * j : 2 * j + 1], (rows, LANES))
    high = jnp.broadcast_to(columns[:, 2 * j + 1 : 2 * j + 2], (rows, LANES))
    return jnp.where(lane_is_low(rows), low, high), low, high


def triangle(rows, keep):
    first = lax.broadcasted_iota(jnp.int32, (rows, rows), 0)
    second = lax.broadcasted_iota(jnp.int32, (rows, rows), 1)
    return keep(first, second)


def decays(rates, rows):
    lower = triangle(rows, lambda t, s: t >= s)
    within = dot(lower.astype(F32), rates, NN, HIGHEST)
    upper = triangle(rows, lambda s, t: s <= t).astype(F32)
    within_t = dot(rates, upper, TN, HIGHEST)
    return within, within_t, lower


def window(column, row, keep):
    rows = row.shape[1]
    return jnp.exp(jnp.where(keep, column[:, :rows] - row, -1e30))


def scan_kernel(
    pairs, x_ref, bc_ref, halo_ref, dt_ref, cw_ref, bias_ref, rate_ref, skip_ref,
    v_ref, y_ref, st_ref, wc_ref, sb_ref, wo_ref, sl_ref, we_ref,
    hal, state, off, off_l,
):
    rows = x_ref.shape[0]
    inner = pairs * LANES

    @pl.when(pl.program_id(1) == 0)
    def _():
        hal[...] = halo_ref[0]
        state[...] = jnp.zeros_like(state)
        off[...] = jnp.zeros_like(off)
        off_l[...] = jnp.zeros_like(off_l)

    def convolve(ref, at, start):
        now = ref[:, start : start + LANES].astype(F32)
        chunk = jnp.concatenate([hal[:, at : at + LANES], now], axis=0)
        hal[:, at : at + LANES] = now[rows - HALO :]
        shift = HALO - KERNEL + 1
        out = cw_ref[0:1, at : at + LANES] * chunk[shift : shift + rows]
        for k in range(1, KERNEL):
            out = out + cw_ref[k : k + 1, at : at + LANES] * chunk[shift + k : shift + k + rows]
        v_ref[:, at : at + LANES] = out
        return out * jax.nn.sigmoid(out)

    bmat = convolve(bc_ref, inner, 0)
    cmat = convolve(bc_ref, inner + LANES, LANES)
    b_half, c_half = bmat.astype(BF16), cmat.astype(BF16)
    scores = dot(cmat, bmat, NT, HIGHEST)
    steps = jax.nn.softplus(dt_ref[...] + bias_ref[...])
    rates = steps * -rate_ref[...]
    within, within_t, lower = decays(rates, rows)
    low_lanes = lane_is_low(rows)
    st_ref[...] = steps
    wc_ref[...] = off[0:1] + within
    off[0:1] = off[0:1] + within[rows - 1 : rows]
    wo_ref[0] = off_l[0:1]
    for j in range(pairs):
        at = slice(j * LANES, (j + 1) * LANES)
        x = convolve(x_ref, j * LANES, j * LANES)
        u = x * spread(steps, j, rows)[0]
        u_half = u.astype(BF16)
        grow, low, high = spread(within, j, rows)
        end = grow[rows - 1 : rows]
        a_low = (window(low, within_t[2 * j : 2 * j + 1], lower) * scores).astype(BF16)
        a_high = (window(high, within_t[2 * j + 1 : 2 * j + 2], lower) * scores).astype(BF16)
        inside = jnp.where(low_lanes, dot(a_low, u_half), dot(a_high, u_half))
        before = state[:, at]
        carried = jnp.exp(grow) * dot(c_half, before.astype(BF16))
        y_ref[:, at] = inside + carried + skip_ref[0:1, at] * x
        tail = (u * jnp.exp(end - grow)).astype(BF16)
        sb_ref[0, :, at] = before
        after = jnp.exp(end) * before + dot(b_half, tail, TN)
        state[:, at] = after
        sl_ref[0, :, at] = after
        ends = off_l[0:1, at] + end
        off_l[0:1, at] = ends
        we_ref[0, :, at] = ends


def gate_kernel(
    pairs, y_ref, vc_ref, s_ref, wc_ref, zp_ref, dmp_ref, gg_ref, na_ref, ca_ref, wz_ref, wo_ref,
    ssd_ref, sq_ref, z_ref, dm_ref
):
    rows = y_ref.shape[0]
    z_ref[...] = zp_ref[...] + dot(na_ref[...], wz_ref[...])
    dm_ref[...] = dmp_ref[...] + dot(ca_ref[...], wo_ref[...])
    vc = vc_ref[...]
    c_half = (vc * jax.nn.sigmoid(vc)).astype(BF16)
    cumulative = wc_ref[...]
    total = jnp.zeros((rows, LANES), F32)
    meet = jnp.zeros((rows, LANES), F32)
    for j in range(pairs):
        at = slice(j * LANES, (j + 1) * LANES)
        grow = jnp.exp(spread(cumulative, j, rows)[0])
        ssd = y_ref[:, at] + grow * dot(c_half, s_ref[0, :, at].astype(BF16))
        ssd_ref[:, at] = ssd
        z = z_ref[:, at]
        gated = ssd * (z * jax.nn.sigmoid(z))
        total = total + gated * gated
        meet = meet + dm_ref[:, at] * gg_ref[0:1, at] * gated
    sq_ref[0, 0:1] = jnp.sum(total.T, axis=0, keepdims=True)
    sq_ref[0, 1:2] = jnp.sum(meet.T, axis=0, keepdims=True)


def as_column(row):
    return jnp.broadcast_to(row, (LANES, row.shape[1])).T


def gate_back_kernel(
    pairs, width, dmp_ref, ssd_ref, zp_ref, gs_ref, ip_ref, gg_ref, wc_ref, vc_ref,
    na_ref, ca_ref, wz_ref, wo_ref,
    dz_ref, dy_ref, ds_ref, zz_ref, gate_ref, mixed_ref, z_ref, dm_ref,
):
    rows = dmp_ref.shape[0]
    z_ref[...] = zp_ref[...] + dot(na_ref[...], wz_ref[...])
    dm_ref[...] = dmp_ref[...] + dot(ca_ref[...], wo_ref[...])

    @pl.when(pl.program_id(1) == 0)
    def _():
        ds_ref[...] = jnp.zeros_like(ds_ref)

    @pl.when((pl.program_id(0) == 0) & (pl.program_id(1) == 0))
    def _():
        gate_ref[...] = jnp.zeros_like(gate_ref)

    scale = as_column(gs_ref[0])
    pull = as_column(gs_ref[0] * gs_ref[0] * gs_ref[0] * ip_ref[0] * (1.0 / width))
    vc = vc_ref[...]
    c_half = (vc * jax.nn.sigmoid(vc)).astype(BF16)
    cumulative = wc_ref[...]
    total = jnp.zeros((rows, LANES), F32)
    for j in range(pairs):
        at = slice(j * LANES, (j + 1) * LANES)
        z = z_ref[:, at]
        ssd = ssd_ref[:, at]
        logistic = jax.nn.sigmoid(z)
        opened = z * logistic
        gated = ssd * opened
        mixed_ref[:, at] = (gated * scale * gg_ref[0:1, at]).astype(BF16)
        scaled = scale * dm_ref[:, at]
        gate_ref[0:1, at] += jnp.sum(scaled * gated, axis=0, keepdims=True)
        d_gated = scaled * gg_ref[0:1, at] - gated * pull
        d_z = (d_gated * ssd * silu_slope(z, logistic)).astype(BF16)
        dz_ref[:, at] = d_z
        total = total + d_z.astype(F32) * z
        dy = d_gated * opened
        dy_ref[:, at] = dy
        grown = (jnp.exp(spread(cumulative, j, rows)[0]) * dy).astype(BF16)
        ds_ref[0, :, at] += dot(c_half, grown, TN)
    zz_ref[0] = jnp.sum(total.T, axis=0, keepdims=True)


def scan_back_kernel(
    pairs, v_ref, dy_ref, st_ref, rate_ref, sb_ref, wo_ref, s_ref,
    du_ref, dbc_ref, grad,
):
    rows = v_ref.shape[0]
    inner = pairs * LANES

    @pl.when(pl.program_id(1) == 0)
    def _():
        grad[...] = jnp.zeros_like(grad)

    def act(at):
        value = v_ref[:, at : at + LANES]
        return value * jax.nn.sigmoid(value)

    bmat, cmat = act(inner), act(inner + LANES)
    b_half, c_half = bmat.astype(BF16), cmat.astype(BF16)
    scores = dot(cmat, bmat, NT, HIGHEST)
    steps = st_ref[...]
    rates = steps * -rate_ref[...]
    within, within_t, lower = decays(rates, rows)
    low_lanes = lane_is_low(rows)
    d_c = jnp.zeros((rows, LANES), F32)
    d_b = jnp.zeros((rows, LANES), F32)
    d_scores = jnp.zeros((rows, rows), F32)
    none = jnp.zeros((rows, LANES), BF16)
    for j in range(pairs):
        at = slice(j * LANES, (j + 1) * LANES)
        x = act(j * LANES)
        u = x * spread(steps, j, rows)[0]
        u_half = u.astype(BF16)
        dy = dy_ref[:, at]
        dy_half = dy.astype(BF16)
        grow, low, high = spread(within, j, rows)
        end = grow[rows - 1 : rows]
        back = jnp.exp(end - grow)
        grown = (jnp.exp(grow) * dy).astype(BF16)
        begun = sb_ref[0, :, at] + jnp.exp(wo_ref[0, :, at]) * s_ref[0, :, at]
        d_c = d_c + dot(grown, begun.astype(BF16), NT)
        later = grad[:, at]
        later_half = later.astype(BF16)
        d_b = d_b + dot((u * back).astype(BF16), later_half, NT)
        w_low = window(low, within_t[2 * j : 2 * j + 1], lower)
        w_high = window(high, within_t[2 * j + 1 : 2 * j + 2], lower)
        d_scores = d_scores + w_low * dot(jnp.where(low_lanes, dy_half, none), u_half, NT)
        d_scores = d_scores + w_high * dot(jnp.where(low_lanes, none, dy_half), u_half, NT)
        a_low = (w_low * scores).astype(BF16)
        a_high = (w_high * scores).astype(BF16)
        inside = jnp.where(low_lanes, dot(a_low, dy_half, TN), dot(a_high, dy_half, TN))
        du_ref[:, at] = inside + back * dot(b_half, later_half)
        grad[:, at] = jnp.exp(end) * later + dot(c_half, grown, TN)
    d_half = d_scores.astype(BF16)
    dbc_ref[:, :LANES] = d_b + dot(d_half, c_half, TN)
    dbc_ref[:, LANES:] = d_c + dot(d_half, b_half)


def put_split(ref, at, value):
    rows = value.shape[0]
    high = value.astype(BF16)
    ref[:rows, at] = high
    ref[rows : 2 * rows, at] = (value - high.astype(F32)).astype(BF16)


def per_head(ref, picker, rows):
    both = dot(ref[: 2 * rows], picker)
    return both[:rows] + both[rows:]


def finish_kernel(
    pairs, v_ref, dy_ref, du_ref, ssd_ref, st_ref, wc_ref, we_ref, la_ref, se_ref, dbc_ref,
    dt_ref, bias_ref, rate_ref, skip_ref, pick_ref,
    dcx_ref, dbo_ref, ddt_ref, dskip_ref, dhead_ref, run, moves, drives,
):
    rows = v_ref.shape[0]
    inner = pairs * LANES
    picker = pick_ref[...]

    @pl.when((pl.program_id(0) == 0) & (pl.program_id(1) == 0))
    def _():
        dskip_ref[...] = jnp.zeros_like(dskip_ref)
        dhead_ref[...] = jnp.zeros_like(dhead_ref)

    @pl.when(pl.program_id(1) == 0)
    def _():
        for j in range(pairs):
            at = slice(j * LANES, (j + 1) * LANES)
            both = jnp.sum(la_ref[0, :, at] * se_ref[0, :, at], axis=0, keepdims=True)
            put_split(moves, at, jnp.broadcast_to(both, (rows, LANES)))
        run[...] = per_head(moves, picker, rows)[0:8]

    value_b = v_ref[:, inner : inner + LANES]
    b_half = (value_b * jax.nn.sigmoid(value_b)).astype(BF16)
    steps = st_ref[...]
    cumulative = wc_ref[...]
    d_b = dbc_ref[:, :LANES]
    for j in range(pairs):
        at = slice(j * LANES, (j + 1) * LANES)
        value = v_ref[:, at]
        logistic = jax.nn.sigmoid(value)
        x = value * logistic
        wide = spread(steps, j, rows)[0]
        u = x * wide
        dy = dy_ref[:, at]
        skip = skip_ref[0:1, at]
        tail = jnp.exp(we_ref[0, :, at] - spread(cumulative, j, rows)[0])
        later = la_ref[0, :, at].astype(BF16)
        du = du_ref[:, at] + tail * dot(b_half, later)
        d_b = d_b + dot((u * tail).astype(BF16), later, NT)
        put_split(moves, at, dy * (ssd_ref[:, at] - skip * x) - u * du)
        put_split(drives, at, x * du)
        dskip_ref[0:1, at] += jnp.sum(dy * x, axis=0, keepdims=True)
        d_inner = wide * du + skip * dy
        dcx_ref[:, at] = (d_inner * silu_slope(value, logistic)).astype(BF16)
    dbo_ref[:, :LANES] = d_b
    dbo_ref[:, LANES:] = dbc_ref[:, LANES:]
    moved = per_head(moves, picker, rows)
    driven = per_head(drives, picker, rows)
    upper = triangle(rows, lambda t, s: s >= t).astype(F32)
    d_rates = dot(upper, moved, NN, HIGHEST) + run[0:1]
    run[0:1] = d_rates[0:1]
    d_steps = driven - rate_ref[...] * d_rates
    d_raw = d_steps * jax.nn.sigmoid(dt_ref[...] + bias_ref[...])
    ddt_ref[...] = d_raw.astype(BF16)
    dhead_ref[0:1] += jnp.sum(d_raw, axis=0, keepdims=True)
    dhead_ref[1:2] -= jnp.sum(steps * d_rates, axis=0, keepdims=True)


def conv_back_kernel(d_ref, in_ref, halo_ref, cw_ref, dx_ref, gw_ref, xx_ref, hal):
    rows, width = d_ref.shape

    @pl.when((pl.program_id(0) == 0) & (pl.program_id(1) == 0))
    def _():
        gw_ref[...] = jnp.zeros_like(gw_ref)

    @pl.when(pl.program_id(1) == 0)
    def _():
        hal[...] = halo_ref[0]

    meet = jnp.zeros((rows, LANES), F32)
    for c in range(width // LANES):
        at = slice(c * LANES, (c + 1) * LANES)
        now = d_ref[:, at].astype(F32)
        chunk = jnp.concatenate([now, hal[:, at]], axis=0)
        hal[:, at] = now[:HALO]
        given = in_ref[:, at].astype(F32)
        total = jnp.zeros((rows, LANES), F32)
        for k in range(KERNEL):
            moved = chunk[KERNEL - 1 - k : KERNEL - 1 - k + rows]
            total = total + cw_ref[k : k + 1, at] * moved
            gw_ref[k : k + 1, at] += jnp.sum(given * moved, axis=0, keepdims=True)
        d_x = total.astype(BF16)
        dx_ref[:, at] = d_x
        meet = meet + d_x.astype(F32) * given
    xx_ref[0] = jnp.sum(meet.T, axis=0, keepdims=True)


def place_blocks(spot_ref, target, items, down, along=slice(None)):
    order = [0]
    for k in range(1, 4):
        order += [8 - k, k]

    rows = down.stop - down.start

    def put(k, shift, block):
        at = pl.multiple_of(spot_ref[k] * rows + shift, LANES)
        target[pl.ds(at, block.shape[0]), :] = block

    for k, item in zip(order, items):
        put(k, 0, item[down, along])
    return put


def in_project_kernel(spot_ref, *refs):
    acts, items, halves = refs[:4], refs[4:11], refs[11:13]
    x_ref, bc_ref, dt_ref, w_ref, r_ref = refs[13:]
    rows = items[0].shape[0]
    inner = x_ref.shape[1]

    @pl.when(pl.program_id(0) == 0)
    def _():
        for target, cut in ((w_ref, slice(0, inner)), (r_ref, slice(inner, None))):
            put = place_blocks(spot_ref, target, items, slice(0, rows), cut)
            put(4, 0, halves[0][:, cut])
            put(4, rows // 2, halves[1][:, cut])

    act = jnp.concatenate([a[...] for a in acts], axis=1)
    x_ref[...] = dot(act, w_ref[...]).astype(BF16)
    rest = dot(act, r_ref[...])
    bc_ref[...] = rest[:, : 2 * N].astype(BF16)
    dt_ref[...] = rest[:, 2 * N :]


def gate_project_kernel(spot_ref, *refs):
    acts, cots, items = refs[:4], refs[4:8], refs[8:15]
    z_ref, dm_ref, wz_ref, wo_ref, na_ref, ca_ref = refs[15:]
    rows = items[0].shape[0] // 2
    last = spot_ref[4]

    @pl.when(pl.program_id(0) == 0)
    def _():
        for target, down in ((wz_ref, slice(0, rows)), (wo_ref, slice(rows, 2 * rows))):
            put = place_blocks(spot_ref, target, items, down)
            put(4, 0, jnp.zeros((rows, target.shape[1]), BF16))

    for i in range(8):

        @pl.when(last == i)
        def _():
            cut = slice((i % 2) * rows, (i % 2 + 1) * rows)
            na_ref[...] = acts[i // 2][:, cut]
            ca_ref[...] = cots[i // 2][:, cut]

    z_ref[...] = dot(jnp.concatenate([a[...] for a in acts], axis=1), wz_ref[...])
    dm_ref[...] = dot(jnp.concatenate([a[...] for a in cots], axis=1), wo_ref[...])


def with_spots(kernel, spots, acts, items, outs, shapes):
    total, width = acts[0].shape
    rows = min(256, total)
    fixed = lambda i, spot: (0, 0)
    return pl.pallas_call(
        kernel,
        grid_spec=pltpu.PrefetchScalarGridSpec(
            num_scalar_prefetch=1,
            grid=(total // rows,),
            in_specs=[pl.BlockSpec((rows, width), lambda i, spot: (i, 0)) for _ in acts]
            + [pl.BlockSpec(item.shape, fixed) for item in items],
            out_specs=[
                pl.BlockSpec((rows, shape.shape[1]), lambda i, spot: (i, 0)) if split
                else pl.BlockSpec(shape.shape, fixed)
                for shape, split in zip(shapes, outs)
            ],
        ),
        out_shape=shapes,
        compiler_params=pltpu.CompilerParams(vmem_limit_bytes=VMEM_LIMIT),
    )(spots, *acts, *items)


def outer_kernel(pairs_of, block_ref, *refs):
    out_ref = refs[-1]
    n = len(pairs_of)
    grads = refs[4 * n : -1]
    width = refs[0].shape[1]
    for a in range(4):

        @pl.when(pl.program_id(0) // 2 == a)
        def _():
            taken = 0
            for i, count in enumerate(pairs_of):
                start = 0
                for grad in grads[taken : taken + count]:
                    wide = grad.shape[1]
                    out_ref[i * width : (i + 1) * width, start : start + wide] = dot(
                        refs[4 * i + a][...], grad[...], TN
                    ).astype(BF16)
                    start += wide
                taken += count


def outer(blocks, *terms):
    total, own = terms[0][0][0].shape
    width = own // 2
    specs, args = [], []
    for acts, _ in terms:
        for a, act in enumerate(acts):
            specs.append(
                pl.BlockSpec((total, width), lambda i, _, a=a: (0, jnp.clip(i - 2 * a, 0, 1)))
            )
            args.append(act)
    for _, grads in terms:
        for grad in grads:
            specs.append(pl.BlockSpec(grad.shape, lambda i, _: (0, 0)))
            args.append(grad)
    columns = sum(g.shape[1] for g in terms[0][1])
    rows = width * len(terms)
    return pl.pallas_call(
        functools.partial(outer_kernel, [len(grads) for _, grads in terms]),
        grid_spec=pltpu.PrefetchScalarGridSpec(
            num_scalar_prefetch=1,
            grid=(8,),
            in_specs=specs,
            out_specs=pl.BlockSpec((rows, columns), lambda i, block: (block[i], 0)),
        ),
        out_shape=shaped(8 * rows, columns, dtype=BF16),
        compiler_params=pltpu.CompilerParams(vmem_limit_bytes=VMEM_LIMIT),
    )(blocks, *args)


def project_kernel(terms, late, spot_ref, *refs):
    out_ref = refs[-1]
    total = None
    for k in range(terms):
        weight = refs[terms + k][...]
        if k < late:
            weight = jnp.where(pl.program_id(0) == spot_ref[4], refs[2 * terms + k][...], weight)
        term = dot(refs[k][...], weight, NT)
        total = term if total is None else total + term
    out_ref[...] = total.astype(out_ref.dtype)


def project(ring, spots, acts, weights, late=()):
    if not ring.on:
        return sum(dot(a, w, NT) for a, w in zip(acts, weights)).astype(BF16)
    rows, width = acts[0].shape[0], 256
    whole = lambda i, spot: (0, 0)
    return pl.pallas_call(
        functools.partial(project_kernel, len(acts), len(late)),
        grid_spec=pltpu.PrefetchScalarGridSpec(
            num_scalar_prefetch=1,
            grid=(weights[0].shape[0] // width,),
            in_specs=[pl.BlockSpec(a.shape, whole) for a in acts]
            + [pl.BlockSpec((width, w.shape[1]), lambda i, spot: (i, 0)) for w in weights]
            + [pl.BlockSpec(w.shape, whole) for w in late],
            out_specs=pl.BlockSpec((rows, width), lambda i, spot: (0, i)),
        ),
        out_shape=shaped(rows, weights[0].shape[0], dtype=BF16),
        compiler_params=pltpu.CompilerParams(vmem_limit_bytes=VMEM_LIMIT),
    )(spots, *acts, *weights, *late)


def shaped(*shape, dtype=F32):
    return jax.ShapeDtypeStruct(shape, dtype)


def call(kernel, grid, ins, outs, shapes, scratch=(), micros=5.0):
    return pl.pallas_call(
        kernel,
        grid=grid,
        in_specs=ins,
        out_specs=outs,
        out_shape=shapes,
        scratch_shapes=list(scratch),
        compiler_params=pltpu.CompilerParams(vmem_limit_bytes=VMEM_LIMIT),
        cost_estimate=pl.CostEstimate(
            flops=0, bytes_accessed=int(micros * 3.3e6), transcendentals=0
        ),
    )


def conv_back(d_conv, given, after, taps, batch, length, rows):
    width = d_conv.shape[1]
    count = length // rows
    turn = lambda b, i: (b * count + count - 1 - i, 0)
    block = pl.BlockSpec((rows, width), turn)
    total = batch * length
    return call(
        conv_back_kernel,
        (batch, count),
        [
            block,
            block,
            pl.BlockSpec((1, HALO, width), lambda b, i: (b, 0, 0)),
            pl.BlockSpec((KERNEL, width), lambda b, i: (0, 0)),
        ],
        [
            block,
            pl.BlockSpec((KERNEL, width), lambda b, i: (0, 0)),
            pl.BlockSpec((1, 1, rows), lambda b, i: (b * count + count - 1 - i, 0, 0)),
        ],
        [
            shaped(total, width, dtype=BF16),
            shaped(KERNEL, width),
            shaped(batch * count, 1, rows),
        ],
        [pltpu.VMEM((HALO, width), F32)],
        micros=8.0 * total * width / 2**20,
    )(d_conv, given, after, taps)


def body(
    tokens, norm_gain, w_z, w_x, w_bc, w_dt, conv_x, conv_bc, dt_bias, decay_rate,
    skip_gain, gate_gain, w_out, grad_out,
):
    ring = Ring(lax.axis_size("seq"))
    batch, length, own_width = tokens.shape
    model = norm_gain.shape[0] * ring.size
    total = batch * length
    inner = w_z.shape[1]
    heads = dt_bias.shape[0]
    inner_all = inner * lax.axis_size("head")
    pairs = heads // 2
    rows = min(SPAN, length)
    count = length // rows
    blocks = batch * count
    margin = KERNEL - 1
    here = lax.axis_index("head")

    slab = tokens.reshape(total, own_width)
    cot_rows = grad_out.reshape(total, own_width)
    bias_row = dt_bias.reshape(1, heads)
    rate_row = decay_rate.reshape(1, heads)
    skip_lanes = jnp.repeat(skip_gain, P_SIZE).reshape(1, inner)
    gate_f = gate_gain.astype(F32).reshape(1, inner)
    conv_xf = conv_x.astype(F32)
    conv_bcf = conv_bc.astype(F32)
    conv_w = jnp.concatenate([conv_xf, conv_bcf], axis=1)

    def edge(arrays, last):
        cut = [array.reshape(batch, length, -1) for array in arrays]
        cut = [array[:, length - margin :] if last else array[:, :margin] for array in cut]
        cut = jnp.concatenate(cut, axis=2)
        moves = [(i, i + 1) for i in range(ring.size - 1)]
        if not last:
            moves = [(b, a) for a, b in moves]
        got = lax.ppermute(cut, "seq", moves).astype(F32)
        pad = ((0, 0), (HALO - margin, 0), (0, 0)) if last else ((0, 0), (0, HALO - margin), (0, 0))
        return jnp.pad(got, pad)

    at = lambda b, i: (b * count + i, 0)
    back = lambda b, i: (b * count + count - 1 - i, 0)
    at3 = lambda b, i: (b * count + i, 0, 0)
    back3 = lambda b, i: (b * count + count - 1 - i, 0, 0)
    seq3 = lambda b, i: (b, 0, 0)
    fixed = lambda b, i: (0, 0)
    row_heads = pl.BlockSpec((1, heads), fixed)
    row_inner = pl.BlockSpec((1, inner), fixed)
    state_spec = pl.BlockSpec((1, N, inner), seq3)
    pair_flops = total * rows * inner

    block_spec = pl.BlockSpec((rows, inner), at)
    row_out = pl.BlockSpec((1, 1, rows), at3)
    c_spec = pl.BlockSpec((rows, LANES), lambda b, i: (b * count + i, inner // LANES + 1))
    head_cols = pl.BlockSpec((rows, heads), at)
    v_back = pl.BlockSpec((rows, inner + 2 * N), back)
    block_back = pl.BlockSpec((rows, inner), back)
    heads_back = pl.BlockSpec((rows, heads), back)
    bc_back = pl.BlockSpec((rows, 2 * N), back)
    def scan(x_in, bc_in, halo, dt_raw):
        conv_out, y_local, steps, cumulative, begun, offsets, left, left_w = call(
            functools.partial(scan_kernel, pairs),
            (batch, count),
            [
                pl.BlockSpec((rows, inner), at),
                pl.BlockSpec((rows, 2 * N), at),
                pl.BlockSpec((1, HALO, inner + 2 * N), seq3),
                pl.BlockSpec((rows, heads), at),
                pl.BlockSpec((KERNEL, inner + 2 * N), fixed),
                row_heads,
                row_heads,
                row_inner,
            ],
            [
                pl.BlockSpec((rows, inner + 2 * N), at),
                pl.BlockSpec((rows, inner), at),
                pl.BlockSpec((rows, heads), at),
                pl.BlockSpec((rows, heads), at),
                pl.BlockSpec((1, N, inner), at3),
                pl.BlockSpec((1, 1, inner), at3),
                state_spec,
                pl.BlockSpec((1, 1, inner), seq3),
            ],
            [
                shaped(total, inner + 2 * N),
                shaped(total, inner),
                shaped(total, heads),
                shaped(total, heads),
                shaped(blocks, N, inner),
                shaped(blocks, 1, inner),
                shaped(batch, N, inner),
                shaped(batch, 1, inner),
            ],
            [
                pltpu.VMEM((HALO, inner + 2 * N), F32),
                pltpu.VMEM((N, inner), F32),
                pltpu.VMEM((8, heads), F32),
                pltpu.VMEM((8, inner), F32),
            ],
            micros=14.5,
        )(x_in, bc_in, halo, dt_raw, conv_w, bias_row, rate_row, skip_lanes)
        return conv_out, y_local, steps, cumulative, begun, offsets, left, left_w

    own_block = model // ring.size
    act_spec = pl.BlockSpec((rows, own_block), at)
    late_spec = pl.BlockSpec((own_block, inner), fixed)
    wide_scratch = [pltpu.VMEM((rows, inner), F32), pltpu.VMEM((rows, inner), F32)]

    def gate(y_local, conv_out, came, cumulative, z_part, dm_part, late):
        return call(
            functools.partial(gate_kernel, pairs),
            (batch, count),
            [
                block_spec, c_spec, state_spec, head_cols, block_spec, block_spec, row_inner,
                act_spec, act_spec, late_spec, late_spec,
            ],
            [block_spec, pl.BlockSpec((1, 2, rows), at3)],
            [shaped(total, inner), shaped(blocks, 2, rows)],
            wide_scratch,
            micros=7.0,
        )(y_local, conv_out, came, cumulative, z_part, dm_part, gate_f, *late)

    def gate_back(dm_part, ssd, z_part, gate_scale, product, cumulative, conv_out, late):
        return call(
            functools.partial(gate_back_kernel, pairs, inner_all),
            (batch, count),
            [
                block_spec, block_spec, block_spec, row_out, row_out, row_inner, head_cols, c_spec,
                act_spec, act_spec, late_spec, late_spec,
            ],
            [block_spec, block_spec, state_spec, row_out, row_inner, block_spec],
            [
                shaped(total, inner, dtype=BF16),
                shaped(total, inner),
                shaped(batch, N, inner),
                shaped(blocks, 1, rows),
                shaped(1, inner),
                shaped(total, inner, dtype=BF16),
            ],
            wide_scratch,
            micros=9.0,
        )(dm_part, ssd, z_part, gate_scale, product, gate_f, cumulative, conv_out, *late)

    def scan_back(conv_out, d_ssd, steps, begun, offsets, came):
        du_local, dbc_local = call(
            functools.partial(scan_back_kernel, pairs),
            (batch, count),
            [
                v_back, block_back, heads_back, row_heads,
                pl.BlockSpec((1, N, inner), back3),
                pl.BlockSpec((1, 1, inner), back3),
                state_spec,
            ],
            [block_back, bc_back],
            [shaped(total, inner), shaped(total, 2 * N)],
            [pltpu.VMEM((N, inner), F32)],
            micros=18.0,
        )(conv_out, d_ssd, steps, rate_row, begun, offsets, came)
        return du_local, dbc_local

    def finish(conv_out, d_ssd, du_local, ssd, steps, cumulative, left_w, later, came, left, dbc_local, dt_raw):
        lane_head = lax.broadcasted_iota(jnp.int32, (inner, heads), 0) // P_SIZE
        picker = (lane_head == lax.broadcasted_iota(jnp.int32, (inner, heads), 1)).astype(BF16)
        at_end = jnp.exp(left_w) * came + left
        d_conv_x, d_bc_part, d_dt, g_skip, g_heads = call(
            functools.partial(finish_kernel, pairs),
            (batch, count),
            [
                v_back, block_back, block_back, block_back, heads_back, heads_back,
                pl.BlockSpec((1, 1, inner), seq3), state_spec, state_spec, bc_back, heads_back,
                row_heads, row_heads, row_inner,
                pl.BlockSpec((inner, heads), fixed),
            ],
            [
                block_back, bc_back, heads_back, row_inner,
                pl.BlockSpec((2, heads), fixed),
            ],
            [
                shaped(total, inner, dtype=BF16),
                shaped(total, 2 * N),
                shaped(total, heads, dtype=BF16),
                shaped(1, inner),
                shaped(2, heads),
            ],
            [
                pltpu.VMEM((8, heads), F32),
                pltpu.VMEM((2 * rows, inner), BF16),
                pltpu.VMEM((2 * rows, inner), BF16),
            ],
            micros=15.0,
        )(
            conv_out, d_ssd, du_local, ssd, steps, cumulative, left_w, later, at_end, dbc_local,
            dt_raw, bias_row, rate_row, skip_lanes, picker,
        )
        return d_conv_x, d_bc_part, d_dt, g_skip, g_heads

    split_pass = ring.on and batch == 2
    forth, back_pass = Passing(ring, 1, inner), Passing(ring, -1, inner)
    slope = lambda v: silu_slope(v, jax.nn.sigmoid(v))

    edge_at = inner + 2 * N
    spare = -(2 * N + heads) % LANES
    per = w_z.shape[0]
    all_in = jnp.concatenate(
        [w_x, w_bc, w_dt, jnp.zeros((w_x.shape[0], spare), BF16)], axis=1
    )
    spots, order = (ring.spots(), ring.blocks()) if ring.on else (None, None)

    def work(all_in, slab):
        own_gain = own_features(ring, norm_gain.astype(F32), own_width)
        block = all_in + 0.0 * own_gain[:1].astype(BF16)
        square = head_sum(jnp.sum(slab * slab, axis=1))
        scale = lax.rsqrt(square / model + EPS)
        own_normed = (slab * scale[:, None] * own_gain).astype(BF16)
        return ring.hop((block, block)), own_gain, scale, own_normed

    hop1, own_gain, scale, own_normed = ring.phase(work, all_in, slab)
    far = across(ring, own_normed)

    def work(hop1, own, w_z, w_out, cot_rows):
        zo_in = jnp.concatenate([w_z, w_out.T], axis=0)
        return ring.hop(hop1), beside(ring, own), zo_in, cot_rows.astype(BF16)

    hop2, near, zo_in, own_cot = ring.phase(work, hop1, own_normed, w_z, w_out, cot_rows)
    hop3 = ring.phase(ring.hop, hop2)
    hop4, both = ring.phase(
        lambda hop3, far: (ring.last_hop(hop3), corner(ring, own_normed, far)), hop3, far
    )
    normed = (both, near, far, own_normed) if ring.on else (both,)

    def work(normed, hop1, hop2, hop3, hop4, zo_in):
        moving = ring.hop((zo_in, zo_in))
        if ring.on:
            x_in, bc_in, dt_raw, x_w, rest_w = with_spots(
                in_project_kernel, spots, normed, [all_in, *hop1, *hop2, *hop3, *hop4],
                [True, True, True, False, False],
                [
                    shaped(total, inner, dtype=BF16), shaped(total, 2 * N, dtype=BF16),
                    shaped(total, all_in.shape[1] - edge_at), shaped(model, inner, dtype=BF16),
                    shaped(model, all_in.shape[1] - inner, dtype=BF16),
                ],
            )
        else:
            x_w = lax.all_gather(w_x, "seq", axis=0, tiled=True)
            rest_w = lax.all_gather(all_in[:, inner:], "seq", axis=0, tiled=True)
            rest = dot(normed[0], rest_w)
            x_in, bc_in = dot(normed[0], x_w).astype(BF16), rest[:, : 2 * N].astype(BF16)
            dt_raw = rest[:, 2 * N :]
        return moving, x_in, bc_in, dt_raw[:, :heads], x_w, rest_w, edge([x_in, bc_in], True)

    hop1, x_in, bc_in, dt_raw, x_w, rest_w, halo = ring.phase(
        work, normed, hop1, hop2, hop3, hop4, zo_in
    )

    def work(hop1, x_in, bc_in, halo, dt_raw, own_cot):
        scanned = scan(x_in, bc_in, halo, dt_raw)
        held = forth.pair(forth.begin(scanned[6], scanned[7])) if split_pass else ()
        return ring.hop(hop1), scanned, held, beside(ring, own_cot), across(ring, own_cot)

    hop2, scanned, held, near, far = ring.phase(work, hop1, x_in, bc_in, halo, dt_raw, own_cot)
    conv_out, y_local, steps, cumulative, begun, offsets, left, left_w = scanned
    first = jnp.where(here == 0, 1.0, 0.0)
    once = lax.broadcasted_iota(jnp.int32, (1, all_in.shape[1]), 1)
    once = jnp.where((once < inner) | (once >= edge_at), 1.0, first)

    def work(hop2, held, far, rest_w):
        held = forth.next_line(held) if split_pass else ()
        return ring.hop(hop2), held, corner(ring, own_cot, far), rest_w * once[:, inner:].astype(BF16)

    hop3, held, both, rest_once = ring.phase(work, hop2, held, far, rest_w)
    cot = (both, near, far, own_cot) if ring.on else (both,)

    def work(hop1, hop2, hop3, held, normed, cot):
        held = forth.further_lines(held) if split_pass else ()
        if ring.on:
            wide, weight = shaped(total, inner), shaped(model, inner, dtype=BF16)
            act = shaped(total, own_block, dtype=BF16)
            given = with_spots(
                gate_project_kernel, spots, (*normed, *cot), [zo_in, *hop1, *hop2, *hop3],
                [True, True, False, False, True, True], [wide, wide, weight, weight, act, act],
            )
        else:
            z_w = lax.all_gather(w_z, "seq", axis=0, tiled=True)
            out_w = lax.all_gather(w_out.T, "seq", axis=0, tiled=True)
            none = jnp.zeros((total, own_block), BF16)
            given = dot(normed[0], z_w), dot(cot[0], out_w), z_w, out_w, none, none
        return ring.last_hop(hop3), held, given

    hop4, held, given = ring.phase(work, hop1, hop2, hop3, held, normed, cot)
    z_part, dm_part, z_w, out_w, normed_last, cot_last = given
    if not ring.on:
        hop4 = (jnp.zeros((own_block, inner), BF16),) * 2
    late = (normed_last, cot_last, *hop4)
    came = ring.phase(
        lambda held: forth.end(held) if split_pass else states_scan(left, left_w, 1), held
    )

    ssd, square_g = gate(y_local, conv_out, came, cumulative, z_part, dm_part, late)
    square_g = head_sum(square_g)
    gate_scale = lax.rsqrt(square_g[:, 0:1] / inner_all + EPS)
    product = square_g[:, 1:2]
    d_z, d_ssd, d_left, met_z, g_gate, mixed = gate_back(
        dm_part, ssd, z_part, gate_scale, product, cumulative, conv_out, late
    )

    def work(d_left, left_w, normed, d_z, mixed, cot):
        held = back_pass.pair(back_pass.begin(d_left, left_w)) if split_pass else ()
        if ring.on:
            g_zo = outer(order, (normed, [d_z]), (cot, [mixed]))
        else:
            g_zo = (dot(normed[0], d_z, TN), dot(cot[0], mixed, TN))
        return held, g_zo

    held, g_zo = ring.phase(work, d_left, left_w, normed, d_z, mixed, cot)

    def work(held, g_zo, conv_out, d_ssd, steps, begun, offsets, came):
        sent = ring.send(g_zo)
        held = back_pass.next_line(held) if split_pass else ()
        back = scan_back(conv_out, d_ssd, steps, begun, offsets, came)
        return held, ring.add(g_zo, sent, 3), back

    held, sums, (du_local, dbc_local) = ring.phase(
        work, held, g_zo, conv_out, d_ssd, steps, begun, offsets, came
    )

    def work(held, mixed, out_w, late_w):
        held = back_pass.further_lines(held) if split_pass else ()
        return held, project(ring, spots, [mixed], [out_w], [late_w])

    held, branch = ring.phase(work, held, mixed, out_w, hop4[1])

    def work(held, branch):
        later = back_pass.end(held) if split_pass else states_scan(d_left, left_w, -1)
        return later, scatter_near(ring, branch)

    later, (out_far, out_own) = ring.phase(work, held, branch)

    def work(later, sums, g_zo, du_local, dbc_local):
        sums = ring.hop(sums)
        d_conv_x, d_bc_part, d_dt, g_skip, g_heads = finish(
            conv_out, d_ssd, du_local, ssd, steps, cumulative, left_w, later, came, left,
            dbc_local, dt_raw,
        )
        after_x = edge([d_conv_x], False)
        v_bc = conv_out[:, inner:]
        if ring.on:
            half, quarter = total // 2, total // 4
            low, high = here & 1, here >> 1
            cut = lambda a, at, n: lax.dynamic_slice_in_dim(a, at, n, 0)
            mine = cut(d_bc_part, low * half, half)
            mine = mine + swap(cut(d_bc_part, (1 - low) * half, half), "head", 1)
            given = swap(cut(mine, (1 - high) * quarter, quarter), "head", 2)
            mine = cut(mine, high * quarter, quarter) + given
            mine = (mine * slope(cut(v_bc, low * half + high * quarter, quarter))).astype(BF16)
            given = swap(mine, "head", 2)
            mine = jnp.where(
                high == 0, jnp.concatenate([mine, given], 0), jnp.concatenate([given, mine], 0)
            )
            given = swap(mine, "head", 1)
            d_conv_bc = jnp.where(
                low == 0, jnp.concatenate([mine, given], 0), jnp.concatenate([given, mine], 0)
            )
        else:
            d_conv_bc = (head_sum(d_bc_part) * slope(v_bc)).astype(BF16)
        after_bc = edge([d_conv_bc], False)
        sums = ring.add(g_zo, sums, 2)
        return sums, d_conv_x, after_x, d_conv_bc, after_bc, d_dt, g_skip, g_heads

    sums, d_conv_x, after_x, d_conv_bc, after_bc, d_dt, g_skip, g_heads = ring.phase(
        work, later, sums, g_zo, du_local, dbc_local
    )
    out_far = across(ring, out_far)

    def work(sums, g_zo, d_conv_x, after_x, d_conv_bc, after_bc, d_dt, normed):
        sums = ring.add(g_zo, ring.hop(sums), 1)
        d_x, g_conv_x, met_x = conv_back(d_conv_x, x_in, after_x, conv_xf, batch, length, rows)
        d_bc, g_conv_bc, met_bc = conv_back(
            d_conv_bc, bc_in, after_bc, conv_bcf, batch, length, rows
        )
        fill = jnp.zeros((total, spare), BF16)
        d_rest = jnp.concatenate([d_bc, d_dt, fill], axis=1)
        if ring.on:
            g_all = outer(order, (normed, [d_x, d_rest]))
        else:
            g_all = jnp.concatenate([dot(normed[0], d, TN) for d in (d_x, d_rest)], axis=1)
        met_dt = jnp.sum(d_dt.astype(F32) * dt_raw, axis=1)
        met = (met_z + met_x + first * met_bc).reshape(total) + met_dt
        return sums, d_x, d_rest, g_conv_x, g_conv_bc, met, g_all

    sums, d_x, d_rest, g_conv_x, g_conv_bc, met, g_all = ring.phase(
        work, sums, g_zo, d_conv_x, after_x, d_conv_bc, after_bc, d_dt, normed
    )
    small = jnp.concatenate(
        [
            g_conv_x.reshape(-1), g_conv_bc.reshape(-1), g_gate.reshape(-1),
            g_skip.reshape(-1), g_heads.reshape(-1),
        ]
    )

    def one_swap(array, bit):
        return array + swap(array, "seq", bit) if ring.on else array

    def work(sums, g_zo, g_all, small, d_z, d_x, d_rest, z_w, x_w, rest_once, late_w, met):
        last = ring.hop(sums)
        sent = ring.send(g_all)
        back = project(ring, spots, [d_z, d_x, d_rest], [z_w, x_w, rest_once], [late_w])
        return (
            ring.total(g_zo, last) if ring.on else [ring.total(g, None) for g in g_zo],
            ring.add(g_all, sent, 3), back, one_swap(small, 1), head_sum(met) / scale,
        )

    g_zo, sums, back_terms, small, dots = ring.phase(
        work, sums, g_zo, g_all, small, d_z, d_x, d_rest, z_w, x_w, rest_once, hop4[0], met
    )
    g_z, g_out = (g_zo[:per], g_zo[per:]) if ring.on else g_zo

    def work(sums, g_all, small, back_terms, out_far, out_own, slab):
        mixed_out = slab + scatter_sum(ring, out_far, out_own)
        return (
            ring.add(g_all, ring.hop(sums), 2), scatter_near(ring, back_terms),
            one_swap(small, 2), mixed_out,
        )

    sums, (far, d_normed), small, mixed_out = ring.phase(
        work, sums, g_all, small, back_terms, out_far, out_own, slab
    )
    far = across(ring, far)

    def work(sums, g_all, small, g_z):
        return (
            ring.add(g_all, ring.hop(sums), 1), one_swap(small, 4),
            jnp.sum(g_z * w_z.astype(F32), axis=1), g_out.T,
        )

    sums, small, met_f, g_out = ring.phase(work, sums, g_all, small, g_z)
    if not ring.on:
        small = lax.psum(small, "seq")

    def work(sums, g_all, far, d_normed, slab, dots, met_f):
        last = ring.hop(sums)
        d_normed = scatter_sum(ring, far, d_normed)
        grad_tokens = (
            cot_rows
            + (scale[:, None] * own_gain) * d_normed
            - slab * (scale * scale * scale * dots / model)[:, None]
        )
        g_all = ring.total(g_all, last)
        met_f = met_f + jnp.sum(g_all * all_in.astype(F32) * once, axis=1)
        g_gain = head_sum(met_f) / norm_gain.astype(F32)
        return (
            g_all[:, :inner], g_all[:, inner:edge_at], g_all[:, edge_at : edge_at + heads],
            grad_tokens, g_gain,
        )

    g_x, g_bc, g_dt, grad_tokens, g_gain = ring.phase(
        work, sums, g_all, far, d_normed, slab, dots, met_f
    )

    cuts = [KERNEL * inner, KERNEL * 2 * N, inner, inner, heads, heads]
    parts, start = [], 0
    for width in cuts:
        parts.append(small[start : start + width])
        start += width
    sum_x, sum_bc, sum_gate, sum_skip, sum_bias, sum_rate = parts

    return (
        mixed_out.reshape(batch, length, own_width),
        grad_tokens.reshape(batch, length, own_width),
        g_gain,
        g_z,
        g_x,
        g_bc,
        g_dt,
        sum_x.reshape(KERNEL, inner),
        sum_bc.reshape(KERNEL, 2 * N),
        sum_bias,
        sum_rate,
        jnp.sum(sum_skip.reshape(heads, P_SIZE), axis=1),
        sum_gate,
        g_out,
    )


def solution(mesh):
    in_specs = (
        P(None, "seq", "head"),
        P("seq"),
        P("seq", "head"),
        P("seq", "head"),
        P("seq", None),
        P("seq", "head"),
        P(None, "head"),
        P(),
        P("head"),
        P("head"),
        P("head"),
        P("head"),
        P("head", "seq"),
        P(None, "seq", "head"),
    )
    out_specs = (
        P(None, "seq", "head"),
        P(None, "seq", "head"),
        P("seq"),
        P("seq", "head"),
        P("seq", "head"),
        P("seq", None),
        P("seq", "head"),
        P(None, "head"),
        P(),
        P("head"),
        P("head"),
        P("head"),
        P("head"),
        P("head", "seq"),
    )
    return jax.shard_map(body, mesh=mesh, in_specs=in_specs, out_specs=out_specs, check_vma=False)
```

time: 702 us -> 583 us (0.83)
  Pallas kernels: 81.3 us -> 183 us
  starting transfers between devices: 159 us -> 71.8 us
  matrix products: 78.8 us -> 0 us
  waiting for transfers between devices: 215 us -> 178 us
  between operations: 13.5 us -> 1.49 us
    pallas_call x6 -> x21, Pallas kernels: 74 us -> 169 us  [the longest x2 29.6 us: with_spots(): pl.pallas_call(kernel, grid_spec=pltpu.PrefetchScalarGridSpec(num_scalar_...]
    dot_general x13 -> x0, matrix products: 78.8 us -> none  [dot(): lax.dot_general(left, right, dims, precision=precision, preferred_element...]
    ppermute x64 -> x32, waiting for transfers between devices: 128 us -> 51.6 us  [shift(): lax.ppermute(array, 'seq', [(order[i], order[(i + by) % size]) for i in r...]
    ppermute x64 -> x32, starting transfers between devices: 104 us -> 37.8 us  [shift(): lax.ppermute(array, 'seq', [(order[i], order[(i + by) % size]) for i in r...]
    ppermute x25 -> x23, waiting for transfers between devices: 52.9 us -> 80.7 us  [swap(): return lax.ppermute(array, axis, [(i, i ^ bit) for i in range(size)])]
    slice x19 -> x18, local copies, waits for them, and re-layouts: 5.51 us -> 18.8 us  [the longest x4 5.78 us: last_hop(): return (self.shift(moving[0][:cut], 1), self.shift(moving[1][cut:], -1))]
    convert_element_type x23 -> x9, other arithmetic: 32.2 us -> 19.8 us  [the longest x4 14.3 us: add(): return (right.astype(BF16), left.astype(BF16))]
    ppermute x10 -> x6, starting transfers between devices: 25.4 us -> 13 us  [the longest x4 9.33 us: shift_flat(): lax.ppermute(array, 'seq', [(i, i + by) for i in range(size) if 0 <= i +...]
  transfers between devices with their start and end apart: 102 -> 64, of which waited for: 31 -> 24; matrix products, arithmetic and copies ran while one was open for 26% -> 10% of each run, Pallas kernels for 12% -> 24%
where the time goes in v2:
time: 583 us; the launch traced here: 573 us
  Pallas kernels  183 us (31%)
  waiting for transfers between devices  178 us (31%)
  starting transfers between devices  71.8 us (12%)
  other arithmetic  55.3 us (9%)
  local copies, waits for them, and re-layouts  51.6 us (9%)
  blocking collectives  31.1 us (5%)
    ppermute x23, waiting for transfers between devices, swap(): return lax.ppermute(array, axis, [(i, i ^ bit) for i in range(size)])  80.7 us
    ppermute x32, waiting for transfers between devices, shift(): lax.ppermute(array, 'seq', [(order[i], order[(i + by) % size]) for i in r...  51.6 us
    ppermute x32, starting transfers between devices, shift(): lax.ppermute(array, 'seq', [(order[i], order[(i + by) % size]) for i in r...  37.8 us
    psum x4, blocking collectives, head_sum(): return lax.psum(array, 'head')  31.1 us
    pallas_call x2, Pallas kernels, with_spots(): pl.pallas_call(kernel, grid_spec=pltpu.PrefetchScalarGridSpec(num_scalar_...  29.6 us
    ppermute x4, waiting for transfers between devices, shift_flat(): lax.ppermute(array, 'seq', [(i, i + by) for i in range(size) if 0 <= i +...  28.3 us
    pallas_call x2, Pallas kernels, outer(): pl.pallas_call(functools.partial(outer_kernel, [len(grads) for _, grads i...  27.1 us
    pallas_call x2, Pallas kernels, project(): pl.pallas_call(functools.partial(project_kernel, len(acts), len(late)), g...  26.7 us
  transfers between devices with their start and end apart: 64, of which 24 were waited for; matrix products, arithmetic and copies ran while one was open for 10% of the time, Pallas kernels for 24%

profile of v2, /device:TPU:0, one launch (start us, length us, event | category | flops | bytes accessed | tf_op | source)
XLA Modules:
  0.0 573.1 jit_solution(16646512717682946182)
XLA Ops:
  3.4 32.2 %conditional.19 = (bf16[256,1408]{1,0:T(8,128)(2,1)}, bf16[256,1408]{1,0:T(8,128)(2,1)}, f32[512]{0:T(512)}, f32[1024]{0:T(1024)}, bf16[1024,512]{1,0:T(8,128)(2,1)S(1)}) conditional(s32[]{:T(128)} %convert_element_type.212, () %tuple.182, (s32[]{:T(128)}, bf16[256]{0:T(256)(128)(2,1)}, bf16[256,1408]{1,0:T(8,128)(2,1)}, f32[1024,512]{1,0:T(8,128)}) %tuple.295), branch_computations={%region_0.1_spmd, %region_1.4_spmd} | conditional | flops 2985474 | bytes 20885750 | solution.py:111
  17.2 13.3 %psum.24 = f32[1024]{0:T(1024)S(1)} all-reduce(f32[1024]{0:T(1024)S(1)} %multiply_reduce_fusion), channel_id=1, replica_groups=mesh['seq'=8,'head'=4] {'head'}, use_global_device_ids=true, to_apply=%region_3.3 | all-reduce | flops 1024 | bytes 8192 | tf_op jit(solution)/shard_map/cond/branch_1_fun/psum | solution.py:120
  39.2 19.4 %conditional.20 = (bf16[256,1408]{1,0:T(8,128)(2,1)}, bf16[256,1408]{1,0:T(8,128)(2,1)}, bf16[1024,512]{1,0:T(8,128)(2,1)}, bf16[512,1024]{0,1:T(8,128)(2,1)}, bf16[1024,512]{1,0:T(8,128)(2,1)S(1)}) conditional(s32[]{:T(128)} %convert_element_type.212, () %tuple.181, (bf16[256,1408]{1,0:T(8,128)(2,1)}, bf16[256,1408]{1,0:T(8,128)(2,1)}, ...), branch_computations={%region_4.5_spmd, %region_5.6_spmd} | conditional | flops 2621440 | bytes 20447448 | solution.py:111
  46.6 12.0 %collective-permute-done.16 = bf16[256,1408]{1,0:T(8,128)(2,1)} collective-permute-done((bf16[256,1408]{1,0:T(8,128)(2,1)}, bf16[256,1408]{1,0:T(8,128)(2,1)}, u32[]{:S(2)}, u32[]{:S(2)}) %collective-permute-start.16) | collective-permute-done | bytes 720928 | tf_op jit(solution)/shard_map/cond/branch_1_fun/ppermute | solution.py:60
  59.6 18.2 %conditional.21 = (bf16[256,1408]{1,0:T(8,128)(2,1)}, bf16[256,1408]{1,0:T(8,128)(2,1)}) conditional(s32[]{:T(128)} %convert_element_type.212, () %tuple.186, (bf16[256,1408]{1,0:T(8,128)(2,1)}, bf16[256,1408]{1,0:T(8,128)(2,1)}) %tuple.187), branch_computations={%region_6.7_spmd, %region_7.8_spmd} | conditional | bytes 5767264 | solution.py:111
  61.6 16.2 %collective-permute-done = bf16[256,1408]{1,0:T(8,128)(2,1)} collective-permute-done((bf16[256,1408]{1,0:T(8,128)(2,1)}, bf16[256,1408]{1,0:T(8,128)(2,1)}, u32[]{:S(2)}, u32[]{:S(2)}) %collective-permute-start) | collective-permute-done | bytes 720928 | tf_op jit(solution)/shard_map/cond/branch_1_fun/ppermute | solution.py:60
  78.4 14.2 %conditional.22 = (bf16[128,1408]{1,0:T(8,128)(2,1)}, bf16[128,1408]{1,0:T(8,128)(2,1)}, bf16[1024,512]{1,0:T(8,128)(2,1)}) conditional(s32[]{:T(128)} %convert_element_type.212, () %tuple.185, (bf16[256,1408]{1,0:T(8,128)(2,1)}, bf16[256,1408]{1,0:T(8,128)(2,1)}, bf16[1024,512]{1,0:T(8,128)(2,1)S(1)}) %tuple.188), branch_computations={%region_8.9_spmd, %region_9.10_spmd} | conditional | bytes 8519824 | solution.py:111
  82.6 7.8 %collective-permute-done.2 = bf16[128,1408]{1,0:T(8,128)(2,1)} collective-permute-done((bf16[128,1408]{1,0:T(8,128)(2,1)S(1)}, bf16[128,1408]{1,0:T(8,128)(2,1)}, u32[]{:S(2)}, u32[]{:S(2)}) %collective-permute-start.2) | collective-permute-done | bytes 360480 | tf_op jit(solution)/shard_map/cond/branch_1_fun/ppermute | solution.py:60
  92.6 28.5 %conditional.23 = (bf16[512,1024]{1,0:T(8,128)(2,1)}, bf16[512,1024]{1,0:T(8,128)(2,1)}, bf16[1024,1024]{1,0:T(8,128)(2,1)}, bf16[1024,256]{1,0:T(8,128)(2,1)}, ...) conditional(s32[]{:T(128)} %convert_element_type.212, ...), branch_computations={%region_10.11_spmd, %region_11.12_spmd} | conditional | flops 51200 | bytes 10706104 | solution.py:111
  96.9 13.2 %branch_1_fun.21 = (bf16[1024,1024]{1,0:T(8,128)(2,1)}, bf16[1024,256]{1,0:T(8,128)(2,1)}, f32[1024,128]{1,0:T(8,128)S(1)}, bf16[2048,1024]{1,0:T(8,128)(2,1)}, bf16[2048,384]{1,0:T(8,128)(2,1)}) custom-call(s32[8]{0:T(128)S(1)} %get-tuple-element.454.spot_ref, bf16[1024,512]{1,0:T(8,128)(2,1)} %get-tuple-element.455.refs_0_, ...), custom_call_target="tpu_custom_call" | custom-call | tf_op jit(solution)/shard_map/cond/branch_1_fun/pallas_call | solution.py:698
  114.2 5.4 collective-permute-done.21
  121.9 33.1 %conditional.24 = (bf16[512,1024]{1,0:T(8,128)(2,1)}, bf16[512,1024]{1,0:T(8,128)(2,1)}, f32[1024,1280]{1,0:T(8,128)}, f32[1024,1024]{1,0:T(8,128)}, f32[1024,16...) conditional(s32[]{:T(128)} %convert_element_type.212, ...), branch_computations={%region_12.13_spmd, %region_13.14_spmd} | conditional | bytes 65807200 | solution.py:111
  124.0 16.2 %branch_1_fun.22 = (f32[1024,1280]{1,0:T(8,128)}, f32[1024,1024]{1,0:T(8,128)}, f32[1024,16]{1,0:T(8,128)}, f32[1024,16]{1,0:T(8,128)}, f32[8,128,1024]{2,1,0:T(...) custom-call(bf16[1024,1024]{1,0:T(8,128)(2,1)} %get-tuple-element.475.x_ref, ...), custom_call_target="tpu_custom_call" | custom-call | bytes 47850000 | tf_op jit(solution)/shard_map/cond/branch_1_fun/pallas_call | solution.py:906
  142.5 11.5 %collective-permute-done.7.got_ref = bf16[144,1024]{1,0:T(8,128)(2,1)S(1)} collective-permute-done((bf16[144,1024]{1,0:T(8,128)(2,1)S(1)}, bf16[144,1024]{1,0:T(8,128)(2,1)S(1)}, u32[]{:S(2)}, u32[]{:S(2)}) %collective-permute-start.7) | collective-permute-done | bytes 294944 | tf_op jit(solution)/shard_map/cond/branch_1_fun/ppermute | solution.py:116
  155.1 30.2 %conditional.25 = (bf16[512,1024]{1,0:T(8,128)(2,1)}, bf16[512,1024]{1,0:T(8,128)(2,1)}, f32[128,1024]{1,0:T(8,128)}, f32[1,1024]{1,0:T(1,128)S(1)}, f32[128,102...) conditional(s32[]{:T(128)} %convert_element_type.212, ...), branch_computations={%region_14.15_spmd, %region_15.16_spmd} | conditional | flops 786432 | bytes 16910824 | solution.py:111
  160.8 23.6 %collective-permute-done.34.got_ref = bf16[144,1024]{1,0:T(8,128)(2,1)S(1)} collective-permute-done((bf16[144,1024]{1,0:T(8,128)(2,1)}, bf16[144,1024]{1,0:T(8,128)(2,1)S(1)}, u32[]{:S(2)}, u32[]{:S(2)}) %collective-permute-start.34) | collective-permute-done | bytes 294944 | tf_op jit(solution)/shard_map/cond/branch_1_fun/ppermute | solution.py:189
  186.5 31.2 %conditional.26 = (bf16[256,1024]{1,0:T(8,128)(2,1)}, bf16[256,1024]{1,0:T(8,128)(2,1)}, f32[128,1024]{1,0:T(8,128)}, bf16[128,1024]{1,0:T(8,128)(2,1)}, f32[102...) conditional(s32[]{:T(128)} %convert_element_type.212, ...), branch_computations={%region_16.17_spmd, %region_17.18_spmd} | conditional | bytes 19660906 | solution.py:111
  199.3 16.4 %branch_1_fun.27 = (f32[1024,1024]{1,0:T(8,128)}, f32[1024,1024]{1,0:T(8,128)}, bf16[2048,1024]{1,0:T(8,128)(2,1)}, bf16[2048,1024]{1,0:T(8,128)(2,1)}, bf16[102...) custom-call(s32[8]{0:T(128)S(1)} %get-tuple-element.525.spot_ref, bf16[1024,512]{1,0:T(8,128)(2,1)} %get-tuple-element.526.refs_0_, ...), custom_call_target="tpu_custom_call" | custom-call | tf_op jit(solution)/shard_map/cond/branch_1_fun/pallas_call | solution.py:698
  217.8 7.8 %conditional.27 = (f32[2,128,1024]{2,1,0:T(8,128)S(1)}) conditional(s32[]{:T(128)} %convert_element_type.212, () %tuple.193, (bf16[128,1024]{1,0:T(8,128)(2,1)}, s32[1]{0:T(128)}, f32[128,1024]{1,0:T(8,128)}) %tuple.194), branch_computations={%region_18.19_spmd, %region_19.20_spmd} | conditional | bytes 1048624 | solution.py:111
  225.6 11.1 %shard_map.246 = (f32[1024,1024]{1,0:T(8,128)}, f32[8,2,128]{2,1,0:T(2,128)S(1)}) custom-call(f32[1024,1024]{1,0:T(8,128)} %get-tuple-element.888.y_ref, f32[1024,1280]{1,0:T(8,128)} %get-tuple-element.889.vc_ref, f32[2,128,1024]{2,1,0:T(8,128)S(1)} %get-tuple-element.1468.s_ref, f32[1024,16]{1,0:T(8,128)} %get-tuple-element.892.wc_ref, ...), custom_call_target="tpu_custom_call" | custom-call | bytes 23100000 | tf_op jit(solution)/shard_map/pallas_call | solution.py:955
  236.7 5.8 %psum.28 = f32[8,2,128]{2,1,0:T(2,128)S(1)} all-reduce(f32[8,2,128]{2,1,0:T(2,128)S(1)} %get-tuple-element.899), channel_id=1, replica_groups=mesh['seq'=8,'head'=4] {'head'}, use_global_device_ids=true, to_apply=%region_20.21 | all-reduce | flops 2048 | bytes 16384 | tf_op jit(solution)/shard_map/psum | solution.py:120
  242.5 13.0 %shard_map.247 = (bf16[1024,1024]{1,0:T(8,128)(2,1)S(1)}, f32[1024,1024]{1,0:T(8,128)}, f32[2,128,1024]{2,1,0:T(8,128)S(1)}, f32[8,1,128]{2,1,0:T(1,128)S(1)}, f...) custom-call(f32[1024,1024]{1,0:T(8,128)} %get-tuple-element.887.dmp_ref, f32[1024,1024]{1,0:T(8,128)} %get-tuple-element.898.ssd_ref, ...), custom_call_target="tpu_custom_call" | custom-call | bytes 29700000 | tf_op jit(solution)/shard_map/pallas_call | solution.py:969
  257.6 18.0 %conditional.28 = (f32[128,1024]{1,0:T(8,128)S(1)}, f32[1,1024]{1,0:T(1,128)S(1)}, f32[128,1024]{1,0:T(8,128)S(1)}, f32[1,1024]{1,0:T(1,128)S(1)}, bf16[144,1024...) conditional(s32[]{:T(128)} %convert_element_type.212, () %tuple.176, (s32[1]{0:T(128)}, s32[1]{0:T(128)}, ...), branch_computations={%region_21.22_spmd, %region_22.23_spmd} | conditional | bytes 9740356 | solution.py:111
  260.1 14.6 %branch_1_fun.31 = bf16[4096,1024]{1,0:T(8,128)(2,1)} custom-call(s32[8]{0:T(128)S(1)} %get-tuple-element.560.block_ref, bf16[1024,512]{1,0:T(8,128)(2,1)} %get-tuple-element.561.refs_0_, bf16[1024,512]{1,0:T(8,128)(2,1)} %get-tuple-element.562.refs_1_, bf16[1024,512]{1,0:T(8,128)(2,1)S(1)} %get-tuple-element.563.refs_2_, ...), custom_call_target="tpu_custom_call" | custom-call | tf_op jit(solution)/shard_map/cond/branch_1_fun/pallas_call | solution.py:753
  275.6 27.0 %conditional.29 = (f32[128,1024]{1,0:T(8,128)S(1)}, f32[1,1024]{1,0:T(1,128)S(1)}, f32[128,1024]{1,0:T(8,128)S(1)}, f32[1,1024]{1,0:T(1,128)S(1)}, bf16[128,1024...) conditional(s32[]{:T(128)} %convert_element_type.212, ...), branch_computations={%region_23.24_spmd, %region_24.25_spmd} | conditional | flops 6291456 | bytes 93085720 | solution.py:111
  280.8 18.5 %branch_1_fun.33 = (f32[1024,1024]{1,0:T(8,128)}, f32[1024,256]{1,0:T(8,128)}) custom-call(f32[1024,1280]{1,0:T(8,128)} %get-tuple-element.582.v_ref, f32[1024,1024]{1,0:T(8,128)} %get-tuple-element.583.dy_ref, f32[1024,16]{1,0:T(8,128)} %get-tuple-element.584.st_ref, f32[1,16]{1,0:T(1,128)S(1)} %get-tuple-element.585.rate_ref, ...), custom_call_target="tpu_custom_call" | custom-call | bytes 59400000 | tf_op jit(solution)/shard_map/cond/branch_1_fun/pallas_call | solution.py:990
  302.5 17.8 %conditional.30 = (f32[128,1024]{1,0:T(8,128)S(1)}, bf16[128,1024]{1,0:T(8,128)(2,1)}, bf16[1024,2048]{1,0:T(8,128)(2,1)S(1)}) conditional(s32[]{:T(128)} %convert_element_type.212, () %tuple.200, (bf16[128,1024]{1,0:T(8,128)(2,1)S(1)}, s32[1]{0:T(128)}, s32[1]{0:T(128)}, f32[128,1024]{1,0:T(8,128)S(1)}, f32[1,1024]{1,0:T(1,128)S(1)}, ...), branch_computations={%region_25.26_spmd, %region_26.27_spmd} | conditional | bytes 4980768 | solution.py:111
  304.1 9.7 %branch_1_fun.35 = bf16[1024,2048]{1,0:T(8,128)(2,1)S(1)} custom-call(s32[8]{0:T(128)S(1)} %get-tuple-element.600.spot_ref, bf16[1024,1024]{1,0:T(8,128)(2,1)} %get-tuple-element.601.refs_0_, bf16[2048,1024]{1,0:T(8,128)(2,1)} %get-tuple-element.602.refs_1_, bf16[256,1024]{1,0:T(8,128)(2,1)} %get-tuple-element.603.refs_2_), custom_call_target="tpu_custom_call" | custom-call | tf_op jit(solution)/shard_map/cond/branch_1_fun/pallas_call | solution.py:783
  320.3 10.7 %conditional.31 = (f32[2,128,1024]{2,1,0:T(8,128)}, bf16[1024,512]{1,0:T(8,128)(2,1)S(1)}, f32[1024,512]{1,0:T(8,128)S(1)}) conditional(s32[]{:T(128)} %convert_element_type.212, () %tuple.199, (bf16[128,1024]{1,0:T(8,128)(2,1)}, s32[1]{0:T(128)}, s32[1]{0:T(128)}, f32[128,1024]{1,0:T(8,128)S(1)}, bf16[1024,2048]{1,0:T(8,128)(2,1)S(1)}) %tuple.202), branch_computations={%region_27.28_spmd, %region_28.29_spmd} | conditional | flops 3670016 | bytes 22020268 | solution.py:111
  322.3 7.1 %collective-permute-done.45.got_ref = bf16[128,1024]{1,0:T(8,128)(2,1)S(1)} collective-permute-done((bf16[128,1024]{1,0:T(8,128)(2,1)S(1)}, bf16[128,1024]{1,0:T(8,128)(2,1)S(1)}, u32[]{:S(2)}, u32[]{:S(2)}) %collective-permute-start.45) | collective-permute-done | bytes 262176 | tf_op jit(solution)/shard_map/cond/branch_1_fun/ppermute | solution.py:116
  332.9 58.0 %conditional.32 = (bf16[512,1024]{1,0:T(8,128)(2,1)}, bf16[512,1024]{1,0:T(8,128)(2,1)}, bf16[1024,1024]{1,0:T(8,128)(2,1)}, f32[2,8,1024]{2,1,0:T(8,128)S(1)}, ...) conditional(s32[]{:T(128)} %convert_element_type.212, ...), branch_computations={%region_29.30_spmd, %region_30.31_spmd} | conditional | flops 9120794 | bytes 89235432 | solution.py:111
  336.0 15.4 %branch_1_fun.37 = (bf16[1024,1024]{1,0:T(8,128)(2,1)}, f32[1024,256]{1,0:T(8,128)S(1)}, bf16[1024,16]{1,0:T(8,128)(2,1)}, f32[1,1024]{1,0:T(1,128)S(1)}, f32[2,16]{1,0:T(2,128)S(1)}) custom-call(f32[1024,1280]{1,0:T(8,128)} %get-tuple-element.612.v_ref, f32[1024,1024]{1,0:T(8,128)} %get-tuple-element.613.dy_ref, f32[1024,1024]{1,0:T(8,128)} %get-tuple-element.614.du_ref, ...), custom_call_target="tpu_custom_call" | custom-call | bytes 49500000 | tf_op jit(solution)/shard_map/cond/branch_1_fun/pallas_call | solution.py:1010
  373.3 10.0 %collective-permute-done.24 = bf16[2,3,1024]{2,1,0:T(4,128)(2,1)S(1)} collective-permute-done((bf16[2,3,1024]{2,1,0:T(4,128)(2,1)S(1)}, bf16[2,3,1024]{2,1,0:T(4,128)(2,1)S(1)}, u32[]{:S(2)}, u32[]{:S(2)}) %collective-permute-start.24) | collective-permute-done | bytes 12320 | tf_op jit(solution)/shard_map/cond/branch_1_fun/ppermute | solution.py:882
  390.9 35.5 %conditional.33 = (bf16[512,1024]{1,0:T(8,128)(2,1)}, bf16[512,1024]{1,0:T(8,128)(2,1)}, bf16[1024,1024]{1,0:T(8,128)(2,1)}, bf16[1024,384]{1,0:T(8,128)(2,1)}, ...) conditional(s32[]{:T(128)} %convert_element_type.212, ...), branch_computations={%region_31.32_spmd, %region_32.34_spmd} | conditional | flops 6605824 | bytes 52736748 | solution.py:111
  394.9 9.6 %branch_1_fun.38 = (bf16[1024,1024]{1,0:T(8,128)(2,1)}, f32[4,1024]{1,0:T(4,128)S(1)}, f32[8,1,128]{2,1,0:T(1,128)S(1)}) custom-call(bf16[1024,1024]{1,0:T(8,128)(2,1)} %get-tuple-element.636.d_ref, bf16[1024,1024]{1,0:T(8,128)(2,1)} %get-tuple-element.637.in_ref, f32[2,8,1024]{2,1,0:T(8,128)S(1)} %get-tuple-element.638.halo_ref, ...), custom_call_target="tpu_custom_call" | custom-call | bytes 26400000 | tf_op jit(solution)/shard_map/cond/branch_1_fun/pallas_call | solution.py:823
  404.5 5.0 branch_1_fun.39
  410.1 12.5 %branch_1_fun.40 = bf16[2048,1408]{1,0:T(8,128)(2,1)} custom-call(s32[8]{0:T(128)S(1)} %get-tuple-element.652.block_ref, bf16[1024,512]{1,0:T(8,128)(2,1)} %get-tuple-element.653.refs_0_, bf16[1024,512]{1,0:T(8,128)(2,1)} %get-tuple-element.654.refs_1_, bf16[1024,512]{1,0:T(8,128)(2,1)S(1)} %get-tuple-element.655.refs_2_, ...), custom_call_target="tpu_custom_call" | custom-call | tf_op jit(solution)/shard_map/cond/branch_1_fun/pallas_call | solution.py:753
  429.4 44.4 %conditional.34 = (f32[512,1024]{1,0:T(8,128)}, bf16[256,1408]{1,0:T(8,128)(2,1)}, bf16[256,1408]{1,0:T(8,128)(2,1)}, bf16[1024,2048]{1,0:T(8,128)(2,1)S(1)}, f3...) conditional(s32[]{:T(128)} %convert_element_type.212, () %tuple.205, ...), branch_computations={%region_34.35_spmd, %region_35.37_spmd} | conditional | flops 6956064 | bytes 50226552 | solution.py:111
  436.8 6.0 %psum.25 = f32[1024]{0:T(1024)S(1)} all-reduce(f32[1024]{0:T(1024)S(1)} %get-tuple-element.672), channel_id=1, replica_groups=mesh['seq'=8,'head'=4] {'head'}, use_global_device_ids=true, to_apply=%region_36.36 | all-reduce | flops 1024 | bytes 8192 | tf_op jit(solution)/shard_map/cond/branch_1_fun/psum | solution.py:120
  443.6 17.0 %branch_1_fun.41 = bf16[1024,2048]{1,0:T(8,128)(2,1)} custom-call(s32[8]{0:T(128)S(1)} %copy-done.42, bf16[1024,1024]{1,0:T(8,128)(2,1)} %get-tuple-element.664.refs_0_, bf16[1024,1024]{1,0:T(8,128)(2,1)} %get-tuple-element.665.refs_1_, bf16[1024,384]{1,0:T(8,128)(2,1)S(1)} %copy-done.18, bf16[2048,1024]{1,0:T(8,128)(2,1)} %get-tuple-element.667.refs_3_, ...), custom_call_target="tpu_custom_call" | custom-call | tf_op jit(solution)/shard_map/cond/branch_1_fun/pallas_call | solution.py:783
  474.4 21.8 %collective-permute-done.62 = bf16[1024,512]{1,0:T(8,128)(2,1)S(1)} collective-permute-done((bf16[1024,512]{1,0:T(8,128)(2,1)}, bf16[1024,512]{1,0:T(8,128)(2,1)S(1)}, u32[]{:S(2)}, u32[]{:S(2)}) %collective-permute-start.62) | collective-permute-done | bytes 1048608 | tf_op jit(solution)/shard_map/ppermute | solution.py:116
  496.3 21.9 %conditional.35 = (bf16[256,1408]{1,0:T(8,128)(2,1)}, bf16[256,1408]{1,0:T(8,128)(2,1)}, bf16[1024,512]{1,0:T(8,128)(2,1)}, f32[1024,512]{1,0:T(8,128)S(1)}, f32...) conditional(s32[]{:T(128)} %convert_element_type.212, () %tuple.174, (bf16[2048,1408]{1,0:T(8,128)(2,1)}, ...), branch_computations={%region_37.38_spmd, %region_38.39_spmd} | conditional | flops 8133664 | bytes 45946004 | solution.py:111
  500.5 13.3 %collective-permute-done.57 = f32[7200]{0:T(1024)S(1)} collective-permute-done((f32[7200]{0:T(1024)S(1)}, f32[7200]{0:T(1024)S(1)}, u32[]{:S(2)}, u32[]{:S(2)}) %collective-permute-start.57) | collective-permute-done | bytes 28832 | tf_op jit(solution)/shard_map/cond/branch_1_fun/ppermute | solution.py:116
  520.2 26.5 %conditional.36 = (bf16[256,1408]{1,0:T(8,128)(2,1)}, bf16[256,1408]{1,0:T(8,128)(2,1)}, f32[7200]{0:T(1024)}, f32[256]{0:T(256)S(1)}, f32[4096]{0:T(1024)}, /*i...) conditional(s32[]{:T(128)} %convert_element_type.212, ...), branch_computations={%region_39.40_spmd, %region_40.43_spmd} | conditional | flops 3677968 | bytes 14076332 | solution.py:111
  526.7 10.3 %collective-permute-done.60 = f32[7200]{0:T(1024)S(1)} collective-permute-done((f32[7200]{0:T(1024)S(1)}, f32[7200]{0:T(1024)S(1)}, u32[]{:S(2)}, u32[]{:S(2)}) %collective-permute-start.60) | collective-permute-done | bytes 28832 | tf_op jit(solution)/shard_map/cond/branch_1_fun/ppermute | solution.py:116
  547.3 24.2 %conditional.37 = (f32[256,1024]{1,0:T(8,128)S(1)}, f32[256,256]{1,0:T(8,128)S(1)}, f32[256]{0:T(256)S(1)}, f32[2,512,512]{2,1,0:T(8,128)}, f32[256,16]{0,1:T(8,128)S(1)}) conditional(s32[]{:T(128)} %convert_element_type.212, () %tuple.208, (bf16[2048,1408]{1,0:T(8,128)(2,1)}, bf16[256,1408]{1,0:T(8,128)(2,1)}, bf16[256,1408]{1,0:T(8,128)(2,1)}, ...), branch_computations={%region_43.44_spmd, %region_44.47_spmd} | conditional | flops 6918912 | bytes 22264956 | solution.py:111
  554.5 6.8 %collective-permute-done.40 = bf16[256,1408]{1,0:T(8,128)(2,1)} collective-permute-done((bf16[256,1408]{1,0:T(8,128)(2,1)}, bf16[256,1408]{1,0:T(8,128)(2,1)}, u32[]{:S(2)}, u32[]{:S(2)}) %collective-permute-start.40) | collective-permute-done | bytes 720928 | tf_op jit(solution)/shard_map/cond/branch_1_fun/ppermute | solution.py:60
  565.6 6.0 %psum.26 = f32[256]{0:T(256)S(1)} all-reduce(f32[256]{0:T(256)S(1)} %add.163), channel_id=1, replica_groups=mesh['seq'=8,'head'=4] {'head'}, use_global_device_ids=true, to_apply=%region_46.46 | all-reduce | flops 256 | bytes 2048 | tf_op jit(solution)/shard_map/cond/branch_1_fun/psum | solution.py:120
  (346 shorter events, 221.5 us)
Async XLA Ops:
  11.6 21.0 %collective-permute-start.38 = (bf16[256,1408]{1,0:T(8,128)(2,1)}, bf16[256,1408]{1,0:T(8,128)(2,1)}, u32[]{:S(2)}, u32[]{:S(2)}) collective-permute-start(bf16[256,1408]{1,0:T(8,128)(2,1)} %broadcast_add_fusion), channel_id=1, source_target_pairs={{0,8},{8,16},{16,24},{24,28},{28,20},{20,12},{12,4},{4,0},{1,9},{9... | collective-permute-start | bytes 2162696 | tf_op jit(solution)/shard_map/cond/branch_1_fun/ppermute | solution.py:60
  15.3 20.2 %collective-permute-start.39 = (bf16[256,1408]{1,0:T(8,128)(2,1)}, bf16[256,1408]{1,0:T(8,128)(2,1)}, u32[]{:S(2)}, u32[]{:S(2)}) collective-permute-start(bf16[256,1408]{1,0:T(8,128)(2,1)} %broadcast_add_fusion), channel_id=1, source_target_pairs={{0,4},{8,0},{16,8},{24,16},{28,24},{20,28},{12,20},{4,12},{1,5},{9... | collective-permute-start | bytes 2162696 | tf_op jit(solution)/shard_map/cond/branch_1_fun/ppermute | solution.py:60
  35.6 42.8 %collective-permute-start.61 = (bf16[1024,512]{1,0:T(8,128)(2,1)S(1)}, bf16[1024,512]{1,0:T(8,128)(2,1)S(1)}, u32[]{:S(2)}, u32[]{:S(2)}) collective-permute-start(bf16[1024,512]{1,0:T(8,128)(2,1)S(1)} %get-tuple-element.852), channel_id=1, source_target_pairs={{0,2},{1,3},{2,0},{3,1},{4,6},{5,7},{6,4},{7,5},{8,10},{9,11},{10,... | collective-permute-start | bytes 3145736 | tf_op jit(solution)/shard_map/ppermute | solution.py:116
  39.2 19.4 %collective-permute-start.18 = (bf16[1024,512]{1,0:T(8,128)(2,1)S(1)}, bf16[1024,512]{1,0:T(8,128)(2,1)}, u32[]{:S(2)}, u32[]{:S(2)}) collective-permute-start(bf16[1024,512]{1,0:T(8,128)(2,1)S(1)} %get-tuple-element.444), channel_id=1, source_target_pairs={{0,1},{1,0},{2,3},{3,2},{4,5},{5,4},{6,7},{7,6},{8,9},{9,8},{10,11... | collective-permute-start | bytes 3145736 | tf_op jit(solution)/shard_map/cond/branch_1_fun/ppermute | solution.py:116
  39.3 19.3 %collective-permute-start.16 = (bf16[256,1408]{1,0:T(8,128)(2,1)}, bf16[256,1408]{1,0:T(8,128)(2,1)}, u32[]{:S(2)}, u32[]{:S(2)}) collective-permute-start(bf16[256,1408]{1,0:T(8,128)(2,1)} %get-tuple-element.442), channel_id=1, source_target_pairs={{0,8},{8,16},{16,24},{24,28},{28,20},{20,12},{12,4},{4,0},{1,9},{9... | collective-permute-start | bytes 2162696 | tf_op jit(solution)/shard_map/cond/branch_1_fun/ppermute | solution.py:60
  39.3 19.3 %collective-permute-start.17 = (bf16[256,1408]{1,0:T(8,128)(2,1)}, bf16[256,1408]{1,0:T(8,128)(2,1)}, u32[]{:S(2)}, u32[]{:S(2)}) collective-permute-start(bf16[256,1408]{1,0:T(8,128)(2,1)} %get-tuple-element.443), channel_id=1, source_target_pairs={{0,4},{8,0},{16,8},{24,16},{28,24},{20,28},{12,20},{4,12},{1,5},{9... | collective-permute-start | bytes 2162696 | tf_op jit(solution)/shard_map/cond/branch_1_fun/ppermute | solution.py:60
  59.6 18.2 %collective-permute-start = (bf16[256,1408]{1,0:T(8,128)(2,1)}, bf16[256,1408]{1,0:T(8,128)(2,1)}, u32[]{:S(2)}, u32[]{:S(2)}) collective-permute-start(bf16[256,1408]{1,0:T(8,128)(2,1)} %get-tuple-element.448), channel_id=1, source_target_pairs={{0,8},{8,16},{16,24},{24,28},{28,20},{20,12},{12,4},{4,0},{1,9},{9... | collective-permute-start | bytes 2162696 | tf_op jit(solution)/shard_map/cond/branch_1_fun/ppermute | solution.py:60
  59.6 18.2 %collective-permute-start.1 = (bf16[256,1408]{1,0:T(8,128)(2,1)}, bf16[256,1408]{1,0:T(8,128)(2,1)}, u32[]{:S(2)}, u32[]{:S(2)}) collective-permute-start(bf16[256,1408]{1,0:T(8,128)(2,1)} %get-tuple-element.449), channel_id=1, source_target_pairs={{0,4},{8,0},{16,8},{24,16},{28,24},{20,28},{12,20},{4,12},{1,5},{9... | collective-permute-start | bytes 2162696 | tf_op jit(solution)/shard_map/cond/branch_1_fun/ppermute | solution.py:60
  78.4 14.2 %collective-permute-start.4 = (bf16[1024,512]{1,0:T(8,128)(2,1)S(1)}, bf16[1024,512]{1,0:T(8,128)(2,1)}, u32[]{:S(2)}, u32[]{:S(2)}) collective-permute-start(bf16[1024,512]{1,0:T(8,128)(2,1)S(1)} %get-tuple-element.452), channel_id=1, source_target_pairs={{0,1},{1,0},{2,3},{3,2},{4,5},{5,4},{6,7},{7,6},{8,9},{9,8},{10,11... | collective-permute-start | bytes 3145736 | tf_op jit(solution)/shard_map/cond/branch_1_fun/ppermute | solution.py:116
  94.9 25.1 %collective-permute-start.19 = (bf16[512,1024]{1,0:T(8,128)(2,1)}, bf16[512,1024]{1,0:T(8,128)(2,1)}, u32[]{:S(2)}, u32[]{:S(2)}) collective-permute-start(bf16[512,1024]{1,0:T(8,128)(2,1)} %copy.43), channel_id=1, source_target_pairs={{0,8},{8,16},{16,24},{24,28},{28,20},{20,12},{12,4},{4,0},{1,9},{9... | collective-permute-start | bytes 3145736 | tf_op jit(solution)/shard_map/cond/branch_1_fun/ppermute | solution.py:60
  96.6 24.5 %collective-permute-start.20 = (bf16[512,1024]{1,0:T(8,128)(2,1)}, bf16[512,1024]{1,0:T(8,128)(2,1)}, u32[]{:S(2)}, u32[]{:S(2)}) collective-permute-start(bf16[512,1024]{1,0:T(8,128)(2,1)} %copy.43), channel_id=1, source_target_pairs={{0,4},{8,0},{16,8},{24,16},{28,24},{20,28},{12,20},{4,12},{1,5},{9... | collective-permute-start | bytes 3145736 | tf_op jit(solution)/shard_map/cond/branch_1_fun/ppermute | solution.py:60
  121.9 33.1 %collective-permute-start.8 = (bf16[1024,512]{1,0:T(8,128)(2,1)}, bf16[1024,512]{1,0:T(8,128)(2,1)}, u32[]{:S(2)}, u32[]{:S(2)}) collective-permute-start(bf16[1024,512]{1,0:T(8,128)(2,1)} %get-tuple-element.500), channel_id=1, source_target_pairs={{0,1},{1,0},{2,3},{3,2},{4,5},{5,4},{6,7},{7,6},{8,9},{9,8},{10,11... | collective-permute-start | bytes 3145736 | tf_op jit(solution)/shard_map/cond/branch_1_fun/ppermute | solution.py:116
  122.0 33.1 %collective-permute-start.9 = (bf16[1024,512]{1,0:T(8,128)(2,1)}, bf16[1024,512]{1,0:T(8,128)(2,1)}, u32[]{:S(2)}, u32[]{:S(2)}) collective-permute-start(bf16[1024,512]{1,0:T(8,128)(2,1)} %get-tuple-element.500), channel_id=1, source_target_pairs={{0,2},{1,3},{2,0},{3,1},{4,6},{5,7},{6,4},{7,5},{8,10},{9,11},{10,... | collective-permute-start | bytes 3145736 | tf_op jit(solution)/shard_map/cond/branch_1_fun/ppermute | solution.py:116
  122.0 33.1 %collective-permute-start.5 = (bf16[512,1024]{1,0:T(8,128)(2,1)}, bf16[512,1024]{1,0:T(8,128)(2,1)}, u32[]{:S(2)}, u32[]{:S(2)}) collective-permute-start(bf16[512,1024]{1,0:T(8,128)(2,1)} %get-tuple-element.473), channel_id=1, source_target_pairs={{0,8},{8,16},{16,24},{24,28},{28,20},{20,12},{12,4},{4,0},{1,9},{9... | collective-permute-start | bytes 3145736 | tf_op jit(solution)/shard_map/cond/branch_1_fun/ppermute | solution.py:60
  123.7 31.4 %collective-permute-start.6 = (bf16[512,1024]{1,0:T(8,128)(2,1)}, bf16[512,1024]{1,0:T(8,128)(2,1)}, u32[]{:S(2)}, u32[]{:S(2)}) collective-permute-start(bf16[512,1024]{1,0:T(8,128)(2,1)} %get-tuple-element.474), channel_id=1, source_target_pairs={{0,4},{8,0},{16,8},{24,16},{28,24},{20,28},{12,20},{4,12},{1,5},{9... | collective-permute-start | bytes 3145736 | tf_op jit(solution)/shard_map/cond/branch_1_fun/ppermute | solution.py:60
  155.1 30.2 %collective-permute-start.32 = (bf16[512,1024]{1,0:T(8,128)(2,1)}, bf16[512,1024]{1,0:T(8,128)(2,1)}, u32[]{:S(2)}, u32[]{:S(2)}) collective-permute-start(bf16[512,1024]{1,0:T(8,128)(2,1)} %get-tuple-element.501), channel_id=1, source_target_pairs={{0,8},{8,16},{16,24},{24,28},{28,20},{20,12},{12,4},{4,0},{1,9},{9... | collective-permute-start | bytes 3145736 | tf_op jit(solution)/shard_map/cond/branch_1_fun/ppermute | solution.py:60
  155.2 30.2 %collective-permute-start.33 = (bf16[512,1024]{1,0:T(8,128)(2,1)}, bf16[512,1024]{1,0:T(8,128)(2,1)}, u32[]{:S(2)}, u32[]{:S(2)}) collective-permute-start(bf16[512,1024]{1,0:T(8,128)(2,1)} %get-tuple-element.502), channel_id=1, source_target_pairs={{0,4},{8,0},{16,8},{24,16},{28,24},{20,28},{12,20},{4,12},{1,5},{9... | collective-permute-start | bytes 3145736 | tf_op jit(solution)/shard_map/cond/branch_1_fun/ppermute | solution.py:60
  157.2 28.1 %collective-permute-start.35 = (bf16[1024,512]{1,0:T(8,128)(2,1)}, bf16[1024,512]{1,0:T(8,128)(2,1)}, u32[]{:S(2)}, u32[]{:S(2)}) collective-permute-start(bf16[1024,512]{1,0:T(8,128)(2,1)} %get-tuple-element.512), channel_id=1, source_target_pairs={{0,1},{1,0},{2,3},{3,2},{4,5},{5,4},{6,7},{7,6},{8,9},{9,8},{10,11... | collective-permute-start | bytes 3145736 | tf_op jit(solution)/shard_map/cond/branch_1_fun/ppermute | solution.py:116
  157.2 27.2 %collective-permute-start.34 = (bf16[144,1024]{1,0:T(8,128)(2,1)}, bf16[144,1024]{1,0:T(8,128)(2,1)S(1)}, u32[]{:S(2)}, u32[]{:S(2)}) collective-permute-start(bf16[144,1024]{1,0:T(8,128)(2,1)} %get-tuple-element.508), channel_id=1, source_target_pairs={{0,8},{4,12},{8,16},{12,20},{16,24},{20,28},{1,9},{5,13},{9,17},{1... | collective-permute-start | bytes 884744 | tf_op jit(solution)/shard_map/cond/branch_1_fun/ppermute | solution.py:189
  188.4 29.4 %collective-permute-start.10 = (bf16[256,1024]{1,0:T(8,128)(2,1)}, bf16[256,1024]{1,0:T(8,128)(2,1)}, u32[]{:S(2)}, u32[]{:S(2)}) collective-permute-start(bf16[256,1024]{1,0:T(8,128)(2,1)} %slice.169), channel_id=1, source_target_pairs={{0,8},{8,16},{16,24},{24,28},{28,20},{20,12},{12,4},{4,0},{1,9},{9... | collective-permute-start | bytes 1572872 | tf_op jit(solution)/shard_map/cond/branch_1_fun/ppermute | solution.py:60
  192.7 25.1 %collective-permute-start.11 = (bf16[256,1024]{1,0:T(8,128)(2,1)}, bf16[256,1024]{1,0:T(8,128)(2,1)}, u32[]{:S(2)}, u32[]{:S(2)}) collective-permute-start(bf16[256,1024]{1,0:T(8,128)(2,1)} %slice.170), channel_id=1, source_target_pairs={{0,4},{8,0},{16,8},{24,16},{28,24},{20,28},{12,20},{4,12},{1,5},{9... | collective-permute-start | bytes 1572872 | tf_op jit(solution)/shard_map/cond/branch_1_fun/ppermute | solution.py:60
  193.2 22.5 %collective-permute-start.12 = (bf16[128,1024]{1,0:T(8,128)(2,1)}, bf16[128,1024]{1,0:T(8,128)(2,1)S(1)}, u32[]{:S(2)}, u32[]{:S(2)}) collective-permute-start(bf16[128,1024]{1,0:T(8,128)(2,1)} %get-tuple-element.522), channel_id=1, source_target_pairs={{0,16},{4,20},{8,24},{12,28},{1,17},{5,21},{9,25},{13,29},{2,18},{... | collective-permute-start | bytes 786440 | tf_op jit(solution)/shard_map/cond/branch_1_fun/ppermute | solution.py:189
  258.4 16.3 %collective-permute-start.14 = (bf16[144,1024]{1,0:T(8,128)(2,1)S(1)}, bf16[144,1024]{1,0:T(8,128)(2,1)S(1)}, u32[]{:S(2)}, u32[]{:S(2)}) collective-permute-start(bf16[144,1024]{1,0:T(8,128)(2,1)S(1)} %get-tuple-element.554), channel_id=1, source_target_pairs={{0,4},{4,0},{8,12},{12,8},{16,20},{20,16},{24,28},{28,24},{1,5},{5... | collective-permute-start | bytes 884744 | tf_op jit(solution)/shard_map/cond/branch_1_fun/ppermute | solution.py:116
  277.4 22.0 %collective-permute-start.43 = (bf16[256,1024]{1,0:T(8,128)(2,1)S(1)}, bf16[256,1024]{1,0:T(8,128)(2,1)S(1)}, u32[]{:S(2)}, u32[]{:S(2)}) collective-permute-start(bf16[256,1024]{1,0:T(8,128)(2,1)S(1)} %get-tuple-element.1165), channel_id=1, source_target_pairs={{0,8},{8,16},{16,24},{24,28},{28,20},{20,12},{12,4},{4,0},{1,9},{9... | collective-permute-start | bytes 1572872 | tf_op jit(solution)/shard_map/cond/branch_1_fun/ppermute | solution.py:60
  278.6 20.8 %collective-permute-start.44 = (bf16[256,1024]{1,0:T(8,128)(2,1)S(1)}, bf16[256,1024]{1,0:T(8,128)(2,1)S(1)}, u32[]{:S(2)}, u32[]{:S(2)}) collective-permute-start(bf16[256,1024]{1,0:T(8,128)(2,1)S(1)} %get-tuple-element.1163), channel_id=1, source_target_pairs={{0,4},{8,0},{16,8},{24,16},{28,24},{20,28},{12,20},{4,12},{1,5},{9... | collective-permute-start | bytes 1572872 | tf_op jit(solution)/shard_map/cond/branch_1_fun/ppermute | solution.py:60
  279.5 19.8 %collective-permute-start.42 = (bf16[144,1024]{1,0:T(8,128)(2,1)}, bf16[144,1024]{1,0:T(8,128)(2,1)S(1)}, u32[]{:S(2)}, u32[]{:S(2)}) collective-permute-start(bf16[144,1024]{1,0:T(8,128)(2,1)} %get-tuple-element.577), channel_id=1, source_target_pairs={{8,0},{12,4},{16,8},{20,12},{24,16},{28,20},{9,1},{13,5},{17,9},{2... | collective-permute-start | bytes 884744 | tf_op jit(solution)/shard_map/cond/branch_1_fun/ppermute | solution.py:189
  302.6 15.9 %collective-permute-start.15 = (bf16[128,1024]{1,0:T(8,128)(2,1)S(1)}, bf16[128,1024]{1,0:T(8,128)(2,1)S(1)}, u32[]{:S(2)}, u32[]{:S(2)}) collective-permute-start(bf16[128,1024]{1,0:T(8,128)(2,1)S(1)} %get-tuple-element.597), channel_id=1, source_target_pairs={{16,0},{20,4},{24,8},{28,12},{17,1},{21,5},{25,9},{29,13},{18,2},{... | collective-permute-start | bytes 786440 | tf_op jit(solution)/shard_map/cond/branch_1_fun/ppermute | solution.py:189
  357.9 28.5 %collective-permute-start.22 = (bf16[512,1024]{1,0:T(8,128)(2,1)}, bf16[512,1024]{1,0:T(8,128)(2,1)}, u32[]{:S(2)}, u32[]{:S(2)}) collective-permute-start(bf16[512,1024]{1,0:T(8,128)(2,1)} %get-tuple-element.610), channel_id=1, source_target_pairs={{0,8},{8,16},{16,24},{24,28},{28,20},{20,12},{12,4},{4,0},{1,9},{9... | collective-permute-start | bytes 3145736 | tf_op jit(solution)/shard_map/cond/branch_1_fun/ppermute | solution.py:60
  357.9 28.5 %collective-permute-start.23 = (bf16[512,1024]{1,0:T(8,128)(2,1)}, bf16[512,1024]{1,0:T(8,128)(2,1)}, u32[]{:S(2)}, u32[]{:S(2)}) collective-permute-start(bf16[512,1024]{1,0:T(8,128)(2,1)} %get-tuple-element.611), channel_id=1, source_target_pairs={{0,4},{8,0},{16,8},{24,16},{28,24},{20,28},{12,20},{4,12},{1,5},{9... | collective-permute-start | bytes 3145736 | tf_op jit(solution)/shard_map/cond/branch_1_fun/ppermute | solution.py:60
  390.9 31.7 %collective-permute-start.30 = (bf16[512,1024]{1,0:T(8,128)(2,1)}, bf16[512,1024]{1,0:T(8,128)(2,1)S(1)}, u32[]{:S(2)}, u32[]{:S(2)}) collective-permute-start(bf16[512,1024]{1,0:T(8,128)(2,1)} %get-tuple-element.634), channel_id=1, source_target_pairs={{0,8},{8,16},{16,24},{24,28},{28,20},{20,12},{12,4},{4,0},{1,9},{9... | collective-permute-start | bytes 3145736 | tf_op jit(solution)/shard_map/cond/branch_1_fun/ppermute | solution.py:60
  394.6 28.0 %collective-permute-start.31 = (bf16[512,1024]{1,0:T(8,128)(2,1)}, bf16[512,1024]{1,0:T(8,128)(2,1)S(1)}, u32[]{:S(2)}, u32[]{:S(2)}) collective-permute-start(bf16[512,1024]{1,0:T(8,128)(2,1)} %get-tuple-element.635), channel_id=1, source_target_pairs={{0,4},{8,0},{16,8},{24,16},{28,24},{20,28},{12,20},{4,12},{1,5},{9... | collective-permute-start | bytes 3145736 | tf_op jit(solution)/shard_map/cond/branch_1_fun/ppermute | solution.py:60
  431.8 32.5 %collective-permute-start.50 = (bf16[128,1408]{1,0:T(8,128)(2,1)}, bf16[128,1408]{1,0:T(8,128)(2,1)}, u32[]{:S(2)}, u32[]{:S(2)}) collective-permute-start(bf16[128,1408]{1,0:T(8,128)(2,1)} %get-tuple-element.1183), channel_id=1, source_target_pairs={{0,8},{8,16},{16,24},{24,28},{28,20},{20,12},{12,4},{4,0},{1,9},{9... | collective-permute-start | bytes 1081352 | tf_op jit(solution)/shard_map/cond/branch_1_fun/ppermute | solution.py:60
  433.8 30.5 %collective-permute-start.51 = (bf16[128,1408]{1,0:T(8,128)(2,1)}, bf16[128,1408]{1,0:T(8,128)(2,1)}, u32[]{:S(2)}, u32[]{:S(2)}) collective-permute-start(bf16[128,1408]{1,0:T(8,128)(2,1)} %get-tuple-element.1181), channel_id=1, source_target_pairs={{0,4},{8,0},{16,8},{24,16},{28,24},{20,28},{12,20},{4,12},{1,5},{9... | collective-permute-start | bytes 1081352 | tf_op jit(solution)/shard_map/cond/branch_1_fun/ppermute | solution.py:60
  433.8 33.2 %collective-permute-start.48 = (bf16[512,1024]{1,0:T(8,128)(2,1)}, bf16[512,1024]{1,0:T(8,128)(2,1)}, u32[]{:S(2)}, u32[]{:S(2)}) collective-permute-start(bf16[512,1024]{1,0:T(8,128)(2,1)} %get-tuple-element.660), channel_id=1, source_target_pairs={{0,8},{8,16},{16,24},{24,28},{28,20},{20,12},{12,4},{4,0},{1,9},{9... | collective-permute-start | bytes 3145736 | tf_op jit(solution)/shard_map/cond/branch_1_fun/ppermute | solution.py:60
  435.8 31.2 %collective-permute-start.49 = (bf16[512,1024]{1,0:T(8,128)(2,1)}, bf16[512,1024]{1,0:T(8,128)(2,1)}, u32[]{:S(2)}, u32[]{:S(2)}) collective-permute-start(bf16[512,1024]{1,0:T(8,128)(2,1)} %get-tuple-element.661), channel_id=1, source_target_pairs={{0,4},{8,0},{16,8},{24,16},{28,24},{20,28},{12,20},{4,12},{1,5},{9... | collective-permute-start | bytes 3145736 | tf_op jit(solution)/shard_map/cond/branch_1_fun/ppermute | solution.py:60
  435.9 27.7 %collective-permute-start.52 = (f32[7200]{0:T(1024)}, f32[7200]{0:T(1024)S(1)}, u32[]{:S(2)}, u32[]{:S(2)}) collective-permute-start(f32[7200]{0:T(1024)} %get-tuple-element.671), channel_id=1, source_target_pairs={{0,4},{4,0},{8,12},{12,8},{16,20},{20,16},{24,28},{28,24},{1,5},{5... | collective-permute-start | bytes 86408 | tf_op jit(solution)/shard_map/cond/branch_1_fun/ppermute | solution.py:116
  473.8 22.5 %collective-permute-start.62 = (bf16[1024,512]{1,0:T(8,128)(2,1)}, bf16[1024,512]{1,0:T(8,128)(2,1)S(1)}, u32[]{:S(2)}, u32[]{:S(2)}) collective-permute-start(bf16[1024,512]{1,0:T(8,128)(2,1)} %copy-done.32), channel_id=1, source_target_pairs={{0,2},{1,3},{2,0},{3,1},{4,6},{5,7},{6,4},{7,5},{8,10},{9,11},{10,... | collective-permute-start | bytes 3145736 | tf_op jit(solution)/shard_map/ppermute | solution.py:116
  496.3 17.5 %collective-permute-start.53 = (bf16[256,1408]{1,0:T(8,128)(2,1)}, bf16[256,1408]{1,0:T(8,128)(2,1)S(1)}, u32[]{:S(2)}, u32[]{:S(2)}) collective-permute-start(bf16[256,1408]{1,0:T(8,128)(2,1)} %get-tuple-element.675), channel_id=1, source_target_pairs={{0,8},{8,16},{16,24},{24,28},{28,20},{20,12},{12,4},{4,0},{1,9},{9... | collective-permute-start | bytes 2162696 | tf_op jit(solution)/shard_map/cond/branch_1_fun/ppermute | solution.py:60
  496.6 17.2 %collective-permute-start.54 = (bf16[256,1408]{1,0:T(8,128)(2,1)}, bf16[256,1408]{1,0:T(8,128)(2,1)S(1)}, u32[]{:S(2)}, u32[]{:S(2)}) collective-permute-start(bf16[256,1408]{1,0:T(8,128)(2,1)} %get-tuple-element.676), channel_id=1, source_target_pairs={{0,4},{8,0},{16,8},{24,16},{28,24},{20,28},{12,20},{4,12},{1,5},{9... | collective-permute-start | bytes 2162696 | tf_op jit(solution)/shard_map/cond/branch_1_fun/ppermute | solution.py:60
  498.5 18.1 %collective-permute-start.55 = (bf16[1024,512]{1,0:T(8,128)(2,1)S(1)}, bf16[1024,512]{1,0:T(8,128)(2,1)S(1)}, u32[]{:S(2)}, u32[]{:S(2)}) collective-permute-start(bf16[1024,512]{1,0:T(8,128)(2,1)S(1)} %get-tuple-element.1195), channel_id=1, source_target_pairs={{0,1},{1,0},{2,3},{3,2},{4,5},{5,4},{6,7},{7,6},{8,9},{9,8},{10,11... | collective-permute-start | bytes 3145736 | tf_op jit(solution)/shard_map/cond/branch_1_fun/ppermute | solution.py:116
  498.6 18.0 %collective-permute-start.56 = (bf16[1024,512]{1,0:T(8,128)(2,1)S(1)}, bf16[1024,512]{1,0:T(8,128)(2,1)S(1)}, u32[]{:S(2)}, u32[]{:S(2)}) collective-permute-start(bf16[1024,512]{1,0:T(8,128)(2,1)S(1)} %get-tuple-element.1194), channel_id=1, source_target_pairs={{0,1},{1,0},{2,3},{3,2},{4,5},{5,4},{6,7},{7,6},{8,9},{9,8},{10,11... | collective-permute-start | bytes 3145736 | tf_op jit(solution)/shard_map/cond/branch_1_fun/ppermute | solution.py:116
  499.1 14.7 %collective-permute-start.57 = (f32[7200]{0:T(1024)S(1)}, f32[7200]{0:T(1024)S(1)}, u32[]{:S(2)}, u32[]{:S(2)}) collective-permute-start(f32[7200]{0:T(1024)S(1)} %get-tuple-element.678), channel_id=1, source_target_pairs={{0,8},{4,12},{8,0},{12,4},{16,24},{20,28},{24,16},{28,20},{1,9},{5... | collective-permute-start | bytes 86408 | tf_op jit(solution)/shard_map/cond/branch_1_fun/ppermute | solution.py:116
  518.1 28.6 %collective-permute-start.63 = (bf16[1024,512]{1,0:T(8,128)(2,1)}, bf16[1024,512]{1,0:T(8,128)(2,1)}, u32[]{:S(2)}, u32[]{:S(2)}) collective-permute-start(bf16[1024,512]{1,0:T(8,128)(2,1)} %get-tuple-element.968), channel_id=1, source_target_pairs={{0,2},{1,3},{2,0},{3,1},{4,6},{5,7},{6,4},{7,5},{8,10},{9,11},{10,... | collective-permute-start | bytes 3145736 | tf_op jit(solution)/shard_map/ppermute | solution.py:116
  520.2 23.3 %collective-permute-start.58 = (bf16[256,1408]{1,0:T(8,128)(2,1)}, bf16[256,1408]{1,0:T(8,128)(2,1)}, u32[]{:S(2)}, u32[]{:S(2)}) collective-permute-start(bf16[256,1408]{1,0:T(8,128)(2,1)} %get-tuple-element.683), channel_id=1, source_target_pairs={{0,8},{8,16},{16,24},{24,28},{28,20},{20,12},{12,4},{4,0},{1,9},{9... | collective-permute-start | bytes 2162696 | tf_op jit(solution)/shard_map/cond/branch_1_fun/ppermute | solution.py:60
  520.4 23.0 %collective-permute-start.59 = (bf16[256,1408]{1,0:T(8,128)(2,1)}, bf16[256,1408]{1,0:T(8,128)(2,1)}, u32[]{:S(2)}, u32[]{:S(2)}) collective-permute-start(bf16[256,1408]{1,0:T(8,128)(2,1)} %get-tuple-element.684), channel_id=1, source_target_pairs={{0,4},{8,0},{16,8},{24,16},{28,24},{20,28},{12,20},{4,12},{1,5},{9... | collective-permute-start | bytes 2162696 | tf_op jit(solution)/shard_map/cond/branch_1_fun/ppermute | solution.py:60
  522.5 14.6 %collective-permute-start.60 = (f32[7200]{0:T(1024)S(1)}, f32[7200]{0:T(1024)S(1)}, u32[]{:S(2)}, u32[]{:S(2)}) collective-permute-start(f32[7200]{0:T(1024)S(1)} %get-tuple-element.685), channel_id=1, source_target_pairs={{0,16},{4,20},{8,24},{12,28},{16,0},{20,4},{24,8},{28,12},{1,17},{... | collective-permute-start | bytes 86408 | tf_op jit(solution)/shard_map/cond/branch_1_fun/ppermute | solution.py:116
  547.3 14.0 %collective-permute-start.40 = (bf16[256,1408]{1,0:T(8,128)(2,1)}, bf16[256,1408]{1,0:T(8,128)(2,1)}, u32[]{:S(2)}, u32[]{:S(2)}) collective-permute-start(bf16[256,1408]{1,0:T(8,128)(2,1)} %get-tuple-element.690), channel_id=1, source_target_pairs={{0,8},{8,16},{16,24},{24,28},{28,20},{20,12},{12,4},{4,0},{1,9},{9... | collective-permute-start | bytes 2162696 | tf_op jit(solution)/shard_map/cond/branch_1_fun/ppermute | solution.py:60
  549.1 14.2 %collective-permute-start.41 = (bf16[256,1408]{1,0:T(8,128)(2,1)}, bf16[256,1408]{1,0:T(8,128)(2,1)}, u32[]{:S(2)}, u32[]{:S(2)}) collective-permute-start(bf16[256,1408]{1,0:T(8,128)(2,1)} %get-tuple-element.691), channel_id=1, source_target_pairs={{0,4},{8,0},{16,8},{24,16},{28,24},{20,28},{12,20},{4,12},{1,5},{9... | collective-permute-start | bytes 2162696 | tf_op jit(solution)/shard_map/cond/branch_1_fun/ppermute | solution.py:60
  (73 other events, 842.9 us)

commit v3 on v2

--- a/solution.py
+++ b/solution.py
@@ -12,6 +12,7 @@
 KERNEL = 4
 SPAN = 128
 HALO = 8
+ADD_STEPS = 2
 LANES = 128
 EPS = 1e-05
 HIGHEST = lax.Precision.HIGHEST
@@ -23,6 +24,10 @@
 TN = (((0,), (0,)), ((), ()))
 
 
+def lasts(micros):
+    return pl.CostEstimate(flops=0, bytes_accessed=int(micros * 3.3e6), transcendentals=0)
+
+
 def dot(left, right, dims=NN, precision=None):
     return lax.dot_general(left, right, dims, precision=precision, preferred_element_type=F32)
 
@@ -75,30 +80,41 @@
         k = k % self.size
         return whole[k * n : (k + 1) * n]
 
-    def send(self, whole):
-        if not self.on:
-            return None
-        far = self.part(whole, self.size // 2)
-        cut = far.shape[0] // 2
-        return self.shift(far[:cut], 1), self.shift(far[cut:], -1)
+    def send(self, first, second):
+        return self.shift(first, 1), self.shift(second, -1)
 
     def add(self, whole, came, k):
         if not self.on:
-            return None
-        right, left = self.part(whole, k).astype(F32), self.part(whole, -k).astype(F32)
-        first, second = came[0].astype(F32), came[1].astype(F32)
-        if k == self.size // 2 - 1:
-            cut = first.shape[0]
-            right = jnp.concatenate([right[:cut] + first, right[cut:]], axis=0)
-            left = jnp.concatenate([left[:cut], left[cut:] + second], axis=0)
-        else:
-            right, left = right + first, left + second
-        return right.astype(BF16), left.astype(BF16)
-
-    def total(self, whole, came):
-        if not self.on:
-            return lax.psum_scatter(whole, "seq", scatter_dimension=0, tiled=True).astype(F32)
-        return self.part(whole, 0).astype(F32) + came[0].astype(F32) + came[1].astype(F32)
+            return ()
+        rows, columns = whole.shape[0] // self.size, whole.shape[1]
+        halves = k == self.size // 2 - 1
+        steps = ADD_STEPS
+        tile = rows // steps
+
+        def kernel(a_ref, b_ref, right_ref, left_ref, out_a_ref, out_b_ref):
+            right, left = right_ref[...].astype(F32), left_ref[...].astype(F32)
+            if halves:
+                upper = pl.program_id(0) < steps // 2
+                right, left = jnp.where(upper, right, 0.0), jnp.where(upper, 0.0, left)
+            out_a_ref[...] = (a_ref[...].astype(F32) + right).astype(BF16)
+            out_b_ref[...] = (b_ref[...].astype(F32) + left).astype(BF16)
+
+        block = lambda at: pl.BlockSpec((tile, columns), at)
+        plain = lambda i: (i, 0)
+        out = jax.ShapeDtypeStruct((rows, columns), BF16)
+        return pl.pallas_call(
+            kernel,
+            grid=(steps,),
+            in_specs=[
+                block(lambda i: (steps * k + i, 0)),
+                block(lambda i: (steps * (self.size - k) + i, 0)),
+                block((lambda i: (jnp.minimum(i, steps // 2 - 1), 0)) if halves else plain),
+                block((lambda i: (jnp.maximum(i - steps // 2, 0), 0)) if halves else plain),
+            ],
+            out_specs=[block(plain), block(plain)],
+            out_shape=[out, out],
+            compiler_params=pltpu.CompilerParams(vmem_limit_bytes=VMEM_LIMIT),
+        )(whole, whole, *came)
 
     def phase(self, work, *args):
         if not self.on:
@@ -544,9 +560,9 @@
 
 
 def finish_kernel(
-    pairs, v_ref, dy_ref, du_ref, ssd_ref, st_ref, wc_ref, we_ref, la_ref, se_ref, dbc_ref,
-    dt_ref, bias_ref, rate_ref, skip_ref, pick_ref,
-    dcx_ref, dbo_ref, ddt_ref, dskip_ref, dhead_ref, run, moves, drives,
+    pairs, split, v_ref, dy_ref, du_ref, ssd_ref, st_ref, wc_ref, we_ref, la_ref, se_ref, dbc_ref,
+    dt_ref, bias_ref, rate_ref, skip_ref, pick_ref, at_ref,
+    dcx_ref, keep_ref, send_ref, ddt_ref, dskip_ref, dhead_ref, run, moves, drives,
 ):
     rows = v_ref.shape[0]
     inner = pairs * LANES
@@ -588,8 +604,20 @@
         dskip_ref[0:1, at] += jnp.sum(dy * x, axis=0, keepdims=True)
         d_inner = wide * du + skip * dy
         dcx_ref[:, at] = (d_inner * silu_slope(value, logistic)).astype(BF16)
-    dbo_ref[:, :LANES] = d_b
-    dbo_ref[:, LANES:] = dbc_ref[:, LANES:]
+    d_c = dbc_ref[:, LANES:]
+    if split:
+        turn = lambda a: pltpu.roll(a, P_SIZE, 1)
+        near, far = jnp.where(at_ref[1] == 0, d_b, d_c), jnp.where(at_ref[1] == 0, d_c, d_b)
+        low, core = lane_is_low(rows), at_ref[0] == 0
+        keep_ref[...] = jnp.where(
+            core, jnp.where(low, near, turn(far)), jnp.where(low, turn(near), far)
+        )
+        send_ref[...] = jnp.where(
+            core, jnp.where(low, turn(near), far), jnp.where(low, near, turn(far))
+        )
+    else:
+        keep_ref[...] = d_b
+        send_ref[...] = d_c
     moved = per_head(moves, picker, rows)
     driven = per_head(drives, picker, rows)
     upper = triangle(rows, lambda t, s: s >= t).astype(F32)
@@ -649,7 +677,7 @@
 
 def in_project_kernel(spot_ref, *refs):
     acts, items, halves = refs[:4], refs[4:11], refs[11:13]
-    x_ref, bc_ref, dt_ref, w_ref, r_ref = refs[13:]
+    x_ref, rest_ref, w_ref, r_ref = refs[13:]
     rows = items[0].shape[0]
     inner = x_ref.shape[1]
 
@@ -662,9 +690,7 @@
 
     act = jnp.concatenate([a[...] for a in acts], axis=1)
     x_ref[...] = dot(act, w_ref[...]).astype(BF16)
-    rest = dot(act, r_ref[...])
-    bc_ref[...] = rest[:, : 2 * N].astype(BF16)
-    dt_ref[...] = rest[:, 2 * N :]
+    rest_ref[...] = dot(act, r_ref[...])
 
 
 def gate_project_kernel(spot_ref, *refs):
@@ -710,17 +736,19 @@
         ),
         out_shape=shapes,
         compiler_params=pltpu.CompilerParams(vmem_limit_bytes=VMEM_LIMIT),
+        cost_estimate=lasts(15.0),
     )(spots, *acts, *items)
 
 
-def outer_kernel(pairs_of, block_ref, *refs):
+def outer_kernel(pairs_of, far_ref, block_ref, *refs):
     out_ref = refs[-1]
     n = len(pairs_of)
     grads = refs[4 * n : -1]
     width = refs[0].shape[1]
+    spot = far_ref[0] ^ (pl.program_id(0) + 1)
     for a in range(4):
 
-        @pl.when(pl.program_id(0) // 2 == a)
+        @pl.when(spot // 2 == a)
         def _():
             taken = 0
             for i, count in enumerate(pairs_of):
@@ -734,33 +762,69 @@
                 taken += count
 
 
-def outer(blocks, *terms):
+def outer(far, blocks, *terms):
     total, own = terms[0][0][0].shape
     width = own // 2
+
+    def pick(i, far, blocks, a):
+        late = i + 1 > 2 * ((far[0] >> 1) ^ a)
+        return 0, jnp.where(late, 1 - (far[0] & 1), far[0] & 1)
+
     specs, args = [], []
     for acts, _ in terms:
         for a, act in enumerate(acts):
-            specs.append(
-                pl.BlockSpec((total, width), lambda i, _, a=a: (0, jnp.clip(i - 2 * a, 0, 1)))
-            )
+            specs.append(pl.BlockSpec((total, width), functools.partial(pick, a=a)))
             args.append(act)
     for _, grads in terms:
         for grad in grads:
-            specs.append(pl.BlockSpec(grad.shape, lambda i, _: (0, 0)))
+            specs.append(pl.BlockSpec(grad.shape, lambda i, far, blocks: (0, 0)))
             args.append(grad)
     columns = sum(g.shape[1] for g in terms[0][1])
     rows = width * len(terms)
     return pl.pallas_call(
         functools.partial(outer_kernel, [len(grads) for _, grads in terms]),
         grid_spec=pltpu.PrefetchScalarGridSpec(
-            num_scalar_prefetch=1,
-            grid=(8,),
+            num_scalar_prefetch=2,
+            grid=(7,),
             in_specs=specs,
-            out_specs=pl.BlockSpec((rows, columns), lambda i, block: (block[i], 0)),
+            out_specs=pl.BlockSpec(
+                (rows, columns), lambda i, far, blocks: (blocks[far[0] ^ (i + 1)], 0)
+            ),
         ),
         out_shape=shaped(8 * rows, columns, dtype=BF16),
         compiler_params=pltpu.CompilerParams(vmem_limit_bytes=VMEM_LIMIT),
-    )(blocks, *args)
+        cost_estimate=lasts(8.0 * rows * columns / 2**18),
+    )(far, blocks, *args)
+
+
+def outer_far(acts, grads):
+    vmem = pl.BlockSpec(memory_space=pltpu.VMEM)
+    columns = grads[0].shape[1] if len(acts) == 2 else sum(g.shape[1] for g in grads)
+    width = acts[0].shape[1]
+
+    def kernel(*refs):
+        first, second = refs[-2:]
+        given = refs[len(acts) : -2]
+        if len(acts) == 2:
+            first[...] = dot(refs[0][...], given[0][...], TN).astype(BF16)
+            second[...] = dot(refs[1][...], given[1][...], TN).astype(BF16)
+            return
+        start = 0
+        for grad in given:
+            wide = grad.shape[1]
+            both = dot(refs[0][...], grad[...], TN).astype(BF16)
+            first[:, start : start + wide] = both[: width // 2]
+            second[:, start : start + wide] = both[width // 2 :]
+            start += wide
+
+    half = shaped(width if len(acts) == 2 else width // 2, columns, dtype=BF16)
+    return pl.pallas_call(
+        kernel,
+        in_specs=[vmem] * (len(acts) + len(grads)),
+        out_specs=[vmem, vmem],
+        out_shape=[half, half],
+        compiler_params=pltpu.CompilerParams(vmem_limit_bytes=VMEM_LIMIT),
+    )(*acts, *grads)
 
 
 def project_kernel(terms, late, spot_ref, *refs):
@@ -792,7 +856,47 @@
         ),
         out_shape=shaped(rows, weights[0].shape[0], dtype=BF16),
         compiler_params=pltpu.CompilerParams(vmem_limit_bytes=VMEM_LIMIT),
+        cost_estimate=lasts(7.0 * sum(a.shape[1] for a in acts) / 1024),
     )(spots, *acts, *weights, *late)
+
+
+def block_total(refs, cut):
+    return sum(ref[cut].astype(F32) for ref in refs)
+
+
+def total_zo_kernel(own_ref, right_ref, left_ref, w_ref, gz_ref, go_ref, met_ref):
+    refs = own_ref, right_ref, left_ref
+    rows = w_ref.shape[0]
+    g_z = block_total(refs, slice(0, rows))
+    gz_ref[...] = g_z
+    go_ref[...] = block_total(refs, slice(rows, 2 * rows)).T
+    met_ref[...] = jnp.sum(g_z * w_ref[...].astype(F32), axis=1, keepdims=True)
+
+
+def total_in_kernel(own_ref, right_ref, left_ref, w_ref, met_in, gx_ref, gb_ref, gd_ref, met_ref):
+    total = block_total((own_ref, right_ref, left_ref), slice(None))
+    inner, heads = gx_ref.shape[1], gd_ref.shape[1]
+    gx_ref[...] = total[:, :inner]
+    gb_ref[...] = total[:, inner : inner + gb_ref.shape[1]]
+    start = inner + gb_ref.shape[1]
+    gd_ref[...] = total[:, start : start + heads]
+    met = jnp.sum(total * w_ref[...].astype(F32), axis=1, keepdims=True)
+    met_ref[...] = met_in[...] + met
+
+
+def totals(kernel, whole, came, others, shapes):
+    rows = came[0].shape[0]
+    fixed = lambda i: (0, 0)
+    arrays = [*came, *others]
+    return pl.pallas_call(
+        kernel,
+        grid=(1,),
+        in_specs=[pl.BlockSpec((rows, whole.shape[1]), fixed)]
+        + [pl.BlockSpec(a.shape, fixed) for a in arrays],
+        out_specs=[pl.BlockSpec(shape.shape, fixed) for shape in shapes],
+        out_shape=shapes,
+        compiler_params=pltpu.CompilerParams(vmem_limit_bytes=VMEM_LIMIT),
+    )(whole, *arrays)
 
 
 def shaped(*shape, dtype=F32):
@@ -808,9 +912,7 @@
         out_shape=shapes,
         scratch_shapes=list(scratch),
         compiler_params=pltpu.CompilerParams(vmem_limit_bytes=VMEM_LIMIT),
-        cost_estimate=pl.CostEstimate(
-            flops=0, bytes_accessed=int(micros * 3.3e6), transcendentals=0
-        ),
+        cost_estimate=lasts(micros),
     )
 
 
@@ -1007,22 +1109,24 @@
         lane_head = lax.broadcasted_iota(jnp.int32, (inner, heads), 0) // P_SIZE
         picker = (lane_head == lax.broadcasted_iota(jnp.int32, (inner, heads), 1)).astype(BF16)
         at_end = jnp.exp(left_w) * came + left
-        d_conv_x, d_bc_part, d_dt, g_skip, g_heads = call(
-            functools.partial(finish_kernel, pairs),
+        d_conv_x, d_bc_keep, d_bc_send, d_dt, g_skip, g_heads = call(
+            functools.partial(finish_kernel, pairs, ring.on),
             (batch, count),
             [
                 v_back, block_back, block_back, block_back, heads_back, heads_back,
                 pl.BlockSpec((1, 1, inner), seq3), state_spec, state_spec, bc_back, heads_back,
                 row_heads, row_heads, row_inner,
-                pl.BlockSpec((inner, heads), fixed),
+                pl.BlockSpec((inner, heads), fixed), pl.BlockSpec(memory_space=pltpu.SMEM),
             ],
             [
-                block_back, bc_back, heads_back, row_inner,
+                block_back, pl.BlockSpec((rows, LANES), back), pl.BlockSpec((rows, LANES), back),
+                heads_back, row_inner,
                 pl.BlockSpec((2, heads), fixed),
             ],
             [
                 shaped(total, inner, dtype=BF16),
-                shaped(total, 2 * N),
+                shaped(total, LANES),
+                shaped(total, LANES),
                 shaped(total, heads, dtype=BF16),
                 shaped(1, inner),
                 shaped(2, heads),
@@ -1036,28 +1140,50 @@
         )(
             conv_out, d_ssd, du_local, ssd, steps, cumulative, left_w, later, at_end, dbc_local,
             dt_raw, bias_row, rate_row, skip_lanes, picker,
+            jnp.stack([here & 1, here >> 1]).astype(jnp.int32),
         )
-        return d_conv_x, d_bc_part, d_dt, g_skip, g_heads
+        return d_conv_x, d_bc_keep, d_bc_send, d_dt, g_skip, g_heads
 
     split_pass = ring.on and batch == 2
     forth, back_pass = Passing(ring, 1, inner), Passing(ring, -1, inner)
     slope = lambda v: silu_slope(v, jax.nn.sigmoid(v))
 
-    edge_at = inner + 2 * N
-    spare = -(2 * N + heads) % LANES
+    group = 2 * N // 4 if ring.on else 2 * N
+    edge_at = inner + group
+    spare = -(group + heads) % LANES
     per = w_z.shape[0]
+    own_columns = lambda a: lax.dynamic_slice_in_dim(a, here * group, group, 1) if ring.on else a
     all_in = jnp.concatenate(
-        [w_x, w_bc, w_dt, jnp.zeros((w_x.shape[0], spare), BF16)], axis=1
-    )
+        [w_x, own_columns(w_bc), w_dt, jnp.zeros((w_x.shape[0], spare), BF16)], axis=1
+    )
+
+    def by_group(pieces):
+        own, near, far, both = pieces
+        return [
+            jnp.where(
+                here == g, own, jnp.where(here == g ^ 1, near, jnp.where(here == g ^ 2, far, both))
+            )
+            for g in range(4)
+        ]
+
+    def gather_groups(own):
+        far = swap(own, "head", 2)
+        return by_group([own, swap(own, "head", 1), far, swap(far, "head", 1)])
+
+    def fold(a):
+        return jnp.concatenate([a[: total // 2], a[total // 2 :]], axis=1)
+
+    def unfold(a):
+        n = a.shape[1] // 2
+        return jnp.concatenate([a[:, :n], a[:, n:]], axis=0)
     spots, order = (ring.spots(), ring.blocks()) if ring.on else (None, None)
 
     def work(all_in, slab):
         own_gain = own_features(ring, norm_gain.astype(F32), own_width)
-        block = all_in + 0.0 * own_gain[:1].astype(BF16)
         square = head_sum(jnp.sum(slab * slab, axis=1))
         scale = lax.rsqrt(square / model + EPS)
         own_normed = (slab * scale[:, None] * own_gain).astype(BF16)
-        return ring.hop((block, block)), own_gain, scale, own_normed
+        return ring.hop((all_in, all_in)), own_gain, scale, own_normed
 
     hop1, own_gain, scale, own_normed = ring.phase(work, all_in, slab)
     far = across(ring, own_normed)
@@ -1073,29 +1199,34 @@
     )
     normed = (both, near, far, own_normed) if ring.on else (both,)
 
-    def work(normed, hop1, hop2, hop3, hop4, zo_in):
-        moving = ring.hop((zo_in, zo_in))
+    def project_in(normed, hop1, hop2, hop3, hop4):
         if ring.on:
-            x_in, bc_in, dt_raw, x_w, rest_w = with_spots(
+            x_in, rest, x_w, rest_w = with_spots(
                 in_project_kernel, spots, normed, [all_in, *hop1, *hop2, *hop3, *hop4],
-                [True, True, True, False, False],
+                [True, True, False, False],
                 [
-                    shaped(total, inner, dtype=BF16), shaped(total, 2 * N, dtype=BF16),
-                    shaped(total, all_in.shape[1] - edge_at), shaped(model, inner, dtype=BF16),
+                    shaped(total, inner, dtype=BF16), shaped(total, all_in.shape[1] - inner),
+                    shaped(model, inner, dtype=BF16),
                     shaped(model, all_in.shape[1] - inner, dtype=BF16),
                 ],
             )
+            groups = gather_groups(fold(rest[:, :group]).astype(BF16))
+            bc_in = jnp.concatenate([unfold(piece) for piece in groups], axis=1)
         else:
             x_w = lax.all_gather(w_x, "seq", axis=0, tiled=True)
             rest_w = lax.all_gather(all_in[:, inner:], "seq", axis=0, tiled=True)
             rest = dot(normed[0], rest_w)
-            x_in, bc_in = dot(normed[0], x_w).astype(BF16), rest[:, : 2 * N].astype(BF16)
-            dt_raw = rest[:, 2 * N :]
-        return moving, x_in, bc_in, dt_raw[:, :heads], x_w, rest_w, edge([x_in, bc_in], True)
-
-    hop1, x_in, bc_in, dt_raw, x_w, rest_w, halo = ring.phase(
+            x_in, bc_in = dot(normed[0], x_w).astype(BF16), rest[:, :group].astype(BF16)
+        bc_own = jnp.pad(rest[:, :group].astype(BF16), ((0, 0), (0, -group % LANES)))
+        return x_in, bc_in, bc_own, rest[:, group : group + heads], x_w, rest_w
+
+    def work(normed, hop1, hop2, hop3, hop4, zo_in):
+        return ring.hop((zo_in, zo_in)), ring.phase(project_in, normed, hop1, hop2, hop3, hop4)
+
+    hop1, (x_in, bc_in, bc_own, dt_raw, x_w, rest_w) = ring.phase(
         work, normed, hop1, hop2, hop3, hop4, zo_in
     )
+    halo = ring.phase(lambda x_in, bc_in: edge([x_in, bc_in], True), x_in, bc_in)
 
     def work(hop1, x_in, bc_in, halo, dt_raw, own_cot):
         scanned = scan(x_in, bc_in, halo, dt_raw)
@@ -1104,15 +1235,18 @@
 
     hop2, scanned, held, near, far = ring.phase(work, hop1, x_in, bc_in, halo, dt_raw, own_cot)
     conv_out, y_local, steps, cumulative, begun, offsets, left, left_w = scanned
-    first = jnp.where(here == 0, 1.0, 0.0)
-    once = lax.broadcasted_iota(jnp.int32, (1, all_in.shape[1]), 1)
-    once = jnp.where((once < inner) | (once >= edge_at), 1.0, first)
-
-    def work(hop2, held, far, rest_w):
+    def work(hop2, held, far, conv_out):
         held = forth.next_line(held) if split_pass else ()
-        return ring.hop(hop2), held, corner(ring, own_cot, far), rest_w * once[:, inner:].astype(BF16)
-
-    hop3, held, both, rest_once = ring.phase(work, hop2, held, far, rest_w)
+        value = conv_out[:, inner:]
+        if ring.on:
+            value = [value[:, g * group : (g + 1) * group] for g in range(4)]
+            value = jnp.where(
+                here < 2, jnp.where(here == 0, value[0], value[1]),
+                jnp.where(here == 2, value[2], value[3]),
+            )
+        return ring.hop(hop2), held, corner(ring, own_cot, far), slope(value)
+
+    hop3, held, both, own_slope = ring.phase(work, hop2, held, far, conv_out)
     cot = (both, near, far, own_cot) if ring.on else (both,)
 
     def work(hop1, hop2, hop3, held, normed, cot):
@@ -1148,31 +1282,35 @@
         dm_part, ssd, z_part, gate_scale, product, cumulative, conv_out, late
     )
 
-    def work(d_left, left_w, normed, d_z, mixed, cot):
+    far_spot = spots[4:5] if ring.on else None
+
+    def work(d_left, left_w, normed, d_z, mixed, cot, normed_last, cot_last):
         held = back_pass.pair(back_pass.begin(d_left, left_w)) if split_pass else ()
         if ring.on:
-            g_zo = outer(order, (normed, [d_z]), (cot, [mixed]))
-        else:
-            g_zo = (dot(normed[0], d_z, TN), dot(cot[0], mixed, TN))
-        return held, g_zo
-
-    held, g_zo = ring.phase(work, d_left, left_w, normed, d_z, mixed, cot)
-
-    def work(held, g_zo, conv_out, d_ssd, steps, begun, offsets, came):
-        sent = ring.send(g_zo)
+            sums = ring.send(*outer_far([normed_last, cot_last], [d_z, mixed]))
+            g_zo = outer(far_spot, order, (normed, [d_z]), (cot, [mixed]))
+            return held, ring.add(g_zo, sums, 3), g_zo
+        return held, (), (dot(normed[0], d_z, TN), dot(cot[0], mixed, TN))
+
+    held, sums, g_zo = ring.phase(
+        work, d_left, left_w, normed, d_z, mixed, cot, normed_last, cot_last
+    )
+
+    def work(held, sums, conv_out, d_ssd, steps, begun, offsets, came):
+        sums = ring.hop(sums)
         held = back_pass.next_line(held) if split_pass else ()
-        back = scan_back(conv_out, d_ssd, steps, begun, offsets, came)
-        return held, ring.add(g_zo, sent, 3), back
+        return held, sums, scan_back(conv_out, d_ssd, steps, begun, offsets, came)
 
     held, sums, (du_local, dbc_local) = ring.phase(
-        work, held, g_zo, conv_out, d_ssd, steps, begun, offsets, came
-    )
-
-    def work(held, mixed, out_w, late_w):
+        work, held, sums, conv_out, d_ssd, steps, begun, offsets, came
+    )
+
+    def work(held, sums, g_zo, mixed, out_w, late_w):
         held = back_pass.further_lines(held) if split_pass else ()
-        return held, project(ring, spots, [mixed], [out_w], [late_w])
-
-    held, branch = ring.phase(work, held, mixed, out_w, hop4[1])
+        branch = project(ring, spots, [mixed], [out_w], [late_w])
+        return held, ring.add(g_zo, sums, 2), branch
+
+    held, sums, branch = ring.phase(work, held, sums, g_zo, mixed, out_w, hop4[1])
 
     def work(held, branch):
         later = back_pass.end(held) if split_pass else states_scan(d_left, left_w, -1)
@@ -1180,61 +1318,66 @@
 
     later, (out_far, out_own) = ring.phase(work, held, branch)
 
-    def work(later, sums, g_zo, du_local, dbc_local):
+    def work(later, sums, du_local, dbc_local):
         sums = ring.hop(sums)
-        d_conv_x, d_bc_part, d_dt, g_skip, g_heads = finish(
+        d_conv_x, mine, send, d_dt, g_skip, g_heads = finish(
             conv_out, d_ssd, du_local, ssd, steps, cumulative, left_w, later, came, left,
             dbc_local, dt_raw,
         )
         after_x = edge([d_conv_x], False)
-        v_bc = conv_out[:, inner:]
         if ring.on:
-            half, quarter = total // 2, total // 4
-            low, high = here & 1, here >> 1
-            cut = lambda a, at, n: lax.dynamic_slice_in_dim(a, at, n, 0)
-            mine = cut(d_bc_part, low * half, half)
-            mine = mine + swap(cut(d_bc_part, (1 - low) * half, half), "head", 1)
-            given = swap(cut(mine, (1 - high) * quarter, quarter), "head", 2)
-            mine = cut(mine, high * quarter, quarter) + given
-            mine = (mine * slope(cut(v_bc, low * half + high * quarter, quarter))).astype(BF16)
-            given = swap(mine, "head", 2)
-            mine = jnp.where(
-                high == 0, jnp.concatenate([mine, given], 0), jnp.concatenate([given, mine], 0)
-            )
-            given = swap(mine, "head", 1)
-            d_conv_bc = jnp.where(
-                low == 0, jnp.concatenate([mine, given], 0), jnp.concatenate([given, mine], 0)
-            )
+            mine = mine + swap(send, "head", 1)
         else:
-            d_conv_bc = (head_sum(d_bc_part) * slope(v_bc)).astype(BF16)
-        after_bc = edge([d_conv_bc], False)
-        sums = ring.add(g_zo, sums, 2)
-        return sums, d_conv_x, after_x, d_conv_bc, after_bc, d_dt, g_skip, g_heads
-
-    sums, d_conv_x, after_x, d_conv_bc, after_bc, d_dt, g_skip, g_heads = ring.phase(
-        work, later, sums, g_zo, du_local, dbc_local
-    )
-    out_far = across(ring, out_far)
-
-    def work(sums, g_zo, d_conv_x, after_x, d_conv_bc, after_bc, d_dt, normed):
-        sums = ring.add(g_zo, ring.hop(sums), 1)
+            mine = jnp.concatenate([mine, send], axis=1)
+        return sums, d_conv_x, after_x, mine, d_dt, g_skip, g_heads
+
+    sums, d_conv_x, after_x, mine, d_dt, g_skip, g_heads = ring.phase(
+        work, later, sums, du_local, dbc_local
+    )
+
+    share = 1.0 if ring.on else jnp.where(here == 0, 1.0, 0.0)
+
+    def work(mine, sums, g_zo, own_slope):
+        if ring.on:
+            mine = mine[:, :group] + unfold(swap(fold(mine[:, group:]), "head", 2))
+        else:
+            mine = head_sum(mine)
+        d_conv_bc = jnp.pad((mine * own_slope).astype(BF16), ((0, 0), (0, -group % LANES)))
+        return d_conv_bc, edge([d_conv_bc], False), ring.add(g_zo, sums, 1)
+
+    d_conv_bc, after_bc, sums = ring.phase(work, mine, sums, g_zo, own_slope)
+    own_taps = jnp.pad(own_columns(conv_bcf), ((0, 0), (0, -group % LANES)))
+
+    def work(
+        sums, g_zo, d_conv_bc, after_bc, d_conv_x, after_x, d_dt, normed, normed_last, out_far
+    ):
         d_x, g_conv_x, met_x = conv_back(d_conv_x, x_in, after_x, conv_xf, batch, length, rows)
         d_bc, g_conv_bc, met_bc = conv_back(
-            d_conv_bc, bc_in, after_bc, conv_bcf, batch, length, rows
+            d_conv_bc, bc_own, after_bc, own_taps, batch, length, rows
         )
         fill = jnp.zeros((total, spare), BF16)
-        d_rest = jnp.concatenate([d_bc, d_dt, fill], axis=1)
+        d_rest = jnp.concatenate([d_bc[:, :group], d_dt, fill], axis=1)
+        last = ring.hop(sums)
         if ring.on:
-            g_all = outer(order, (normed, [d_x, d_rest]))
+            sums = ring.send(*outer_far([normed_last], [d_x, d_rest]))
+            g_all = outer(far_spot, order, (normed, [d_x, d_rest]))
+            sums = ring.add(g_all, sums, 3)
         else:
+            sums = ()
             g_all = jnp.concatenate([dot(normed[0], d, TN) for d in (d_x, d_rest)], axis=1)
         met_dt = jnp.sum(d_dt.astype(F32) * dt_raw, axis=1)
-        met = (met_z + met_x + first * met_bc).reshape(total) + met_dt
-        return sums, d_x, d_rest, g_conv_x, g_conv_bc, met, g_all
-
-    sums, d_x, d_rest, g_conv_x, g_conv_bc, met, g_all = ring.phase(
-        work, sums, g_zo, d_conv_x, after_x, d_conv_bc, after_bc, d_dt, normed
-    )
+        met = (met_z + met_x + share * met_bc).reshape(total) + met_dt
+        return (
+            last, sums, d_x, d_rest, g_conv_x, g_conv_bc, met, g_all, across(ring, out_far),
+        )
+
+    last, sums, d_x, d_rest, g_conv_x, g_conv_bc, met, g_all, out_far = ring.phase(
+        work, sums, g_zo, d_conv_bc, after_bc, d_conv_x, after_x, d_dt, normed, normed_last, out_far
+    )
+    g_conv_bc = g_conv_bc[:, :group]
+    if ring.on:
+        none = jnp.zeros((KERNEL, 2 * N), F32)
+        g_conv_bc = lax.dynamic_update_slice(none, g_conv_bc, (0, here * group))
     small = jnp.concatenate(
         [
             g_conv_x.reshape(-1), g_conv_bc.reshape(-1), g_gate.reshape(-1),
@@ -1245,68 +1388,86 @@
     def one_swap(array, bit):
         return array + swap(array, "seq", bit) if ring.on else array
 
-    def work(sums, g_zo, g_all, small, d_z, d_x, d_rest, z_w, x_w, rest_once, late_w, met):
+    def work(sums, small, d_z, d_x, d_rest, z_w, x_w, rest_w, late_w, met):
+        sums = ring.hop(sums)
+        met = met + swap(met, "head", 1) if ring.on else head_sum(met)
+        if not ring.on:
+            columns = lax.broadcasted_iota(jnp.int32, (1, rest_w.shape[1]), 1)
+            rest_w = jnp.where((columns < group) & (here > 0), 0.0, rest_w.astype(F32)).astype(BF16)
+        back = project(ring, spots, [d_z, d_x, d_rest], [z_w, x_w, rest_w], [late_w])
+        return sums, back, one_swap(small, 1), met
+
+    sums, back_terms, small, met = ring.phase(
+        work, sums, small, d_z, d_x, d_rest, z_w, x_w, rest_w, hop4[0], met
+    )
+
+    def work(sums, g_all, back_terms, met):
+        far, d_normed = scatter_near(ring, back_terms)
+        met = met + swap(met, "head", 2) if ring.on else met
+        return ring.add(g_all, sums, 2), far, d_normed, met / scale
+
+    sums, far, d_normed, dots = ring.phase(work, sums, g_all, back_terms, met)
+
+    def work(sums, g_all, small, far, out_far, out_own, slab, g_zo, last):
+        far = across(ring, far)
+        mixed_out = slab + scatter_sum(ring, out_far, out_own)
+        block, column = shaped(per, inner), shaped(per, 1)
+        if ring.on:
+            g_z, g_out, met_f = totals(
+                total_zo_kernel, g_zo, last, [w_z], [block, shaped(inner, per), column]
+            )
+        else:
+            g_z, g_out = (
+                lax.psum_scatter(g.astype(BF16), "seq", scatter_dimension=0, tiled=True).astype(F32)
+                for g in g_zo
+            )
+            g_out, met_f = g_out.T, jnp.sum(g_z * w_z.astype(F32), axis=1, keepdims=True)
+        return (
+            ring.add(g_all, ring.hop(sums), 1), far, one_swap(small, 2), mixed_out,
+            g_z, g_out, met_f,
+        )
+
+    sums, far, small, mixed_out, g_z, g_out, met_f = ring.phase(
+        work, sums, g_all, small, far, out_far, out_own, slab, g_zo, last
+    )
+
+    def work(sums, g_all, far, d_normed, slab, dots, met_f, small):
         last = ring.hop(sums)
-        sent = ring.send(g_all)
-        back = project(ring, spots, [d_z, d_x, d_rest], [z_w, x_w, rest_once], [late_w])
-        return (
-            ring.total(g_zo, last) if ring.on else [ring.total(g, None) for g in g_zo],
-            ring.add(g_all, sent, 3), back, one_swap(small, 1), head_sum(met) / scale,
-        )
-
-    g_zo, sums, back_terms, small, dots = ring.phase(
-        work, sums, g_zo, g_all, small, d_z, d_x, d_rest, z_w, x_w, rest_once, hop4[0], met
-    )
-    g_z, g_out = (g_zo[:per], g_zo[per:]) if ring.on else g_zo
-
-    def work(sums, g_all, small, back_terms, out_far, out_own, slab):
-        mixed_out = slab + scatter_sum(ring, out_far, out_own)
-        return (
-            ring.add(g_all, ring.hop(sums), 2), scatter_near(ring, back_terms),
-            one_swap(small, 2), mixed_out,
-        )
-
-    sums, (far, d_normed), small, mixed_out = ring.phase(
-        work, sums, g_all, small, back_terms, out_far, out_own, slab
-    )
-    far = across(ring, far)
-
-    def work(sums, g_all, small, g_z):
-        return (
-            ring.add(g_all, ring.hop(sums), 1), one_swap(small, 4),
-            jnp.sum(g_z * w_z.astype(F32), axis=1), g_out.T,
-        )
-
-    sums, small, met_f, g_out = ring.phase(work, sums, g_all, small, g_z)
-    if not ring.on:
-        small = lax.psum(small, "seq")
-
-    def work(sums, g_all, far, d_normed, slab, dots, met_f):
-        last = ring.hop(sums)
+        small = one_swap(small, 4)
         d_normed = scatter_sum(ring, far, d_normed)
         grad_tokens = (
             cot_rows
             + (scale[:, None] * own_gain) * d_normed
             - slab * (scale * scale * scale * dots / model)[:, None]
         )
-        g_all = ring.total(g_all, last)
-        met_f = met_f + jnp.sum(g_all * all_in.astype(F32) * once, axis=1)
-        g_gain = head_sum(met_f) / norm_gain.astype(F32)
-        return (
-            g_all[:, :inner], g_all[:, inner:edge_at], g_all[:, edge_at : edge_at + heads],
-            grad_tokens, g_gain,
-        )
-
-    g_x, g_bc, g_dt, grad_tokens, g_gain = ring.phase(
-        work, sums, g_all, far, d_normed, slab, dots, met_f
-    )
-
+        shapes = [shaped(per, inner), shaped(per, group), shaped(per, heads), shaped(per, 1)]
+        if ring.on:
+            g_x, g_bc, g_dt, met_f = totals(
+                total_in_kernel, g_all, last, [all_in, met_f], shapes
+            )
+            g_bc = jnp.concatenate(gather_groups(g_bc), axis=1)
+        else:
+            g = lax.psum_scatter(g_all.astype(BF16), "seq", scatter_dimension=0, tiled=True)
+            g = g.astype(F32)
+            g_x, g_bc, g_dt = g[:, :inner], g[:, inner:edge_at], g[:, edge_at : edge_at + heads]
+            columns = lax.broadcasted_iota(jnp.int32, (1, g.shape[1]), 1)
+            once = jnp.where((columns >= inner) & (columns < edge_at), share, 1.0)
+            met_f = met_f + jnp.sum(g * all_in.astype(F32) * once, axis=1, keepdims=True)
+            small = lax.psum(small, "seq")
+        maps = small[KERNEL * inner : KERNEL * (inner + 2 * N)]
+        both = head_sum(jnp.concatenate([met_f[:, 0], maps if ring.on else maps * (1.0 / lax.axis_size("head"))]))
+        g_gain = both[:per] / norm_gain.astype(F32)
+        return g_x, g_bc, g_dt, grad_tokens, g_gain, small, both[per:]
+
+    g_x, g_bc, g_dt, grad_tokens, g_gain, small, sum_bc = ring.phase(
+        work, sums, g_all, far, d_normed, slab, dots, met_f, small
+    )
     cuts = [KERNEL * inner, KERNEL * 2 * N, inner, inner, heads, heads]
     parts, start = [], 0
     for width in cuts:
         parts.append(small[start : start + width])
         start += width
-    sum_x, sum_bc, sum_gate, sum_skip, sum_bias, sum_rate = parts
+    sum_x, _, sum_gate, sum_skip, sum_bias, sum_rate = parts
 
     return (
         mixed_out.reshape(batch, length, own_width),

time: 583 us -> 506 us (0.87)
  waiting for transfers between devices: 178 us -> 130 us
  other arithmetic: 55.3 us -> 26.9 us
  local copies, waits for them, and re-layouts: 51.6 us -> 28 us
  Pallas kernels: 183 us -> 203 us
  starting transfers between devices: 71.8 us -> 82.6 us
  blocking collectives: 31.1 us -> 22.6 us
    pallas_call x1 -> x11, Pallas kernels: 15.4 us -> 41.4 us  [the longest x1 15.6 us: finish(): call(functools.partial(finish_kernel, pairs, ring.on), (batch, count), [v...]
    ppermute x23 -> x29, waiting for transfers between devices: 80.7 us -> 55.3 us  [swap(): return lax.ppermute(array, axis, [(i, i ^ bit) for i in range(size)])]
    ppermute x32, waiting for transfers between devices: 51.6 us -> 35.5 us  [shift(): lax.ppermute(array, 'seq', [(order[i], order[(i + by) % size]) for i in r...]
    convert_element_type x5 -> x1, other arithmetic: 15.4 us -> 0.13 us  [work(): (mine * own_slope).astype(BF16)]
    ppermute x23 -> x29, starting transfers between devices: 15.8 us -> 25.7 us  [swap(): return lax.ppermute(array, axis, [(i, i ^ bit) for i in range(size)])]
    ppermute x3, waiting for transfers between devices: 15.4 us -> 6.66 us  [edge(): got = lax.ppermute(cut, 'seq', moves).astype(F32)]
    psum x4 -> x3, blocking collectives: 31.1 us -> 22.6 us  [head_sum(): return lax.psum(array, 'head')]
    slice x8 -> x9, local copies, waits for them, and re-layouts: 9.66 us -> 2.33 us  [the longest x1 1.03 us: project_in(): return (x_in, bc_in, bc_own, rest[:, group:group + heads], x_w, rest_w)]
  transfers between devices with their start and end apart: 64 -> 70, of which waited for: 24 -> 26; matrix products, arithmetic and copies ran while one was open for 10% -> 7% of each run, Pallas kernels for 24% -> 34%
where the time goes in v3:
time: 506 us; the launch traced here: 496 us
  Pallas kernels  203 us (40%)
  waiting for transfers between devices  130 us (26%)
  starting transfers between devices  82.6 us (16%)
  local copies, waits for them, and re-layouts  28 us (6%)
  other arithmetic  26.9 us (5%)
  blocking collectives  22.6 us (4%)
    ppermute x29, waiting for transfers between devices, swap(): return lax.ppermute(array, axis, [(i, i ^ bit) for i in range(size)])  55.3 us
    ppermute x32, starting transfers between devices, shift(): lax.ppermute(array, 'seq', [(order[i], order[(i + by) % size]) for i in r...  37.7 us
    ppermute x32, waiting for transfers between devices, shift(): lax.ppermute(array, 'seq', [(order[i], order[(i + by) % size]) for i in r...  35.5 us
    ppermute x4, waiting for transfers between devices, shift_flat(): lax.ppermute(array, 'seq', [(i, i + by) for i in range(size) if 0 <= i +...  32.3 us
    pallas_call x2, Pallas kernels, with_spots(): pl.pallas_call(kernel, grid_spec=pltpu.PrefetchScalarGridSpec(num_scalar_...  29.3 us
    pallas_call x2, Pallas kernels, outer(): pl.pallas_call(functools.partial(outer_kernel, [len(grads) for _, grads i...  26 us
    ppermute x29, starting transfers between devices, swap(): return lax.ppermute(array, axis, [(i, i ^ bit) for i in range(size)])  25.7 us
    pallas_call x2, Pallas kernels, project(): pl.pallas_call(functools.partial(project_kernel, len(acts), len(late)), g...  24.7 us
  transfers between devices with their start and end apart: 70, of which 26 were waited for; matrix products, arithmetic and copies ran while one was open for 7% of the time, Pallas kernels for 34%

profile of v3, /device:TPU:0, one launch (start us, length us, event | category | flops | bytes accessed | tf_op | source)
XLA Modules:
  0.0 495.9 jit_solution(5905700229739976123)
XLA Ops:
  3.6 24.4 %conditional.22 = (bf16[256,1152]{1,0:T(8,128)(2,1)}, bf16[256,1152]{1,0:T(8,128)(2,1)}, f32[512]{0:T(512)}, f32[1024]{0:T(1024)}, bf16[1024,512]{1,0:T(8,128)(2,1)S(1)}) conditional(s32[]{:T(128)} %convert_element_type.80, () %tuple.209, (bf16[256,1152]{1,0:T(8,128)(2,1)}, s32[]{:T(128)}, bf16[256]{0:T(256)(128)(2,1)}, f32[1024,512]{1,0:T(8,128)}) %tuple.330), branch_computations={%region_0.1_spmd, %region_1.4_spmd} | conditional | flops 2624769 | bytes 18394862 | solution.py:127
  13.9 9.6 %psum.18 = f32[1024]{0:T(1024)S(1)} all-reduce(f32[1024]{0:T(1024)S(1)} %multiply_reduce_fusion), channel_id=1, replica_groups=mesh['seq'=8,'head'=4] {'head'}, use_global_device_ids=true, to_apply=%region_3.3 | all-reduce | flops 1024 | bytes 8192 | tf_op jit(solution)/shard_map/cond/branch_1_fun/psum | solution.py:136
  31.1 16.1 %conditional.23 = (bf16[256,1152]{1,0:T(8,128)(2,1)}, bf16[256,1152]{1,0:T(8,128)(2,1)}, bf16[1024,512]{1,0:T(8,128)(2,1)}, bf16[512,1024]{0,1:T(8,128)(2,1)}, bf16[1024,512]{1,0:T(8,128)(2,1)}) conditional(s32[]{:T(128)} %convert_element_type.80, () %tuple.208, (bf16[256,1152]{1,0:T(8,128)(2,1)}, bf16[256,1152]{1,0:T(8,128)(2,1)}, ...), branch_computations={%region_4.5_spmd, %region_5.6_spmd} | conditional | flops 2621440 | bytes 17301692 | solution.py:127
  38.2 9.0 %collective-permute-done.29 = bf16[256,1152]{1,0:T(8,128)(2,1)} collective-permute-done((bf16[256,1152]{1,0:T(8,128)(2,1)}, bf16[256,1152]{1,0:T(8,128)(2,1)}, u32[]{:S(2)}, u32[]{:S(2)}) %collective-permute-start.29) | collective-permute-done | bytes 589856 | tf_op jit(solution)/shard_map/cond/branch_1_fun/ppermute | solution.py:65
  47.2 16.1 %conditional.24 = (bf16[256,1152]{1,0:T(8,128)(2,1)}, bf16[256,1152]{1,0:T(8,128)(2,1)}) conditional(s32[]{:T(128)} %convert_element_type.80, () %tuple.213, (bf16[256,1152]{1,0:T(8,128)(2,1)}, bf16[256,1152]{1,0:T(8,128)(2,1)}) %tuple.214), branch_computations={%region_6.7_spmd, %region_7.8_spmd} | conditional | bytes 4718688 | solution.py:127
  49.3 13.2 %collective-permute-done = bf16[256,1152]{1,0:T(8,128)(2,1)} collective-permute-done((bf16[256,1152]{1,0:T(8,128)(2,1)}, bf16[256,1152]{1,0:T(8,128)(2,1)}, u32[]{:S(2)}, u32[]{:S(2)}) %collective-permute-start) | collective-permute-done | bytes 589856 | tf_op jit(solution)/shard_map/cond/branch_1_fun/ppermute | solution.py:65
  63.3 12.1 %conditional.25 = (bf16[128,1152]{1,0:T(8,128)(2,1)}, bf16[128,1152]{1,0:T(8,128)(2,1)}, bf16[1024,512]{1,0:T(8,128)(2,1)}) conditional(s32[]{:T(128)} %convert_element_type.80, () %tuple.212, (bf16[256,1152]{1,0:T(8,128)(2,1)}, bf16[256,1152]{1,0:T(8,128)(2,1)}, bf16[1024,512]{1,0:T(8,128)(2,1)S(1)}) %tuple.215), branch_computations={%region_8.9_spmd, %region_9.10_spmd} | conditional | bytes 7733392 | solution.py:127
  67.7 6.2 %collective-permute-done.2 = bf16[128,1152]{1,0:T(8,128)(2,1)} collective-permute-done((bf16[128,1152]{1,0:T(8,128)(2,1)S(1)}, bf16[128,1152]{1,0:T(8,128)(2,1)}, u32[]{:S(2)}, u32[]{:S(2)}) %collective-permute-start.2) | collective-permute-done | bytes 294944 | tf_op jit(solution)/shard_map/cond/branch_1_fun/ppermute | solution.py:65
  75.4 27.1 %conditional.26 = (bf16[512,1024]{1,0:T(8,128)(2,1)}, bf16[512,1024]{1,0:T(8,128)(2,1)}, bf16[1024,1024]{1,0:T(8,128)(2,1)}, bf16[1024,256]{1,0:T(8,128)(2,1)}, ...) conditional(s32[]{:T(128)} %convert_element_type.80, () %tuple.207, ...), branch_computations={%region_10.11_spmd, %region_11.14_spmd} | conditional | flops 5767177 | bytes 66409472 | solution.py:127
  79.7 20.2 %conditional = (bf16[1024,1024]{1,0:T(8,128)(2,1)}, bf16[1024,256]{1,0:T(8,128)(2,1)}, bf16[1024,128]{1,0:T(8,128)(2,1)}, f32[1024,16]{1,0:T(8,128)}, bf16[2048,...) conditional(s32[]{:T(128)} %convert_element_type.46, () %tuple.121, (s32[8]{0:T(128)S(1)}, ...), branch_computations={%region_12.12_spmd, %region_13.13_spmd} | conditional | flops 5767172 | bytes 55923400 | solution.py:127
  79.7 11.3 %branch_1_fun.31 = (bf16[1024,1024]{1,0:T(8,128)(2,1)}, f32[1024,128]{1,0:T(8,128)S(1)}, bf16[2048,1024]{1,0:T(8,128)(2,1)}, bf16[2048,128]{1,0:T(8,128)(2,1)}) custom-call(s32[8]{0:T(128)S(1)} %get-tuple-element.521.spot_ref, bf16[1024,512]{1,0:T(8,128)(2,1)} %get-tuple-element.522.refs_0_, bf16[1024,512]{1,0:T(8,128)(2,1)} %get-tuple-element.523.refs_1_, ...), custom_call_target="tpu_custom_call" | custom-call | bytes 49500000 | tf_op jit(solution)/shard_map/cond/branch_1_fun/cond/branch_1_fun/pallas_call | solution.py:724
  102.4 6.4 %conditional.27 = (f32[2,8,1280]{2,1,0:T(8,128)S(1)}) conditional(s32[]{:T(128)} %convert_element_type.80, () %tuple.217, (bf16[1024,1024]{1,0:T(8,128)(2,1)}, bf16[1024,256]{1,0:T(8,128)(2,1)}) %tuple.218), branch_computations={%region_14.15_spmd, %region_15.16_spmd} | conditional | flops 51200 | bytes 220208 | solution.py:127
  108.8 35.4 %conditional.28 = (bf16[512,1024]{1,0:T(8,128)(2,1)}, bf16[512,1024]{1,0:T(8,128)(2,1)}, f32[1024,1280]{1,0:T(8,128)}, f32[1024,1024]{1,0:T(8,128)}, f32[1024,16...) conditional(s32[]{:T(128)} %convert_element_type.80, () %tuple.206, ...), branch_computations={%region_16.17_spmd, %region_17.18_spmd} | conditional | bytes 65807200 | solution.py:127
  113.3 16.1 %branch_1_fun.32 = (f32[1024,1280]{1,0:T(8,128)}, f32[1024,1024]{1,0:T(8,128)}, f32[1024,16]{1,0:T(8,128)}, f32[1024,16]{1,0:T(8,128)}, f32[8,128,1024]{2,1,0:T(...) custom-call(bf16[1024,1024]{1,0:T(8,128)(2,1)} %get-tuple-element.566.x_ref, ...), custom_call_target="tpu_custom_call" | custom-call | bytes 47850000 | tf_op jit(solution)/shard_map/cond/branch_1_fun/pallas_call | solution.py:1008
  132.8 10.5 %collective-permute-done.7.got_ref = bf16[144,1024]{1,0:T(8,128)(2,1)S(1)} collective-permute-done((bf16[144,1024]{1,0:T(8,128)(2,1)S(1)}, bf16[144,1024]{1,0:T(8,128)(2,1)S(1)}, u32[]{:S(2)}, u32[]{:S(2)}) %collective-permute-start.7) | collective-permute-done | bytes 294944 | tf_op jit(solution)/shard_map/cond/branch_1_fun/ppermute | solution.py:132
  144.2 30.0 %conditional.29 = (bf16[512,1024]{1,0:T(8,128)(2,1)}, bf16[512,1024]{1,0:T(8,128)(2,1)}, f32[128,1024]{1,0:T(8,128)}, f32[1,1024]{1,0:T(1,128)S(1)}, f32[128,102...) conditional(s32[]{:T(128)} %convert_element_type.80, () %tuple.205, ...), branch_computations={%region_18.19_spmd, %region_19.20_spmd} | conditional | flops 655363 | bytes 15073542 | solution.py:127
  150.3 23.1 %collective-permute-done.35.got_ref = bf16[144,1024]{1,0:T(8,128)(2,1)S(1)} collective-permute-done((bf16[144,1024]{1,0:T(8,128)(2,1)S(1)}, bf16[144,1024]{1,0:T(8,128)(2,1)S(1)}, u32[]{:S(2)}, u32[]{:S(2)}) %collective-permute-start.35) | collective-permute-done | bytes 294944 | tf_op jit(solution)/shard_map/cond/branch_1_fun/ppermute | solution.py:205
  175.0 33.3 %conditional.30 = (bf16[256,1024]{1,0:T(8,128)(2,1)}, bf16[256,1024]{1,0:T(8,128)(2,1)}, f32[128,1024]{1,0:T(8,128)}, bf16[128,1024]{1,0:T(8,128)(2,1)}, f32[102...) conditional(s32[]{:T(128)} %convert_element_type.80, () %tuple.204, ...), branch_computations={%region_20.21_spmd, %region_21.22_spmd} | conditional | bytes 61034564 | solution.py:127
  188.1 18.1 %branch_1_fun.37 = (f32[1024,1024]{1,0:T(8,128)}, f32[1024,1024]{1,0:T(8,128)}, bf16[2048,1024]{1,0:T(8,128)(2,1)}, bf16[2048,1024]{1,0:T(8,128)(2,1)}, bf16[102...) custom-call(s32[8]{0:T(128)S(1)} %get-tuple-element.616.spot_ref, bf16[1024,512]{1,0:T(8,128)(2,1)} %get-tuple-element.617.refs_0_, ...), custom_call_target="tpu_custom_call" | custom-call | bytes 49500000 | tf_op jit(solution)/shard_map/cond/branch_1_fun/pallas_call | solution.py:724
  208.3 7.8 %conditional.31 = (f32[2,128,1024]{2,1,0:T(8,128)S(1)}) conditional(s32[]{:T(128)} %convert_element_type.80, () %tuple.222, (bf16[128,1024]{1,0:T(8,128)(2,1)}, s32[1]{0:T(128)}, f32[128,1024]{1,0:T(8,128)}) %tuple.223), branch_computations={%region_22.23_spmd, %region_23.24_spmd} | conditional | bytes 1048624 | solution.py:127
  209.8 5.2 %collective-permute-done.13.got_ref = bf16[128,1024]{1,0:T(8,128)(2,1)S(1)} collective-permute-done((bf16[128,1024]{1,0:T(8,128)(2,1)}, bf16[128,1024]{1,0:T(8,128)(2,1)S(1)}, u32[]{:S(2)}, u32[]{:S(2)}) %collective-permute-start.13) | collective-permute-done | bytes 262176 | tf_op jit(solution)/shard_map/cond/branch_1_fun/ppermute | solution.py:132
  216.1 11.2 %shard_map.246 = (f32[1024,1024]{1,0:T(8,128)}, f32[8,2,128]{2,1,0:T(2,128)S(1)}) custom-call(f32[1024,1024]{1,0:T(8,128)} %get-tuple-element.1027.y_ref, f32[1024,1280]{1,0:T(8,128)} %get-tuple-element.1014.vc_ref, f32[2,128,1024]{2,1,0:T(8,128)S(1)} %get-tuple-element.1709.s_ref, f32[1024,16]{1,0:T(8,128)} %get-tuple-element.1030.wc_ref, ...), custom_call_target="tpu_custom_call" | custom-call | bytes 23100000 | tf_op jit(solution)/shard_map/pallas_call | solution.py:1057
  227.3 5.8 %psum.21 = f32[8,2,128]{2,1,0:T(2,128)S(1)} all-reduce(f32[8,2,128]{2,1,0:T(2,128)S(1)} %get-tuple-element.1037), channel_id=1, replica_groups=mesh['seq'=8,'head'=4] {'head'}, use_global_device_ids=true, to_apply=%region_24.25 | all-reduce | flops 2048 | bytes 16384 | tf_op jit(solution)/shard_map/psum | solution.py:136
  233.1 13.6 %shard_map.247 = (bf16[1024,1024]{1,0:T(8,128)(2,1)}, f32[1024,1024]{1,0:T(8,128)}, f32[2,128,1024]{2,1,0:T(8,128)S(1)}, f32[8,1,128]{2,1,0:T(1,128)S(1)}, f32[1...) custom-call(f32[1024,1024]{1,0:T(8,128)} %get-tuple-element.1026.dmp_ref, f32[1024,1024]{1,0:T(8,128)} %get-tuple-element.1036.ssd_ref, ...), custom_call_target="tpu_custom_call" | custom-call | bytes 29700000 | tf_op jit(solution)/shard_map/pallas_call | solution.py:1071
  246.8 26.1 %conditional.32 = (f32[128,1024]{1,0:T(8,128)S(1)}, f32[1,1024]{1,0:T(1,128)S(1)}, f32[128,1024]{1,0:T(8,128)S(1)}, f32[1,1024]{1,0:T(1,128)S(1)}, bf16[144,1024...) conditional(s32[]{:T(128)} %convert_element_type.80, () %tuple.203, ...), branch_computations={%region_25.26_spmd, %region_26.27_spmd} | conditional | bytes 58174136 | solution.py:127
  255.1 15.6 %branch_1_fun.41.a_ref.b_ref = bf16[4096,1024]{1,0:T(8,128)(2,1)} custom-call(s32[1]{0:T(128)} %get-tuple-element.651.far_ref, s32[8]{0:T(128)S(1)} %get-tuple-element.652.block_ref, bf16[1024,512]{1,0:T(8,128)(2,1)} %get-tuple-element.653.refs_0_, bf16[1024,512]{1,0:T(8,128)(2,1)} %get-tuple-element.654.refs_1_, ...), custom_call_target="tpu_custom_call" | custom-call | bytes 52800000 | tf_op jit(solution)/shard_map/cond/branch_1_fun/pallas_call | solution.py:784
  272.9 32.2 %conditional.33 = (f32[128,1024]{1,0:T(8,128)S(1)}, f32[1,1024]{1,0:T(1,128)S(1)}, f32[128,1024]{1,0:T(8,128)}, f32[1,1024]{1,0:T(1,128)S(1)}, bf16[128,1024]{1,...) conditional(s32[]{:T(128)} %convert_element_type.80, () %tuple.202, ...), branch_computations={%region_27.28_spmd, %region_28.29_spmd} | conditional | bytes 68968448 | solution.py:127
  276.6 18.6 %branch_1_fun.45 = (f32[1024,1024]{1,0:T(8,128)}, f32[1024,256]{1,0:T(8,128)}) custom-call(f32[1024,1280]{1,0:T(8,128)} %get-tuple-element.681.v_ref, f32[1024,1024]{1,0:T(8,128)} %get-tuple-element.682.dy_ref, f32[1024,16]{1,0:T(8,128)S(1)} %get-tuple-element.683.st_ref, f32[1,16]{1,0:T(1,128)S(1)} %get-tuple-element.684.rate_ref, ...), custom_call_target="tpu_custom_call" | custom-call | bytes 59400000 | tf_op jit(solution)/shard_map/cond/branch_1_fun/pallas_call | solution.py:1092
  295.2 9.1 %collective-permute-done.17.got_ref = bf16[144,1024]{1,0:T(8,128)(2,1)S(1)} collective-permute-done((bf16[144,1024]{1,0:T(8,128)(2,1)S(1)}, bf16[144,1024]{1,0:T(8,128)(2,1)S(1)}, u32[]{:S(2)}, u32[]{:S(2)}) %collective-permute-start.17) | collective-permute-done | bytes 294944 | tf_op jit(solution)/shard_map/cond/branch_1_fun/ppermute | solution.py:205
  305.2 14.6 %conditional.34 = (f32[128,1024]{1,0:T(8,128)S(1)}, bf16[128,1024]{1,0:T(8,128)(2,1)S(1)}, bf16[512,1024]{1,0:T(8,128)(2,1)}, bf16[512,1024]{1,0:T(8,128)(2,1)}, bf16[1024,2048]{1,0:T(8,128)(2,1)S(1)}) conditional(s32[]{:T(128)} %convert_element_type.80, () %tuple.201, (bf16[128,1024]{1,0:T(8,128)(2,1)S(1)}, s32[1]{0:T(128)}, s32[1]{0:T(128)}, ...), branch_computations={%region_29.30_spmd, %region_30.31_spmd} | conditional | bytes 30440196 | solution.py:127
  309.8 9.7 %branch_1_fun.48 = bf16[1024,2048]{1,0:T(8,128)(2,1)S(1)} custom-call(s32[8]{0:T(128)S(1)} %get-tuple-element.704.spot_ref, bf16[1024,1024]{1,0:T(8,128)(2,1)} %get-tuple-element.705.refs_0_, bf16[2048,1024]{1,0:T(8,128)(2,1)} %get-tuple-element.706.refs_1_, bf16[256,1024]{1,0:T(8,128)(2,1)} %get-tuple-element.707.refs_2_), custom_call_target="tpu_custom_call" | custom-call | bytes 23100000 | tf_op jit(solution)/shard_map/cond/branch_1_fun/pallas_call | solution.py:847
  319.8 10.8 %conditional.35 = (f32[2,128,1024]{2,1,0:T(8,128)}, bf16[1024,512]{1,0:T(8,128)(2,1)S(1)}, f32[1024,512]{1,0:T(8,128)S(1)}) conditional(s32[]{:T(128)} %convert_element_type.80, () %tuple.227, (bf16[128,1024]{1,0:T(8,128)(2,1)S(1)}, s32[1]{0:T(128)}, s32[1]{0:T(128)}, f32[128,1024]{1,0:T(8,128)S(1)}, bf16[1024,2048]{1,0:T(8,128)(2,1)S(1)}) %tuple.228), branch_computations={%region_31.32_spmd, %region_32.33_spmd} | conditional | flops 3670016 | bytes 20971664 | solution.py:127
  321.8 7.1 %collective-permute-done.55.got_ref = bf16[128,1024]{1,0:T(8,128)(2,1)S(1)} collective-permute-done((bf16[128,1024]{1,0:T(8,128)(2,1)S(1)}, bf16[128,1024]{1,0:T(8,128)(2,1)S(1)}, u32[]{:S(2)}, u32[]{:S(2)}) %collective-permute-start.55) | collective-permute-done | bytes 262176 | tf_op jit(solution)/shard_map/cond/branch_1_fun/ppermute | solution.py:132
  332.2 27.5 %conditional.36 = (bf16[512,1024]{1,0:T(8,128)(2,1)}, bf16[512,1024]{1,0:T(8,128)(2,1)}, bf16[1024,1024]{1,0:T(8,128)(2,1)}, f32[2,8,1024]{2,1,0:T(8,128)S(1)}, ...) conditional(s32[]{:T(128)} %convert_element_type.80, () %tuple.200, ...), branch_computations={%region_33.34_spmd, %region_34.35_spmd} | conditional | flops 728068 | bytes 69667264 | solution.py:127
  337.5 15.6 %branch_1_fun.50 = (bf16[1024,1024]{1,0:T(8,128)(2,1)}, f32[1024,128]{1,0:T(8,128)S(1)}, f32[1024,128]{1,0:T(8,128)S(1)}, bf16[1024,16]{1,0:T(8,128)(2,1)}, f32[1,1024]{1,0:T(1,128)S(1)}, /*index=5*/f32[2,16]{1,0:T(2,128)S(1)}) custom-call(f32[1024,1280]{1,0:T(8,128)} %get-tuple-element.715.v_ref, f32[1024,1024]{1,0:T(8,128)} %get-tuple-element.716.dy_ref, ...), custom_call_target="tpu_custom_call" | custom-call | bytes 49500000 | tf_op jit(solution)/shard_map/cond/branch_1_fun/pallas_call | solution.py:1112
  359.7 15.2 %conditional.37 = (bf16[1024,128]{1,0:T(8,128)(2,1)}, f32[2,8,128]{2,1,0:T(8,128)S(1)}, bf16[512,1024]{1,0:T(8,128)(2,1)}, bf16[512,1024]{1,0:T(8,128)(2,1)}) conditional(s32[]{:T(128)} %convert_element_type.80, () %tuple.199, (f32[1024,128]{1,0:T(8,128)S(1)}, f32[1024,64]{1,0:T(8,128)}, bf16[4096,1024]{1,0:T(8,128)(2,1)}, ...), branch_computations={%region_35.36_spmd, %region_36.37_spmd} | conditional | flops 329728 | bytes 4999822 | solution.py:127
  361.7 6.0 %collective-permute-done.58 = f32[512,128]{1,0:T(8,128)S(1)} collective-permute-done((f32[512,128]{1,0:T(8,128)S(1)}, f32[512,128]{1,0:T(8,128)S(1)}, u32[]{:S(2)}, u32[]{:S(2)}) %collective-permute-start.58) | collective-permute-done | bytes 262176 | tf_op jit(solution)/shard_map/cond/branch_1_fun/ppermute | solution.py:132
  375.0 35.5 %conditional.38 = (bf16[512,1024]{1,0:T(8,128)(2,1)}, bf16[512,1024]{1,0:T(8,128)(2,1)}, bf16[256,1152]{1,0:T(8,128)(2,1)}, bf16[256,1152]{1,0:T(8,128)(2,1)}, b...) conditional(s32[]{:T(128)} %convert_element_type.80, () %tuple.198, ...), branch_computations={%region_37.38_spmd, %region_38.40_spmd} | conditional | flops 837632 | bytes 106526744 | solution.py:127
  383.9 9.0 %branch_1_fun.52 = (bf16[1024,1024]{1,0:T(8,128)(2,1)S(1)}, f32[4,1024]{1,0:T(4,128)S(1)}, f32[8,1,128]{2,1,0:T(1,128)S(1)}) custom-call(bf16[1024,1024]{1,0:T(8,128)(2,1)} %get-tuple-element.752.d_ref, bf16[1024,1024]{1,0:T(8,128)(2,1)} %get-tuple-element.753.in_ref, f32[2,8,1024]{2,1,0:T(8,128)S(1)} %get-tuple-element.754.halo_ref, ...), custom_call_target="tpu_custom_call" | custom-call | bytes 26400000 | tf_op jit(solution)/shard_map/cond/branch_1_fun/pallas_call | solution.py:925
  397.7 10.4 %branch_1_fun.54.a_ref.b_ref = bf16[2048,1152]{1,0:T(8,128)(2,1)} custom-call(s32[1]{0:T(128)} %get-tuple-element.746.far_ref, s32[8]{0:T(128)S(1)} %get-tuple-element.747.block_ref, bf16[1024,512]{1,0:T(8,128)(2,1)} %get-tuple-element.748.refs_0_, bf16[1024,512]{1,0:T(8,128)(2,1)} %get-tuple-element.749.refs_1_, bf16[1024,512]{1,0:T(8,128)(2,1)S(1)} %copy-done.12, ...), custom_call_target="tpu_custom_call" | custom-call | bytes 29700000 | tf_op jit(solution)/shard_map/cond/branch_1_fun/pallas_call | solution.py:784
  410.7 19.0 %conditional.39 = (bf16[256,1152]{1,0:T(8,128)(2,1)}, bf16[256,1152]{1,0:T(8,128)(2,1)}, bf16[1024,2048]{1,0:T(8,128)(2,1)S(1)}, f32[7200]{0:T(1024)S(1)}, f32[1024]{0:T(1024)S(1)}) conditional(s32[]{:T(128)} %convert_element_type.80, () %tuple.232, (bf16[256,1152]{1,0:T(8,128)(2,1)}, bf16[256,1152]{1,0:T(8,128)(2,1)}, s32[8]{0:T(128)S(1)}, ...), branch_computations={%region_40.41_spmd, %region_41.42_spmd} | conditional | flops 8224 | bytes 54036564 | solution.py:127
  414.7 15.0 %branch_1_fun.57 = bf16[1024,2048]{1,0:T(8,128)(2,1)S(1)} custom-call(s32[8]{0:T(128)S(1)} %get-tuple-element.778.spot_ref, bf16[1024,1024]{1,0:T(8,128)(2,1)} %get-tuple-element.779.refs_0_, bf16[1024,1024]{1,0:T(8,128)(2,1)S(1)} %get-tuple-element.780.refs_1_, bf16[1024,128]{1,0:T(8,128)(2,1)S(1)} %get-tuple-element.781.refs_2_, ...), custom_call_target="tpu_custom_call" | custom-call | bytes 49087500 | tf_op jit(solution)/shard_map/cond/branch_1_fun/pallas_call | solution.py:847
  429.8 5.8 %conditional.40 = (bf16[256,1152]{1,0:T(8,128)(2,1)S(1)}, bf16[256,1152]{1,0:T(8,128)(2,1)S(1)}, bf16[1024,512]{1,0:T(8,128)(2,1)S(1)}, f32[1024,512]{1,0:T(8,128)S(1)}, f32[1024]{0:T(1024)S(1)}) conditional(s32[]{:T(128)} %convert_element_type.80, () %tuple.197, (bf16[2048,1152]{1,0:T(8,128)(2,1)}, bf16[256,1152]{1,0:T(8,128)(2,1)}, ...), branch_computations={%region_42.43_spmd, %region_43.44_spmd} | conditional | flops 3672064 | bytes 19955872 | solution.py:127
  436.9 24.9 %conditional.41 = (bf16[256,1152]{1,0:T(8,128)(2,1)}, bf16[256,1152]{1,0:T(8,128)(2,1)}, bf16[1024,512]{1,0:T(8,128)(2,1)}, f32[7200]{0:T(1024)S(1)}, f32[256,10...) conditional(s32[]{:T(128)} %convert_element_type.80, () %tuple.196, ...), branch_computations={%region_44.45_spmd, %region_45.46_spmd} | conditional | flops 1580064 | bytes 16454752 | solution.py:127
  447.5 7.1 %collective-permute-done.49 = f32[7200]{0:T(1024)S(1)} collective-permute-done((f32[7200]{0:T(1024)S(1)}, f32[7200]{0:T(1024)S(1)}, u32[]{:S(2)}, u32[]{:S(2)}) %collective-permute-start.49) | collective-permute-done | bytes 28832 | tf_op jit(solution)/shard_map/cond/branch_1_fun/ppermute | solution.py:132
  463.2 31.2 %conditional.42 = (f32[256,1024]{1,0:T(8,128)}, f32[256,256]{1,0:T(8,128)S(1)}, f32[256]{0:T(256)S(1)}, f32[7200]{0:T(1024)}, f32[2,512,512]{2,1,0:T(8,128)}, /*...) conditional(s32[]{:T(128)} %convert_element_type.80, () %tuple.236, ...), branch_computations={%region_46.47_spmd, %region_47.50_spmd} | conditional | flops 4078612 | bytes 16589476 | solution.py:127
  473.4 8.4 %collective-permute-done.68 = f32[7200]{0:T(1024)S(1)} collective-permute-done((f32[7200]{0:T(1024)S(1)}, f32[7200]{0:T(1024)S(1)}, u32[]{:S(2)}, u32[]{:S(2)}) %collective-permute-start.68) | collective-permute-done | bytes 28832 | tf_op jit(solution)/shard_map/cond/branch_1_fun/ppermute | solution.py:132
  485.5 7.2 %psum.19 = f32[1280]{0:T(1024)S(1)} all-reduce(f32[1280]{0:T(1024)S(1)} %pad_maximum_fusion.6), channel_id=1, replica_groups=mesh['seq'=8,'head'=4] {'head'}, use_global_device_ids=true, to_apply=%region_48.48 | all-reduce | flops 1280 | bytes 10240 | tf_op jit(solution)/shard_map/cond/branch_1_fun/psum | solution.py:136
  (363 shorter events, 201.7 us)
Async XLA Ops:
  4.4 19.7 %collective-permute-start.27 = (f32[256]{0:T(256)S(1)}, f32[256]{0:T(256)S(1)}, u32[]{:S(2)}, u32[]{:S(2)}) collective-permute-start(f32[256]{0:T(256)S(1)} %convert_element_type.31), channel_id=1, source_target_pairs={{0,0},{8,1},{16,2},{24,3},{4,4},{12,5},{20,6},{28,7},{1,8},{9,9},{... | collective-permute-start | bytes 3080 | tf_op jit(solution)/shard_map/cond/branch_1_fun/ppermute | solution.py:156
  5.1 19.0 %collective-permute-start.28 = (f32[256]{0:T(256)S(1)}, f32[256]{0:T(256)S(1)}, u32[]{:S(2)}, u32[]{:S(2)}) collective-permute-start(f32[256]{0:T(256)S(1)} %convert_element_type.31), channel_id=1, source_target_pairs={{4,0},{12,1},{20,2},{28,3},{0,4},{8,5},{16,6},{24,7},{5,8},{13,9},... | collective-permute-start | bytes 3080 | tf_op jit(solution)/shard_map/cond/branch_1_fun/ppermute | solution.py:156
  8.1 17.6 %collective-permute-start.25 = (bf16[256,1152]{1,0:T(8,128)(2,1)}, bf16[256,1152]{1,0:T(8,128)(2,1)}, u32[]{:S(2)}, u32[]{:S(2)}) collective-permute-start(bf16[256,1152]{1,0:T(8,128)(2,1)} %get-tuple-element.506), channel_id=1, source_target_pairs={{0,8},{8,16},{16,24},{24,28},{28,20},{20,12},{12,4},{4,0},{1,9},{9... | collective-permute-start | bytes 1769480 | tf_op jit(solution)/shard_map/cond/branch_1_fun/ppermute | solution.py:65
  12.1 15.9 %collective-permute-start.26 = (bf16[256,1152]{1,0:T(8,128)(2,1)}, bf16[256,1152]{1,0:T(8,128)(2,1)}, u32[]{:S(2)}, u32[]{:S(2)}) collective-permute-start(bf16[256,1152]{1,0:T(8,128)(2,1)} %get-tuple-element.506), channel_id=1, source_target_pairs={{0,4},{8,0},{16,8},{24,16},{28,24},{20,28},{12,20},{4,12},{1,5},{9... | collective-permute-start | bytes 1769480 | tf_op jit(solution)/shard_map/cond/branch_1_fun/ppermute | solution.py:65
  28.0 35.3 %collective-permute-start.69 = (bf16[1024,512]{1,0:T(8,128)(2,1)S(1)}, bf16[1024,512]{1,0:T(8,128)(2,1)S(1)}, u32[]{:S(2)}, u32[]{:S(2)}) collective-permute-start(bf16[1024,512]{1,0:T(8,128)(2,1)S(1)} %get-tuple-element.992), channel_id=1, source_target_pairs={{0,2},{1,3},{2,0},{3,1},{4,6},{5,7},{6,4},{7,5},{8,10},{9,11},{10,... | collective-permute-start | bytes 3145736 | tf_op jit(solution)/shard_map/ppermute | solution.py:132
  31.1 16.1 %collective-permute-start.31 = (bf16[1024,512]{1,0:T(8,128)(2,1)S(1)}, bf16[1024,512]{1,0:T(8,128)(2,1)}, u32[]{:S(2)}, u32[]{:S(2)}) collective-permute-start(bf16[1024,512]{1,0:T(8,128)(2,1)S(1)} %get-tuple-element.512), channel_id=1, source_target_pairs={{0,1},{1,0},{2,3},{3,2},{4,5},{5,4},{6,7},{7,6},{8,9},{9,8},{10,11... | collective-permute-start | bytes 3145736 | tf_op jit(solution)/shard_map/cond/branch_1_fun/ppermute | solution.py:132
  31.1 16.1 %collective-permute-start.29 = (bf16[256,1152]{1,0:T(8,128)(2,1)}, bf16[256,1152]{1,0:T(8,128)(2,1)}, u32[]{:S(2)}, u32[]{:S(2)}) collective-permute-start(bf16[256,1152]{1,0:T(8,128)(2,1)} %get-tuple-element.510), channel_id=1, source_target_pairs={{0,8},{8,16},{16,24},{24,28},{28,20},{20,12},{12,4},{4,0},{1,9},{9... | collective-permute-start | bytes 1769480 | tf_op jit(solution)/shard_map/cond/branch_1_fun/ppermute | solution.py:65
  31.4 15.8 %collective-permute-start.30 = (bf16[256,1152]{1,0:T(8,128)(2,1)}, bf16[256,1152]{1,0:T(8,128)(2,1)}, u32[]{:S(2)}, u32[]{:S(2)}) collective-permute-start(bf16[256,1152]{1,0:T(8,128)(2,1)} %get-tuple-element.511), channel_id=1, source_target_pairs={{0,4},{8,0},{16,8},{24,16},{28,24},{20,28},{12,20},{4,12},{1,5},{9... | collective-permute-start | bytes 1769480 | tf_op jit(solution)/shard_map/cond/branch_1_fun/ppermute | solution.py:65
  47.2 15.3 %collective-permute-start = (bf16[256,1152]{1,0:T(8,128)(2,1)}, bf16[256,1152]{1,0:T(8,128)(2,1)}, u32[]{:S(2)}, u32[]{:S(2)}) collective-permute-start(bf16[256,1152]{1,0:T(8,128)(2,1)} %get-tuple-element.516), channel_id=1, source_target_pairs={{0,8},{8,16},{16,24},{24,28},{28,20},{20,12},{12,4},{4,0},{1,9},{9... | collective-permute-start | bytes 1769480 | tf_op jit(solution)/shard_map/cond/branch_1_fun/ppermute | solution.py:65
  48.6 14.7 %collective-permute-start.1 = (bf16[256,1152]{1,0:T(8,128)(2,1)}, bf16[256,1152]{1,0:T(8,128)(2,1)}, u32[]{:S(2)}, u32[]{:S(2)}) collective-permute-start(bf16[256,1152]{1,0:T(8,128)(2,1)} %get-tuple-element.517), channel_id=1, source_target_pairs={{0,4},{8,0},{16,8},{24,16},{28,24},{20,28},{12,20},{4,12},{1,5},{9... | collective-permute-start | bytes 1769480 | tf_op jit(solution)/shard_map/cond/branch_1_fun/ppermute | solution.py:65
  77.7 24.5 %collective-permute-start.53 = (bf16[512,1024]{1,0:T(8,128)(2,1)}, bf16[512,1024]{1,0:T(8,128)(2,1)}, u32[]{:S(2)}, u32[]{:S(2)}) collective-permute-start(bf16[512,1024]{1,0:T(8,128)(2,1)} %copy.46), channel_id=1, source_target_pairs={{0,8},{8,16},{16,24},{24,28},{28,20},{20,12},{12,4},{4,0},{1,9},{9... | collective-permute-start | bytes 3145736 | tf_op jit(solution)/shard_map/cond/branch_1_fun/ppermute | solution.py:65
  78.2 24.2 %collective-permute-start.54 = (bf16[512,1024]{1,0:T(8,128)(2,1)}, bf16[512,1024]{1,0:T(8,128)(2,1)}, u32[]{:S(2)}, u32[]{:S(2)}) collective-permute-start(bf16[512,1024]{1,0:T(8,128)(2,1)} %copy.46), channel_id=1, source_target_pairs={{0,4},{8,0},{16,8},{24,16},{28,24},{20,28},{12,20},{4,12},{1,5},{9... | collective-permute-start | bytes 3145736 | tf_op jit(solution)/shard_map/cond/branch_1_fun/ppermute | solution.py:65
  108.8 35.4 %collective-permute-start.8 = (bf16[1024,512]{1,0:T(8,128)(2,1)}, bf16[1024,512]{1,0:T(8,128)(2,1)}, u32[]{:S(2)}, u32[]{:S(2)}) collective-permute-start(bf16[1024,512]{1,0:T(8,128)(2,1)} %get-tuple-element.591), channel_id=1, source_target_pairs={{0,1},{1,0},{2,3},{3,2},{4,5},{5,4},{6,7},{7,6},{8,9},{9,8},{10,11... | collective-permute-start | bytes 3145736 | tf_op jit(solution)/shard_map/cond/branch_1_fun/ppermute | solution.py:132
  108.9 35.3 %collective-permute-start.9 = (bf16[1024,512]{1,0:T(8,128)(2,1)}, bf16[1024,512]{1,0:T(8,128)(2,1)}, u32[]{:S(2)}, u32[]{:S(2)}) collective-permute-start(bf16[1024,512]{1,0:T(8,128)(2,1)} %get-tuple-element.591), channel_id=1, source_target_pairs={{0,2},{1,3},{2,0},{3,1},{4,6},{5,7},{6,4},{7,5},{8,10},{9,11},{10,... | collective-permute-start | bytes 3145736 | tf_op jit(solution)/shard_map/cond/branch_1_fun/ppermute | solution.py:132
  111.0 33.2 %collective-permute-start.5 = (bf16[512,1024]{1,0:T(8,128)(2,1)}, bf16[512,1024]{1,0:T(8,128)(2,1)}, u32[]{:S(2)}, u32[]{:S(2)}) collective-permute-start(bf16[512,1024]{1,0:T(8,128)(2,1)} %get-tuple-element.564), channel_id=1, source_target_pairs={{0,8},{8,16},{16,24},{24,28},{28,20},{20,12},{12,4},{4,0},{1,9},{9... | collective-permute-start | bytes 3145736 | tf_op jit(solution)/shard_map/cond/branch_1_fun/ppermute | solution.py:65
  113.0 31.2 %collective-permute-start.6 = (bf16[512,1024]{1,0:T(8,128)(2,1)}, bf16[512,1024]{1,0:T(8,128)(2,1)}, u32[]{:S(2)}, u32[]{:S(2)}) collective-permute-start(bf16[512,1024]{1,0:T(8,128)(2,1)} %get-tuple-element.565), channel_id=1, source_target_pairs={{0,4},{8,0},{16,8},{24,16},{28,24},{20,28},{12,20},{4,12},{1,5},{9... | collective-permute-start | bytes 3145736 | tf_op jit(solution)/shard_map/cond/branch_1_fun/ppermute | solution.py:65
  130.7 12.6 %collective-permute-start.7 = (bf16[144,1024]{1,0:T(8,128)(2,1)S(1)}, bf16[144,1024]{1,0:T(8,128)(2,1)S(1)}, u32[]{:S(2)}, u32[]{:S(2)}) collective-permute-start(bf16[144,1024]{1,0:T(8,128)(2,1)S(1)} %get-tuple-element.585), channel_id=1, source_target_pairs={{0,4},{4,0},{8,12},{12,8},{16,20},{20,16},{24,28},{28,24},{1,5},{5... | collective-permute-start | bytes 884744 | tf_op jit(solution)/shard_map/cond/branch_1_fun/ppermute | solution.py:132
  144.2 30.0 %collective-permute-start.33 = (bf16[512,1024]{1,0:T(8,128)(2,1)}, bf16[512,1024]{1,0:T(8,128)(2,1)}, u32[]{:S(2)}, u32[]{:S(2)}) collective-permute-start(bf16[512,1024]{1,0:T(8,128)(2,1)} %get-tuple-element.592), channel_id=1, source_target_pairs={{0,8},{8,16},{16,24},{24,28},{28,20},{20,12},{12,4},{4,0},{1,9},{9... | collective-permute-start | bytes 3145736 | tf_op jit(solution)/shard_map/cond/branch_1_fun/ppermute | solution.py:65
  144.3 29.9 %collective-permute-start.34 = (bf16[512,1024]{1,0:T(8,128)(2,1)}, bf16[512,1024]{1,0:T(8,128)(2,1)}, u32[]{:S(2)}, u32[]{:S(2)}) collective-permute-start(bf16[512,1024]{1,0:T(8,128)(2,1)} %get-tuple-element.593), channel_id=1, source_target_pairs={{0,4},{8,0},{16,8},{24,16},{28,24},{20,28},{12,20},{4,12},{1,5},{9... | collective-permute-start | bytes 3145736 | tf_op jit(solution)/shard_map/cond/branch_1_fun/ppermute | solution.py:65
  146.3 27.9 %collective-permute-start.36 = (bf16[1024,512]{1,0:T(8,128)(2,1)}, bf16[1024,512]{1,0:T(8,128)(2,1)}, u32[]{:S(2)}, u32[]{:S(2)}) collective-permute-start(bf16[1024,512]{1,0:T(8,128)(2,1)} %get-tuple-element.603), channel_id=1, source_target_pairs={{0,1},{1,0},{2,3},{3,2},{4,5},{5,4},{6,7},{7,6},{8,9},{9,8},{10,11... | collective-permute-start | bytes 3145736 | tf_op jit(solution)/shard_map/cond/branch_1_fun/ppermute | solution.py:132
  146.3 27.0 %collective-permute-start.35 = (bf16[144,1024]{1,0:T(8,128)(2,1)S(1)}, bf16[144,1024]{1,0:T(8,128)(2,1)S(1)}, u32[]{:S(2)}, u32[]{:S(2)}) collective-permute-start(bf16[144,1024]{1,0:T(8,128)(2,1)S(1)} %get-tuple-element.599), channel_id=1, source_target_pairs={{0,8},{4,12},{8,16},{12,20},{16,24},{20,28},{1,9},{5,13},{9,17},{1... | collective-permute-start | bytes 884744 | tf_op jit(solution)/shard_map/cond/branch_1_fun/ppermute | solution.py:205
  176.9 31.4 %collective-permute-start.10 = (bf16[256,1024]{1,0:T(8,128)(2,1)}, bf16[256,1024]{1,0:T(8,128)(2,1)}, u32[]{:S(2)}, u32[]{:S(2)}) collective-permute-start(bf16[256,1024]{1,0:T(8,128)(2,1)} %slice.156), channel_id=1, source_target_pairs={{0,8},{8,16},{16,24},{24,28},{28,20},{20,12},{12,4},{4,0},{1,9},{9... | collective-permute-start | bytes 1572872 | tf_op jit(solution)/shard_map/cond/branch_1_fun/ppermute | solution.py:65
  181.3 27.0 %collective-permute-start.11 = (bf16[256,1024]{1,0:T(8,128)(2,1)}, bf16[256,1024]{1,0:T(8,128)(2,1)}, u32[]{:S(2)}, u32[]{:S(2)}) collective-permute-start(bf16[256,1024]{1,0:T(8,128)(2,1)} %slice.157), channel_id=1, source_target_pairs={{0,4},{8,0},{16,8},{24,16},{28,24},{20,28},{12,20},{4,12},{1,5},{9... | collective-permute-start | bytes 1572872 | tf_op jit(solution)/shard_map/cond/branch_1_fun/ppermute | solution.py:65
  181.7 24.5 %collective-permute-start.12 = (bf16[128,1024]{1,0:T(8,128)(2,1)S(1)}, bf16[128,1024]{1,0:T(8,128)(2,1)S(1)}, u32[]{:S(2)}, u32[]{:S(2)}) collective-permute-start(bf16[128,1024]{1,0:T(8,128)(2,1)S(1)} %get-tuple-element.613), channel_id=1, source_target_pairs={{0,16},{4,20},{8,24},{12,28},{1,17},{5,21},{9,25},{13,29},{2,18},{... | collective-permute-start | bytes 786440 | tf_op jit(solution)/shard_map/cond/branch_1_fun/ppermute | solution.py:205
  250.7 20.2 %collective-permute-start.15 = (bf16[256,1024]{1,0:T(8,128)(2,1)S(1)}, bf16[256,1024]{1,0:T(8,128)(2,1)S(1)}, u32[]{:S(2)}, u32[]{:S(2)}) collective-permute-start(bf16[256,1024]{1,0:T(8,128)(2,1)S(1)} %get-tuple-element.665), channel_id=1, source_target_pairs={{0,8},{8,16},{16,24},{24,28},{28,20},{20,12},{12,4},{4,0},{1,9},{9... | collective-permute-start | bytes 1572872 | tf_op jit(solution)/shard_map/cond/branch_1_fun/ppermute | solution.py:65
  252.8 18.2 %collective-permute-start.16 = (bf16[256,1024]{1,0:T(8,128)(2,1)S(1)}, bf16[256,1024]{1,0:T(8,128)(2,1)S(1)}, u32[]{:S(2)}, u32[]{:S(2)}) collective-permute-start(bf16[256,1024]{1,0:T(8,128)(2,1)S(1)} %get-tuple-element.666), channel_id=1, source_target_pairs={{0,4},{8,0},{16,8},{24,16},{28,24},{20,28},{12,20},{4,12},{1,5},{9... | collective-permute-start | bytes 1572872 | tf_op jit(solution)/shard_map/cond/branch_1_fun/ppermute | solution.py:65
  253.6 17.1 %collective-permute-start.14 = (bf16[144,1024]{1,0:T(8,128)(2,1)S(1)}, bf16[144,1024]{1,0:T(8,128)(2,1)S(1)}, u32[]{:S(2)}, u32[]{:S(2)}) collective-permute-start(bf16[144,1024]{1,0:T(8,128)(2,1)S(1)} %get-tuple-element.645), channel_id=1, source_target_pairs={{0,4},{4,0},{8,12},{12,8},{16,20},{20,16},{24,28},{28,24},{1,5},{5... | collective-permute-start | bytes 884744 | tf_op jit(solution)/shard_map/cond/branch_1_fun/ppermute | solution.py:132
  272.9 32.2 %collective-permute-start.18 = (bf16[512,1024]{1,0:T(8,128)(2,1)S(1)}, bf16[512,1024]{1,0:T(8,128)(2,1)}, u32[]{:S(2)}, u32[]{:S(2)}) collective-permute-start(bf16[512,1024]{1,0:T(8,128)(2,1)S(1)} %get-tuple-element.679), channel_id=1, source_target_pairs={{0,8},{8,16},{16,24},{24,28},{28,20},{20,12},{12,4},{4,0},{1,9},{9... | collective-permute-start | bytes 3145736 | tf_op jit(solution)/shard_map/cond/branch_1_fun/ppermute | solution.py:65
  274.2 31.0 %collective-permute-start.19 = (bf16[512,1024]{1,0:T(8,128)(2,1)S(1)}, bf16[512,1024]{1,0:T(8,128)(2,1)}, u32[]{:S(2)}, u32[]{:S(2)}) collective-permute-start(bf16[512,1024]{1,0:T(8,128)(2,1)S(1)} %get-tuple-element.680), channel_id=1, source_target_pairs={{0,4},{8,0},{16,8},{24,16},{28,24},{20,28},{12,20},{4,12},{1,5},{9... | collective-permute-start | bytes 3145736 | tf_op jit(solution)/shard_map/cond/branch_1_fun/ppermute | solution.py:65
  275.1 29.2 %collective-permute-start.17 = (bf16[144,1024]{1,0:T(8,128)(2,1)S(1)}, bf16[144,1024]{1,0:T(8,128)(2,1)S(1)}, u32[]{:S(2)}, u32[]{:S(2)}) collective-permute-start(bf16[144,1024]{1,0:T(8,128)(2,1)S(1)} %get-tuple-element.675), channel_id=1, source_target_pairs={{8,0},{12,4},{16,8},{20,12},{24,16},{28,20},{9,1},{13,5},{17,9},{2... | collective-permute-start | bytes 884744 | tf_op jit(solution)/shard_map/cond/branch_1_fun/ppermute | solution.py:205
  305.2 14.4 %collective-permute-start.20 = (bf16[128,1024]{1,0:T(8,128)(2,1)S(1)}, bf16[128,1024]{1,0:T(8,128)(2,1)S(1)}, u32[]{:S(2)}, u32[]{:S(2)}) collective-permute-start(bf16[128,1024]{1,0:T(8,128)(2,1)S(1)} %get-tuple-element.696), channel_id=1, source_target_pairs={{16,0},{20,4},{24,8},{28,12},{17,1},{21,5},{25,9},{29,13},{18,2},{... | collective-permute-start | bytes 786440 | tf_op jit(solution)/shard_map/cond/branch_1_fun/ppermute | solution.py:205
  332.2 27.5 %collective-permute-start.37 = (bf16[512,1024]{1,0:T(8,128)(2,1)}, bf16[512,1024]{1,0:T(8,128)(2,1)}, u32[]{:S(2)}, u32[]{:S(2)}) collective-permute-start(bf16[512,1024]{1,0:T(8,128)(2,1)} %get-tuple-element.713), channel_id=1, source_target_pairs={{0,8},{8,16},{16,24},{24,28},{28,20},{20,12},{12,4},{4,0},{1,9},{9... | collective-permute-start | bytes 3145736 | tf_op jit(solution)/shard_map/cond/branch_1_fun/ppermute | solution.py:65
  333.0 26.7 %collective-permute-start.38 = (bf16[512,1024]{1,0:T(8,128)(2,1)}, bf16[512,1024]{1,0:T(8,128)(2,1)}, u32[]{:S(2)}, u32[]{:S(2)}) collective-permute-start(bf16[512,1024]{1,0:T(8,128)(2,1)} %get-tuple-element.714), channel_id=1, source_target_pairs={{0,4},{8,0},{16,8},{24,16},{28,24},{20,28},{12,20},{4,12},{1,5},{9... | collective-permute-start | bytes 3145736 | tf_op jit(solution)/shard_map/cond/branch_1_fun/ppermute | solution.py:65
  375.0 35.5 %collective-permute-start.41 = (bf16[512,1024]{1,0:T(8,128)(2,1)}, bf16[512,1024]{1,0:T(8,128)(2,1)}, u32[]{:S(2)}, u32[]{:S(2)}) collective-permute-start(bf16[512,1024]{1,0:T(8,128)(2,1)} %get-tuple-element.744), channel_id=1, source_target_pairs={{0,8},{8,16},{16,24},{24,28},{28,20},{20,12},{12,4},{4,0},{1,9},{9... | collective-permute-start | bytes 3145736 | tf_op jit(solution)/shard_map/cond/branch_1_fun/ppermute | solution.py:65
  378.3 32.2 %collective-permute-start.42 = (bf16[512,1024]{1,0:T(8,128)(2,1)}, bf16[512,1024]{1,0:T(8,128)(2,1)}, u32[]{:S(2)}, u32[]{:S(2)}) collective-permute-start(bf16[512,1024]{1,0:T(8,128)(2,1)} %get-tuple-element.745), channel_id=1, source_target_pairs={{0,4},{8,0},{16,8},{24,16},{28,24},{20,28},{12,20},{4,12},{1,5},{9... | collective-permute-start | bytes 3145736 | tf_op jit(solution)/shard_map/cond/branch_1_fun/ppermute | solution.py:65
  378.3 32.2 %collective-permute-start.45 = (bf16[1024,512]{1,0:T(8,128)(2,1)}, bf16[1024,512]{1,0:T(8,128)(2,1)}, u32[]{:S(2)}, u32[]{:S(2)}) collective-permute-start(bf16[1024,512]{1,0:T(8,128)(2,1)} %get-tuple-element.773), channel_id=1, source_target_pairs={{0,2},{1,3},{2,0},{3,1},{4,6},{5,7},{6,4},{7,5},{8,10},{9,11},{10,... | collective-permute-start | bytes 3145736 | tf_op jit(solution)/shard_map/cond/branch_1_fun/ppermute | solution.py:132
  394.0 14.0 %collective-permute-start.43 = (bf16[128,1152]{1,0:T(8,128)(2,1)S(1)}, bf16[128,1152]{1,0:T(8,128)(2,1)S(1)}, u32[]{:S(2)}, u32[]{:S(2)}) collective-permute-start(bf16[128,1152]{1,0:T(8,128)(2,1)S(1)} %get-tuple-element.765), channel_id=1, source_target_pairs={{0,8},{8,16},{16,24},{24,28},{28,20},{20,12},{12,4},{4,0},{1,9},{9... | collective-permute-start | bytes 884744 | tf_op jit(solution)/shard_map/cond/branch_1_fun/ppermute | solution.py:65
  410.7 19.0 %collective-permute-start.21 = (bf16[256,1152]{1,0:T(8,128)(2,1)}, bf16[256,1152]{1,0:T(8,128)(2,1)}, u32[]{:S(2)}, u32[]{:S(2)}) collective-permute-start(bf16[256,1152]{1,0:T(8,128)(2,1)} %get-tuple-element.776), channel_id=1, source_target_pairs={{0,8},{8,16},{16,24},{24,28},{28,20},{20,12},{12,4},{4,0},{1,9},{9... | collective-permute-start | bytes 1769480 | tf_op jit(solution)/shard_map/cond/branch_1_fun/ppermute | solution.py:65
  413.0 16.8 %collective-permute-start.22 = (bf16[256,1152]{1,0:T(8,128)(2,1)}, bf16[256,1152]{1,0:T(8,128)(2,1)}, u32[]{:S(2)}, u32[]{:S(2)}) collective-permute-start(bf16[256,1152]{1,0:T(8,128)(2,1)} %get-tuple-element.777), channel_id=1, source_target_pairs={{0,4},{8,0},{16,8},{24,16},{28,24},{20,28},{12,20},{4,12},{1,5},{9... | collective-permute-start | bytes 1769480 | tf_op jit(solution)/shard_map/cond/branch_1_fun/ppermute | solution.py:65
  413.0 16.8 %collective-permute-start.23 = (f32[7200]{0:T(1024)S(1)}, f32[7200]{0:T(1024)S(1)}, u32[]{:S(2)}, u32[]{:S(2)}) collective-permute-start(f32[7200]{0:T(1024)S(1)} %get-tuple-element.786), channel_id=1, source_target_pairs={{0,4},{4,0},{8,12},{12,8},{16,20},{20,16},{24,28},{28,24},{1,5},{5... | collective-permute-start | bytes 86408 | tf_op jit(solution)/shard_map/cond/branch_1_fun/ppermute | solution.py:132
  414.7 15.0 %collective-permute-start.24 = (f32[1024]{0:T(1024)S(1)}, f32[1024]{0:T(1024)S(1)}, u32[]{:S(2)}, u32[]{:S(2)}) collective-permute-start(f32[1024]{0:T(1024)S(1)} %get-tuple-element.787), channel_id=1, source_target_pairs={{0,1},{1,0},{2,3},{3,2},{4,5},{5,4},{6,7},{7,6},{8,9},{9,8},{10,11... | collective-permute-start | bytes 12296 | tf_op jit(solution)/shard_map/cond/branch_1_fun/ppermute | solution.py:132
  436.9 24.9 %collective-permute-start.48 = (bf16[1024,512]{1,0:T(8,128)(2,1)S(1)}, bf16[1024,512]{1,0:T(8,128)(2,1)}, u32[]{:S(2)}, u32[]{:S(2)}) collective-permute-start(bf16[1024,512]{1,0:T(8,128)(2,1)S(1)} %get-tuple-element.801), channel_id=1, source_target_pairs={{0,2},{1,3},{2,0},{3,1},{4,6},{5,7},{6,4},{7,5},{8,10},{9,11},{10,... | collective-permute-start | bytes 3145736 | tf_op jit(solution)/shard_map/cond/branch_1_fun/ppermute | solution.py:132
  437.4 17.2 %collective-permute-start.46 = (bf16[256,1152]{1,0:T(8,128)(2,1)S(1)}, bf16[256,1152]{1,0:T(8,128)(2,1)S(1)}, u32[]{:S(2)}, u32[]{:S(2)}) collective-permute-start(bf16[256,1152]{1,0:T(8,128)(2,1)S(1)} %get-tuple-element.797), channel_id=1, source_target_pairs={{0,8},{8,16},{16,24},{24,28},{28,20},{20,12},{12,4},{4,0},{1,9},{9... | collective-permute-start | bytes 1769480 | tf_op jit(solution)/shard_map/cond/branch_1_fun/ppermute | solution.py:65
  439.4 15.3 %collective-permute-start.47 = (bf16[256,1152]{1,0:T(8,128)(2,1)S(1)}, bf16[256,1152]{1,0:T(8,128)(2,1)S(1)}, u32[]{:S(2)}, u32[]{:S(2)}) collective-permute-start(bf16[256,1152]{1,0:T(8,128)(2,1)S(1)} %get-tuple-element.798), channel_id=1, source_target_pairs={{0,4},{8,0},{16,8},{24,16},{28,24},{20,28},{12,20},{4,12},{1,5},{9... | collective-permute-start | bytes 1769480 | tf_op jit(solution)/shard_map/cond/branch_1_fun/ppermute | solution.py:65
  439.4 15.2 %collective-permute-start.49 = (f32[7200]{0:T(1024)S(1)}, f32[7200]{0:T(1024)S(1)}, u32[]{:S(2)}, u32[]{:S(2)}) collective-permute-start(f32[7200]{0:T(1024)S(1)} %get-tuple-element.802), channel_id=1, source_target_pairs={{0,8},{4,12},{8,0},{12,4},{16,24},{20,28},{24,16},{28,20},{1,9},{5... | collective-permute-start | bytes 86408 | tf_op jit(solution)/shard_map/cond/branch_1_fun/ppermute | solution.py:132
  463.2 18.9 %collective-permute-start.63 = (bf16[256,1152]{1,0:T(8,128)(2,1)}, bf16[256,1152]{1,0:T(8,128)(2,1)S(1)}, u32[]{:S(2)}, u32[]{:S(2)}) collective-permute-start(bf16[256,1152]{1,0:T(8,128)(2,1)} %get-tuple-element.814), channel_id=1, source_target_pairs={{0,8},{8,16},{16,24},{24,28},{28,20},{20,12},{12,4},{4,0},{1,9},{9... | collective-permute-start | bytes 1769480 | tf_op jit(solution)/shard_map/cond/branch_1_fun/ppermute | solution.py:65
  465.1 17.0 %collective-permute-start.64 = (bf16[256,1152]{1,0:T(8,128)(2,1)}, bf16[256,1152]{1,0:T(8,128)(2,1)S(1)}, u32[]{:S(2)}, u32[]{:S(2)}) collective-permute-start(bf16[256,1152]{1,0:T(8,128)(2,1)} %get-tuple-element.815), channel_id=1, source_target_pairs={{0,4},{8,0},{16,8},{24,16},{28,24},{20,28},{12,20},{4,12},{1,5},{9... | collective-permute-start | bytes 1769480 | tf_op jit(solution)/shard_map/cond/branch_1_fun/ppermute | solution.py:65
  465.2 16.6 %collective-permute-start.68 = (f32[7200]{0:T(1024)S(1)}, f32[7200]{0:T(1024)S(1)}, u32[]{:S(2)}, u32[]{:S(2)}) collective-permute-start(f32[7200]{0:T(1024)S(1)} %get-tuple-element.823), channel_id=1, source_target_pairs={{0,16},{4,20},{8,24},{12,28},{16,0},{20,4},{24,8},{28,12},{1,17},{... | collective-permute-start | bytes 86408 | tf_op jit(solution)/shard_map/cond/branch_1_fun/ppermute | solution.py:132
  (77 other events, 689.0 us)

commit v4 on v3

--- a/solution.py
+++ b/solution.py
@@ -86,7 +86,7 @@
     def add(self, whole, came, k):
         if not self.on:
             return ()
-        rows, columns = whole.shape[0] // self.size, whole.shape[1]
+        rows, columns = 2 * came[0].shape[0] if k == 3 else came[0].shape[0], whole.shape[1]
         halves = k == self.size // 2 - 1
         steps = ADD_STEPS
         tile = rows // steps
@@ -693,32 +693,48 @@
     rest_ref[...] = dot(act, r_ref[...])
 
 
+LATE = (4, 3, 5)
+
+
 def gate_project_kernel(spot_ref, *refs):
-    acts, cots, items = refs[:4], refs[4:8], refs[8:15]
-    z_ref, dm_ref, wz_ref, wo_ref, na_ref, ca_ref = refs[15:]
+    acts, cots, items = refs[:4], refs[4:8], refs[8:13]
+    z_ref, dm_ref, wz_ref, wo_ref, na_ref, ca_ref = refs[13:]
     rows = items[0].shape[0] // 2
-    last = spot_ref[4]
 
     @pl.when(pl.program_id(0) == 0)
     def _():
         for target, down in ((wz_ref, slice(0, rows)), (wo_ref, slice(rows, 2 * rows))):
             put = place_blocks(spot_ref, target, items, down)
-            put(4, 0, jnp.zeros((rows, target.shape[1]), BF16))
-
-    for i in range(8):
-
-        @pl.when(last == i)
-        def _():
-            cut = slice((i % 2) * rows, (i % 2 + 1) * rows)
-            na_ref[...] = acts[i // 2][:, cut]
-            ca_ref[...] = cots[i // 2][:, cut]
+            for k in LATE:
+                put(k, 0, jnp.zeros((rows, target.shape[1]), BF16))
+
+    for n, k in enumerate(LATE):
+        to = slice(n * rows, (n + 1) * rows)
+        for i in range(8):
+
+            @pl.when(spot_ref[k] == i)
+            def _():
+                cut = slice((i % 2) * rows, (i % 2 + 1) * rows)
+                na_ref[:, to] = acts[i // 2][:, cut]
+                ca_ref[:, to] = cots[i // 2][:, cut]
 
     z_ref[...] = dot(jnp.concatenate([a[...] for a in acts], axis=1), wz_ref[...])
     dm_ref[...] = dot(jnp.concatenate([a[...] for a in cots], axis=1), wo_ref[...])
 
 
+def gate_more_kernel(spot_ref, z_ref, dm_ref, na_ref, ca_ref, five_ref, three_ref, z_out, dm_out):
+    rows = five_ref.shape[0] // 2
+    one, two = slice(rows, 2 * rows), slice(2 * rows, 3 * rows)
+    z_out[...] = z_ref[...] + (
+        dot(na_ref[:, one], three_ref[:rows]) + dot(na_ref[:, two], five_ref[:rows])
+    )
+    dm_out[...] = dm_ref[...] + (
+        dot(ca_ref[:, one], three_ref[rows:]) + dot(ca_ref[:, two], five_ref[rows:])
+    )
+
+
 def with_spots(kernel, spots, acts, items, outs, shapes):
-    total, width = acts[0].shape
+    total = acts[0].shape[0]
     rows = min(256, total)
     fixed = lambda i, spot: (0, 0)
     return pl.pallas_call(
@@ -726,7 +742,7 @@
         grid_spec=pltpu.PrefetchScalarGridSpec(
             num_scalar_prefetch=1,
             grid=(total // rows,),
-            in_specs=[pl.BlockSpec((rows, width), lambda i, spot: (i, 0)) for _ in acts]
+            in_specs=[pl.BlockSpec((rows, act.shape[1]), lambda i, spot: (i, 0)) for act in acts]
             + [pl.BlockSpec(item.shape, fixed) for item in items],
             out_specs=[
                 pl.BlockSpec((rows, shape.shape[1]), lambda i, spot: (i, 0)) if split
@@ -798,9 +814,10 @@
 
 
 def outer_far(acts, grads):
-    vmem = pl.BlockSpec(memory_space=pltpu.VMEM)
     columns = grads[0].shape[1] if len(acts) == 2 else sum(g.shape[1] for g in grads)
-    width = acts[0].shape[1]
+    total, width = acts[0].shape[0], acts[0].shape[1] // len(LATE)
+    first_block = pl.BlockSpec((total, width), lambda i: (0, 0))
+    whole = lambda a: pl.BlockSpec(a.shape, lambda i: (0, 0))
 
     def kernel(*refs):
         first, second = refs[-2:]
@@ -820,8 +837,9 @@
     half = shaped(width if len(acts) == 2 else width // 2, columns, dtype=BF16)
     return pl.pallas_call(
         kernel,
-        in_specs=[vmem] * (len(acts) + len(grads)),
-        out_specs=[vmem, vmem],
+        grid=(1,),
+        in_specs=[first_block] * len(acts) + [whole(grad) for grad in grads],
+        out_specs=[whole(half), whole(half)],
         out_shape=[half, half],
         compiler_params=pltpu.CompilerParams(vmem_limit_bytes=VMEM_LIMIT),
     )(*acts, *grads)
@@ -832,18 +850,21 @@
     total = None
     for k in range(terms):
         weight = refs[terms + k][...]
-        if k < late:
-            weight = jnp.where(pl.program_id(0) == spot_ref[4], refs[2 * terms + k][...], weight)
+        if k == 0:
+            for n in range(late):
+                here = pl.program_id(0) == spot_ref[LATE[n]]
+                weight = jnp.where(here, refs[2 * terms + n][...], weight)
         term = dot(refs[k][...], weight, NT)
         total = term if total is None else total + term
     out_ref[...] = total.astype(out_ref.dtype)
 
 
-def project(ring, spots, acts, weights, late=()):
+def project(ring, spots, acts, weights, late, second):
     if not ring.on:
         return sum(dot(a, w, NT) for a, w in zip(acts, weights)).astype(BF16)
     rows, width = acts[0].shape[0], 256
     whole = lambda i, spot: (0, 0)
+    half = lambda i, spot: (second, 0)
     return pl.pallas_call(
         functools.partial(project_kernel, len(acts), len(late)),
         grid_spec=pltpu.PrefetchScalarGridSpec(
@@ -851,7 +872,10 @@
             grid=(weights[0].shape[0] // width,),
             in_specs=[pl.BlockSpec(a.shape, whole) for a in acts]
             + [pl.BlockSpec((width, w.shape[1]), lambda i, spot: (i, 0)) for w in weights]
-            + [pl.BlockSpec(w.shape, whole) for w in late],
+            + [
+                pl.BlockSpec((width, w.shape[1]), half if w.shape[0] > width else whole)
+                for w in late
+            ],
             out_specs=pl.BlockSpec((rows, width), lambda i, spot: (0, i)),
         ),
         out_shape=shaped(rows, weights[0].shape[0], dtype=BF16),
@@ -1049,20 +1073,27 @@
         return conv_out, y_local, steps, cumulative, begun, offsets, left, left_w
 
     own_block = model // ring.size
-    act_spec = pl.BlockSpec((rows, own_block), at)
+    g_rows = min(256, length)
+    g_count = length // g_rows
+    g_at = lambda b, i: (b * g_count + i, 0)
+    g_at3 = lambda b, i: (b * g_count + i, 0, 0)
+    g_block, g_row = pl.BlockSpec((g_rows, inner), g_at), pl.BlockSpec((1, 1, g_rows), g_at3)
+    g_c = pl.BlockSpec((g_rows, LANES), lambda b, i: (b * g_count + i, inner // LANES + 1))
+    g_heads_spec = pl.BlockSpec((g_rows, heads), g_at)
+    act_spec = pl.BlockSpec((g_rows, own_block), g_at)
     late_spec = pl.BlockSpec((own_block, inner), fixed)
-    wide_scratch = [pltpu.VMEM((rows, inner), F32), pltpu.VMEM((rows, inner), F32)]
+    wide_scratch = [pltpu.VMEM((g_rows, inner), F32), pltpu.VMEM((g_rows, inner), F32)]
 
     def gate(y_local, conv_out, came, cumulative, z_part, dm_part, late):
         return call(
             functools.partial(gate_kernel, pairs),
-            (batch, count),
+            (batch, g_count),
             [
-                block_spec, c_spec, state_spec, head_cols, block_spec, block_spec, row_inner,
+                g_block, g_c, state_spec, g_heads_spec, g_block, g_block, row_inner,
                 act_spec, act_spec, late_spec, late_spec,
             ],
-            [block_spec, pl.BlockSpec((1, 2, rows), at3)],
-            [shaped(total, inner), shaped(blocks, 2, rows)],
+            [g_block, pl.BlockSpec((1, 2, g_rows), g_at3)],
+            [shaped(total, inner), shaped(batch * g_count, 2, g_rows)],
             wide_scratch,
             micros=7.0,
         )(y_local, conv_out, came, cumulative, z_part, dm_part, gate_f, *late)
@@ -1070,17 +1101,17 @@
     def gate_back(dm_part, ssd, z_part, gate_scale, product, cumulative, conv_out, late):
         return call(
             functools.partial(gate_back_kernel, pairs, inner_all),
-            (batch, count),
+            (batch, g_count),
             [
-                block_spec, block_spec, block_spec, row_out, row_out, row_inner, head_cols, c_spec,
+                g_block, g_block, g_block, g_row, g_row, row_inner, g_heads_spec, g_c,
                 act_spec, act_spec, late_spec, late_spec,
             ],
-            [block_spec, block_spec, state_spec, row_out, row_inner, block_spec],
+            [g_block, g_block, state_spec, g_row, row_inner, g_block],
             [
                 shaped(total, inner, dtype=BF16),
                 shaped(total, inner),
                 shaped(batch, N, inner),
-                shaped(blocks, 1, rows),
+                shaped(batch * g_count, 1, g_rows),
                 shaped(1, inner),
                 shaped(total, inner, dtype=BF16),
             ],
@@ -1105,22 +1136,24 @@
         )(conv_out, d_ssd, steps, rate_row, begun, offsets, came)
         return du_local, dbc_local
 
-    def finish(conv_out, d_ssd, du_local, ssd, steps, cumulative, left_w, later, came, left, dbc_local, dt_raw):
+    def finish(conv_out, d_ssd, du_local, ssd, steps, cumulative, left_w, later, at_end, dbc_local, dt_raw):
+        f_back = lambda b, i: (b * g_count + g_count - 1 - i, 0)
+        f_spec = lambda width: pl.BlockSpec((g_rows, width), f_back)
+        f_v, f_block, f_heads = f_spec(inner + 2 * N), f_spec(inner), f_spec(heads)
+        f_maps, f_lanes = f_spec(2 * N), f_spec(LANES)
         lane_head = lax.broadcasted_iota(jnp.int32, (inner, heads), 0) // P_SIZE
         picker = (lane_head == lax.broadcasted_iota(jnp.int32, (inner, heads), 1)).astype(BF16)
-        at_end = jnp.exp(left_w) * came + left
         d_conv_x, d_bc_keep, d_bc_send, d_dt, g_skip, g_heads = call(
             functools.partial(finish_kernel, pairs, ring.on),
-            (batch, count),
+            (batch, g_count),
             [
-                v_back, block_back, block_back, block_back, heads_back, heads_back,
-                pl.BlockSpec((1, 1, inner), seq3), state_spec, state_spec, bc_back, heads_back,
+                f_v, f_block, f_block, f_block, f_heads, f_heads,
+                pl.BlockSpec((1, 1, inner), seq3), state_spec, state_spec, f_maps, f_heads,
                 row_heads, row_heads, row_inner,
                 pl.BlockSpec((inner, heads), fixed), pl.BlockSpec(memory_space=pltpu.SMEM),
             ],
             [
-                block_back, pl.BlockSpec((rows, LANES), back), pl.BlockSpec((rows, LANES), back),
-                heads_back, row_inner,
+                f_block, f_lanes, f_lanes, f_heads, row_inner,
                 pl.BlockSpec((2, heads), fixed),
             ],
             [
@@ -1133,8 +1166,8 @@
             ],
             [
                 pltpu.VMEM((8, heads), F32),
-                pltpu.VMEM((2 * rows, inner), BF16),
-                pltpu.VMEM((2 * rows, inner), BF16),
+                pltpu.VMEM((2 * g_rows, inner), BF16),
+                pltpu.VMEM((2 * g_rows, inner), BF16),
             ],
             micros=15.0,
         )(
@@ -1190,10 +1223,10 @@
 
     def work(hop1, own, w_z, w_out, cot_rows):
         zo_in = jnp.concatenate([w_z, w_out.T], axis=0)
-        return ring.hop(hop1), beside(ring, own), zo_in, cot_rows.astype(BF16)
-
-    hop2, near, zo_in, own_cot = ring.phase(work, hop1, own_normed, w_z, w_out, cot_rows)
-    hop3 = ring.phase(ring.hop, hop2)
+        hop2 = ring.hop(hop1)
+        return hop2, ring.hop(hop2), beside(ring, own), zo_in, cot_rows.astype(BF16)
+
+    hop2, hop3, near, zo_in, own_cot = ring.phase(work, hop1, own_normed, w_z, w_out, cot_rows)
     hop4, both = ring.phase(
         lambda hop3, far: (ring.last_hop(hop3), corner(ring, own_normed, far)), hop3, far
     )
@@ -1235,44 +1268,56 @@
 
     hop2, scanned, held, near, far = ring.phase(work, hop1, x_in, bc_in, halo, dt_raw, own_cot)
     conv_out, y_local, steps, cumulative, begun, offsets, left, left_w = scanned
-    def work(hop2, held, far, conv_out):
+    def work(hop1, hop2, held, far, conv_out, normed):
+        moving = ring.hop(hop2)
+        value = conv_out[:, inner:]
+        if not ring.on:
+            z_w = lax.all_gather(w_z, "seq", axis=0, tiled=True)
+            out_w = lax.all_gather(w_out.T, "seq", axis=0, tiled=True)
+            cot = (corner(ring, own_cot, far),)
+            none = jnp.zeros((total, own_block), BF16)
+            given = dot(normed[0], z_w), dot(cot[0], out_w), z_w, out_w, none, none
+            return moving, held, cot, given, slope(value)
+        value = [value[:, g * group : (g + 1) * group] for g in range(4)]
+        value = jnp.where(
+            here < 2, jnp.where(here == 0, value[0], value[1]),
+            jnp.where(here == 2, value[2], value[3]),
+        )
+        both = ring.phase(lambda far: corner(ring, own_cot, far), far)
+        wide, weight = shaped(total, inner), shaped(model, inner, dtype=BF16)
+        act = shaped(total, len(LATE) * own_block, dtype=BF16)
+        given = with_spots(
+            gate_project_kernel, spots, (*normed, both, near, far, own_cot), [zo_in, *hop1, *hop2],
+            [True, True, False, False, True, True], [wide, wide, weight, weight, act, act],
+        )
         held = forth.next_line(held) if split_pass else ()
-        value = conv_out[:, inner:]
-        if ring.on:
-            value = [value[:, g * group : (g + 1) * group] for g in range(4)]
-            value = jnp.where(
-                here < 2, jnp.where(here == 0, value[0], value[1]),
-                jnp.where(here == 2, value[2], value[3]),
-            )
-        return ring.hop(hop2), held, corner(ring, own_cot, far), slope(value)
-
-    hop3, held, both, own_slope = ring.phase(work, hop2, held, far, conv_out)
-    cot = (both, near, far, own_cot) if ring.on else (both,)
-
-    def work(hop1, hop2, hop3, held, normed, cot):
+        return moving, held, both, given, slope(value)
+
+    hop3, held, cot, given, own_slope = ring.phase(
+        work, hop1, hop2, held, far, conv_out, normed
+    )
+    if ring.on:
+        cot = (cot, near, far, own_cot)
+    z_part, dm_part, z_w, out_w, normed_late, cot_late = given
+
+    def work(hop3, held, z_part, dm_part, normed_late, cot_late):
         held = forth.further_lines(held) if split_pass else ()
         if ring.on:
-            wide, weight = shaped(total, inner), shaped(model, inner, dtype=BF16)
-            act = shaped(total, own_block, dtype=BF16)
-            given = with_spots(
-                gate_project_kernel, spots, (*normed, *cot), [zo_in, *hop1, *hop2, *hop3],
-                [True, True, False, False, True, True], [wide, wide, weight, weight, act, act],
+            wide = shaped(total, inner)
+            z_part, dm_part = with_spots(
+                gate_more_kernel, spots, (z_part, dm_part, normed_late, cot_late), hop3,
+                [True, True], [wide, wide],
             )
-        else:
-            z_w = lax.all_gather(w_z, "seq", axis=0, tiled=True)
-            out_w = lax.all_gather(w_out.T, "seq", axis=0, tiled=True)
-            none = jnp.zeros((total, own_block), BF16)
-            given = dot(normed[0], z_w), dot(cot[0], out_w), z_w, out_w, none, none
-        return ring.last_hop(hop3), held, given
-
-    hop4, held, given = ring.phase(work, hop1, hop2, hop3, held, normed, cot)
-    z_part, dm_part, z_w, out_w, normed_last, cot_last = given
+        came = forth.end(held) if split_pass else states_scan(left, left_w, 1)
+        return ring.last_hop(hop3), came, z_part, dm_part
+
+    hop4, came, z_part, dm_part = ring.phase(
+        work, hop3, held, z_part, dm_part, normed_late, cot_late
+    )
     if not ring.on:
         hop4 = (jnp.zeros((own_block, inner), BF16),) * 2
-    late = (normed_last, cot_last, *hop4)
-    came = ring.phase(
-        lambda held: forth.end(held) if split_pass else states_scan(left, left_w, 1), held
-    )
+    late = (normed_late, cot_late, *hop4)
+    late_z, late_out = ([half, hop3[1], hop3[0]] if ring.on else [] for half in hop4)
 
     ssd, square_g = gate(y_local, conv_out, came, cumulative, z_part, dm_part, late)
     square_g = head_sum(square_g)
@@ -1284,33 +1329,34 @@
 
     far_spot = spots[4:5] if ring.on else None
 
-    def work(d_left, left_w, normed, d_z, mixed, cot, normed_last, cot_last):
+    def work(d_left, left_w, normed, d_z, mixed, cot, normed_late, cot_late):
         held = back_pass.pair(back_pass.begin(d_left, left_w)) if split_pass else ()
         if ring.on:
-            sums = ring.send(*outer_far([normed_last, cot_last], [d_z, mixed]))
+            sums = ring.send(*outer_far([normed_late, cot_late], [d_z, mixed]))
             g_zo = outer(far_spot, order, (normed, [d_z]), (cot, [mixed]))
             return held, ring.add(g_zo, sums, 3), g_zo
         return held, (), (dot(normed[0], d_z, TN), dot(cot[0], mixed, TN))
 
     held, sums, g_zo = ring.phase(
-        work, d_left, left_w, normed, d_z, mixed, cot, normed_last, cot_last
+        work, d_left, left_w, normed, d_z, mixed, cot, normed_late, cot_late
     )
 
     def work(held, sums, conv_out, d_ssd, steps, begun, offsets, came):
         sums = ring.hop(sums)
         held = back_pass.next_line(held) if split_pass else ()
-        return held, sums, scan_back(conv_out, d_ssd, steps, begun, offsets, came)
-
-    held, sums, (du_local, dbc_local) = ring.phase(
+        at_end = jnp.exp(left_w) * came + left
+        return held, sums, scan_back(conv_out, d_ssd, steps, begun, offsets, came), at_end
+
+    held, sums, (du_local, dbc_local), at_end = ring.phase(
         work, held, sums, conv_out, d_ssd, steps, begun, offsets, came
     )
 
-    def work(held, sums, g_zo, mixed, out_w, late_w):
+    def work(held, sums, g_zo, mixed, out_w, late_out):
         held = back_pass.further_lines(held) if split_pass else ()
-        branch = project(ring, spots, [mixed], [out_w], [late_w])
+        branch = project(ring, spots, [mixed], [out_w], late_out, 1)
         return held, ring.add(g_zo, sums, 2), branch
 
-    held, sums, branch = ring.phase(work, held, sums, g_zo, mixed, out_w, hop4[1])
+    held, sums, branch = ring.phase(work, held, sums, g_zo, mixed, out_w, late_out)
 
     def work(held, branch):
         later = back_pass.end(held) if split_pass else states_scan(d_left, left_w, -1)
@@ -1321,7 +1367,7 @@
     def work(later, sums, du_local, dbc_local):
         sums = ring.hop(sums)
         d_conv_x, mine, send, d_dt, g_skip, g_heads = finish(
-            conv_out, d_ssd, du_local, ssd, steps, cumulative, left_w, later, came, left,
+            conv_out, d_ssd, du_local, ssd, steps, cumulative, left_w, later, at_end,
             dbc_local, dt_raw,
         )
         after_x = edge([d_conv_x], False)
@@ -1349,30 +1395,30 @@
     own_taps = jnp.pad(own_columns(conv_bcf), ((0, 0), (0, -group % LANES)))
 
     def work(
-        sums, g_zo, d_conv_bc, after_bc, d_conv_x, after_x, d_dt, normed, normed_last, out_far
+        sums, g_zo, d_conv_bc, after_bc, d_conv_x, after_x, d_dt, normed, normed_late, out_far
     ):
-        d_x, g_conv_x, met_x = conv_back(d_conv_x, x_in, after_x, conv_xf, batch, length, rows)
+        d_x, g_conv_x, met_x = conv_back(d_conv_x, x_in, after_x, conv_xf, batch, length, g_rows)
         d_bc, g_conv_bc, met_bc = conv_back(
-            d_conv_bc, bc_own, after_bc, own_taps, batch, length, rows
+            d_conv_bc, bc_own, after_bc, own_taps, batch, length, g_rows
         )
         fill = jnp.zeros((total, spare), BF16)
         d_rest = jnp.concatenate([d_bc[:, :group], d_dt, fill], axis=1)
         last = ring.hop(sums)
         if ring.on:
-            sums = ring.send(*outer_far([normed_last], [d_x, d_rest]))
+            sums = ring.send(*outer_far([normed_late], [d_x, d_rest]))
             g_all = outer(far_spot, order, (normed, [d_x, d_rest]))
             sums = ring.add(g_all, sums, 3)
         else:
             sums = ()
             g_all = jnp.concatenate([dot(normed[0], d, TN) for d in (d_x, d_rest)], axis=1)
         met_dt = jnp.sum(d_dt.astype(F32) * dt_raw, axis=1)
-        met = (met_z + met_x + share * met_bc).reshape(total) + met_dt
+        met = met_z.reshape(total) + (met_x + share * met_bc).reshape(total) + met_dt
         return (
             last, sums, d_x, d_rest, g_conv_x, g_conv_bc, met, g_all, across(ring, out_far),
         )
 
     last, sums, d_x, d_rest, g_conv_x, g_conv_bc, met, g_all, out_far = ring.phase(
-        work, sums, g_zo, d_conv_bc, after_bc, d_conv_x, after_x, d_dt, normed, normed_last, out_far
+        work, sums, g_zo, d_conv_bc, after_bc, d_conv_x, after_x, d_dt, normed, normed_late, out_far
     )
     g_conv_bc = g_conv_bc[:, :group]
     if ring.on:
@@ -1388,17 +1434,17 @@
     def one_swap(array, bit):
         return array + swap(array, "seq", bit) if ring.on else array
 
-    def work(sums, small, d_z, d_x, d_rest, z_w, x_w, rest_w, late_w, met):
+    def work(sums, small, d_z, d_x, d_rest, z_w, x_w, rest_w, late_z, met):
         sums = ring.hop(sums)
         met = met + swap(met, "head", 1) if ring.on else head_sum(met)
         if not ring.on:
             columns = lax.broadcasted_iota(jnp.int32, (1, rest_w.shape[1]), 1)
             rest_w = jnp.where((columns < group) & (here > 0), 0.0, rest_w.astype(F32)).astype(BF16)
-        back = project(ring, spots, [d_z, d_x, d_rest], [z_w, x_w, rest_w], [late_w])
+        back = project(ring, spots, [d_z, d_x, d_rest], [z_w, x_w, rest_w], late_z, 0)
         return sums, back, one_swap(small, 1), met
 
     sums, back_terms, small, met = ring.phase(
-        work, sums, small, d_z, d_x, d_rest, z_w, x_w, rest_w, hop4[0], met
+        work, sums, small, d_z, d_x, d_rest, z_w, x_w, rest_w, late_z, met
     )
 
     def work(sums, g_all, back_terms, met):
@@ -1408,8 +1454,7 @@
 
     sums, far, d_normed, dots = ring.phase(work, sums, g_all, back_terms, met)
 
-    def work(sums, g_all, small, far, out_far, out_own, slab, g_zo, last):
-        far = across(ring, far)
+    def third(sums, g_all, small, out_far, out_own, g_zo, last):
         mixed_out = slab + scatter_sum(ring, out_far, out_own)
         block, column = shaped(per, inner), shaped(per, 1)
         if ring.on:
@@ -1422,24 +1467,16 @@
                 for g in g_zo
             )
             g_out, met_f = g_out.T, jnp.sum(g_z * w_z.astype(F32), axis=1, keepdims=True)
-        return (
-            ring.add(g_all, ring.hop(sums), 1), far, one_swap(small, 2), mixed_out,
-            g_z, g_out, met_f,
-        )
-
-    sums, far, small, mixed_out, g_z, g_out, met_f = ring.phase(
-        work, sums, g_all, small, far, out_far, out_own, slab, g_zo, last
-    )
-
-    def work(sums, g_all, far, d_normed, slab, dots, met_f, small):
+        sums = ring.add(g_all, ring.hop(sums), 1)
+        small = one_swap(one_swap(small, 2), 4) if ring.on else lax.psum(small, "seq")
+        parts, start = [], 0
+        for width in [KERNEL * inner, KERNEL * 2 * N, inner, inner, heads, heads]:
+            parts.append(small[start : start + width])
+            start += width
+        return sums, parts, mixed_out, g_z, g_out, met_f
+
+    def fourth(sums, g_all, met_f, sum_bc):
         last = ring.hop(sums)
-        small = one_swap(small, 4)
-        d_normed = scatter_sum(ring, far, d_normed)
-        grad_tokens = (
-            cot_rows
-            + (scale[:, None] * own_gain) * d_normed
-            - slab * (scale * scale * scale * dots / model)[:, None]
-        )
         shapes = [shaped(per, inner), shaped(per, group), shaped(per, heads), shaped(per, 1)]
         if ring.on:
             g_x, g_bc, g_dt, met_f = totals(
@@ -1453,21 +1490,28 @@
             columns = lax.broadcasted_iota(jnp.int32, (1, g.shape[1]), 1)
             once = jnp.where((columns >= inner) & (columns < edge_at), share, 1.0)
             met_f = met_f + jnp.sum(g * all_in.astype(F32) * once, axis=1, keepdims=True)
-            small = lax.psum(small, "seq")
-        maps = small[KERNEL * inner : KERNEL * (inner + 2 * N)]
-        both = head_sum(jnp.concatenate([met_f[:, 0], maps if ring.on else maps * (1.0 / lax.axis_size("head"))]))
+            sum_bc = sum_bc * (1.0 / lax.axis_size("head"))
+        both = head_sum(jnp.concatenate([met_f[:, 0], sum_bc]))
         g_gain = both[:per] / norm_gain.astype(F32)
-        return g_x, g_bc, g_dt, grad_tokens, g_gain, small, both[per:]
-
-    g_x, g_bc, g_dt, grad_tokens, g_gain, small, sum_bc = ring.phase(
-        work, sums, g_all, far, d_normed, slab, dots, met_f, small
-    )
-    cuts = [KERNEL * inner, KERNEL * 2 * N, inner, inner, heads, heads]
-    parts, start = [], 0
-    for width in cuts:
-        parts.append(small[start : start + width])
-        start += width
+        return g_x, g_bc, g_dt, g_gain, both[per:]
+
+    def work(sums, g_all, small, far, d_normed, dots, out_far, out_own, g_zo, last):
+        far = across(ring, far)
+        sums, parts, *given = third(sums, g_all, small, out_far, out_own, g_zo, last)
+        ends = fourth(sums, g_all, given[-1], parts[1])
+        d_normed = scatter_sum(ring, far, d_normed)
+        grad_tokens = (
+            cot_rows
+            + (scale[:, None] * own_gain) * d_normed
+            - slab * (scale * scale * scale * dots / model)[:, None]
+        )
+        return parts, given, ends, grad_tokens
+
+    parts, (mixed_out, g_z, g_out, _), ends, grad_tokens = ring.phase(
+        work, sums, g_all, small, far, d_normed, dots, out_far, out_own, g_zo, last
+    )
     sum_x, _, sum_gate, sum_skip, sum_bias, sum_rate = parts
+    g_x, g_bc, g_dt, g_gain, sum_bc = ends
 
     return (
         mixed_out.reshape(batch, length, own_width),

time: 506 us -> 483 us (0.955)
  waiting for transfers between devices: 130 us -> 104 us
    ppermute x4, waiting for transfers between devices: 32.3 us -> 9.95 us  [shift_flat(): lax.ppermute(array, 'seq', [(i, i + by) for i in range(size) if 0 <= i +...]
    pallas_call x2 -> x3, Pallas kernels: 29.3 us -> 36.8 us  [with_spots(): pl.pallas_call(kernel, grid_spec=pltpu.PrefetchScalarGridSpec(num_scalar_...]
    ppermute x29, starting transfers between devices: 25.7 us -> 19.2 us  [swap(): return lax.ppermute(array, axis, [(i, i ^ bit) for i in range(size)])]
  transfers between devices with their start and end apart: 70 -> 70, of which waited for: 26 -> 26; matrix products, arithmetic and copies ran while one was open for 7% -> 8% of each run, Pallas kernels for 34% -> 38%
where the time goes in v4:
time: 483 us; the launch traced here: 474 us
  Pallas kernels  207 us (43%)
  waiting for transfers between devices  104 us (22%)
  starting transfers between devices  79.1 us (16%)
  other arithmetic  30.4 us (6%)
  local copies, waits for them, and re-layouts  28.5 us (6%)
  blocking collectives  22 us (5%)
    ppermute x29, waiting for transfers between devices, swap(): return lax.ppermute(array, axis, [(i, i ^ bit) for i in range(size)])  50.7 us
    ppermute x32, starting transfers between devices, shift(): lax.ppermute(array, 'seq', [(order[i], order[(i + by) % size]) for i in r...  37.9 us
    ppermute x32, waiting for transfers between devices, shift(): lax.ppermute(array, 'seq', [(order[i], order[(i + by) % size]) for i in r...  37.2 us
    pallas_call x3, Pallas kernels, with_spots(): pl.pallas_call(kernel, grid_spec=pltpu.PrefetchScalarGridSpec(num_scalar_...  36.8 us
    pallas_call x2, Pallas kernels, outer(): pl.pallas_call(functools.partial(outer_kernel, [len(grads) for _, grads i...  25.3 us
    pallas_call x2, Pallas kernels, project(): pl.pallas_call(functools.partial(project_kernel, len(acts), len(late)), g...  25.3 us
    psum x3, blocking collectives, head_sum(): return lax.psum(array, 'head')  22 us
    ppermute x29, starting transfers between devices, swap(): return lax.ppermute(array, axis, [(i, i ^ bit) for i in range(size)])  19.2 us
  transfers between devices with their start and end apart: 70, of which 26 were waited for; matrix products, arithmetic and copies ran while one was open for 8% of the time, Pallas kernels for 38%

profile of v4, /device:TPU:0, one launch (start us, length us, event | category | flops | bytes accessed | tf_op | source)
XLA Modules:
  0.0 474.0 jit_solution(8326148698847463926)
XLA Ops:
  2.9 24.2 %conditional.20 = (bf16[256,1152]{1,0:T(8,128)(2,1)}, bf16[256,1152]{1,0:T(8,128)(2,1)}, f32[512]{0:T(512)}, f32[1024]{0:T(1024)}, bf16[1024,512]{1,0:T(8,128)(2,1)S(1)}) conditional(s32[]{:T(128)} %convert_element_type.106, () %tuple.195, (bf16[256,1152]{1,0:T(8,128)(2,1)S(1)}, s32[]{:T(128)}, bf16[256]{0:T(256)(128)(2,1)}, ...), branch_computations={%region_0.1_spmd, %region_1.4_spmd} | conditional | flops 2624769 | bytes 10006226 | solution.py:127
  13.3 9.6 %psum.18 = f32[1024]{0:T(1024)S(1)} all-reduce(f32[1024]{0:T(1024)S(1)} %multiply_reduce_fusion), channel_id=1, replica_groups=mesh['seq'=8,'head'=4] {'head'}, use_global_device_ids=true, to_apply=%region_3.3 | all-reduce | flops 1024 | bytes 8192 | tf_op jit(solution)/shard_map/cond/branch_1_fun/psum | solution.py:136
  30.2 29.0 %conditional.21 = (bf16[256,1152]{1,0:T(8,128)(2,1)}, bf16[256,1152]{1,0:T(8,128)(2,1)}, bf16[256,1152]{1,0:T(8,128)(2,1)}, bf16[256,1152]{1,0:T(8,128)(2,1)}, b...) conditional(s32[]{:T(128)} %convert_element_type.106, () %tuple.194, ...), branch_computations={%region_4.5_spmd, %region_5.6_spmd} | conditional | flops 2621440 | bytes 22020380 | solution.py:127
  32.2 12.8 %collective-permute-done.25 = bf16[256,1152]{1,0:T(8,128)(2,1)} collective-permute-done((bf16[256,1152]{1,0:T(8,128)(2,1)}, bf16[256,1152]{1,0:T(8,128)(2,1)}, u32[]{:S(2)}, u32[]{:S(2)}) %collective-permute-start.25) | collective-permute-done | bytes 589856 | tf_op jit(solution)/shard_map/cond/branch_1_fun/ppermute | solution.py:65
  52.1 6.8 %collective-permute-done.27 = bf16[256,1152]{1,0:T(8,128)(2,1)} collective-permute-done((bf16[256,1152]{1,0:T(8,128)(2,1)}, bf16[256,1152]{1,0:T(8,128)(2,1)}, u32[]{:S(2)}, u32[]{:S(2)}) %collective-permute-start.27) | collective-permute-done | bytes 589856 | tf_op jit(solution)/shard_map/cond/branch_1_fun/ppermute | solution.py:65
  59.2 11.7 %conditional.22 = (bf16[128,1152]{1,0:T(8,128)(2,1)}, bf16[128,1152]{1,0:T(8,128)(2,1)}, bf16[1024,512]{1,0:T(8,128)(2,1)}) conditional(s32[]{:T(128)} %convert_element_type.106, () %tuple.198, (bf16[256,1152]{1,0:T(8,128)(2,1)}, bf16[256,1152]{1,0:T(8,128)(2,1)}, bf16[1024,512]{1,0:T(8,128)(2,1)S(1)}) %tuple.199), branch_computations={%region_6.7_spmd, %region_7.8_spmd} | conditional | bytes 7733392 | solution.py:127
  63.6 6.2 %collective-permute-done = bf16[128,1152]{1,0:T(8,128)(2,1)} collective-permute-done((bf16[128,1152]{1,0:T(8,128)(2,1)S(1)}, bf16[128,1152]{1,0:T(8,128)(2,1)}, u32[]{:S(2)}, u32[]{:S(2)}) %collective-permute-start) | collective-permute-done | bytes 294944 | tf_op jit(solution)/shard_map/cond/branch_1_fun/ppermute | solution.py:65
  70.9 26.8 %conditional.23 = (bf16[512,1024]{1,0:T(8,128)(2,1)}, bf16[512,1024]{1,0:T(8,128)(2,1)}, bf16[1024,1024]{1,0:T(8,128)(2,1)}, bf16[1024,256]{1,0:T(8,128)(2,1)}, ...) conditional(s32[]{:T(128)} %convert_element_type.106, ...), branch_computations={%region_8.9_spmd, %region_9.12_spmd} | conditional | flops 5767177 | bytes 66409472 | solution.py:127
  75.3 20.2 %conditional = (bf16[1024,1024]{1,0:T(8,128)(2,1)}, bf16[1024,256]{1,0:T(8,128)(2,1)}, bf16[1024,128]{1,0:T(8,128)(2,1)}, f32[1024,16]{1,0:T(8,128)}, bf16[2048,...) conditional(s32[]{:T(128)} %convert_element_type.48, () %tuple.114, (s32[8]{0:T(128)S(1)}, ...), branch_computations={%region_10.10_spmd, %region_11.11_spmd} | conditional | flops 5767172 | bytes 55923400 | solution.py:127
  75.3 11.3 %branch_1_fun.32 = (bf16[1024,1024]{1,0:T(8,128)(2,1)}, f32[1024,128]{1,0:T(8,128)S(1)}, bf16[2048,1024]{1,0:T(8,128)(2,1)}, bf16[2048,128]{1,0:T(8,128)(2,1)}) custom-call(s32[8]{0:T(128)S(1)} %get-tuple-element.502.spot_ref, bf16[1024,512]{1,0:T(8,128)(2,1)} %get-tuple-element.503.refs_0_, bf16[1024,512]{1,0:T(8,128)(2,1)} %get-tuple-element.504.refs_1_, ...), custom_call_target="tpu_custom_call" | custom-call | bytes 49500000 | tf_op jit(solution)/shard_map/cond/branch_1_fun/cond/branch_1_fun/pallas_call | solution.py:740
  87.9 4.5 collective-permute-done.47
  97.8 6.6 %conditional.24 = (f32[2,8,1280]{2,1,0:T(8,128)S(1)}) conditional(s32[]{:T(128)} %convert_element_type.106, () %tuple.201, (bf16[1024,1024]{1,0:T(8,128)(2,1)}, bf16[1024,256]{1,0:T(8,128)(2,1)}) %tuple.202), branch_computations={%region_12.13_spmd, %region_13.14_spmd} | conditional | flops 51200 | bytes 220208 | solution.py:127
  104.4 34.1 %conditional.25 = (bf16[512,1024]{1,0:T(8,128)(2,1)}, bf16[512,1024]{1,0:T(8,128)(2,1)}, f32[1024,1280]{1,0:T(8,128)}, f32[1024,1024]{1,0:T(8,128)}, f32[1024,16...) conditional(s32[]{:T(128)} %convert_element_type.106, ...), branch_computations={%region_14.15_spmd, %region_15.16_spmd} | conditional | bytes 65807200 | solution.py:127
  107.9 16.2 %branch_1_fun.33 = (f32[1024,1280]{1,0:T(8,128)}, f32[1024,1024]{1,0:T(8,128)}, f32[1024,16]{1,0:T(8,128)}, f32[1024,16]{1,0:T(8,128)S(1)}, f32[8,128,1024]{2,1,...) custom-call(bf16[1024,1024]{1,0:T(8,128)(2,1)} %get-tuple-element.547.x_ref, ...), custom_call_target="tpu_custom_call" | custom-call | bytes 47850000 | tf_op jit(solution)/shard_map/cond/branch_1_fun/pallas_call | solution.py:1032
  127.0 10.3 %collective-permute-done.5.got_ref = bf16[144,1024]{1,0:T(8,128)(2,1)S(1)} collective-permute-done((bf16[144,1024]{1,0:T(8,128)(2,1)S(1)}, bf16[144,1024]{1,0:T(8,128)(2,1)S(1)}, u32[]{:S(2)}, u32[]{:S(2)}) %collective-permute-start.5) | collective-permute-done | bytes 294944 | tf_op jit(solution)/shard_map/cond/branch_1_fun/ppermute | solution.py:132
  138.6 31.3 %conditional.26 = (bf16[512,1024]{1,0:T(8,128)(2,1)}, bf16[512,1024]{1,0:T(8,128)(2,1)}, f32[128,1024]{1,0:T(8,128)}, f32[1,1024]{1,0:T(1,128)S(1)}, f32[128,102...) conditional(s32[]{:T(128)} %convert_element_type.106, ...), branch_computations={%region_16.17_spmd, %region_17.20_spmd} | conditional | flops 655368 | bytes 72962304 | solution.py:127
  147.7 18.4 %branch_1_fun.37 = (f32[1024,1024]{1,0:T(8,128)}, f32[1024,1024]{1,0:T(8,128)}, bf16[2048,1024]{1,0:T(8,128)(2,1)}, bf16[2048,1024]{1,0:T(8,128)(2,1)}, bf16[102...) custom-call(s32[8]{0:T(128)S(1)} %get-tuple-element.585.spot_ref, bf16[1024,512]{1,0:T(8,128)(2,1)} %get-tuple-element.586.refs_0_, ...), custom_call_target="tpu_custom_call" | custom-call | bytes 49500000 | tf_op jit(solution)/shard_map/cond/branch_1_fun/pallas_call | solution.py:740
  169.8 29.3 %conditional.27 = (bf16[256,1024]{1,0:T(8,128)(2,1)}, bf16[256,1024]{1,0:T(8,128)(2,1)}, f32[2,128,1024]{2,1,0:T(8,128)S(1)}, f32[1024,1024]{1,0:T(8,128)S(1)}, f32[1024,1024]{1,0:T(8,128)S(1)}) conditional(s32[]{:T(128)} %convert_element_type.106, () %tuple.190, (bf16[512,1024]{1,0:T(8,128)(2,1)}, bf16[512,1024]{1,0:T(8,128)(2,1)}, ...), branch_computations={%region_20.21_spmd, %region_21.22_spmd} | conditional | bytes 59985988 | solution.py:127
  169.8 7.5 %collective-permute-start.11 = (bf16[128,1024]{1,0:T(8,128)(2,1)}, bf16[128,1024]{1,0:T(8,128)(2,1)S(1)}, u32[]{:S(2)}, u32[]{:S(2)}) collective-permute-start(bf16[128,1024]{1,0:T(8,128)(2,1)} %get-tuple-element.610), channel_id=1, source_target_pairs={{0,16},{4,20},{8,24},{12,28},{1,17},{5,21},{9,25},{13,29},{2,18},{... | collective-permute-start | bytes 786440 | tf_op jit(solution)/shard_map/cond/branch_1_fun/ppermute | solution.py:205
  185.9 7.2 %branch_1_fun.40 = (f32[1024,1024]{1,0:T(8,128)S(1)}, f32[1024,1024]{1,0:T(8,128)S(1)}) custom-call(s32[8]{0:T(128)S(1)} %get-tuple-element.613.spot_ref, f32[1024,1024]{1,0:T(8,128)} %get-tuple-element.614.z_ref, f32[1024,1024]{1,0:T(8,128)} %get-tuple-element.615.dm_ref, bf16[1024,768]{1,0:T(8,128)(2,1)S(1)} %get-tuple-element.616.na_ref, ...), custom_call_target="tpu_custom_call" | custom-call | bytes 49500000 | tf_op jit(solution)/shard_map/cond/branch_1_fun/pallas_call | solution.py:740
  193.1 5.8 %collective-permute-done.12.got_ref = bf16[128,1024]{1,0:T(8,128)(2,1)S(1)} collective-permute-done((bf16[128,1024]{1,0:T(8,128)(2,1)S(1)}, bf16[128,1024]{1,0:T(8,128)(2,1)S(1)}, u32[]{:S(2)}, u32[]{:S(2)}) %collective-permute-start.12) | collective-permute-done | bytes 262176 | tf_op jit(solution)/shard_map/cond/branch_1_fun/ppermute | solution.py:132
  199.1 9.5 %shard_map.246 = (f32[1024,1024]{1,0:T(8,128)}, f32[4,2,256]{2,1,0:T(2,128)S(1)}) custom-call(f32[1024,1024]{1,0:T(8,128)} %get-tuple-element.1006.y_ref, f32[1024,1280]{1,0:T(8,128)} %get-tuple-element.991.vc_ref, f32[2,128,1024]{2,1,0:T(8,128)S(1)} %get-tuple-element.1007.s_ref, f32[1024,16]{1,0:T(8,128)S(1)} %get-tuple-element.1008.wc_ref, ...), custom_call_target="tpu_custom_call" | custom-call | bytes 23100000 | tf_op jit(solution)/shard_map/pallas_call | solution.py:1088
  208.7 5.8 %psum.21 = f32[4,2,256]{2,1,0:T(2,128)S(1)} all-reduce(f32[4,2,256]{2,1,0:T(2,128)S(1)} %get-tuple-element.1013), channel_id=1, replica_groups=mesh['seq'=8,'head'=4] {'head'}, use_global_device_ids=true, to_apply=%region_22.23 | all-reduce | flops 2048 | bytes 16384 | tf_op jit(solution)/shard_map/psum | solution.py:136
  214.5 11.2 %shard_map.247 = (bf16[1024,1024]{1,0:T(8,128)(2,1)S(1)}, f32[1024,1024]{1,0:T(8,128)}, f32[2,128,1024]{2,1,0:T(8,128)S(1)}, f32[4,1,256]{2,1,0:T(1,128)}, f32[1...) custom-call(f32[1024,1024]{1,0:T(8,128)} %copy-done.3, f32[1024,1024]{1,0:T(8,128)} %get-tuple-element.1012.ssd_ref, ...), custom_call_target="tpu_custom_call" | custom-call | bytes 29700000 | tf_op jit(solution)/shard_map/pallas_call | solution.py:1102
  227.7 25.9 %conditional.28 = (f32[128,1024]{1,0:T(8,128)}, f32[1,1024]{1,0:T(1,128)S(1)}, f32[128,1024]{1,0:T(8,128)S(1)}, f32[1,1024]{1,0:T(1,128)S(1)}, bf16[144,1024]{1,...) conditional(s32[]{:T(128)} %convert_element_type.106, ...), branch_computations={%region_23.24_spmd, %region_24.25_spmd} | conditional | bytes 58174136 | solution.py:127
  233.3 14.2 %branch_1_fun.43.a_ref.b_ref = bf16[4096,1024]{1,0:T(8,128)(2,1)} custom-call(s32[1]{0:T(128)} %get-tuple-element.632.far_ref, s32[8]{0:T(128)S(1)} %get-tuple-element.633.block_ref, bf16[1024,512]{1,0:T(8,128)(2,1)} %get-tuple-element.634.refs_0_, bf16[1024,512]{1,0:T(8,128)(2,1)} %get-tuple-element.635.refs_1_, ...), custom_call_target="tpu_custom_call" | custom-call | bytes 52800000 | tf_op jit(solution)/shard_map/cond/branch_1_fun/pallas_call | solution.py:800
  253.7 30.8 %conditional.29 = (f32[128,1024]{1,0:T(8,128)}, f32[1,1024]{1,0:T(1,128)S(1)}, f32[128,1024]{1,0:T(8,128)S(1)}, f32[1,1024]{1,0:T(1,128)S(1)}, bf16[128,1024]{1,...) conditional(s32[]{:T(128)} %convert_element_type.106, ...), branch_computations={%region_25.26_spmd, %region_26.27_spmd} | conditional | flops 524288 | bytes 76333096 | solution.py:127
  257.0 19.2 %branch_1_fun.47 = (f32[1024,1024]{1,0:T(8,128)}, f32[1024,256]{1,0:T(8,128)}) custom-call(f32[1024,1280]{1,0:T(8,128)} %get-tuple-element.662.v_ref, f32[1024,1024]{1,0:T(8,128)} %get-tuple-element.663.dy_ref, f32[1024,16]{1,0:T(8,128)} %get-tuple-element.664.st_ref, f32[1,16]{1,0:T(1,128)S(1)} %get-tuple-element.665.rate_ref, ...), custom_call_target="tpu_custom_call" | custom-call | bytes 59400000 | tf_op jit(solution)/shard_map/cond/branch_1_fun/pallas_call | solution.py:1123
  278.4 5.9 %collective-permute-done.34.got_ref = bf16[144,1024]{1,0:T(8,128)(2,1)S(1)} collective-permute-done((bf16[144,1024]{1,0:T(8,128)(2,1)S(1)}, bf16[144,1024]{1,0:T(8,128)(2,1)S(1)}, u32[]{:S(2)}, u32[]{:S(2)}) %collective-permute-start.34) | collective-permute-done | bytes 294944 | tf_op jit(solution)/shard_map/cond/branch_1_fun/ppermute | solution.py:205
  285.4 16.7 %conditional.30 = (f32[128,1024]{1,0:T(8,128)S(1)}, bf16[128,1024]{1,0:T(8,128)(2,1)S(1)}, bf16[512,1024]{1,0:T(8,128)(2,1)}, bf16[512,1024]{1,0:T(8,128)(2,1)}, bf16[1024,2048]{1,0:T(8,128)(2,1)S(1)}) conditional(s32[]{:T(128)} %convert_element_type.106, () %tuple.187, (bf16[128,1024]{1,0:T(8,128)(2,1)S(1)}, s32[1]{0:T(128)}, s32[1]{0:T(128)}, ...), branch_computations={%region_27.28_spmd, %region_28.29_spmd} | conditional | bytes 32537292 | solution.py:127
  290.2 9.4 %branch_1_fun.50 = bf16[1024,2048]{1,0:T(8,128)(2,1)S(1)} custom-call(s32[8]{0:T(128)S(1)} %get-tuple-element.687.spot_ref, bf16[1024,1024]{1,0:T(8,128)(2,1)S(1)} %copy-done.10, bf16[2048,1024]{1,0:T(8,128)(2,1)} %get-tuple-element.689.refs_1_, bf16[256,1024]{1,0:T(8,128)(2,1)} %get-tuple-element.690.refs_2_, bf16[512,1024]{1,0:T(8,128)(2,1)} %get-tuple-element.691.refs_3_, ...), custom_call_target="tpu_custom_call" | custom-call | bytes 23100000 | tf_op jit(solution)/shard_map/cond/branch_1_fun/pallas_call | solution.py:868
  302.1 10.8 %conditional.31 = (f32[2,128,1024]{2,1,0:T(8,128)}, bf16[1024,512]{1,0:T(8,128)(2,1)S(1)}, f32[1024,512]{1,0:T(8,128)S(1)}) conditional(s32[]{:T(128)} %convert_element_type.106, () %tuple.209, (bf16[128,1024]{1,0:T(8,128)(2,1)S(1)}, s32[1]{0:T(128)}, s32[1]{0:T(128)}, f32[128,1024]{1,0:T(8,128)S(1)}, bf16[1024,2048]{1,0:T(8,128)(2,1)S(1)}) %tuple.210), branch_computations={%region_29.30_spmd, %region_30.31_spmd} | conditional | flops 3670016 | bytes 20971664 | solution.py:127
  302.9 8.2 %collective-permute-done.51.got_ref = bf16[128,1024]{1,0:T(8,128)(2,1)S(1)} collective-permute-done((bf16[128,1024]{1,0:T(8,128)(2,1)S(1)}, bf16[128,1024]{1,0:T(8,128)(2,1)S(1)}, u32[]{:S(2)}, u32[]{:S(2)}) %collective-permute-start.51) | collective-permute-done | bytes 262176 | tf_op jit(solution)/shard_map/cond/branch_1_fun/ppermute | solution.py:132
  314.5 26.9 %conditional.32 = (bf16[512,1024]{1,0:T(8,128)(2,1)}, bf16[512,1024]{1,0:T(8,128)(2,1)}, bf16[1024,1024]{1,0:T(8,128)(2,1)}, f32[2,8,1024]{2,1,0:T(8,128)S(1)}, ...) conditional(s32[]{:T(128)} %convert_element_type.106, () %tuple.186, ...), branch_computations={%region_31.32_spmd, %region_32.33_spmd} | conditional | flops 203780 | bytes 61761896 | solution.py:127
  317.8 16.2 %branch_1_fun.52 = (bf16[1024,1024]{1,0:T(8,128)(2,1)}, f32[1024,128]{1,0:T(8,128)S(1)}, f32[1024,128]{1,0:T(8,128)S(1)}, bf16[1024,16]{1,0:T(8,128)(2,1)}, f32[1,1024]{1,0:T(1,128)S(1)}, /*index=5*/f32[2,16]{1,0:T(2,128)S(1)}) custom-call(f32[1024,1280]{1,0:T(8,128)} %get-tuple-element.700.v_ref, f32[1024,1024]{1,0:T(8,128)} %get-tuple-element.701.dy_ref, ...), custom_call_target="tpu_custom_call" | custom-call | bytes 49500000 | tf_op jit(solution)/shard_map/cond/branch_1_fun/pallas_call | solution.py:1146
  341.9 17.8 %conditional.33 = (bf16[1024,128]{1,0:T(8,128)(2,1)}, f32[2,8,128]{2,1,0:T(8,128)S(1)}, bf16[512,1024]{1,0:T(8,128)(2,1)}, bf16[512,1024]{1,0:T(8,128)(2,1)}) conditional(s32[]{:T(128)} %convert_element_type.106, () %tuple.185, (f32[1024,128]{1,0:T(8,128)}, f32[1024,64]{1,0:T(8,128)}, bf16[4096,1024]{1,0:T(8,128)(2,1)}, ...), branch_computations={%region_33.34_spmd, %region_34.35_spmd} | conditional | flops 329728 | bytes 3951218 | solution.py:127
  344.2 7.1 %collective-permute-done.54 = f32[512,128]{1,0:T(8,128)S(1)} collective-permute-done((f32[512,128]{1,0:T(8,128)S(1)}, f32[512,128]{1,0:T(8,128)S(1)}, u32[]{:S(2)}, u32[]{:S(2)}) %collective-permute-start.54) | collective-permute-done | bytes 262176 | tf_op jit(solution)/shard_map/cond/branch_1_fun/ppermute | solution.py:132
  359.7 35.5 %conditional.34 = (bf16[512,1024]{1,0:T(8,128)(2,1)}, bf16[512,1024]{1,0:T(8,128)(2,1)}, bf16[256,1152]{1,0:T(8,128)(2,1)}, bf16[256,1152]{1,0:T(8,128)(2,1)}, b...) conditional(s32[]{:T(128)} %convert_element_type.106, ...), branch_computations={%region_35.36_spmd, %region_36.38_spmd} | conditional | flops 837632 | bytes 81360792 | solution.py:127
  366.4 9.0 %branch_1_fun.54 = (bf16[1024,1024]{1,0:T(8,128)(2,1)}, f32[4,1024]{1,0:T(4,128)S(1)}, f32[4,1,256]{2,1,0:T(1,128)S(1)}) custom-call(bf16[1024,1024]{1,0:T(8,128)(2,1)} %get-tuple-element.736.d_ref, bf16[1024,1024]{1,0:T(8,128)(2,1)} %get-tuple-element.737.in_ref, f32[2,8,1024]{2,1,0:T(8,128)S(1)} %get-tuple-element.738.halo_ref, ...), custom_call_target="tpu_custom_call" | custom-call | bytes 26400000 | tf_op jit(solution)/shard_map/cond/branch_1_fun/pallas_call | solution.py:949
  381.9 11.1 %branch_1_fun.56.a_ref.b_ref = bf16[2048,1152]{1,0:T(8,128)(2,1)} custom-call(s32[1]{0:T(128)} %get-tuple-element.730.far_ref, s32[8]{0:T(128)S(1)} %get-tuple-element.731.block_ref, bf16[1024,512]{1,0:T(8,128)(2,1)} %get-tuple-element.732.refs_0_, bf16[1024,512]{1,0:T(8,128)(2,1)} %get-tuple-element.733.refs_1_, bf16[1024,512]{1,0:T(8,128)(2,1)S(1)} %copy-done.16, ...), custom_call_target="tpu_custom_call" | custom-call | bytes 29700000 | tf_op jit(solution)/shard_map/cond/branch_1_fun/pallas_call | solution.py:800
  395.5 20.0 %conditional.35 = (bf16[256,1152]{1,0:T(8,128)(2,1)}, bf16[256,1152]{1,0:T(8,128)(2,1)}, bf16[1024,2048]{1,0:T(8,128)(2,1)S(1)}, f32[7200]{0:T(1024)S(1)}, f32[1024]{0:T(1024)S(1)}) conditional(s32[]{:T(128)} %convert_element_type.106, () %tuple.183, (bf16[256,1152]{1,0:T(8,128)(2,1)}, bf16[256,1152]{1,0:T(8,128)(2,1)}, s32[8]{0:T(128)S(1)}, ...), branch_computations={%region_38.39_spmd, %region_39.40_spmd} | conditional | flops 8224 | bytes 54036564 | solution.py:127
  399.6 15.9 %branch_1_fun.59 = bf16[1024,2048]{1,0:T(8,128)(2,1)S(1)} custom-call(s32[8]{0:T(128)S(1)} %get-tuple-element.762.spot_ref, bf16[1024,1024]{1,0:T(8,128)(2,1)} %get-tuple-element.763.refs_0_, bf16[1024,1024]{1,0:T(8,128)(2,1)} %get-tuple-element.764.refs_1_, bf16[1024,128]{1,0:T(8,128)(2,1)S(1)} %get-tuple-element.765.refs_2_, ...), custom_call_target="tpu_custom_call" | custom-call | bytes 49087500 | tf_op jit(solution)/shard_map/cond/branch_1_fun/pallas_call | solution.py:868
  415.6 6.8 %conditional.36 = (bf16[256,1152]{1,0:T(8,128)(2,1)S(1)}, bf16[256,1152]{1,0:T(8,128)(2,1)}, bf16[1024,512]{1,0:T(8,128)(2,1)}, f32[1024,512]{1,0:T(8,128)S(1)}, f32[1024]{0:T(1024)S(1)}) conditional(s32[]{:T(128)} %convert_element_type.106, () %tuple.215, (bf16[2048,1152]{1,0:T(8,128)(2,1)}, bf16[256,1152]{1,0:T(8,128)(2,1)}, ...), branch_computations={%region_40.41_spmd, %region_41.42_spmd} | conditional | flops 3672064 | bytes 19955872 | solution.py:127
  422.4 50.1 %conditional.37 = (f32[1024]{0:T(1024)S(1)}, f32[16]{0:T(128)}, f32[16]{0:T(128)}, f32[256,1024]{1,0:T(8,128)}, f32[1024,256]{1,0:T(8,128)}, /*index=5*/f32[256,...) conditional(s32[]{:T(128)} %convert_element_type.106, ...), branch_computations={%region_42.43_spmd, %region_43.46_spmd} | conditional | flops 5658676 | bytes 72695064 | solution.py:127
  435.1 8.6 %collective-permute-done.60 = f32[7200]{0:T(1024)S(1)} collective-permute-done((f32[7200]{0:T(1024)S(1)}, f32[7200]{0:T(1024)S(1)}, u32[]{:S(2)}, u32[]{:S(2)}) %collective-permute-start.60) | collective-permute-done | bytes 28832 | tf_op jit(solution)/shard_map/cond/branch_1_fun/ppermute | solution.py:132
  449.4 4.4 multiply_subtract_fusion
  453.9 5.8 %collective-permute-done.63.right_ref = bf16[256,1152]{1,0:T(8,128)(2,1)S(1)} collective-permute-done((bf16[256,1152]{1,0:T(8,128)(2,1)S(1)}, bf16[256,1152]{1,0:T(8,128)(2,1)S(1)}, u32[]{:S(2)}, u32[]{:S(2)}) %collective-permute-start.63) | collective-permute-done | bytes 589856 | tf_op jit(solution)/shard_map/cond/branch_1_fun/ppermute | solution.py:65
  464.1 6.7 %psum.19 = f32[1280]{0:T(1024)S(1)} all-reduce(f32[1280]{0:T(1024)S(1)} %pad_maximum_fusion.6), channel_id=1, replica_groups=mesh['seq'=8,'head'=4] {'head'}, use_global_device_ids=true, to_apply=%region_44.44 | all-reduce | flops 1280 | bytes 10240 | tf_op jit(solution)/shard_map/cond/branch_1_fun/psum | solution.py:136
  (343 shorter events, 189.5 us)
Async XLA Ops:
  3.8 19.7 %collective-permute-start.23 = (f32[256]{0:T(256)S(1)}, f32[256]{0:T(256)S(1)}, u32[]{:S(2)}, u32[]{:S(2)}) collective-permute-start(f32[256]{0:T(256)S(1)} %convert_element_type.32), channel_id=1, source_target_pairs={{0,0},{8,1},{16,2},{24,3},{4,4},{12,5},{20,6},{28,7},{1,8},{9,9},{... | collective-permute-start | bytes 3080 | tf_op jit(solution)/shard_map/cond/branch_1_fun/ppermute | solution.py:156
  4.5 19.0 %collective-permute-start.24 = (f32[256]{0:T(256)S(1)}, f32[256]{0:T(256)S(1)}, u32[]{:S(2)}, u32[]{:S(2)}) collective-permute-start(f32[256]{0:T(256)S(1)} %convert_element_type.32), channel_id=1, source_target_pairs={{4,0},{12,1},{20,2},{28,3},{0,4},{8,5},{16,6},{24,7},{5,8},{13,9},... | collective-permute-start | bytes 3080 | tf_op jit(solution)/shard_map/cond/branch_1_fun/ppermute | solution.py:156
  7.5 18.5 %collective-permute-start.21 = (bf16[256,1152]{1,0:T(8,128)(2,1)S(1)}, bf16[256,1152]{1,0:T(8,128)(2,1)}, u32[]{:S(2)}, u32[]{:S(2)}) collective-permute-start(bf16[256,1152]{1,0:T(8,128)(2,1)S(1)} %get-tuple-element.489), channel_id=1, source_target_pairs={{0,8},{8,16},{16,24},{24,28},{28,20},{20,12},{12,4},{4,0},{1,9},{9... | collective-permute-start | bytes 1769480 | tf_op jit(solution)/shard_map/cond/branch_1_fun/ppermute | solution.py:65
  11.5 15.6 %collective-permute-start.22 = (bf16[256,1152]{1,0:T(8,128)(2,1)S(1)}, bf16[256,1152]{1,0:T(8,128)(2,1)}, u32[]{:S(2)}, u32[]{:S(2)}) collective-permute-start(bf16[256,1152]{1,0:T(8,128)(2,1)S(1)} %get-tuple-element.489), channel_id=1, source_target_pairs={{0,4},{8,0},{16,8},{24,16},{28,24},{20,28},{12,20},{4,12},{1,5},{9... | collective-permute-start | bytes 1769480 | tf_op jit(solution)/shard_map/cond/branch_1_fun/ppermute | solution.py:65
  27.2 32.0 %collective-permute-start.69 = (bf16[1024,512]{1,0:T(8,128)(2,1)S(1)}, bf16[1024,512]{1,0:T(8,128)(2,1)S(1)}, u32[]{:S(2)}, u32[]{:S(2)}) collective-permute-start(bf16[1024,512]{1,0:T(8,128)(2,1)S(1)} %get-tuple-element.968), channel_id=1, source_target_pairs={{0,2},{1,3},{2,0},{3,1},{4,6},{5,7},{6,4},{7,5},{8,10},{9,11},{10,... | collective-permute-start | bytes 3145736 | tf_op jit(solution)/shard_map/ppermute | solution.py:132
  30.2 14.8 %collective-permute-start.25 = (bf16[256,1152]{1,0:T(8,128)(2,1)}, bf16[256,1152]{1,0:T(8,128)(2,1)}, u32[]{:S(2)}, u32[]{:S(2)}) collective-permute-start(bf16[256,1152]{1,0:T(8,128)(2,1)} %get-tuple-element.493), channel_id=1, source_target_pairs={{0,8},{8,16},{16,24},{24,28},{28,20},{20,12},{12,4},{4,0},{1,9},{9... | collective-permute-start | bytes 1769480 | tf_op jit(solution)/shard_map/cond/branch_1_fun/ppermute | solution.py:65
  30.5 14.9 %collective-permute-start.26 = (bf16[256,1152]{1,0:T(8,128)(2,1)}, bf16[256,1152]{1,0:T(8,128)(2,1)}, u32[]{:S(2)}, u32[]{:S(2)}) collective-permute-start(bf16[256,1152]{1,0:T(8,128)(2,1)} %get-tuple-element.494), channel_id=1, source_target_pairs={{0,4},{8,0},{16,8},{24,16},{28,24},{20,28},{12,20},{4,12},{1,5},{9... | collective-permute-start | bytes 1769480 | tf_op jit(solution)/shard_map/cond/branch_1_fun/ppermute | solution.py:65
  32.2 19.9 %collective-permute-start.29 = (bf16[1024,512]{1,0:T(8,128)(2,1)S(1)}, bf16[1024,512]{1,0:T(8,128)(2,1)}, u32[]{:S(2)}, u32[]{:S(2)}) collective-permute-start(bf16[1024,512]{1,0:T(8,128)(2,1)S(1)} %get-tuple-element.495), channel_id=1, source_target_pairs={{0,1},{1,0},{2,3},{3,2},{4,5},{5,4},{6,7},{7,6},{8,9},{9,8},{10,11... | collective-permute-start | bytes 3145736 | tf_op jit(solution)/shard_map/cond/branch_1_fun/ppermute | solution.py:132
  45.0 13.9 %collective-permute-start.27 = (bf16[256,1152]{1,0:T(8,128)(2,1)}, bf16[256,1152]{1,0:T(8,128)(2,1)}, u32[]{:S(2)}, u32[]{:S(2)}) collective-permute-start(bf16[256,1152]{1,0:T(8,128)(2,1)} %collective-permute-done.25), channel_id=1, source_target_pairs={{0,8},{8,16},{16,24},{24,28},{28,20},{20,12},{12,4},{4,0},{1,9},{9... | collective-permute-start | bytes 1769480 | tf_op jit(solution)/shard_map/cond/branch_1_fun/ppermute | solution.py:65
  45.5 13.7 %collective-permute-start.28 = (bf16[256,1152]{1,0:T(8,128)(2,1)}, bf16[256,1152]{1,0:T(8,128)(2,1)}, u32[]{:S(2)}, u32[]{:S(2)}) collective-permute-start(bf16[256,1152]{1,0:T(8,128)(2,1)} %collective-permute-done.26), channel_id=1, source_target_pairs={{0,4},{8,0},{16,8},{24,16},{28,24},{20,28},{12,20},{4,12},{1,5},{9... | collective-permute-start | bytes 1769480 | tf_op jit(solution)/shard_map/cond/branch_1_fun/ppermute | solution.py:65
  73.2 24.5 %collective-permute-start.49 = (bf16[512,1024]{1,0:T(8,128)(2,1)}, bf16[512,1024]{1,0:T(8,128)(2,1)}, u32[]{:S(2)}, u32[]{:S(2)}) collective-permute-start(bf16[512,1024]{1,0:T(8,128)(2,1)} %copy.43), channel_id=1, source_target_pairs={{0,8},{8,16},{16,24},{24,28},{28,20},{20,12},{12,4},{4,0},{1,9},{9... | collective-permute-start | bytes 3145736 | tf_op jit(solution)/shard_map/cond/branch_1_fun/ppermute | solution.py:65
  73.5 24.2 %collective-permute-start.50 = (bf16[512,1024]{1,0:T(8,128)(2,1)}, bf16[512,1024]{1,0:T(8,128)(2,1)}, u32[]{:S(2)}, u32[]{:S(2)}) collective-permute-start(bf16[512,1024]{1,0:T(8,128)(2,1)} %copy.43), channel_id=1, source_target_pairs={{0,4},{8,0},{16,8},{24,16},{28,24},{20,28},{12,20},{4,12},{1,5},{9... | collective-permute-start | bytes 3145736 | tf_op jit(solution)/shard_map/cond/branch_1_fun/ppermute | solution.py:65
  104.4 34.1 %collective-permute-start.6 = (bf16[1024,512]{1,0:T(8,128)(2,1)}, bf16[1024,512]{1,0:T(8,128)(2,1)}, u32[]{:S(2)}, u32[]{:S(2)}) collective-permute-start(bf16[1024,512]{1,0:T(8,128)(2,1)} %get-tuple-element.572), channel_id=1, source_target_pairs={{0,1},{1,0},{2,3},{3,2},{4,5},{5,4},{6,7},{7,6},{8,9},{9,8},{10,11... | collective-permute-start | bytes 3145736 | tf_op jit(solution)/shard_map/cond/branch_1_fun/ppermute | solution.py:132
  104.5 34.0 %collective-permute-start.7 = (bf16[1024,512]{1,0:T(8,128)(2,1)}, bf16[1024,512]{1,0:T(8,128)(2,1)}, u32[]{:S(2)}, u32[]{:S(2)}) collective-permute-start(bf16[1024,512]{1,0:T(8,128)(2,1)} %get-tuple-element.572), channel_id=1, source_target_pairs={{0,2},{1,3},{2,0},{3,1},{4,6},{5,7},{6,4},{7,5},{8,10},{9,11},{10,... | collective-permute-start | bytes 3145736 | tf_op jit(solution)/shard_map/cond/branch_1_fun/ppermute | solution.py:132
  105.0 33.5 %collective-permute-start.3 = (bf16[512,1024]{1,0:T(8,128)(2,1)}, bf16[512,1024]{1,0:T(8,128)(2,1)}, u32[]{:S(2)}, u32[]{:S(2)}) collective-permute-start(bf16[512,1024]{1,0:T(8,128)(2,1)} %get-tuple-element.545), channel_id=1, source_target_pairs={{0,8},{8,16},{16,24},{24,28},{28,20},{20,12},{12,4},{4,0},{1,9},{9... | collective-permute-start | bytes 3145736 | tf_op jit(solution)/shard_map/cond/branch_1_fun/ppermute | solution.py:65
  107.9 30.7 %collective-permute-start.4 = (bf16[512,1024]{1,0:T(8,128)(2,1)}, bf16[512,1024]{1,0:T(8,128)(2,1)}, u32[]{:S(2)}, u32[]{:S(2)}) collective-permute-start(bf16[512,1024]{1,0:T(8,128)(2,1)} %get-tuple-element.546), channel_id=1, source_target_pairs={{0,4},{8,0},{16,8},{24,16},{28,24},{20,28},{12,20},{4,12},{1,5},{9... | collective-permute-start | bytes 3145736 | tf_op jit(solution)/shard_map/cond/branch_1_fun/ppermute | solution.py:65
  125.5 11.8 %collective-permute-start.5 = (bf16[144,1024]{1,0:T(8,128)(2,1)S(1)}, bf16[144,1024]{1,0:T(8,128)(2,1)S(1)}, u32[]{:S(2)}, u32[]{:S(2)}) collective-permute-start(bf16[144,1024]{1,0:T(8,128)(2,1)S(1)} %get-tuple-element.566), channel_id=1, source_target_pairs={{0,4},{4,0},{8,12},{12,8},{16,20},{20,16},{24,28},{28,24},{1,5},{5... | collective-permute-start | bytes 884744 | tf_op jit(solution)/shard_map/cond/branch_1_fun/ppermute | solution.py:132
  138.6 31.2 %collective-permute-start.31 = (bf16[512,1024]{1,0:T(8,128)(2,1)}, bf16[512,1024]{1,0:T(8,128)(2,1)}, u32[]{:S(2)}, u32[]{:S(2)}) collective-permute-start(bf16[512,1024]{1,0:T(8,128)(2,1)} %get-tuple-element.573.refs_11_), channel_id=1, source_target_pairs={{0,8},{8,16},{16,24},{24,28},{28,20},{20,12},{12,4},{4,0},{1,9},{9... | collective-permute-start | bytes 3145736 | tf_op jit(solution)/shard_map/cond/branch_1_fun/ppermute | solution.py:65
  138.6 31.2 %collective-permute-start.32 = (bf16[512,1024]{1,0:T(8,128)(2,1)}, bf16[512,1024]{1,0:T(8,128)(2,1)}, u32[]{:S(2)}, u32[]{:S(2)}) collective-permute-start(bf16[512,1024]{1,0:T(8,128)(2,1)} %get-tuple-element.574.refs_12_), channel_id=1, source_target_pairs={{0,4},{8,0},{16,8},{24,16},{28,24},{20,28},{12,20},{4,12},{1,5},{9... | collective-permute-start | bytes 3145736 | tf_op jit(solution)/shard_map/cond/branch_1_fun/ppermute | solution.py:65
  141.0 27.8 %collective-permute-start.33 = (bf16[144,1024]{1,0:T(8,128)(2,1)}, bf16[144,1024]{1,0:T(8,128)(2,1)S(1)}, u32[]{:S(2)}, u32[]{:S(2)}) collective-permute-start(bf16[144,1024]{1,0:T(8,128)(2,1)} %get-tuple-element.580), channel_id=1, source_target_pairs={{0,8},{4,12},{8,16},{12,20},{16,24},{20,28},{1,9},{5,13},{9,17},{1... | collective-permute-start | bytes 884744 | tf_op jit(solution)/shard_map/cond/branch_1_fun/ppermute | solution.py:205
  169.8 14.5 %collective-permute-start.11 = (bf16[128,1024]{1,0:T(8,128)(2,1)}, bf16[128,1024]{1,0:T(8,128)(2,1)S(1)}, u32[]{:S(2)}, u32[]{:S(2)}) collective-permute-start(bf16[128,1024]{1,0:T(8,128)(2,1)} %get-tuple-element.610), channel_id=1, source_target_pairs={{0,16},{4,20},{8,24},{12,28},{1,17},{5,21},{9,25},{13,29},{2,18},{... | collective-permute-start | bytes 786440 | tf_op jit(solution)/shard_map/cond/branch_1_fun/ppermute | solution.py:205
  178.4 20.6 %collective-permute-start.10 = (bf16[256,1024]{1,0:T(8,128)(2,1)S(1)}, bf16[256,1024]{1,0:T(8,128)(2,1)}, u32[]{:S(2)}, u32[]{:S(2)}) collective-permute-start(bf16[256,1024]{1,0:T(8,128)(2,1)S(1)} %slice.144), channel_id=1, source_target_pairs={{0,4},{8,0},{16,8},{24,16},{28,24},{20,28},{12,20},{4,12},{1,5},{9... | collective-permute-start | bytes 1572872 | tf_op jit(solution)/shard_map/cond/branch_1_fun/ppermute | solution.py:65
  179.9 19.2 %collective-permute-start.9 = (bf16[256,1024]{1,0:T(8,128)(2,1)S(1)}, bf16[256,1024]{1,0:T(8,128)(2,1)}, u32[]{:S(2)}, u32[]{:S(2)}) collective-permute-start(bf16[256,1024]{1,0:T(8,128)(2,1)S(1)} %slice.143), channel_id=1, source_target_pairs={{0,8},{8,16},{16,24},{24,28},{28,20},{20,12},{12,4},{4,0},{1,9},{9... | collective-permute-start | bytes 1572872 | tf_op jit(solution)/shard_map/cond/branch_1_fun/ppermute | solution.py:65
  185.6 13.4 %collective-permute-start.12 = (bf16[128,1024]{1,0:T(8,128)(2,1)S(1)}, bf16[128,1024]{1,0:T(8,128)(2,1)S(1)}, u32[]{:S(2)}, u32[]{:S(2)}) collective-permute-start(bf16[128,1024]{1,0:T(8,128)(2,1)S(1)} %get-tuple-element.612), channel_id=1, source_target_pairs={{0,4},{4,0},{8,12},{12,8},{16,20},{20,16},{24,28},{28,24},{1,5},{5... | collective-permute-start | bytes 786440 | tf_op jit(solution)/shard_map/cond/branch_1_fun/ppermute | solution.py:132
  230.1 21.0 %collective-permute-start.14 = (bf16[256,1024]{1,0:T(8,128)(2,1)S(1)}, bf16[256,1024]{1,0:T(8,128)(2,1)S(1)}, u32[]{:S(2)}, u32[]{:S(2)}) collective-permute-start(bf16[256,1024]{1,0:T(8,128)(2,1)S(1)} %get-tuple-element.646), channel_id=1, source_target_pairs={{0,8},{8,16},{16,24},{24,28},{28,20},{20,12},{12,4},{4,0},{1,9},{9... | collective-permute-start | bytes 1572872 | tf_op jit(solution)/shard_map/cond/branch_1_fun/ppermute | solution.py:65
  230.8 20.3 %collective-permute-start.15 = (bf16[256,1024]{1,0:T(8,128)(2,1)S(1)}, bf16[256,1024]{1,0:T(8,128)(2,1)S(1)}, u32[]{:S(2)}, u32[]{:S(2)}) collective-permute-start(bf16[256,1024]{1,0:T(8,128)(2,1)S(1)} %get-tuple-element.647), channel_id=1, source_target_pairs={{0,4},{8,0},{16,8},{24,16},{28,24},{20,28},{12,20},{4,12},{1,5},{9... | collective-permute-start | bytes 1572872 | tf_op jit(solution)/shard_map/cond/branch_1_fun/ppermute | solution.py:65
  233.2 17.0 %collective-permute-start.13 = (bf16[144,1024]{1,0:T(8,128)(2,1)S(1)}, bf16[144,1024]{1,0:T(8,128)(2,1)S(1)}, u32[]{:S(2)}, u32[]{:S(2)}) collective-permute-start(bf16[144,1024]{1,0:T(8,128)(2,1)S(1)} %get-tuple-element.626), channel_id=1, source_target_pairs={{0,4},{4,0},{8,12},{12,8},{16,20},{20,16},{24,28},{28,24},{1,5},{5... | collective-permute-start | bytes 884744 | tf_op jit(solution)/shard_map/cond/branch_1_fun/ppermute | solution.py:132
  253.7 30.8 %collective-permute-start.35 = (bf16[512,1024]{1,0:T(8,128)(2,1)S(1)}, bf16[512,1024]{1,0:T(8,128)(2,1)}, u32[]{:S(2)}, u32[]{:S(2)}) collective-permute-start(bf16[512,1024]{1,0:T(8,128)(2,1)S(1)} %get-tuple-element.660), channel_id=1, source_target_pairs={{0,8},{8,16},{16,24},{24,28},{28,20},{20,12},{12,4},{4,0},{1,9},{9... | collective-permute-start | bytes 3145736 | tf_op jit(solution)/shard_map/cond/branch_1_fun/ppermute | solution.py:65
  253.7 30.8 %collective-permute-start.36 = (bf16[512,1024]{1,0:T(8,128)(2,1)}, bf16[512,1024]{1,0:T(8,128)(2,1)}, u32[]{:S(2)}, u32[]{:S(2)}) collective-permute-start(bf16[512,1024]{1,0:T(8,128)(2,1)} %get-tuple-element.661), channel_id=1, source_target_pairs={{0,4},{8,0},{16,8},{24,16},{28,24},{20,28},{12,20},{4,12},{1,5},{9... | collective-permute-start | bytes 3145736 | tf_op jit(solution)/shard_map/cond/branch_1_fun/ppermute | solution.py:65
  255.7 28.6 %collective-permute-start.34 = (bf16[144,1024]{1,0:T(8,128)(2,1)S(1)}, bf16[144,1024]{1,0:T(8,128)(2,1)S(1)}, u32[]{:S(2)}, u32[]{:S(2)}) collective-permute-start(bf16[144,1024]{1,0:T(8,128)(2,1)S(1)} %get-tuple-element.656), channel_id=1, source_target_pairs={{8,0},{12,4},{16,8},{20,12},{24,16},{28,20},{9,1},{13,5},{17,9},{2... | collective-permute-start | bytes 884744 | tf_op jit(solution)/shard_map/cond/branch_1_fun/ppermute | solution.py:205
  285.4 15.5 %collective-permute-start.16 = (bf16[128,1024]{1,0:T(8,128)(2,1)S(1)}, bf16[128,1024]{1,0:T(8,128)(2,1)S(1)}, u32[]{:S(2)}, u32[]{:S(2)}) collective-permute-start(bf16[128,1024]{1,0:T(8,128)(2,1)S(1)} %get-tuple-element.679), channel_id=1, source_target_pairs={{16,0},{20,4},{24,8},{28,12},{17,1},{21,5},{25,9},{29,13},{18,2},{... | collective-permute-start | bytes 786440 | tf_op jit(solution)/shard_map/cond/branch_1_fun/ppermute | solution.py:205
  314.5 26.9 %collective-permute-start.37 = (bf16[512,1024]{1,0:T(8,128)(2,1)}, bf16[512,1024]{1,0:T(8,128)(2,1)}, u32[]{:S(2)}, u32[]{:S(2)}) collective-permute-start(bf16[512,1024]{1,0:T(8,128)(2,1)} %get-tuple-element.698), channel_id=1, source_target_pairs={{0,8},{8,16},{16,24},{24,28},{28,20},{20,12},{12,4},{4,0},{1,9},{9... | collective-permute-start | bytes 3145736 | tf_op jit(solution)/shard_map/cond/branch_1_fun/ppermute | solution.py:65
  316.7 24.8 %collective-permute-start.38 = (bf16[512,1024]{1,0:T(8,128)(2,1)}, bf16[512,1024]{1,0:T(8,128)(2,1)}, u32[]{:S(2)}, u32[]{:S(2)}) collective-permute-start(bf16[512,1024]{1,0:T(8,128)(2,1)} %get-tuple-element.699), channel_id=1, source_target_pairs={{0,4},{8,0},{16,8},{24,16},{28,24},{20,28},{12,20},{4,12},{1,5},{9... | collective-permute-start | bytes 3145736 | tf_op jit(solution)/shard_map/cond/branch_1_fun/ppermute | solution.py:65
  359.7 35.5 %collective-permute-start.41 = (bf16[512,1024]{1,0:T(8,128)(2,1)}, bf16[512,1024]{1,0:T(8,128)(2,1)}, u32[]{:S(2)}, u32[]{:S(2)}) collective-permute-start(bf16[512,1024]{1,0:T(8,128)(2,1)} %get-tuple-element.728), channel_id=1, source_target_pairs={{0,8},{8,16},{16,24},{24,28},{28,20},{20,12},{12,4},{4,0},{1,9},{9... | collective-permute-start | bytes 3145736 | tf_op jit(solution)/shard_map/cond/branch_1_fun/ppermute | solution.py:65
  362.6 32.6 %collective-permute-start.42 = (bf16[512,1024]{1,0:T(8,128)(2,1)}, bf16[512,1024]{1,0:T(8,128)(2,1)}, u32[]{:S(2)}, u32[]{:S(2)}) collective-permute-start(bf16[512,1024]{1,0:T(8,128)(2,1)} %get-tuple-element.729), channel_id=1, source_target_pairs={{0,4},{8,0},{16,8},{24,16},{28,24},{20,28},{12,20},{4,12},{1,5},{9... | collective-permute-start | bytes 3145736 | tf_op jit(solution)/shard_map/cond/branch_1_fun/ppermute | solution.py:65
  362.6 32.6 %collective-permute-start.45 = (bf16[1024,512]{1,0:T(8,128)(2,1)}, bf16[1024,512]{1,0:T(8,128)(2,1)}, u32[]{:S(2)}, u32[]{:S(2)}) collective-permute-start(bf16[1024,512]{1,0:T(8,128)(2,1)} %get-tuple-element.757), channel_id=1, source_target_pairs={{0,2},{1,3},{2,0},{3,1},{4,6},{5,7},{6,4},{7,5},{8,10},{9,11},{10,... | collective-permute-start | bytes 3145736 | tf_op jit(solution)/shard_map/cond/branch_1_fun/ppermute | solution.py:132
  378.2 14.8 %collective-permute-start.43 = (bf16[128,1152]{1,0:T(8,128)(2,1)S(1)}, bf16[128,1152]{1,0:T(8,128)(2,1)S(1)}, u32[]{:S(2)}, u32[]{:S(2)}) collective-permute-start(bf16[128,1152]{1,0:T(8,128)(2,1)S(1)} %get-tuple-element.749), channel_id=1, source_target_pairs={{0,8},{8,16},{16,24},{24,28},{28,20},{20,12},{12,4},{4,0},{1,9},{9... | collective-permute-start | bytes 884744 | tf_op jit(solution)/shard_map/cond/branch_1_fun/ppermute | solution.py:65
  380.3 12.7 %collective-permute-start.44 = (bf16[128,1152]{1,0:T(8,128)(2,1)S(1)}, bf16[128,1152]{1,0:T(8,128)(2,1)S(1)}, u32[]{:S(2)}, u32[]{:S(2)}) collective-permute-start(bf16[128,1152]{1,0:T(8,128)(2,1)S(1)} %get-tuple-element.750), channel_id=1, source_target_pairs={{0,4},{8,0},{16,8},{24,16},{28,24},{20,28},{12,20},{4,12},{1,5},{9... | collective-permute-start | bytes 884744 | tf_op jit(solution)/shard_map/cond/branch_1_fun/ppermute | solution.py:65
  395.5 20.0 %collective-permute-start.17 = (bf16[256,1152]{1,0:T(8,128)(2,1)}, bf16[256,1152]{1,0:T(8,128)(2,1)}, u32[]{:S(2)}, u32[]{:S(2)}) collective-permute-start(bf16[256,1152]{1,0:T(8,128)(2,1)} %get-tuple-element.760), channel_id=1, source_target_pairs={{0,8},{8,16},{16,24},{24,28},{28,20},{20,12},{12,4},{4,0},{1,9},{9... | collective-permute-start | bytes 1769480 | tf_op jit(solution)/shard_map/cond/branch_1_fun/ppermute | solution.py:65
  397.8 17.8 %collective-permute-start.18 = (bf16[256,1152]{1,0:T(8,128)(2,1)}, bf16[256,1152]{1,0:T(8,128)(2,1)}, u32[]{:S(2)}, u32[]{:S(2)}) collective-permute-start(bf16[256,1152]{1,0:T(8,128)(2,1)} %get-tuple-element.761), channel_id=1, source_target_pairs={{0,4},{8,0},{16,8},{24,16},{28,24},{20,28},{12,20},{4,12},{1,5},{9... | collective-permute-start | bytes 1769480 | tf_op jit(solution)/shard_map/cond/branch_1_fun/ppermute | solution.py:65
  397.8 17.8 %collective-permute-start.19 = (f32[7200]{0:T(1024)S(1)}, f32[7200]{0:T(1024)S(1)}, u32[]{:S(2)}, u32[]{:S(2)}) collective-permute-start(f32[7200]{0:T(1024)S(1)} %get-tuple-element.772), channel_id=1, source_target_pairs={{0,4},{4,0},{8,12},{12,8},{16,20},{20,16},{24,28},{28,24},{1,5},{5... | collective-permute-start | bytes 86408 | tf_op jit(solution)/shard_map/cond/branch_1_fun/ppermute | solution.py:132
  399.6 15.9 %collective-permute-start.20 = (f32[1024]{0:T(1024)S(1)}, f32[1024]{0:T(1024)S(1)}, u32[]{:S(2)}, u32[]{:S(2)}) collective-permute-start(f32[1024]{0:T(1024)S(1)} %get-tuple-element.773), channel_id=1, source_target_pairs={{0,1},{1,0},{2,3},{3,2},{4,5},{5,4},{6,7},{7,6},{8,9},{9,8},{10,11... | collective-permute-start | bytes 12296 | tf_op jit(solution)/shard_map/cond/branch_1_fun/ppermute | solution.py:132
  422.4 26.9 %collective-permute-start.68 = (bf16[1024,512]{1,0:T(8,128)(2,1)}, bf16[1024,512]{1,0:T(8,128)(2,1)}, u32[]{:S(2)}, u32[]{:S(2)}) collective-permute-start(bf16[1024,512]{1,0:T(8,128)(2,1)} %get-tuple-element.809), channel_id=1, source_target_pairs={{0,2},{1,3},{2,0},{3,1},{4,6},{5,7},{6,4},{7,5},{8,10},{9,11},{10,... | collective-permute-start | bytes 3145736 | tf_op jit(solution)/shard_map/cond/branch_1_fun/ppermute | solution.py:132
  425.5 20.1 %collective-permute-start.61 = (bf16[256,1152]{1,0:T(8,128)(2,1)S(1)}, bf16[256,1152]{1,0:T(8,128)(2,1)S(1)}, u32[]{:S(2)}, u32[]{:S(2)}) collective-permute-start(bf16[256,1152]{1,0:T(8,128)(2,1)S(1)} %get-tuple-element.790), channel_id=1, source_target_pairs={{0,8},{8,16},{16,24},{24,28},{28,20},{20,12},{12,4},{4,0},{1,9},{9... | collective-permute-start | bytes 1769480 | tf_op jit(solution)/shard_map/cond/branch_1_fun/ppermute | solution.py:65
  425.6 20.0 %collective-permute-start.62 = (bf16[256,1152]{1,0:T(8,128)(2,1)}, bf16[256,1152]{1,0:T(8,128)(2,1)S(1)}, u32[]{:S(2)}, u32[]{:S(2)}) collective-permute-start(bf16[256,1152]{1,0:T(8,128)(2,1)} %get-tuple-element.791), channel_id=1, source_target_pairs={{0,4},{8,0},{16,8},{24,16},{28,24},{20,28},{12,20},{4,12},{1,5},{9... | collective-permute-start | bytes 1769480 | tf_op jit(solution)/shard_map/cond/branch_1_fun/ppermute | solution.py:65
  427.6 16.1 %collective-permute-start.60 = (f32[7200]{0:T(1024)S(1)}, f32[7200]{0:T(1024)S(1)}, u32[]{:S(2)}, u32[]{:S(2)}) collective-permute-start(f32[7200]{0:T(1024)S(1)} %add.96), channel_id=1, source_target_pairs={{0,16},{4,20},{8,24},{12,28},{16,0},{20,4},{24,8},{28,12},{1,17},{... | collective-permute-start | bytes 86408 | tf_op jit(solution)/shard_map/cond/branch_1_fun/ppermute | solution.py:132
  447.2 12.5 %collective-permute-start.63 = (bf16[256,1152]{1,0:T(8,128)(2,1)S(1)}, bf16[256,1152]{1,0:T(8,128)(2,1)S(1)}, u32[]{:S(2)}, u32[]{:S(2)}) collective-permute-start(bf16[256,1152]{1,0:T(8,128)(2,1)S(1)} %get-tuple-element.792), channel_id=1, source_target_pairs={{0,8},{8,16},{16,24},{24,28},{28,20},{20,12},{12,4},{4,0},{1,9},{9... | collective-permute-start | bytes 1769480 | tf_op jit(solution)/shard_map/cond/branch_1_fun/ppermute | solution.py:65
  447.7 12.7 %collective-permute-start.64 = (bf16[256,1152]{1,0:T(8,128)(2,1)S(1)}, bf16[256,1152]{1,0:T(8,128)(2,1)S(1)}, u32[]{:S(2)}, u32[]{:S(2)}) collective-permute-start(bf16[256,1152]{1,0:T(8,128)(2,1)S(1)} %get-tuple-element.793), channel_id=1, source_target_pairs={{0,4},{8,0},{16,8},{24,16},{28,24},{20,28},{12,20},{4,12},{1,5},{9... | collective-permute-start | bytes 1769480 | tf_op jit(solution)/shard_map/cond/branch_1_fun/ppermute | solution.py:65
  (69 other events, 761.7 us)

commit v5 on v4

--- a/solution.py
+++ b/solution.py
@@ -1251,15 +1251,17 @@
             rest = dot(normed[0], rest_w)
             x_in, bc_in = dot(normed[0], x_w).astype(BF16), rest[:, :group].astype(BF16)
         bc_own = jnp.pad(rest[:, :group].astype(BF16), ((0, 0), (0, -group % LANES)))
-        return x_in, bc_in, bc_own, rest[:, group : group + heads], x_w, rest_w
+        return (
+            x_in, bc_in, bc_own, rest[:, group : group + heads], x_w, rest_w,
+            edge([x_in, bc_in], True),
+        )
 
     def work(normed, hop1, hop2, hop3, hop4, zo_in):
         return ring.hop((zo_in, zo_in)), ring.phase(project_in, normed, hop1, hop2, hop3, hop4)
 
-    hop1, (x_in, bc_in, bc_own, dt_raw, x_w, rest_w) = ring.phase(
+    hop1, (x_in, bc_in, bc_own, dt_raw, x_w, rest_w, halo) = ring.phase(
         work, normed, hop1, hop2, hop3, hop4, zo_in
     )
-    halo = ring.phase(lambda x_in, bc_in: edge([x_in, bc_in], True), x_in, bc_in)
 
     def work(hop1, x_in, bc_in, halo, dt_raw, own_cot):
         scanned = scan(x_in, bc_in, halo, dt_raw)
@@ -1364,34 +1366,31 @@
 
     later, (out_far, out_own) = ring.phase(work, held, branch)
 
-    def work(later, sums, du_local, dbc_local):
-        sums = ring.hop(sums)
+    def finish_maps(later, du_local, dbc_local, own_slope):
         d_conv_x, mine, send, d_dt, g_skip, g_heads = finish(
             conv_out, d_ssd, du_local, ssd, steps, cumulative, left_w, later, at_end,
             dbc_local, dt_raw,
         )
-        after_x = edge([d_conv_x], False)
         if ring.on:
             mine = mine + swap(send, "head", 1)
-        else:
-            mine = jnp.concatenate([mine, send], axis=1)
-        return sums, d_conv_x, after_x, mine, d_dt, g_skip, g_heads
-
-    sums, d_conv_x, after_x, mine, d_dt, g_skip, g_heads = ring.phase(
-        work, later, sums, du_local, dbc_local
-    )
-
-    share = 1.0 if ring.on else jnp.where(here == 0, 1.0, 0.0)
-
-    def work(mine, sums, g_zo, own_slope):
-        if ring.on:
             mine = mine[:, :group] + unfold(swap(fold(mine[:, group:]), "head", 2))
         else:
-            mine = head_sum(mine)
+            mine = head_sum(jnp.concatenate([mine, send], axis=1))
         d_conv_bc = jnp.pad((mine * own_slope).astype(BF16), ((0, 0), (0, -group % LANES)))
-        return d_conv_bc, edge([d_conv_bc], False), ring.add(g_zo, sums, 1)
-
-    d_conv_bc, after_bc, sums = ring.phase(work, mine, sums, g_zo, own_slope)
+        after = edge([d_conv_x, d_conv_bc], False)
+        return d_conv_x, d_conv_bc, d_dt, g_skip, g_heads, after
+
+    def work(later, sums, g_zo, du_local, dbc_local, own_slope):
+        sums = ring.hop(sums)
+        given = ring.phase(finish_maps, later, du_local, dbc_local, own_slope)
+        return ring.add(g_zo, sums, 1), given
+
+    sums, (d_conv_x, d_conv_bc, d_dt, g_skip, g_heads, after) = ring.phase(
+        work, later, sums, g_zo, du_local, dbc_local, own_slope
+    )
+
+    share = 1.0 if ring.on else jnp.where(here == 0, 1.0, 0.0)
+    after_x, after_bc = after[:, :, :inner], after[:, :, inner:]
     own_taps = jnp.pad(own_columns(conv_bcf), ((0, 0), (0, -group % LANES)))
 
     def work(

time: 483 us -> 474 us (0.981)
  Pallas kernels: 207 us -> 200 us
  transfers between devices with their start and end apart: 70 -> 69, of which waited for: 26 -> 25; matrix products, arithmetic and copies ran while one was open for 8% -> 10% of each run, Pallas kernels for 38% -> 37%
where the time goes in v5:
time: 474 us; the launch traced here: 465 us
  Pallas kernels  200 us (42%)
  waiting for transfers between devices  104 us (22%)
  starting transfers between devices  75.2 us (16%)
  other arithmetic  31.6 us (7%)
  local copies, waits for them, and re-layouts  30.3 us (6%)
  blocking collectives  22 us (5%)
    ppermute x29, waiting for transfers between devices, swap(): return lax.ppermute(array, axis, [(i, i ^ bit) for i in range(size)])  52.7 us
    ppermute x32, waiting for transfers between devices, shift(): lax.ppermute(array, 'seq', [(order[i], order[(i + by) % size]) for i in r...  36.9 us
    pallas_call x3, Pallas kernels, with_spots(): pl.pallas_call(kernel, grid_spec=pltpu.PrefetchScalarGridSpec(num_scalar_...  36.8 us
    ppermute x32, starting transfers between devices, shift(): lax.ppermute(array, 'seq', [(order[i], order[(i + by) % size]) for i in r...  35.9 us
    pallas_call x2, Pallas kernels, project(): pl.pallas_call(functools.partial(project_kernel, len(acts), len(late)), g...  24.8 us
    pallas_call x2, Pallas kernels, outer(): pl.pallas_call(functools.partial(outer_kernel, [len(grads) for _, grads i...  24.4 us
    psum x3, blocking collectives, head_sum(): return lax.psum(array, 'head')  22 us
    ppermute x29, starting transfers between devices, swap(): return lax.ppermute(array, axis, [(i, i ^ bit) for i in range(size)])  19.3 us
  transfers between devices with their start and end apart: 69, of which 25 were waited for; matrix products, arithmetic and copies ran while one was open for 10% of the time, Pallas kernels for 37%

profile of v5, /device:TPU:0, one launch (start us, length us, event | category | flops | bytes accessed | tf_op | source)
XLA Modules:
  0.0 465.1 jit_solution(6605400750652111304)
XLA Ops:
  2.9 24.2 %conditional.19 = (bf16[256,1152]{1,0:T(8,128)(2,1)}, bf16[256,1152]{1,0:T(8,128)(2,1)}, f32[512]{0:T(512)}, f32[1024]{0:T(1024)}, bf16[1024,512]{1,0:T(8,128)(2,1)S(1)}) conditional(s32[]{:T(128)} %convert_element_type.104, () %tuple.194, (bf16[256,1152]{1,0:T(8,128)(2,1)S(1)}, s32[]{:T(128)}, bf16[256]{0:T(256)(128)(2,1)}, ...), branch_computations={%region_0.1_spmd, %region_1.4_spmd} | conditional | flops 2624769 | bytes 10006226 | solution.py:127
  7.5 4.0 collective-permute-start.21
  13.3 9.6 %psum.18 = f32[1024]{0:T(1024)S(1)} all-reduce(f32[1024]{0:T(1024)S(1)} %multiply_reduce_fusion), channel_id=1, replica_groups=mesh['seq'=8,'head'=4] {'head'}, use_global_device_ids=true, to_apply=%region_3.3 | all-reduce | flops 1024 | bytes 8192 | tf_op jit(solution)/shard_map/cond/branch_1_fun/psum | solution.py:136
  30.2 29.0 %conditional.20 = (bf16[256,1152]{1,0:T(8,128)(2,1)}, bf16[256,1152]{1,0:T(8,128)(2,1)}, bf16[256,1152]{1,0:T(8,128)(2,1)}, bf16[256,1152]{1,0:T(8,128)(2,1)}, b...) conditional(s32[]{:T(128)} %convert_element_type.104, () %tuple.193, ...), branch_computations={%region_4.5_spmd, %region_5.6_spmd} | conditional | flops 2621440 | bytes 22020380 | solution.py:127
  32.2 12.8 %collective-permute-done.25 = bf16[256,1152]{1,0:T(8,128)(2,1)} collective-permute-done((bf16[256,1152]{1,0:T(8,128)(2,1)}, bf16[256,1152]{1,0:T(8,128)(2,1)}, u32[]{:S(2)}, u32[]{:S(2)}) %collective-permute-start.25) | collective-permute-done | bytes 589856 | tf_op jit(solution)/shard_map/cond/branch_1_fun/ppermute | solution.py:65
  52.1 6.8 %collective-permute-done.27 = bf16[256,1152]{1,0:T(8,128)(2,1)} collective-permute-done((bf16[256,1152]{1,0:T(8,128)(2,1)}, bf16[256,1152]{1,0:T(8,128)(2,1)}, u32[]{:S(2)}, u32[]{:S(2)}) %collective-permute-start.27) | collective-permute-done | bytes 589856 | tf_op jit(solution)/shard_map/cond/branch_1_fun/ppermute | solution.py:65
  59.2 11.7 %conditional.21 = (bf16[128,1152]{1,0:T(8,128)(2,1)}, bf16[128,1152]{1,0:T(8,128)(2,1)}, bf16[1024,512]{1,0:T(8,128)(2,1)}) conditional(s32[]{:T(128)} %convert_element_type.104, () %tuple.197, (bf16[256,1152]{1,0:T(8,128)(2,1)}, bf16[256,1152]{1,0:T(8,128)(2,1)}, bf16[1024,512]{1,0:T(8,128)(2,1)S(1)}) %tuple.198), branch_computations={%region_6.7_spmd, %region_7.8_spmd} | conditional | bytes 7733392 | solution.py:127
  63.6 6.2 %collective-permute-done = bf16[128,1152]{1,0:T(8,128)(2,1)} collective-permute-done((bf16[128,1152]{1,0:T(8,128)(2,1)S(1)}, bf16[128,1152]{1,0:T(8,128)(2,1)}, u32[]{:S(2)}, u32[]{:S(2)}) %collective-permute-start) | collective-permute-done | bytes 294944 | tf_op jit(solution)/shard_map/cond/branch_1_fun/ppermute | solution.py:65
  70.9 31.0 %conditional.22 = (bf16[512,1024]{1,0:T(8,128)(2,1)}, bf16[512,1024]{1,0:T(8,128)(2,1)}, bf16[1024,1024]{1,0:T(8,128)(2,1)}, bf16[1024,256]{1,0:T(8,128)(2,1)}, ...) conditional(s32[]{:T(128)} %convert_element_type.104, ...), branch_computations={%region_8.9_spmd, %region_9.12_spmd} | conditional | flops 5818377 | bytes 66629688 | solution.py:127
  75.2 26.7 %conditional = (bf16[1024,1024]{1,0:T(8,128)(2,1)}, bf16[1024,256]{1,0:T(8,128)(2,1)}, bf16[1024,128]{1,0:T(8,128)(2,1)}, f32[1024,16]{1,0:T(8,128)}, bf16[2048,...) conditional(s32[]{:T(128)} %convert_element_type.34, () %tuple.116, ...), branch_computations={%region_10.10_spmd, %region_11.11_spmd} | conditional | flops 5818372 | bytes 56143608 | solution.py:127
  75.2 11.3 %branch_1_fun.32 = (bf16[1024,1024]{1,0:T(8,128)(2,1)}, f32[1024,128]{1,0:T(8,128)S(1)}, bf16[2048,1024]{1,0:T(8,128)(2,1)}, bf16[2048,128]{1,0:T(8,128)(2,1)}) custom-call(s32[8]{0:T(128)S(1)} %get-tuple-element.525.spot_ref, bf16[1024,512]{1,0:T(8,128)(2,1)} %get-tuple-element.526.refs_0_, bf16[1024,512]{1,0:T(8,128)(2,1)} %get-tuple-element.527.refs_1_, ...), custom_call_target="tpu_custom_call" | custom-call | bytes 49500000 | tf_op jit(solution)/shard_map/cond/branch_1_fun/cond/branch_1_fun/pallas_call | solution.py:740
  87.9 4.5 collective-permute-done.42
  102.0 34.0 %conditional.23 = (bf16[512,1024]{1,0:T(8,128)(2,1)}, bf16[512,1024]{1,0:T(8,128)(2,1)}, f32[1024,1280]{1,0:T(8,128)}, f32[1024,1024]{1,0:T(8,128)}, f32[1024,16...) conditional(s32[]{:T(128)} %convert_element_type.104, ...), branch_computations={%region_12.13_spmd, %region_13.14_spmd} | conditional | bytes 65807200 | solution.py:127
  104.8 16.1 %branch_1_fun.33 = (f32[1024,1280]{1,0:T(8,128)}, f32[1024,1024]{1,0:T(8,128)}, f32[1024,16]{1,0:T(8,128)}, f32[1024,16]{1,0:T(8,128)}, f32[8,128,1024]{2,1,0:T(...) custom-call(bf16[1024,1024]{1,0:T(8,128)(2,1)} %get-tuple-element.569.x_ref, ...), custom_call_target="tpu_custom_call" | custom-call | bytes 47850000 | tf_op jit(solution)/shard_map/cond/branch_1_fun/pallas_call | solution.py:1032
  124.4 10.4 %collective-permute-done.5.got_ref = bf16[144,1024]{1,0:T(8,128)(2,1)S(1)} collective-permute-done((bf16[144,1024]{1,0:T(8,128)(2,1)S(1)}, bf16[144,1024]{1,0:T(8,128)(2,1)S(1)}, u32[]{:S(2)}, u32[]{:S(2)}) %collective-permute-start.5) | collective-permute-done | bytes 294944 | tf_op jit(solution)/shard_map/cond/branch_1_fun/ppermute | solution.py:132
  136.0 31.2 %conditional.24 = (bf16[512,1024]{1,0:T(8,128)(2,1)}, bf16[512,1024]{1,0:T(8,128)(2,1)}, f32[128,1024]{1,0:T(8,128)}, f32[1,1024]{1,0:T(1,128)S(1)}, f32[128,102...) conditional(s32[]{:T(128)} %convert_element_type.104, ...), branch_computations={%region_14.15_spmd, %region_15.18_spmd} | conditional | flops 655368 | bytes 77156632 | solution.py:127
  145.1 18.4 %branch_1_fun.37 = (f32[1024,1024]{1,0:T(8,128)}, f32[1024,1024]{1,0:T(8,128)}, bf16[2048,1024]{1,0:T(8,128)(2,1)}, bf16[2048,1024]{1,0:T(8,128)(2,1)}, bf16[102...) custom-call(s32[8]{0:T(128)S(1)} %get-tuple-element.607.spot_ref, bf16[1024,512]{1,0:T(8,128)(2,1)} %get-tuple-element.608.refs_0_, ...), custom_call_target="tpu_custom_call" | custom-call | bytes 49500000 | tf_op jit(solution)/shard_map/cond/branch_1_fun/pallas_call | solution.py:740
  167.2 28.1 %conditional.25 = (bf16[256,1024]{1,0:T(8,128)(2,1)}, bf16[256,1024]{1,0:T(8,128)(2,1)}, f32[2,128,1024]{2,1,0:T(8,128)S(1)}, f32[1024,1024]{1,0:T(8,128)S(1)}, f32[1024,1024]{1,0:T(8,128)S(1)}) conditional(s32[]{:T(128)} %convert_element_type.104, () %tuple.189, (bf16[512,1024]{1,0:T(8,128)(2,1)}, bf16[512,1024]{1,0:T(8,128)(2,1)}, ...), branch_computations={%region_18.19_spmd, %region_19.20_spmd} | conditional | bytes 59985988 | solution.py:127
  167.2 6.4 %collective-permute-start.11 = (bf16[128,1024]{1,0:T(8,128)(2,1)}, bf16[128,1024]{1,0:T(8,128)(2,1)S(1)}, u32[]{:S(2)}, u32[]{:S(2)}) collective-permute-start(bf16[128,1024]{1,0:T(8,128)(2,1)} %get-tuple-element.632), channel_id=1, source_target_pairs={{0,16},{4,20},{8,24},{12,28},{1,17},{5,21},{9,25},{13,29},{2,18},{... | collective-permute-start | bytes 786440 | tf_op jit(solution)/shard_map/cond/branch_1_fun/ppermute | solution.py:205
  182.2 7.2 %branch_1_fun.40 = (f32[1024,1024]{1,0:T(8,128)S(1)}, f32[1024,1024]{1,0:T(8,128)S(1)}) custom-call(s32[8]{0:T(128)S(1)} %get-tuple-element.635.spot_ref, f32[1024,1024]{1,0:T(8,128)} %get-tuple-element.636.z_ref, f32[1024,1024]{1,0:T(8,128)} %get-tuple-element.637.dm_ref, bf16[1024,768]{1,0:T(8,128)(2,1)S(1)} %get-tuple-element.638.na_ref, ...), custom_call_target="tpu_custom_call" | custom-call | bytes 49500000 | tf_op jit(solution)/shard_map/cond/branch_1_fun/pallas_call | solution.py:740
  189.4 5.8 %collective-permute-done.12.got_ref = bf16[128,1024]{1,0:T(8,128)(2,1)S(1)} collective-permute-done((bf16[128,1024]{1,0:T(8,128)(2,1)S(1)}, bf16[128,1024]{1,0:T(8,128)(2,1)S(1)}, u32[]{:S(2)}, u32[]{:S(2)}) %collective-permute-start.12) | collective-permute-done | bytes 262176 | tf_op jit(solution)/shard_map/cond/branch_1_fun/ppermute | solution.py:132
  195.4 9.4 %shard_map.246 = (f32[1024,1024]{1,0:T(8,128)}, f32[4,2,256]{2,1,0:T(2,128)S(1)}) custom-call(f32[1024,1024]{1,0:T(8,128)} %get-tuple-element.1046.y_ref, f32[1024,1280]{1,0:T(8,128)} %get-tuple-element.1031.vc_ref, f32[2,128,1024]{2,1,0:T(8,128)S(1)} %get-tuple-element.1047.s_ref, f32[1024,16]{1,0:T(8,128)S(1)} %copy-done.26, ...), custom_call_target="tpu_custom_call" | custom-call | bytes 23100000 | tf_op jit(solution)/shard_map/pallas_call | solution.py:1088
  204.8 5.8 %psum.21 = f32[4,2,256]{2,1,0:T(2,128)S(1)} all-reduce(f32[4,2,256]{2,1,0:T(2,128)S(1)} %get-tuple-element.1053), channel_id=1, replica_groups=mesh['seq'=8,'head'=4] {'head'}, use_global_device_ids=true, to_apply=%region_20.21 | all-reduce | flops 2048 | bytes 16384 | tf_op jit(solution)/shard_map/psum | solution.py:136
  210.6 11.1 %shard_map.247 = (bf16[1024,1024]{1,0:T(8,128)(2,1)S(1)}, f32[1024,1024]{1,0:T(8,128)}, f32[2,128,1024]{2,1,0:T(8,128)S(1)}, f32[4,1,256]{2,1,0:T(1,128)S(1)}, f...) custom-call(f32[1024,1024]{1,0:T(8,128)} %copy-done.5, f32[1024,1024]{1,0:T(8,128)} %get-tuple-element.1052.ssd_ref, ...), custom_call_target="tpu_custom_call" | custom-call | bytes 29700000 | tf_op jit(solution)/shard_map/pallas_call | solution.py:1102
  223.7 26.1 %conditional.26 = (f32[128,1024]{1,0:T(8,128)}, f32[1,1024]{1,0:T(1,128)S(1)}, f32[128,1024]{1,0:T(8,128)}, f32[1,1024]{1,0:T(1,128)S(1)}, bf16[144,1024]{1,0:T(...) conditional(s32[]{:T(128)} %convert_element_type.104, ...), branch_computations={%region_21.22_spmd, %region_22.23_spmd} | conditional | bytes 58174136 | solution.py:127
  229.3 14.1 %branch_1_fun.43.a_ref.b_ref = bf16[4096,1024]{1,0:T(8,128)(2,1)} custom-call(s32[1]{0:T(128)} %get-tuple-element.654.far_ref, s32[8]{0:T(128)S(1)} %get-tuple-element.655.block_ref, bf16[1024,512]{1,0:T(8,128)(2,1)} %get-tuple-element.656.refs_0_, bf16[1024,512]{1,0:T(8,128)(2,1)} %get-tuple-element.657.refs_1_, ...), custom_call_target="tpu_custom_call" | custom-call | bytes 52800000 | tf_op jit(solution)/shard_map/cond/branch_1_fun/pallas_call | solution.py:800
  249.7 31.6 %conditional.27 = (f32[128,1024]{1,0:T(8,128)}, f32[1,1024]{1,0:T(1,128)S(1)}, f32[128,1024]{1,0:T(8,128)}, f32[1,1024]{1,0:T(1,128)S(1)}, bf16[128,1024]{1,0:T(...) conditional(s32[]{:T(128)} %convert_element_type.104, ...), branch_computations={%region_23.24_spmd, %region_24.25_spmd} | conditional | flops 524288 | bytes 78430264 | solution.py:127
  253.1 19.2 %branch_1_fun.47 = (f32[1024,1024]{1,0:T(8,128)}, f32[1024,256]{1,0:T(8,128)}) custom-call(f32[1024,1280]{1,0:T(8,128)} %get-tuple-element.684.v_ref, f32[1024,1024]{1,0:T(8,128)} %get-tuple-element.685.dy_ref, f32[1024,16]{1,0:T(8,128)} %get-tuple-element.686.st_ref, f32[1,16]{1,0:T(1,128)S(1)} %get-tuple-element.687.rate_ref, ...), custom_call_target="tpu_custom_call" | custom-call | bytes 59400000 | tf_op jit(solution)/shard_map/cond/branch_1_fun/pallas_call | solution.py:1123
  274.5 5.9 %collective-permute-done.33.got_ref = bf16[144,1024]{1,0:T(8,128)(2,1)S(1)} collective-permute-done((bf16[144,1024]{1,0:T(8,128)(2,1)S(1)}, bf16[144,1024]{1,0:T(8,128)(2,1)S(1)}, u32[]{:S(2)}, u32[]{:S(2)}) %collective-permute-start.33) | collective-permute-done | bytes 294944 | tf_op jit(solution)/shard_map/cond/branch_1_fun/ppermute | solution.py:205
  282.3 15.6 %conditional.28 = (f32[128,1024]{1,0:T(8,128)S(1)}, bf16[128,1024]{1,0:T(8,128)(2,1)S(1)}, bf16[512,1024]{1,0:T(8,128)(2,1)}, bf16[512,1024]{1,0:T(8,128)(2,1)}, bf16[1024,2048]{1,0:T(8,128)(2,1)S(1)}) conditional(s32[]{:T(128)} %convert_element_type.104, () %tuple.186, (bf16[128,1024]{1,0:T(8,128)(2,1)S(1)}, s32[1]{0:T(128)}, s32[1]{0:T(128)}, ...), branch_computations={%region_25.26_spmd, %region_26.27_spmd} | conditional | bytes 28343016 | solution.py:127
  286.9 9.4 %branch_1_fun.50 = bf16[1024,2048]{1,0:T(8,128)(2,1)S(1)} custom-call(s32[8]{0:T(128)S(1)} %get-tuple-element.709.spot_ref, bf16[1024,1024]{1,0:T(8,128)(2,1)S(1)} %get-tuple-element.710.refs_0_, bf16[2048,1024]{1,0:T(8,128)(2,1)} %get-tuple-element.711.refs_1_, bf16[256,1024]{1,0:T(8,128)(2,1)} %get-tuple-element.712.refs_2_, ...), custom_call_target="tpu_custom_call" | custom-call | bytes 23100000 | tf_op jit(solution)/shard_map/cond/branch_1_fun/pallas_call | solution.py:868
  297.8 9.8 %conditional.29 = (f32[2,128,1024]{2,1,0:T(8,128)S(1)}, bf16[1024,512]{1,0:T(8,128)(2,1)S(1)}, f32[1024,512]{1,0:T(8,128)S(1)}) conditional(s32[]{:T(128)} %convert_element_type.104, () %tuple.206, (bf16[128,1024]{1,0:T(8,128)(2,1)S(1)}, s32[1]{0:T(128)}, s32[1]{0:T(128)}, f32[128,1024]{1,0:T(8,128)S(1)}, bf16[1024,2048]{1,0:T(8,128)(2,1)S(1)}) %tuple.207), branch_computations={%region_27.28_spmd, %region_28.29_spmd} | conditional | flops 3670016 | bytes 20971664 | solution.py:127
  298.6 8.3 %collective-permute-done.47.got_ref = bf16[128,1024]{1,0:T(8,128)(2,1)S(1)} collective-permute-done((bf16[128,1024]{1,0:T(8,128)(2,1)S(1)}, bf16[128,1024]{1,0:T(8,128)(2,1)S(1)}, u32[]{:S(2)}, u32[]{:S(2)}) %collective-permute-start.47) | collective-permute-done | bytes 262176 | tf_op jit(solution)/shard_map/cond/branch_1_fun/ppermute | solution.py:132
  309.3 43.6 %conditional.30 = (bf16[512,1024]{1,0:T(8,128)(2,1)S(1)}, bf16[512,1024]{1,0:T(8,128)(2,1)S(1)}, bf16[1024,1024]{1,0:T(8,128)(2,1)}, bf16[1024,128]{1,0:T(8,128)...) conditional(s32[]{:T(128)} %convert_element_type.104, ...), branch_computations={%region_29.30_spmd, %region_30.33_spmd} | conditional | flops 561161 | bytes 70082728 | solution.py:127
  311.5 39.6 %conditional.2 = (bf16[1024,1024]{1,0:T(8,128)(2,1)}, bf16[1024,128]{1,0:T(8,128)(2,1)}, bf16[1024,16]{1,0:T(8,128)(2,1)}, f32[2,8,1152]{2,1,0:T(8,128)}, f32[10...) conditional(s32[]{:T(128)} %convert_element_type.64, () %tuple.137, (s32[]{:T(128)}, ...), branch_computations={%region_31.31_spmd, %region_32.32_spmd} | conditional | flops 561156 | bytes 57499456 | solution.py:127
  312.5 16.1 %branch_1_fun.52 = (bf16[1024,1024]{1,0:T(8,128)(2,1)}, f32[1024,128]{1,0:T(8,128)S(1)}, f32[1024,128]{1,0:T(8,128)S(1)}, bf16[1024,16]{1,0:T(8,128)(2,1)}, f32[1,1024]{1,0:T(1,128)}, /*index=5*/f32[2,16]{1,0:T(2,128)S(1)}) custom-call(f32[1024,1280]{1,0:T(8,128)} %get-tuple-element.720.v_ref, f32[1024,1024]{1,0:T(8,128)} %get-tuple-element.721.dy_ref, ...), custom_call_target="tpu_custom_call" | custom-call | bytes 49500000 | tf_op jit(solution)/shard_map/cond/branch_1_fun/cond/branch_1_fun/pallas_call | solution.py:1146
  332.7 6.7 %collective-permute-done.51 = f32[512,128]{1,0:T(8,128)S(1)} collective-permute-done((f32[512,128]{1,0:T(8,128)S(1)}, f32[512,128]{1,0:T(8,128)S(1)}, u32[]{:S(2)}, u32[]{:S(2)}) %collective-permute-start.51) | collective-permute-done | bytes 262176 | tf_op jit(solution)/shard_map/cond/branch_1_fun/cond/branch_1_fun/ppermute | solution.py:132
  352.9 33.9 %conditional.31 = (bf16[512,1024]{1,0:T(8,128)(2,1)}, bf16[512,1024]{1,0:T(8,128)(2,1)}, bf16[256,1152]{1,0:T(8,128)(2,1)}, bf16[256,1152]{1,0:T(8,128)(2,1)}, b...) conditional(s32[]{:T(128)} %convert_element_type.104, ...), branch_computations={%region_33.34_spmd, %region_34.36_spmd} | conditional | flops 837632 | bytes 104298472 | solution.py:127
  359.0 8.3 %branch_1_fun.54 = (bf16[1024,1024]{1,0:T(8,128)(2,1)S(1)}, f32[4,1024]{1,0:T(4,128)S(1)}, f32[4,1,256]{2,1,0:T(1,128)S(1)}) custom-call(bf16[1024,1024]{1,0:T(8,128)(2,1)} %get-tuple-element.777.d_ref, bf16[1024,1024]{1,0:T(8,128)(2,1)} %get-tuple-element.778.in_ref, f32[2,8,1024]{2,1,0:T(8,128)} %get-tuple-element.779.halo_ref, ...), custom_call_target="tpu_custom_call" | custom-call | bytes 26400000 | tf_op jit(solution)/shard_map/cond/branch_1_fun/pallas_call | solution.py:949
  373.3 10.3 %branch_1_fun.56.a_ref.b_ref = bf16[2048,1152]{1,0:T(8,128)(2,1)} custom-call(s32[1]{0:T(128)} %get-tuple-element.771.far_ref, s32[8]{0:T(128)S(1)} %get-tuple-element.772.block_ref, bf16[1024,512]{1,0:T(8,128)(2,1)} %get-tuple-element.773.refs_0_, bf16[1024,512]{1,0:T(8,128)(2,1)} %get-tuple-element.774.refs_1_, bf16[1024,512]{1,0:T(8,128)(2,1)S(1)} %copy-done.20, ...), custom_call_target="tpu_custom_call" | custom-call | bytes 29700000 | tf_op jit(solution)/shard_map/cond/branch_1_fun/pallas_call | solution.py:800
  388.4 18.8 %conditional.32 = (bf16[256,1152]{1,0:T(8,128)(2,1)}, bf16[256,1152]{1,0:T(8,128)(2,1)}, bf16[1024,2048]{1,0:T(8,128)(2,1)S(1)}, f32[7200]{0:T(1024)S(1)}, f32[1024]{0:T(1024)S(1)}) conditional(s32[]{:T(128)} %convert_element_type.104, () %tuple.183, (bf16[256,1152]{1,0:T(8,128)(2,1)}, bf16[256,1152]{1,0:T(8,128)(2,1)}, s32[8]{0:T(128)S(1)}, ...), branch_computations={%region_36.37_spmd, %region_37.38_spmd} | conditional | flops 8224 | bytes 54036564 | solution.py:127
  391.8 15.4 %branch_1_fun.59 = bf16[1024,2048]{1,0:T(8,128)(2,1)S(1)} custom-call(s32[8]{0:T(128)S(1)} %get-tuple-element.803.spot_ref, bf16[1024,1024]{1,0:T(8,128)(2,1)} %get-tuple-element.804.refs_0_, bf16[1024,1024]{1,0:T(8,128)(2,1)S(1)} %get-tuple-element.805.refs_1_, bf16[1024,128]{1,0:T(8,128)(2,1)S(1)} %get-tuple-element.806.refs_2_, ...), custom_call_target="tpu_custom_call" | custom-call | bytes 49087500 | tf_op jit(solution)/shard_map/cond/branch_1_fun/pallas_call | solution.py:868
  407.3 6.8 %conditional.33 = (bf16[256,1152]{1,0:T(8,128)(2,1)}, bf16[256,1152]{1,0:T(8,128)(2,1)}, bf16[1024,512]{1,0:T(8,128)(2,1)}, f32[1024,512]{1,0:T(8,128)S(1)}, f32[1024]{0:T(1024)S(1)}) conditional(s32[]{:T(128)} %convert_element_type.104, () %tuple.211, (bf16[2048,1152]{1,0:T(8,128)(2,1)}, bf16[256,1152]{1,0:T(8,128)(2,1)}, ...), branch_computations={%region_38.39_spmd, %region_39.40_spmd} | conditional | flops 3672064 | bytes 19955872 | solution.py:127
  414.0 49.6 %conditional.34 = (f32[1024]{0:T(1024)S(1)}, f32[16]{0:T(128)}, f32[16]{0:T(128)}, f32[256,1024]{1,0:T(8,128)}, f32[1024,256]{1,0:T(8,128)}, /*index=5*/f32[256,...) conditional(s32[]{:T(128)} %convert_element_type.104, ...), branch_computations={%region_40.41_spmd, %region_41.44_spmd} | conditional | flops 5658676 | bytes 66665752 | solution.py:127
  426.7 8.0 %collective-permute-done.59 = f32[7200]{0:T(1024)S(1)} collective-permute-done((f32[7200]{0:T(1024)S(1)}, f32[7200]{0:T(1024)S(1)}, u32[]{:S(2)}, u32[]{:S(2)}) %collective-permute-start.59) | collective-permute-done | bytes 28832 | tf_op jit(solution)/shard_map/cond/branch_1_fun/ppermute | solution.py:132
  439.8 4.3 multiply_subtract_fusion
  444.1 6.5 %collective-permute-done.62.right_ref = bf16[256,1152]{1,0:T(8,128)(2,1)S(1)} collective-permute-done((bf16[256,1152]{1,0:T(8,128)(2,1)S(1)}, bf16[256,1152]{1,0:T(8,128)(2,1)S(1)}, u32[]{:S(2)}, u32[]{:S(2)}) %collective-permute-start.62) | collective-permute-done | bytes 589856 | tf_op jit(solution)/shard_map/cond/branch_1_fun/ppermute | solution.py:65
  455.3 6.6 %psum.19 = f32[1280]{0:T(1024)S(1)} all-reduce(f32[1280]{0:T(1024)S(1)} %pad_maximum_fusion.7), channel_id=1, replica_groups=mesh['seq'=8,'head'=4] {'head'}, use_global_device_ids=true, to_apply=%region_42.42 | all-reduce | flops 1280 | bytes 10240 | tf_op jit(solution)/shard_map/cond/branch_1_fun/psum | solution.py:136
  (354 shorter events, 180.8 us)
Async XLA Ops:
  3.8 19.7 %collective-permute-start.23 = (f32[256]{0:T(256)S(1)}, f32[256]{0:T(256)S(1)}, u32[]{:S(2)}, u32[]{:S(2)}) collective-permute-start(f32[256]{0:T(256)S(1)} %convert_element_type.31), channel_id=1, source_target_pairs={{0,0},{8,1},{16,2},{24,3},{4,4},{12,5},{20,6},{28,7},{1,8},{9,9},{... | collective-permute-start | bytes 3080 | tf_op jit(solution)/shard_map/cond/branch_1_fun/ppermute | solution.py:156
  4.5 19.0 %collective-permute-start.24 = (f32[256]{0:T(256)S(1)}, f32[256]{0:T(256)S(1)}, u32[]{:S(2)}, u32[]{:S(2)}) collective-permute-start(f32[256]{0:T(256)S(1)} %convert_element_type.31), channel_id=1, source_target_pairs={{4,0},{12,1},{20,2},{28,3},{0,4},{8,5},{16,6},{24,7},{5,8},{13,9},... | collective-permute-start | bytes 3080 | tf_op jit(solution)/shard_map/cond/branch_1_fun/ppermute | solution.py:156
  7.5 18.4 %collective-permute-start.21 = (bf16[256,1152]{1,0:T(8,128)(2,1)S(1)}, bf16[256,1152]{1,0:T(8,128)(2,1)}, u32[]{:S(2)}, u32[]{:S(2)}) collective-permute-start(bf16[256,1152]{1,0:T(8,128)(2,1)S(1)} %get-tuple-element.512), channel_id=1, source_target_pairs={{0,8},{8,16},{16,24},{24,28},{28,20},{20,12},{12,4},{4,0},{1,9},{9... | collective-permute-start | bytes 1769480 | tf_op jit(solution)/shard_map/cond/branch_1_fun/ppermute | solution.py:65
  11.5 15.6 %collective-permute-start.22 = (bf16[256,1152]{1,0:T(8,128)(2,1)S(1)}, bf16[256,1152]{1,0:T(8,128)(2,1)}, u32[]{:S(2)}, u32[]{:S(2)}) collective-permute-start(bf16[256,1152]{1,0:T(8,128)(2,1)S(1)} %get-tuple-element.512), channel_id=1, source_target_pairs={{0,4},{8,0},{16,8},{24,16},{28,24},{20,28},{12,20},{4,12},{1,5},{9... | collective-permute-start | bytes 1769480 | tf_op jit(solution)/shard_map/cond/branch_1_fun/ppermute | solution.py:65
  27.2 32.0 %collective-permute-start.68 = (bf16[1024,512]{1,0:T(8,128)(2,1)S(1)}, bf16[1024,512]{1,0:T(8,128)(2,1)S(1)}, u32[]{:S(2)}, u32[]{:S(2)}) collective-permute-start(bf16[1024,512]{1,0:T(8,128)(2,1)S(1)} %get-tuple-element.1007), channel_id=1, source_target_pairs={{0,2},{1,3},{2,0},{3,1},{4,6},{5,7},{6,4},{7,5},{8,10},{9,11},{10,... | collective-permute-start | bytes 3145736 | tf_op jit(solution)/shard_map/ppermute | solution.py:132
  30.2 14.8 %collective-permute-start.25 = (bf16[256,1152]{1,0:T(8,128)(2,1)}, bf16[256,1152]{1,0:T(8,128)(2,1)}, u32[]{:S(2)}, u32[]{:S(2)}) collective-permute-start(bf16[256,1152]{1,0:T(8,128)(2,1)} %get-tuple-element.516), channel_id=1, source_target_pairs={{0,8},{8,16},{16,24},{24,28},{28,20},{20,12},{12,4},{4,0},{1,9},{9... | collective-permute-start | bytes 1769480 | tf_op jit(solution)/shard_map/cond/branch_1_fun/ppermute | solution.py:65
  30.5 14.9 %collective-permute-start.26 = (bf16[256,1152]{1,0:T(8,128)(2,1)}, bf16[256,1152]{1,0:T(8,128)(2,1)}, u32[]{:S(2)}, u32[]{:S(2)}) collective-permute-start(bf16[256,1152]{1,0:T(8,128)(2,1)} %get-tuple-element.517), channel_id=1, source_target_pairs={{0,4},{8,0},{16,8},{24,16},{28,24},{20,28},{12,20},{4,12},{1,5},{9... | collective-permute-start | bytes 1769480 | tf_op jit(solution)/shard_map/cond/branch_1_fun/ppermute | solution.py:65
  32.2 19.9 %collective-permute-start.29 = (bf16[1024,512]{1,0:T(8,128)(2,1)S(1)}, bf16[1024,512]{1,0:T(8,128)(2,1)}, u32[]{:S(2)}, u32[]{:S(2)}) collective-permute-start(bf16[1024,512]{1,0:T(8,128)(2,1)S(1)} %get-tuple-element.518), channel_id=1, source_target_pairs={{0,1},{1,0},{2,3},{3,2},{4,5},{5,4},{6,7},{7,6},{8,9},{9,8},{10,11... | collective-permute-start | bytes 3145736 | tf_op jit(solution)/shard_map/cond/branch_1_fun/ppermute | solution.py:132
  45.0 13.9 %collective-permute-start.27 = (bf16[256,1152]{1,0:T(8,128)(2,1)}, bf16[256,1152]{1,0:T(8,128)(2,1)}, u32[]{:S(2)}, u32[]{:S(2)}) collective-permute-start(bf16[256,1152]{1,0:T(8,128)(2,1)} %collective-permute-done.25), channel_id=1, source_target_pairs={{0,8},{8,16},{16,24},{24,28},{28,20},{20,12},{12,4},{4,0},{1,9},{9... | collective-permute-start | bytes 1769480 | tf_op jit(solution)/shard_map/cond/branch_1_fun/ppermute | solution.py:65
  45.5 13.7 %collective-permute-start.28 = (bf16[256,1152]{1,0:T(8,128)(2,1)}, bf16[256,1152]{1,0:T(8,128)(2,1)}, u32[]{:S(2)}, u32[]{:S(2)}) collective-permute-start(bf16[256,1152]{1,0:T(8,128)(2,1)} %collective-permute-done.26), channel_id=1, source_target_pairs={{0,4},{8,0},{16,8},{24,16},{28,24},{20,28},{12,20},{4,12},{1,5},{9... | collective-permute-start | bytes 1769480 | tf_op jit(solution)/shard_map/cond/branch_1_fun/ppermute | solution.py:65
  73.2 28.7 %collective-permute-start.45 = (bf16[512,1024]{1,0:T(8,128)(2,1)}, bf16[512,1024]{1,0:T(8,128)(2,1)}, u32[]{:S(2)}, u32[]{:S(2)}) collective-permute-start(bf16[512,1024]{1,0:T(8,128)(2,1)} %copy.43), channel_id=1, source_target_pairs={{0,8},{8,16},{16,24},{24,28},{28,20},{20,12},{12,4},{4,0},{1,9},{9... | collective-permute-start | bytes 3145736 | tf_op jit(solution)/shard_map/cond/branch_1_fun/ppermute | solution.py:65
  73.5 28.4 %collective-permute-start.46 = (bf16[512,1024]{1,0:T(8,128)(2,1)}, bf16[512,1024]{1,0:T(8,128)(2,1)}, u32[]{:S(2)}, u32[]{:S(2)}) collective-permute-start(bf16[512,1024]{1,0:T(8,128)(2,1)} %copy.43), channel_id=1, source_target_pairs={{0,4},{8,0},{16,8},{24,16},{28,24},{20,28},{12,20},{4,12},{1,5},{9... | collective-permute-start | bytes 3145736 | tf_op jit(solution)/shard_map/cond/branch_1_fun/ppermute | solution.py:65
  102.0 34.0 %collective-permute-start.6 = (bf16[1024,512]{1,0:T(8,128)(2,1)}, bf16[1024,512]{1,0:T(8,128)(2,1)}, u32[]{:S(2)}, u32[]{:S(2)}) collective-permute-start(bf16[1024,512]{1,0:T(8,128)(2,1)} %get-tuple-element.594), channel_id=1, source_target_pairs={{0,1},{1,0},{2,3},{3,2},{4,5},{5,4},{6,7},{7,6},{8,9},{9,8},{10,11... | collective-permute-start | bytes 3145736 | tf_op jit(solution)/shard_map/cond/branch_1_fun/ppermute | solution.py:132
  102.1 33.9 %collective-permute-start.7 = (bf16[1024,512]{1,0:T(8,128)(2,1)}, bf16[1024,512]{1,0:T(8,128)(2,1)}, u32[]{:S(2)}, u32[]{:S(2)}) collective-permute-start(bf16[1024,512]{1,0:T(8,128)(2,1)} %get-tuple-element.594), channel_id=1, source_target_pairs={{0,2},{1,3},{2,0},{3,1},{4,6},{5,7},{6,4},{7,5},{8,10},{9,11},{10,... | collective-permute-start | bytes 3145736 | tf_op jit(solution)/shard_map/cond/branch_1_fun/ppermute | solution.py:132
  102.5 33.4 %collective-permute-start.3 = (bf16[512,1024]{1,0:T(8,128)(2,1)}, bf16[512,1024]{1,0:T(8,128)(2,1)}, u32[]{:S(2)}, u32[]{:S(2)}) collective-permute-start(bf16[512,1024]{1,0:T(8,128)(2,1)} %get-tuple-element.567), channel_id=1, source_target_pairs={{0,8},{8,16},{16,24},{24,28},{28,20},{20,12},{12,4},{4,0},{1,9},{9... | collective-permute-start | bytes 3145736 | tf_op jit(solution)/shard_map/cond/branch_1_fun/ppermute | solution.py:65
  104.4 31.5 %collective-permute-start.4 = (bf16[512,1024]{1,0:T(8,128)(2,1)}, bf16[512,1024]{1,0:T(8,128)(2,1)}, u32[]{:S(2)}, u32[]{:S(2)}) collective-permute-start(bf16[512,1024]{1,0:T(8,128)(2,1)} %get-tuple-element.568), channel_id=1, source_target_pairs={{0,4},{8,0},{16,8},{24,16},{28,24},{20,28},{12,20},{4,12},{1,5},{9... | collective-permute-start | bytes 3145736 | tf_op jit(solution)/shard_map/cond/branch_1_fun/ppermute | solution.py:65
  122.3 12.5 %collective-permute-start.5 = (bf16[144,1024]{1,0:T(8,128)(2,1)S(1)}, bf16[144,1024]{1,0:T(8,128)(2,1)S(1)}, u32[]{:S(2)}, u32[]{:S(2)}) collective-permute-start(bf16[144,1024]{1,0:T(8,128)(2,1)S(1)} %get-tuple-element.588), channel_id=1, source_target_pairs={{0,4},{4,0},{8,12},{12,8},{16,20},{20,16},{24,28},{28,24},{1,5},{5... | collective-permute-start | bytes 884744 | tf_op jit(solution)/shard_map/cond/branch_1_fun/ppermute | solution.py:132
  136.0 31.2 %collective-permute-start.30 = (bf16[512,1024]{1,0:T(8,128)(2,1)}, bf16[512,1024]{1,0:T(8,128)(2,1)}, u32[]{:S(2)}, u32[]{:S(2)}) collective-permute-start(bf16[512,1024]{1,0:T(8,128)(2,1)} %get-tuple-element.595.refs_11_), channel_id=1, source_target_pairs={{0,8},{8,16},{16,24},{24,28},{28,20},{20,12},{12,4},{4,0},{1,9},{9... | collective-permute-start | bytes 3145736 | tf_op jit(solution)/shard_map/cond/branch_1_fun/ppermute | solution.py:65
  136.1 31.1 %collective-permute-start.31 = (bf16[512,1024]{1,0:T(8,128)(2,1)}, bf16[512,1024]{1,0:T(8,128)(2,1)}, u32[]{:S(2)}, u32[]{:S(2)}) collective-permute-start(bf16[512,1024]{1,0:T(8,128)(2,1)} %get-tuple-element.596.refs_12_), channel_id=1, source_target_pairs={{0,4},{8,0},{16,8},{24,16},{28,24},{20,28},{12,20},{4,12},{1,5},{9... | collective-permute-start | bytes 3145736 | tf_op jit(solution)/shard_map/cond/branch_1_fun/ppermute | solution.py:65
  138.1 28.2 %collective-permute-start.32 = (bf16[144,1024]{1,0:T(8,128)(2,1)S(1)}, bf16[144,1024]{1,0:T(8,128)(2,1)S(1)}, u32[]{:S(2)}, u32[]{:S(2)}) collective-permute-start(bf16[144,1024]{1,0:T(8,128)(2,1)S(1)} %get-tuple-element.602), channel_id=1, source_target_pairs={{0,8},{4,12},{8,16},{12,20},{16,24},{20,28},{1,9},{5,13},{9,17},{1... | collective-permute-start | bytes 884744 | tf_op jit(solution)/shard_map/cond/branch_1_fun/ppermute | solution.py:205
  167.2 13.4 %collective-permute-start.11 = (bf16[128,1024]{1,0:T(8,128)(2,1)}, bf16[128,1024]{1,0:T(8,128)(2,1)S(1)}, u32[]{:S(2)}, u32[]{:S(2)}) collective-permute-start(bf16[128,1024]{1,0:T(8,128)(2,1)} %get-tuple-element.632), channel_id=1, source_target_pairs={{0,16},{4,20},{8,24},{12,28},{1,17},{5,21},{9,25},{13,29},{2,18},{... | collective-permute-start | bytes 786440 | tf_op jit(solution)/shard_map/cond/branch_1_fun/ppermute | solution.py:205
  174.7 20.6 %collective-permute-start.10 = (bf16[256,1024]{1,0:T(8,128)(2,1)S(1)}, bf16[256,1024]{1,0:T(8,128)(2,1)}, u32[]{:S(2)}, u32[]{:S(2)}) collective-permute-start(bf16[256,1024]{1,0:T(8,128)(2,1)S(1)} %slice.154), channel_id=1, source_target_pairs={{0,4},{8,0},{16,8},{24,16},{28,24},{20,28},{12,20},{4,12},{1,5},{9... | collective-permute-start | bytes 1572872 | tf_op jit(solution)/shard_map/cond/branch_1_fun/ppermute | solution.py:65
  176.1 19.2 %collective-permute-start.9 = (bf16[256,1024]{1,0:T(8,128)(2,1)S(1)}, bf16[256,1024]{1,0:T(8,128)(2,1)}, u32[]{:S(2)}, u32[]{:S(2)}) collective-permute-start(bf16[256,1024]{1,0:T(8,128)(2,1)S(1)} %slice.153), channel_id=1, source_target_pairs={{0,8},{8,16},{16,24},{24,28},{28,20},{20,12},{12,4},{4,0},{1,9},{9... | collective-permute-start | bytes 1572872 | tf_op jit(solution)/shard_map/cond/branch_1_fun/ppermute | solution.py:65
  181.8 13.4 %collective-permute-start.12 = (bf16[128,1024]{1,0:T(8,128)(2,1)S(1)}, bf16[128,1024]{1,0:T(8,128)(2,1)S(1)}, u32[]{:S(2)}, u32[]{:S(2)}) collective-permute-start(bf16[128,1024]{1,0:T(8,128)(2,1)S(1)} %get-tuple-element.634), channel_id=1, source_target_pairs={{0,4},{4,0},{8,12},{12,8},{16,20},{20,16},{24,28},{28,24},{1,5},{5... | collective-permute-start | bytes 786440 | tf_op jit(solution)/shard_map/cond/branch_1_fun/ppermute | solution.py:132
  226.0 21.2 %collective-permute-start.14 = (bf16[256,1024]{1,0:T(8,128)(2,1)S(1)}, bf16[256,1024]{1,0:T(8,128)(2,1)S(1)}, u32[]{:S(2)}, u32[]{:S(2)}) collective-permute-start(bf16[256,1024]{1,0:T(8,128)(2,1)S(1)} %get-tuple-element.668), channel_id=1, source_target_pairs={{0,8},{8,16},{16,24},{24,28},{28,20},{20,12},{12,4},{4,0},{1,9},{9... | collective-permute-start | bytes 1572872 | tf_op jit(solution)/shard_map/cond/branch_1_fun/ppermute | solution.py:65
  226.7 20.6 %collective-permute-start.15 = (bf16[256,1024]{1,0:T(8,128)(2,1)S(1)}, bf16[256,1024]{1,0:T(8,128)(2,1)S(1)}, u32[]{:S(2)}, u32[]{:S(2)}) collective-permute-start(bf16[256,1024]{1,0:T(8,128)(2,1)S(1)} %get-tuple-element.669), channel_id=1, source_target_pairs={{0,4},{8,0},{16,8},{24,16},{28,24},{20,28},{12,20},{4,12},{1,5},{9... | collective-permute-start | bytes 1572872 | tf_op jit(solution)/shard_map/cond/branch_1_fun/ppermute | solution.py:65
  229.1 17.1 %collective-permute-start.13 = (bf16[144,1024]{1,0:T(8,128)(2,1)S(1)}, bf16[144,1024]{1,0:T(8,128)(2,1)S(1)}, u32[]{:S(2)}, u32[]{:S(2)}) collective-permute-start(bf16[144,1024]{1,0:T(8,128)(2,1)S(1)} %get-tuple-element.648), channel_id=1, source_target_pairs={{0,4},{4,0},{8,12},{12,8},{16,20},{20,16},{24,28},{28,24},{1,5},{5... | collective-permute-start | bytes 884744 | tf_op jit(solution)/shard_map/cond/branch_1_fun/ppermute | solution.py:132
  249.7 31.6 %collective-permute-start.34 = (bf16[512,1024]{1,0:T(8,128)(2,1)S(1)}, bf16[512,1024]{1,0:T(8,128)(2,1)}, u32[]{:S(2)}, u32[]{:S(2)}) collective-permute-start(bf16[512,1024]{1,0:T(8,128)(2,1)S(1)} %get-tuple-element.682), channel_id=1, source_target_pairs={{0,8},{8,16},{16,24},{24,28},{28,20},{20,12},{12,4},{4,0},{1,9},{9... | collective-permute-start | bytes 3145736 | tf_op jit(solution)/shard_map/cond/branch_1_fun/ppermute | solution.py:65
  249.7 31.6 %collective-permute-start.35 = (bf16[512,1024]{1,0:T(8,128)(2,1)}, bf16[512,1024]{1,0:T(8,128)(2,1)}, u32[]{:S(2)}, u32[]{:S(2)}) collective-permute-start(bf16[512,1024]{1,0:T(8,128)(2,1)} %get-tuple-element.683), channel_id=1, source_target_pairs={{0,4},{8,0},{16,8},{24,16},{28,24},{20,28},{12,20},{4,12},{1,5},{9... | collective-permute-start | bytes 3145736 | tf_op jit(solution)/shard_map/cond/branch_1_fun/ppermute | solution.py:65
  251.8 28.7 %collective-permute-start.33 = (bf16[144,1024]{1,0:T(8,128)(2,1)S(1)}, bf16[144,1024]{1,0:T(8,128)(2,1)S(1)}, u32[]{:S(2)}, u32[]{:S(2)}) collective-permute-start(bf16[144,1024]{1,0:T(8,128)(2,1)S(1)} %get-tuple-element.678), channel_id=1, source_target_pairs={{8,0},{12,4},{16,8},{20,12},{24,16},{28,20},{9,1},{13,5},{17,9},{2... | collective-permute-start | bytes 884744 | tf_op jit(solution)/shard_map/cond/branch_1_fun/ppermute | solution.py:205
  282.3 15.4 %collective-permute-start.16 = (bf16[128,1024]{1,0:T(8,128)(2,1)S(1)}, bf16[128,1024]{1,0:T(8,128)(2,1)S(1)}, u32[]{:S(2)}, u32[]{:S(2)}) collective-permute-start(bf16[128,1024]{1,0:T(8,128)(2,1)S(1)} %get-tuple-element.701), channel_id=1, source_target_pairs={{16,0},{20,4},{24,8},{28,12},{17,1},{21,5},{25,9},{29,13},{18,2},{... | collective-permute-start | bytes 786440 | tf_op jit(solution)/shard_map/cond/branch_1_fun/ppermute | solution.py:205
  309.3 41.8 %collective-permute-start.53 = (bf16[512,1024]{1,0:T(8,128)(2,1)}, bf16[512,1024]{1,0:T(8,128)(2,1)S(1)}, u32[]{:S(2)}, u32[]{:S(2)}) collective-permute-start(bf16[512,1024]{1,0:T(8,128)(2,1)} %get-tuple-element.743), channel_id=1, source_target_pairs={{0,8},{8,16},{16,24},{24,28},{28,20},{20,12},{12,4},{4,0},{1,9},{9... | collective-permute-start | bytes 3145736 | tf_op jit(solution)/shard_map/cond/branch_1_fun/ppermute | solution.py:65
  311.3 39.8 %collective-permute-start.54 = (bf16[512,1024]{1,0:T(8,128)(2,1)}, bf16[512,1024]{1,0:T(8,128)(2,1)S(1)}, u32[]{:S(2)}, u32[]{:S(2)}) collective-permute-start(bf16[512,1024]{1,0:T(8,128)(2,1)} %get-tuple-element.744), channel_id=1, source_target_pairs={{0,4},{8,0},{16,8},{24,16},{28,24},{20,28},{12,20},{4,12},{1,5},{9... | collective-permute-start | bytes 3145736 | tf_op jit(solution)/shard_map/cond/branch_1_fun/ppermute | solution.py:65
  352.9 33.9 %collective-permute-start.36 = (bf16[512,1024]{1,0:T(8,128)(2,1)S(1)}, bf16[512,1024]{1,0:T(8,128)(2,1)}, u32[]{:S(2)}, u32[]{:S(2)}) collective-permute-start(bf16[512,1024]{1,0:T(8,128)(2,1)S(1)} %get-tuple-element.769), channel_id=1, source_target_pairs={{0,8},{8,16},{16,24},{24,28},{28,20},{20,12},{12,4},{4,0},{1,9},{9... | collective-permute-start | bytes 3145736 | tf_op jit(solution)/shard_map/cond/branch_1_fun/ppermute | solution.py:65
  355.0 31.8 %collective-permute-start.37 = (bf16[512,1024]{1,0:T(8,128)(2,1)S(1)}, bf16[512,1024]{1,0:T(8,128)(2,1)}, u32[]{:S(2)}, u32[]{:S(2)}) collective-permute-start(bf16[512,1024]{1,0:T(8,128)(2,1)S(1)} %get-tuple-element.770), channel_id=1, source_target_pairs={{0,4},{8,0},{16,8},{24,16},{28,24},{20,28},{12,20},{4,12},{1,5},{9... | collective-permute-start | bytes 3145736 | tf_op jit(solution)/shard_map/cond/branch_1_fun/ppermute | solution.py:65
  355.2 31.6 %collective-permute-start.40 = (bf16[1024,512]{1,0:T(8,128)(2,1)}, bf16[1024,512]{1,0:T(8,128)(2,1)}, u32[]{:S(2)}, u32[]{:S(2)}) collective-permute-start(bf16[1024,512]{1,0:T(8,128)(2,1)} %get-tuple-element.798), channel_id=1, source_target_pairs={{0,2},{1,3},{2,0},{3,1},{4,6},{5,7},{6,4},{7,5},{8,10},{9,11},{10,... | collective-permute-start | bytes 3145736 | tf_op jit(solution)/shard_map/cond/branch_1_fun/ppermute | solution.py:132
  369.6 14.0 %collective-permute-start.38 = (bf16[128,1152]{1,0:T(8,128)(2,1)S(1)}, bf16[128,1152]{1,0:T(8,128)(2,1)S(1)}, u32[]{:S(2)}, u32[]{:S(2)}) collective-permute-start(bf16[128,1152]{1,0:T(8,128)(2,1)S(1)} %get-tuple-element.790), channel_id=1, source_target_pairs={{0,8},{8,16},{16,24},{24,28},{28,20},{20,12},{12,4},{4,0},{1,9},{9... | collective-permute-start | bytes 884744 | tf_op jit(solution)/shard_map/cond/branch_1_fun/ppermute | solution.py:65
  371.5 13.1 %collective-permute-start.39 = (bf16[128,1152]{1,0:T(8,128)(2,1)S(1)}, bf16[128,1152]{1,0:T(8,128)(2,1)S(1)}, u32[]{:S(2)}, u32[]{:S(2)}) collective-permute-start(bf16[128,1152]{1,0:T(8,128)(2,1)S(1)} %get-tuple-element.791), channel_id=1, source_target_pairs={{0,4},{8,0},{16,8},{24,16},{28,24},{20,28},{12,20},{4,12},{1,5},{9... | collective-permute-start | bytes 884744 | tf_op jit(solution)/shard_map/cond/branch_1_fun/ppermute | solution.py:65
  388.4 18.8 %collective-permute-start.17 = (bf16[256,1152]{1,0:T(8,128)(2,1)}, bf16[256,1152]{1,0:T(8,128)(2,1)}, u32[]{:S(2)}, u32[]{:S(2)}) collective-permute-start(bf16[256,1152]{1,0:T(8,128)(2,1)} %get-tuple-element.801), channel_id=1, source_target_pairs={{0,8},{8,16},{16,24},{24,28},{28,20},{20,12},{12,4},{4,0},{1,9},{9... | collective-permute-start | bytes 1769480 | tf_op jit(solution)/shard_map/cond/branch_1_fun/ppermute | solution.py:65
  390.4 16.8 %collective-permute-start.18 = (bf16[256,1152]{1,0:T(8,128)(2,1)}, bf16[256,1152]{1,0:T(8,128)(2,1)}, u32[]{:S(2)}, u32[]{:S(2)}) collective-permute-start(bf16[256,1152]{1,0:T(8,128)(2,1)} %get-tuple-element.802), channel_id=1, source_target_pairs={{0,4},{8,0},{16,8},{24,16},{28,24},{20,28},{12,20},{4,12},{1,5},{9... | collective-permute-start | bytes 1769480 | tf_op jit(solution)/shard_map/cond/branch_1_fun/ppermute | solution.py:65
  390.4 16.8 %collective-permute-start.19 = (f32[7200]{0:T(1024)S(1)}, f32[7200]{0:T(1024)S(1)}, u32[]{:S(2)}, u32[]{:S(2)}) collective-permute-start(f32[7200]{0:T(1024)S(1)} %get-tuple-element.813), channel_id=1, source_target_pairs={{0,4},{4,0},{8,12},{12,8},{16,20},{20,16},{24,28},{28,24},{1,5},{5... | collective-permute-start | bytes 86408 | tf_op jit(solution)/shard_map/cond/branch_1_fun/ppermute | solution.py:132
  391.8 15.4 %collective-permute-start.20 = (f32[1024]{0:T(1024)S(1)}, f32[1024]{0:T(1024)S(1)}, u32[]{:S(2)}, u32[]{:S(2)}) collective-permute-start(f32[1024]{0:T(1024)S(1)} %get-tuple-element.814), channel_id=1, source_target_pairs={{0,1},{1,0},{2,3},{3,2},{4,5},{5,4},{6,7},{7,6},{8,9},{9,8},{10,11... | collective-permute-start | bytes 12296 | tf_op jit(solution)/shard_map/cond/branch_1_fun/ppermute | solution.py:132
  414.0 25.7 %collective-permute-start.67 = (bf16[1024,512]{1,0:T(8,128)(2,1)}, bf16[1024,512]{1,0:T(8,128)(2,1)}, u32[]{:S(2)}, u32[]{:S(2)}) collective-permute-start(bf16[1024,512]{1,0:T(8,128)(2,1)} %get-tuple-element.850), channel_id=1, source_target_pairs={{0,2},{1,3},{2,0},{3,1},{4,6},{5,7},{6,4},{7,5},{8,10},{9,11},{10,... | collective-permute-start | bytes 3145736 | tf_op jit(solution)/shard_map/cond/branch_1_fun/ppermute | solution.py:132
  417.1 18.9 %collective-permute-start.60 = (bf16[256,1152]{1,0:T(8,128)(2,1)}, bf16[256,1152]{1,0:T(8,128)(2,1)S(1)}, u32[]{:S(2)}, u32[]{:S(2)}) collective-permute-start(bf16[256,1152]{1,0:T(8,128)(2,1)} %get-tuple-element.831), channel_id=1, source_target_pairs={{0,8},{8,16},{16,24},{24,28},{28,20},{20,12},{12,4},{4,0},{1,9},{9... | collective-permute-start | bytes 1769480 | tf_op jit(solution)/shard_map/cond/branch_1_fun/ppermute | solution.py:65
  417.2 18.9 %collective-permute-start.61 = (bf16[256,1152]{1,0:T(8,128)(2,1)}, bf16[256,1152]{1,0:T(8,128)(2,1)S(1)}, u32[]{:S(2)}, u32[]{:S(2)}) collective-permute-start(bf16[256,1152]{1,0:T(8,128)(2,1)} %get-tuple-element.832), channel_id=1, source_target_pairs={{0,4},{8,0},{16,8},{24,16},{28,24},{20,28},{12,20},{4,12},{1,5},{9... | collective-permute-start | bytes 1769480 | tf_op jit(solution)/shard_map/cond/branch_1_fun/ppermute | solution.py:65
  419.2 15.6 %collective-permute-start.59 = (f32[7200]{0:T(1024)S(1)}, f32[7200]{0:T(1024)S(1)}, u32[]{:S(2)}, u32[]{:S(2)}) collective-permute-start(f32[7200]{0:T(1024)S(1)} %add.94), channel_id=1, source_target_pairs={{0,16},{4,20},{8,24},{12,28},{16,0},{20,4},{24,8},{28,12},{1,17},{... | collective-permute-start | bytes 86408 | tf_op jit(solution)/shard_map/cond/branch_1_fun/ppermute | solution.py:132
  437.7 13.0 %collective-permute-start.62 = (bf16[256,1152]{1,0:T(8,128)(2,1)S(1)}, bf16[256,1152]{1,0:T(8,128)(2,1)S(1)}, u32[]{:S(2)}, u32[]{:S(2)}) collective-permute-start(bf16[256,1152]{1,0:T(8,128)(2,1)S(1)} %get-tuple-element.833), channel_id=1, source_target_pairs={{0,8},{8,16},{16,24},{24,28},{28,20},{20,12},{12,4},{4,0},{1,9},{9... | collective-permute-start | bytes 1769480 | tf_op jit(solution)/shard_map/cond/branch_1_fun/ppermute | solution.py:65
  438.6 12.9 %collective-permute-start.63 = (bf16[256,1152]{1,0:T(8,128)(2,1)S(1)}, bf16[256,1152]{1,0:T(8,128)(2,1)S(1)}, u32[]{:S(2)}, u32[]{:S(2)}) collective-permute-start(bf16[256,1152]{1,0:T(8,128)(2,1)S(1)} %get-tuple-element.834), channel_id=1, source_target_pairs={{0,4},{8,0},{16,8},{24,16},{28,24},{20,28},{12,20},{4,12},{1,5},{9... | collective-permute-start | bytes 1769480 | tf_op jit(solution)/shard_map/cond/branch_1_fun/ppermute | solution.py:65
  (74 other events, 893.1 us)
